TPU v7x, 128 devices: a whole 4x4x4 slice. The times are simulated.
128 devices in a mesh: gx: 16 (over x_lo, z, core), gy: 8 (over x_hi, y).
Axes of the slice: x: 4 (x_hi: 2, x_lo: 2; x = x_hi * 2 + x_lo), y: 4, z: 4, core: 2. Of those that a mesh axis runs over, the one named last changes fastest.
Arguments:
- pdf_old: float32 [16384, 19, 256], P(('gx', 'gy')), may hold values from -3 to 3
- tile_target: int32 [16384], P(('gx', 'gy')), may hold values from 0 to 16383, as said below
- porosity: float32 [256, 128, 128], P(('gx', 'gy')), may hold values from 0 to 0.6
- relaxation: float32 [256, 128, 128], P(('gx', 'gy')), may hold values from 0.6 to 1.8
- solid_mask: int32 [256, 128, 128], P('gx', 'gy'), may hold values 0 or 1
- force: float32 [3], replicated, may hold values from -0.1 to 0.1
Outputs:
- deviation_out: float32 [19, 256, 128, 128], P(None, 'gx', 'gy')
Inputs may be any that keep to these rules, and one draw needn't show every extreme that they name: tile_target holds every tile index once. The tiles of one device go to at most 2 of their number to any one device (device = tile index // 128), and in every draw some device sends exactly 2 tiles to some device.
All inputs are finite; a program needn't handle non-finite values. No bound on the sum of `solid_mask` on one device may be relied on, other than what follows from the above.
Results may differ from a plain program's by a relative error of at most 0.00023.
Values sent between devices are 32-bit elements; how exact they have to be, the bound alone decides.
No kernel may reach another device: no remote copies, remote signals or barrier semaphores. Data moves between devices by JAX's collectives and lax.ppermute only.
A program may use at most 64 MiB of HBM per device.

v0:
```python
from functools import reduce

import jax
import jax.numpy as jnp
from jax import lax
from jax.sharding import PartitionSpec as P

STEPS = 2


VELOCITY = (
    (0, 0, 0),
    (1, 0, 0),
    (-1, 0, 0),
    (0, 1, 0),
    (0, -1, 0),
    (0, 0, 1),
    (0, 0, -1),
    (1, 1, 0),
    (-1, -1, 0),
    (1, -1, 0),
    (-1, 1, 0),
    (1, 0, 1),
    (-1, 0, -1),
    (1, 0, -1),
    (-1, 0, 1),
    (0, 1, 1),
    (0, -1, -1),
    (0, 1, -1),
    (0, -1, 1),
)
OPPOSITE = [0, 2, 1, 4, 3, 6, 5, 8, 7, 10, 9, 12, 11, 14, 13, 16, 15, 18, 17]
WEIGHT_LIST = [1.0 / 3.0] + [1.0 / 18.0] * 6 + [1.0 / 36.0] * 12
MAGIC = 0.1875


def padded_2(x, sides, width):
    for axis, dim in sides:
        size, length = (lax.axis_size(axis), x.shape[dim])
        up = [(i, (i + 1) % size) for i in range(size)]
        down = [(j, i) for i, j in up]
        last = lax.slice_in_dim(x, length - width, length, axis=dim)
        initial = lax.slice_in_dim(x, 0, width, axis=dim)
        before = lax.ppermute(last, axis, up)
        after = lax.ppermute(initial, axis, down)
        x = jnp.concatenate([before, x, after], axis=dim)
    return x


def lattice_weights(ndim):
    return jnp.array(WEIGHT_LIST, jnp.float32).reshape((19,) + (1,) * (ndim - 1))


def pick(array, index_list):
    return jnp.concatenate([array[index : index + 1] for index in index_list], axis=0)


def component(dist, axis_pos):
    plus_list = [index for index in range(19) if VELOCITY[index][axis_pos] == 1]
    minus_list = [index for index in range(19) if VELOCITY[index][axis_pos] == -1]
    return reduce(lambda left, right: left + right, [dist[index] for index in plus_list]) - reduce(
        lambda left, right: left + right, [dist[index] for index in minus_list]
    )


def collide(dist, porosity, omega_plus, solid_mask, force):
    weights = lattice_weights(dist.ndim)
    density = jnp.sum(dist, axis=0)
    flow = [component(dist, axis_pos) + 0.5 * force[axis_pos] for axis_pos in range(3)]
    speed_sq = flow[0] * flow[0] + flow[1] * flow[1] + flow[2] * flow[2]
    along = jnp.stack(
        [
            VELOCITY[index][0] * flow[0]
            + VELOCITY[index][1] * flow[1]
            + VELOCITY[index][2] * flow[2]
            for index in range(19)
        ]
    )
    push = jnp.stack(
        [
            VELOCITY[index][0] * force[0]
            + VELOCITY[index][1] * force[1]
            + VELOCITY[index][2] * force[2]
            for index in range(19)
        ]
    )
    push = push.reshape((19,) + (1,) * (dist.ndim - 1))
    reversed_dist = pick(dist, OPPOSITE)
    even_part = 0.5 * (dist + reversed_dist)
    odd_part = 0.5 * (dist - reversed_dist)
    eq_even = weights * (density + 4.5 * along * along - 1.5 * speed_sq)
    eq_odd = 3.0 * weights * along
    omega_minus = 1.0 / (MAGIC / (1.0 / omega_plus - 0.5) + 0.5)
    relaxed = (
        dist
        - omega_plus * (even_part - eq_even)
        - omega_minus * (odd_part - eq_odd)
        + 3.0 * weights * push
    )
    solid = porosity + solid_mask.astype(jnp.float32) * (1.0 - porosity)
    return (1.0 - solid) * relaxed + solid * reversed_dist


def extend(post):
    return padded_2(post, (("gx", 1), ("gy", 2)), 1)


def stream(padded, block_x, block_y):
    moved = []
    for index in range(19):
        step_x, step_y, step_z = VELOCITY[index]
        window = padded[
            index, 1 - step_x : 1 - step_x + block_x, 1 - step_y : 1 - step_y + block_y, :
        ]
        moved.append(jnp.roll(window, step_z, axis=2))
    return jnp.stack(moved)


def local(pdf_old, tile_target, porosity, relaxation, solid_mask, force):
    devices_all = lax.axis_size(("gx", "gy"))
    held = pdf_old.shape[0]
    tile_cells = pdf_old.shape[2]
    capacity = 2 * held // devices_all
    slot_count = devices_all * capacity
    block_x, block_y, depth = solid_mask.shape
    tile_rows = tile_cells // depth
    poro_block, relax_block = (
        lax.all_to_all(porosity, "gy", split_axis=1, concat_axis=0, tiled=True),
        lax.all_to_all(relaxation, "gy", split_axis=1, concat_axis=0, tiled=True),
    )
    owner = tile_target // held
    slot_local = tile_target % held
    member = (owner[:, None] == jnp.arange(devices_all, dtype=jnp.int32)[None, :]).astype(jnp.int32)
    earlier = jnp.cumsum(member, axis=0) - member
    rank_in = jnp.sum(earlier * member, axis=1)
    position = owner * capacity + rank_in
    send_table = (position[:, None] == jnp.arange(slot_count, dtype=jnp.int32)[None, :]).astype(
        jnp.float32
    )
    outgoing = jnp.einsum("kp,kqc->pqc", send_table, pdf_old, precision=lax.Precision.HIGHEST)
    labels = (
        jnp.dot(slot_local.astype(jnp.float32) + 1.0, send_table, precision=lax.Precision.HIGHEST)
        - 1.0
    )
    arrived, arrived_labels = (
        lax.all_to_all(
            outgoing.reshape(devices_all, capacity, 19, tile_cells),
            ("gx", "gy"),
            split_axis=0,
            concat_axis=0,
            tiled=True,
        ),
        lax.all_to_all(
            labels.reshape(devices_all, capacity),
            ("gx", "gy"),
            split_axis=0,
            concat_axis=0,
            tiled=True,
        ),
    )
    arrived = arrived.reshape(slot_count, 19, tile_cells)
    where_to = arrived_labels.reshape(slot_count).astype(jnp.int32)
    place_table = (where_to[:, None] == jnp.arange(held, dtype=jnp.int32)[None, :]).astype(
        jnp.float32
    )
    placed = jnp.einsum("rs,rqc->qsc", place_table, arrived, precision=lax.Precision.HIGHEST)
    deviation = placed.reshape(19, block_x, block_y // tile_rows, tile_rows, depth).reshape(
        19, block_x, block_y, depth
    )
    weights = lattice_weights(4)
    dist = weights * (1.0 + deviation)
    for step_index in range(STEPS):
        relaxed = collide(dist, poro_block, relax_block, solid_mask, force)
        dist = stream(extend(relaxed), block_x, block_y)
    return dist / weights - 1.0


def solution(mesh):
    return jax.shard_map(
        local,
        mesh=mesh,
        in_specs=(
            P(("gx", "gy"), None, None),
            P(("gx", "gy")),
            P(("gx", "gy"), None, None),
            P(("gx", "gy"), None, None),
            P("gx", "gy", None),
            P(),
        ),
        out_specs=P(None, "gx", "gy", None),
        check_vma=False,
    )
```

profile of v0, /device:TPU:0, one launch (start us, length us, event | category | flops | bytes accessed | tf_op | source)
XLA Modules:
  0.0 209.6 jit_solution(13636026356029546145)
XLA Ops:
  3.6 11.1 %all-to-all-start.2 = ((f32[128,1,2]{2,1,0:T(1,128)}), f32[128,1,2]{2,1,0:T(1,128)S(1)}, u32[]{:S(2)}, u32[]{:S(2)}) async-start(f32[128,1,2]{2,1,0:T(1,128)} %bitcast.6), calls=%async_computation.2 | async-start | bytes 131072 | tf_op jit(solution)/shard_map/all_to_all | solution.py:153
  16.4 7.6 %all-to-all-done.2 = f32[128,1,2]{2,1,0:T(1,128)S(1)} async-done(((f32[128,1,2]{2,1,0:T(1,128)}), f32[128,1,2]{2,1,0:T(1,128)S(1)}, u32[]{:S(2)}, u32[]{:S(2)}) %all-to-all-start.2) | async-done | bytes 1056 | tf_op jit(solution)/shard_map/all_to_all | solution.py:153
  24.0 3.4 %all-to-all-start = ((f32[2,128,128]{2,0,1:T(2,128)}), f32[2,128,128]{2,0,1:T(2,128)S(1)}, u32[]{:S(2)}, u32[]{:S(2)}) async-start(f32[2,128,128]{2,0,1:T(2,128)} %copy.313), calls=%async_computation | async-start | bytes 262144 | tf_op jit(solution)/shard_map/all_to_all | solution.py:128
  29.0 6.3 %all-to-all-done = f32[2,128,128]{2,0,1:T(2,128)S(1)} async-done(((f32[2,128,128]{2,0,1:T(2,128)}), f32[2,128,128]{2,0,1:T(2,128)S(1)}, u32[]{:S(2)}, u32[]{:S(2)}) %all-to-all-start) | async-done | bytes 131104 | tf_op jit(solution)/shard_map/all_to_all | solution.py:128
  35.4 3.4 %all-to-all-start.3 = ((f32[2,128,128]{2,0,1:T(2,128)}), f32[2,128,128]{2,0,1:T(2,128)S(1)}, u32[]{:S(2)}, u32[]{:S(2)}) async-start(f32[2,128,128]{2,0,1:T(2,128)} %copy.320), calls=%async_computation.3 | async-start | bytes 262144 | tf_op jit(solution)/shard_map/all_to_all | solution.py:129
  38.8 4.4 %fusion.39 = f32[256,19,256]{2,0,1:T(8,128)} fusion(f32[128,19,256]{2,0,1:T(8,128)S(1)} %copy-done, s32[128]{0:T(128)S(1)} %multiply_add_fusion.11), kind=kOutput, calls=%fused_computation.244 | convolution fusion | flops 1912635392 | bytes 7471616 | tf_op jit(solution)/shard_map/kp,kqc->pqc/dot_general | solution.py:140
  43.2 7.1 %reshape.970 = f32[128,2,19,256]{3,1,0,2:T(2,128)} reshape(f32[256,19,256]{2,0,1:T(8,128)} %fusion.39) | data formatting | bytes 9961472 | tf_op jit(solution)/shard_map/reshape | solution.py:147
  50.3 6.4 %copy.315 = f32[128,2,19,256]{3,1,2,0:T(2,128)} copy(f32[128,2,19,256]{3,1,0,2:T(2,128)} %reshape.970) | data formatting | bytes 9961472 | tf_op jit(solution)/shard_map/reshape | solution.py:147
  56.6 9.3 %all-to-all-start.1 = ((f32[128,2,19,256]{3,1,2,0:T(2,128)}), f32[128,2,19,256]{3,1,2,0:T(2,128)}, u32[]{:S(2)}, u32[]{:S(2)}) async-start(f32[128,2,19,256]{3,1,2,0:T(2,128)} %copy.315), calls=%async_computation.1 | async-start | bytes 9961472 | tf_op jit(solution)/shard_map/all_to_all | solution.py:146
  80.3 47.2 %all-to-all-done.1 = f32[128,2,19,256]{3,1,2,0:T(2,128)} async-done(((f32[128,2,19,256]{3,1,2,0:T(2,128)}), f32[128,2,19,256]{3,1,2,0:T(2,128)}, u32[]{:S(2)}, u32[]{:S(2)}) %all-to-all-start.1) | async-done | bytes 4980768 | tf_op jit(solution)/shard_map/all_to_all | solution.py:146
  127.6 7.3 %copy.316 = f32[128,2,19,256]{3,1,0,2:T(2,128)} copy(f32[128,2,19,256]{3,1,2,0:T(2,128)} %all-to-all-done.1) | data formatting | bytes 9961472 | tf_op jit(solution)/shard_map/all_to_all | solution.py:146
  134.9 7.3 %reshape.971 = f32[256,19,256]{2,0,1:T(8,128)} reshape(f32[128,2,19,256]{3,1,0,2:T(2,128)} %copy.316) | data formatting | bytes 9961472 | tf_op jit(solution)/shard_map/reshape | solution.py:161
  142.2 6.6 %multiply_reduce_fusion = (f32[256,128]{1,0:T(8,128)S(1)}, f32[19,128,256]{1,2,0:T(8,128)S(1)}) fusion(f32[19]{0:T(128)S(1)} %copy-done.3, f32[256,19,256]{2,0,1:T(8,128)} %reshape.971, s32[256]{0:T(256)S(1)} %convert_element_type.26), kind=kOutput, calls=%fused_computation.23 | convolution fusion | flops 1914470400 | bytes 7603276 | tf_op jit(solution)/shard_map/rs,rqc->qsc/dot_general | solution.py:166
  148.9 2.0 copy.319
  151.0 2.4 %add.1902 = f32[19,16,16,128]{3,2,1,0:T(8,128)S(1)} reshape(f32[19,128,256]{2,1,0:T(8,128)} %copy.319) | data formatting | bytes 4980736 | tf_op jit(solution)/shard_map/add | solution.py:171
  157.0 3.8 %collective-permute-start.1 = (f32[19,1,16,128]{3,2,1,0:T(8,128)S(1)}, f32[19,1,16,128]{3,2,1,0:T(8,128)S(1)}, u32[]{:S(2)}, u32[]{:S(2)}) collective-permute-start(f32[19,1,16,128]{3,2,1,0:T(8,128)S(1)} %get-tuple-element.61), channel_id=1, source_target_pairs={{8,0},{16,8},{24,16},{32,24},{40,32},{48,40},{56,48},{64,56},{72,6... | collective-permute-start | bytes 466952 | tf_op jit(solution)/shard_map/ppermute | solution.py:45
  160.8 2.9 %collective-permute-done = f32[19,1,16,128]{3,2,1,0:T(8,128)S(1)} collective-permute-done((f32[19,1,16,128]{3,2,1,0:T(8,128)S(1)}, f32[19,1,16,128]{3,2,1,0:T(8,128)S(1)}, u32[]{:S(2)}, u32[]{:S(2)}) %collective-permute-start) | collective-permute-done | bytes 155680 | tf_op jit(solution)/shard_map/ppermute | solution.py:44
  165.2 5.3 %collective-permute-start.3 = (f32[19,18,1,128]{3,2,1,0:T(1,128)S(1)}, f32[19,18,1,128]{3,2,1,0:T(1,128)S(1)}, u32[]{:S(2)}, u32[]{:S(2)}) collective-permute-start(f32[19,18,1,128]{3,2,1,0:T(1,128)S(1)} %get-tuple-element.39), channel_id=1, source_target_pairs={{1,0},{2,1},{3,2},{4,3},{5,4},{6,5},{7,6},{0,7},{9,8},{10,9},{11,1... | collective-permute-start | bytes 525320 | tf_op jit(solution)/shard_map/ppermute | solution.py:45
  170.8 3.1 %collective-permute-done.2 = f32[19,18,1,128]{3,2,1,0:T(1,128)S(1)} collective-permute-done((f32[19,18,1,128]{3,2,1,0:T(1,128)S(1)}, f32[19,18,1,128]{3,2,1,0:T(1,128)S(1)}, u32[]{:S(2)}, u32[]{:S(2)}) %collective-permute-start.2) | collective-permute-done | bytes 175136 | tf_op jit(solution)/shard_map/ppermute | solution.py:44
  180.0 2.8 %collective-permute-start.5 = (f32[19,1,16,128]{3,2,1,0:T(8,128)S(1)}, f32[19,1,16,128]{3,2,1,0:T(8,128)S(1)}, u32[]{:S(2)}, u32[]{:S(2)}) collective-permute-start(f32[19,1,16,128]{3,2,1,0:T(8,128)S(1)} %get-tuple-element.51), channel_id=1, source_target_pairs={{8,0},{16,8},{24,16},{32,24},{40,32},{48,40},{56,48},{64,56},{72,6... | collective-permute-start | bytes 466952 | tf_op jit(solution)/shard_map/ppermute | solution.py:45
  182.8 2.7 %collective-permute-done.5 = f32[19,1,16,128]{3,2,1,0:T(8,128)S(1)} collective-permute-done((f32[19,1,16,128]{3,2,1,0:T(8,128)S(1)}, f32[19,1,16,128]{3,2,1,0:T(8,128)S(1)}, u32[]{:S(2)}, u32[]{:S(2)}) %collective-permute-start.5) | collective-permute-done | bytes 155680 | tf_op jit(solution)/shard_map/ppermute | solution.py:45
  185.5 4.0 %collective-permute-done.4 = f32[19,1,16,128]{3,2,1,0:T(8,128)S(1)} collective-permute-done((f32[19,1,16,128]{3,2,1,0:T(8,128)S(1)}, f32[19,1,16,128]{3,2,1,0:T(8,128)S(1)}, u32[]{:S(2)}, u32[]{:S(2)}) %collective-permute-start.4) | collective-permute-done | bytes 155680 | tf_op jit(solution)/shard_map/ppermute | solution.py:44
  189.8 6.0 %collective-permute-start.7 = (f32[19,18,1,128]{3,2,1,0:T(1,128)S(1)}, f32[19,18,1,128]{3,2,1,0:T(1,128)S(1)}, u32[]{:S(2)}, u32[]{:S(2)}) collective-permute-start(f32[19,18,1,128]{3,2,1,0:T(1,128)S(1)} %get-tuple-element.34), channel_id=1, source_target_pairs={{1,0},{2,1},{3,2},{4,3},{5,4},{6,5},{7,6},{0,7},{9,8},{10,9},{11,1... | collective-permute-start | bytes 525320 | tf_op jit(solution)/shard_map/ppermute | solution.py:45
  195.8 9.0 %collective-permute-done.6 = f32[19,18,1,128]{3,2,1,0:T(1,128)S(1)} collective-permute-done((f32[19,18,1,128]{3,2,1,0:T(1,128)S(1)}, f32[19,18,1,128]{3,2,1,0:T(1,128)S(1)}, u32[]{:S(2)}, u32[]{:S(2)}) %collective-permute-start.6) | collective-permute-done | bytes 175136 | tf_op jit(solution)/shard_map/ppermute | solution.py:44
  (189 shorter events, 23.8 us)
Async XLA Ops:
  0.0 38.8 %copy-start = (f32[128,19,256]{2,0,1:T(8,128)S(1)}, f32[128,19,256]{2,0,1:T(8,128)}, u32[]{:S(2)}) copy-start(f32[128,19,256]{2,0,1:T(8,128)} %param.9) | copy-start | bytes 7471108
  3.6 20.4 %all-to-all-start.2 = ((f32[128,1,2]{2,1,0:T(1,128)}), f32[128,1,2]{2,1,0:T(1,128)S(1)}, u32[]{:S(2)}, u32[]{:S(2)}) async-start(f32[128,1,2]{2,1,0:T(1,128)} %bitcast.6), calls=%async_computation.2 | async-start | bytes 131072 | tf_op jit(solution)/shard_map/all_to_all | solution.py:153
  24.0 11.4 %all-to-all-start = ((f32[2,128,128]{2,0,1:T(2,128)}), f32[2,128,128]{2,0,1:T(2,128)S(1)}, u32[]{:S(2)}, u32[]{:S(2)}) async-start(f32[2,128,128]{2,0,1:T(2,128)} %copy.313), calls=%async_computation | async-start | bytes 262144 | tf_op jit(solution)/shard_map/all_to_all | solution.py:128
  35.4 21.2 %all-to-all-start.3 = ((f32[2,128,128]{2,0,1:T(2,128)}), f32[2,128,128]{2,0,1:T(2,128)S(1)}, u32[]{:S(2)}, u32[]{:S(2)}) async-start(f32[2,128,128]{2,0,1:T(2,128)} %copy.320), calls=%async_computation.3 | async-start | bytes 262144 | tf_op jit(solution)/shard_map/all_to_all | solution.py:129
  56.6 9.3 %copy-start.4 = (f32[3]{0:T(128)S(1)}, f32[3]{0:T(128)}, u32[]{:S(2)}) copy-start(f32[3]{0:T(128)} %param.14) | copy-start | bytes 40
  56.6 23.2 %copy-start.5 = (f32[19]{0:T(128)S(1)}, f32[19]{0:T(128)}, u32[]{:S(2)}) copy-start(f32[19]{0:T(128)} %constant.68) | copy-start | bytes 232
  56.6 23.7 %copy-start.2 = (s32[16,16,128]{2,1,0:T(8,128)S(1)}, s32[16,16,128]{2,1,0:T(8,128)}, u32[]{:S(2)}) copy-start(s32[16,16,128]{2,1,0:T(8,128)} %param.13) | copy-start | bytes 393220
  56.6 70.9 %all-to-all-start.1 = ((f32[128,2,19,256]{3,1,2,0:T(2,128)}), f32[128,2,19,256]{3,1,2,0:T(2,128)}, u32[]{:S(2)}, u32[]{:S(2)}) async-start(f32[128,2,19,256]{3,1,2,0:T(2,128)} %copy.315), calls=%async_computation.1 | async-start | bytes 9961472 | tf_op jit(solution)/shard_map/all_to_all | solution.py:146
  134.9 7.3 %copy-start.3 = (f32[19]{0:T(128)S(1)}, f32[19]{0:T(128)}, u32[]{:S(2)}) copy-start(f32[19]{0:T(128)} %constant.64.clone) | copy-start | bytes 232
  156.9 6.8 %collective-permute-start = (f32[19,1,16,128]{3,2,1,0:T(8,128)S(1)}, f32[19,1,16,128]{3,2,1,0:T(8,128)S(1)}, u32[]{:S(2)}, u32[]{:S(2)}) collective-permute-start(f32[19,1,16,128]{3,2,1,0:T(8,128)S(1)} %get-tuple-element.60), channel_id=1, source_target_pairs={{0,8},{8,16},{16,24},{24,32},{32,40},{40,48},{48,56},{56,64},{64,7... | collective-permute-start | bytes 466952 | tf_op jit(solution)/shard_map/ppermute | solution.py:44
  157.0 6.8 %collective-permute-start.1 = (f32[19,1,16,128]{3,2,1,0:T(8,128)S(1)}, f32[19,1,16,128]{3,2,1,0:T(8,128)S(1)}, u32[]{:S(2)}, u32[]{:S(2)}) collective-permute-start(f32[19,1,16,128]{3,2,1,0:T(8,128)S(1)} %get-tuple-element.61), channel_id=1, source_target_pairs={{8,0},{16,8},{24,16},{32,24},{40,32},{48,40},{56,48},{64,56},{72,6... | collective-permute-start | bytes 466952 | tf_op jit(solution)/shard_map/ppermute | solution.py:45
  164.7 9.1 %collective-permute-start.2 = (f32[19,18,1,128]{3,2,1,0:T(1,128)S(1)}, f32[19,18,1,128]{3,2,1,0:T(1,128)S(1)}, u32[]{:S(2)}, u32[]{:S(2)}) collective-permute-start(f32[19,18,1,128]{3,2,1,0:T(1,128)S(1)} %get-tuple-element.38), channel_id=1, source_target_pairs={{0,1},{1,2},{2,3},{3,4},{4,5},{5,6},{6,7},{7,0},{8,9},{9,10},{10,1... | collective-permute-start | bytes 525320 | tf_op jit(solution)/shard_map/ppermute | solution.py:44
  165.2 8.7 %collective-permute-start.3 = (f32[19,18,1,128]{3,2,1,0:T(1,128)S(1)}, f32[19,18,1,128]{3,2,1,0:T(1,128)S(1)}, u32[]{:S(2)}, u32[]{:S(2)}) collective-permute-start(f32[19,18,1,128]{3,2,1,0:T(1,128)S(1)} %get-tuple-element.39), channel_id=1, source_target_pairs={{1,0},{2,1},{3,2},{4,3},{5,4},{6,5},{7,6},{0,7},{9,8},{10,9},{11,1... | collective-permute-start | bytes 525320 | tf_op jit(solution)/shard_map/ppermute | solution.py:45
  180.0 5.5 %collective-permute-start.5 = (f32[19,1,16,128]{3,2,1,0:T(8,128)S(1)}, f32[19,1,16,128]{3,2,1,0:T(8,128)S(1)}, u32[]{:S(2)}, u32[]{:S(2)}) collective-permute-start(f32[19,1,16,128]{3,2,1,0:T(8,128)S(1)} %get-tuple-element.51), channel_id=1, source_target_pairs={{8,0},{16,8},{24,16},{32,24},{40,32},{48,40},{56,48},{64,56},{72,6... | collective-permute-start | bytes 466952 | tf_op jit(solution)/shard_map/ppermute | solution.py:45
  182.8 6.8 %collective-permute-start.4 = (f32[19,1,16,128]{3,2,1,0:T(8,128)S(1)}, f32[19,1,16,128]{3,2,1,0:T(8,128)S(1)}, u32[]{:S(2)}, u32[]{:S(2)}) collective-permute-start(f32[19,1,16,128]{3,2,1,0:T(8,128)S(1)} %get-tuple-element.52), channel_id=1, source_target_pairs={{0,8},{8,16},{16,24},{24,32},{32,40},{40,48},{48,56},{56,64},{64,7... | collective-permute-start | bytes 466952 | tf_op jit(solution)/shard_map/ppermute | solution.py:44
  189.8 15.1 %collective-permute-start.7 = (f32[19,18,1,128]{3,2,1,0:T(1,128)S(1)}, f32[19,18,1,128]{3,2,1,0:T(1,128)S(1)}, u32[]{:S(2)}, u32[]{:S(2)}) collective-permute-start(f32[19,18,1,128]{3,2,1,0:T(1,128)S(1)} %get-tuple-element.34), channel_id=1, source_target_pairs={{1,0},{2,1},{3,2},{4,3},{5,4},{6,5},{7,6},{0,7},{9,8},{10,9},{11,1... | collective-permute-start | bytes 525320 | tf_op jit(solution)/shard_map/ppermute | solution.py:45
  195.8 9.1 %collective-permute-start.6 = (f32[19,18,1,128]{3,2,1,0:T(1,128)S(1)}, f32[19,18,1,128]{3,2,1,0:T(1,128)S(1)}, u32[]{:S(2)}, u32[]{:S(2)}) collective-permute-start(f32[19,18,1,128]{3,2,1,0:T(1,128)S(1)} %get-tuple-element.35), channel_id=1, source_target_pairs={{0,1},{1,2},{2,3},{3,4},{4,5},{5,6},{6,7},{7,0},{8,9},{9,10},{10,1... | collective-permute-start | bytes 525320 | tf_op jit(solution)/shard_map/ppermute | solution.py:44
  205.7 1.6 copy-start.6
  207.1 2.5 %copy-start.1 = (f32[128,19,256]{2,0,1:T(8,128)S(1)}, f32[128,19,256]{2,0,1:T(8,128)}, u32[]{:S(2)}) copy-start(f32[128,19,256]{2,0,1:T(8,128)} %param.9) | copy-start | bytes 7471108
where the time goes:
time: 211 us; the launch traced here: 210 us
  waiting for transfers between devices  82.9 us (39%)
  starting transfers between devices  45.6 us (22%)
  local copies, waits for them, and re-layouts  41.1 us (19%)
  between operations  14.3 us (7%)
  other arithmetic  13.9 us (7%)
  matrix products  11.8 us (6%)
    all_to_all x1, waiting for transfers between devices, local(): lax.all_to_all(outgoing.reshape(devices_all, capacity, 19, tile_cells), (...  47.2 us
    ppermute x4, waiting for transfers between devices, padded_2(): before = lax.ppermute(last, axis, up)  19 us
    ppermute x4, starting transfers between devices, padded_2(): after = lax.ppermute(initial, axis, down)  17.9 us
    reshape x2, local copies, waits for them, and re-layouts, local(): outgoing.reshape(devices_all, capacity, 19, tile_cells)  13.5 us
    all_to_all x1, starting transfers between devices, local(): lax.all_to_all(labels.reshape(devices_all, capacity), ('gx', 'gy'), split...  11.1 us
    all_to_all x1, starting transfers between devices, local(): lax.all_to_all(outgoing.reshape(devices_all, capacity, 19, tile_cells), (...  9.31 us
    all_to_all x1, waiting for transfers between devices, local(): lax.all_to_all(labels.reshape(devices_all, capacity), ('gx', 'gy'), split...  7.61 us
    all_to_all x1, local copies, waits for them, and re-layouts, local(): lax.all_to_all(outgoing.reshape(devices_all, capacity, 19, tile_cells), (...  7.3 us
  transfers between devices with their start and end apart: 12, of which 8 were waited for; matrix products, arithmetic and copies ran while one was open for 11% of the time, Pallas kernels for 0%

commit v1 on v0

v1 whole, which is shorter than its diff:
```python
import jax
import jax.numpy as jnp
from jax import lax
from jax.experimental import pallas as pl
from jax.experimental.pallas import tpu as pltpu
from jax.sharding import PartitionSpec as P

VELOCITY = (
    (0, 0, 0),
    (1, 0, 0),
    (-1, 0, 0),
    (0, 1, 0),
    (0, -1, 0),
    (0, 0, 1),
    (0, 0, -1),
    (1, 1, 0),
    (-1, -1, 0),
    (1, -1, 0),
    (-1, 1, 0),
    (1, 0, 1),
    (-1, 0, -1),
    (1, 0, -1),
    (-1, 0, 1),
    (0, 1, 1),
    (0, -1, -1),
    (0, 1, -1),
    (0, -1, 1),
)
WEIGHT = [1.0 / 3.0] + [1.0 / 18.0] * 6 + [1.0 / 36.0] * 12
INVERSE = [3.0] + [18.0] * 6 + [36.0] * 12
DEVICES = 128
HELD = 128
CAP = 2
ROWS = 40
EXT = 20
VMEM_LIMIT = 48 * 1024 * 1024
F32 = jnp.float32


def entries(axis, sign):
    far = [(q, 1) for q in range(19) if VELOCITY[q][axis] == sign]
    near = [(q, 0) for q in range(19) if VELOCITY[q][axis] in (0, sign)]
    return far + near


COUNT = 21


def collide(dist, solid, omega, force):
    plus = [None] * 19
    minus = [None] * 19
    for i in range(1, 19, 2):
        plus[i] = dist[i] + dist[i + 1]
        minus[i] = dist[i] - dist[i + 1]
    density = dist[0]
    for i in range(1, 19, 2):
        density = density + plus[i]
    flow = []
    for axis in range(3):
        total = None
        for i in range(1, 19, 2):
            c = VELOCITY[i][axis]
            if c:
                if total is None:
                    total = minus[i]
                else:
                    total = total + minus[i] if c == 1 else total - minus[i]
        flow.append(total + 0.5 * force[axis])
    base = density - 1.5 * (flow[0] * flow[0] + flow[1] * flow[1] + flow[2] * flow[2])
    open_ = 1.0 - solid
    a = open_ * omega
    b = open_ * ((2.0 - omega) / (1.0 - 0.125 * omega))
    keep = 0.5 - 0.5 * a
    turn = 0.5 - solid - 0.5 * b
    post = [None] * 19
    at = a * base
    post[0] = (keep + keep) * dist[0] + at * (1.0 / 3.0)
    drive = [b * flow[axis] + open_ * force[axis] for axis in range(3)]
    for group, w in ((range(1, 7, 2), 1.0 / 18.0), (range(7, 19, 2), 1.0 / 36.0)):
        even_base = at * w
        square = a * (4.5 * w)
        pull = [drive[axis] * (3.0 * w) for axis in range(3)]
        for i in group:
            along = None
            odd = None
            for axis in range(3):
                c = VELOCITY[i][axis]
                if c:
                    if along is None:
                        along, odd = flow[axis], pull[axis]
                    elif c == 1:
                        along, odd = along + flow[axis], odd + pull[axis]
                    else:
                        along, odd = along - flow[axis], odd - pull[axis]
            even = keep * plus[i] + (even_base + square * (along * along))
            odd = turn * minus[i] + odd
            post[i] = even + odd
            post[i + 1] = even - odd
    return post


def shift_z(value, q):
    c = VELOCITY[q][2]
    return value if c == 0 else pltpu.roll(value, c % 128, 1)


def pack_kernel(target, pdf, out, used):
    def clear(i, _):
        used[i] = 0
        return 0

    lax.fori_loop(0, DEVICES, clear, 0, unroll=8)
    empty = jnp.full((1, 128), -1.0, F32)

    def blank(i, _):
        out[pl.ds(i * ROWS + 38, 1), :] = empty
        return 0

    lax.fori_loop(0, DEVICES * CAP, blank, 0, unroll=8)

    def place(group, _):
        near = pdf.at[:, pl.ds(pl.multiple_of(group * 8, 8), 8), :]
        for i in range(8):
            t = target[group * 8 + i]
            owner = lax.shift_right_logical(t, 7)
            rank = used[owner]
            used[owner] = rank + 1
            start = (owner * CAP + rank) * ROWS
            for q in range(19):
                for r in range(2):
                    value = near[q, i : i + 1, r * 128 : (r + 1) * 128]
                    out[pl.ds(start + 2 * q + r, 1), :] = value
            out[pl.ds(start + 38, 1), :] = jnp.full((1, 128), (t & 127).astype(F32), F32)
        return 0

    lax.fori_loop(0, HELD // 8, place, 0)


def pack(target, pdf):
    return pl.pallas_call(
        pack_kernel,
        out_shape=jax.ShapeDtypeStruct((DEVICES * CAP * ROWS, 128), F32),
        in_specs=[
            pl.BlockSpec(memory_space=pltpu.SMEM),
            pl.BlockSpec(memory_space=pltpu.VMEM),
        ],
        out_specs=pl.BlockSpec(memory_space=pltpu.VMEM),
        scratch_shapes=[pltpu.SMEM((DEVICES,), jnp.int32)],
        compiler_params=pltpu.CompilerParams(vmem_limit_bytes=VMEM_LIMIT),
        cost_estimate=pl.CostEstimate(flops=0, bytes_accessed=8_000_000, transcendentals=0),
    )(target, pdf)


def first_kernel(source, force, arrived, coef, post, xup, xdn, yup, ydn, tiles, sems):
    def fetch(s, _):
        p = source[s]
        pltpu.make_async_copy(
            arrived.at[pl.ds(pl.multiple_of(p * ROWS, 8), ROWS), :],
            tiles.at[pl.ds(pl.multiple_of(s * ROWS, 8), ROWS), :],
            sems.at[lax.shift_right_logical(s, 3)],
        ).start()
        return 0

    lax.fori_loop(0, HELD, fetch, 0, unroll=4)
    f = [force[axis] for axis in range(3)]

    def plane(x, _):
        whole = pl.ds(pl.multiple_of(x * (8 * ROWS), 8), 8 * ROWS)
        pltpu.make_async_copy(
            arrived.at[pl.ds(0, 8 * ROWS), :], tiles.at[whole, :], sems.at[x]
        ).wait()
        for r in range(2):
            dist = []
            for q in range(19):
                value = tiles[pl.ds(x * (8 * ROWS) + 2 * q + r, 8, stride=ROWS), :]
                dist.append(WEIGHT[q] * value + WEIGHT[q])
            solid = coef[0, x, pl.ds(r, 8, stride=2), :]
            omega = coef[1, x, pl.ds(r, 8, stride=2), :]
            after = collide(dist, solid, omega, f)
            for q in range(19):
                post[q, x, pl.ds(r, 8, stride=2), :] = shift_z(after[q], q)
        return 0

    lax.fori_loop(0, 16, plane, 0)
    for out, sign in ((xup, 1), (xdn, -1)):
        for i, (q, layer) in enumerate(entries(0, sign)):
            out[i] = post[q, 15 - layer if sign == 1 else layer]
        for j in range(2):
            out[19 + j] = coef[j, 15 if sign == 1 else 0]
    for out, sign in ((yup, 1), (ydn, -1)):
        for i, (q, layer) in enumerate(entries(1, sign)):
            row = 15 - layer if sign == 1 else layer
            for x in range(16):
                out[i, x : x + 1, :] = post[q, x, row : row + 1, :]
        row = 15 if sign == 1 else 0
        for j in range(2):
            for x in range(16):
                out[19 + j, x : x + 1, :] = coef[j, x, row : row + 1, :]


def first(source, force, arrived, coef):
    face = jax.ShapeDtypeStruct((COUNT, 16, 128), F32)
    vmem = pl.BlockSpec(memory_space=pltpu.VMEM)
    smem = pl.BlockSpec(memory_space=pltpu.SMEM)
    return pl.pallas_call(
        first_kernel,
        out_shape=[jax.ShapeDtypeStruct((19, 16, 16, 128), F32)] + [face] * 4,
        in_specs=[smem, smem, pl.BlockSpec(memory_space=pl.ANY), vmem],
        out_specs=[vmem] * 5,
        scratch_shapes=[
            pltpu.VMEM((HELD * ROWS, 128), F32),
            pltpu.SemaphoreType.DMA((16,)),
        ],
        compiler_params=pltpu.CompilerParams(vmem_limit_bytes=VMEM_LIMIT),
        cost_estimate=pl.CostEstimate(flops=10_000_000, bytes_accessed=8_000_000, transcendentals=0),
    )(source, force, arrived, coef)


def join_kernel(left, right, yup, ydn, up, dn):
    zero = jnp.zeros((1, 128), F32)
    for own, out, sign in ((yup, up, 1), (ydn, dn, -1)):
        listed = entries(1, sign) + [(19, 0), (20, 0)]
        for i, (q, layer) in enumerate(listed):
            row = 15 - layer if sign == 1 else layer
            out[i * EXT + 2 : i * EXT + 18, :] = own[i]
            for half, toward in ((left, 1), (right, -1)):
                have = {e: n for n, e in enumerate(entries(0, toward) + [(19, 0), (20, 0)])}
                for deep in range(2):
                    at = (1 - deep) if toward == 1 else 18 + deep
                    n = have.get((q, deep))
                    value = zero if n is None else half[n, row : row + 1, :]
                    out[i * EXT + at : i * EXT + at + 1, :] = value
    for out in (up, dn):
        out[COUNT * EXT : COUNT * EXT + 4, :] = jnp.zeros((4, 128), F32)


def join(left, right, yup, ydn):
    side = jax.ShapeDtypeStruct((COUNT * EXT + 4, 128), F32)
    vmem = pl.BlockSpec(memory_space=pltpu.VMEM)
    return pl.pallas_call(
        join_kernel,
        out_shape=[side] * 2,
        in_specs=[vmem] * 4,
        out_specs=[vmem] * 2,
        compiler_params=pltpu.CompilerParams(vmem_limit_bytes=VMEM_LIMIT),
        cost_estimate=pl.CostEstimate(flops=0, bytes_accessed=1_000_000, transcendentals=0),
    )(left, right, yup, ydn)


def second_kernel(force, post, coef, left, right, below, above, out, wide, wcoef, again, sem):
    own = pltpu.make_async_copy(post, wide.at[:, pl.ds(2, 16), pl.ds(8, 16), :], sem)
    own.start()
    for x in range(16):
        for j in range(2):
            wcoef[j, x + 1, 8:24, :] = coef[j, x]
    for half, sign in ((left, 1), (right, -1)):
        for i, (q, layer) in enumerate(entries(0, sign)):
            wide[q, 1 - layer if sign == 1 else 18 + layer, 8:24, :] = half[i]
        for j in range(2):
            wcoef[j, 0 if sign == 1 else 17, 8:24, :] = half[19 + j]
    for half, sign in ((below, 1), (above, -1)):
        for i, (q, layer) in enumerate(entries(1, sign)):
            row = 7 - layer if sign == 1 else 24 + layer
            for x in range(EXT):
                wide[q, x, row : row + 1, :] = half[i * EXT + x : i * EXT + x + 1, :]
        row = 7 if sign == 1 else 24
        for j in range(2):
            for x in range(18):
                at = (19 + j) * EXT + x + 1
                wcoef[j, x, row : row + 1, :] = half[at : at + 1, :]
    f = [force[axis] for axis in range(3)]
    own.wait()

    def plane(x, _):
        for block in range(3):
            dist = []
            for q in range(19):
                cx, cy, _z = VELOCITY[q]
                dist.append(wide[q, x + 1 - cx, 7 + 8 * block - cy : 15 + 8 * block - cy, :])
            rows = slice(7 + 8 * block, 15 + 8 * block)
            after = collide(dist, wcoef[0, x, rows, :], wcoef[1, x, rows, :], f)
            for q in range(19):
                again[q, x, 8 * block : 8 * block + 8, :] = shift_z(after[q], q)
        return 0

    lax.fori_loop(0, 18, plane, 0)

    def finish(x, _):
        for q in range(19):
            cx, cy, _z = VELOCITY[q]
            for block in range(2):
                start = 8 * block + 1 - cy
                value = again[q, x + 1 - cx, start : start + 8, :]
                out[q, x, 8 * block : 8 * block + 8, :] = value * INVERSE[q] - 1.0
        return 0

    lax.fori_loop(0, 16, finish, 0)


def second(force, post, coef, left, right, below, above):
    vmem = pl.BlockSpec(memory_space=pltpu.VMEM)
    smem = pl.BlockSpec(memory_space=pltpu.SMEM)
    return pl.pallas_call(
        second_kernel,
        out_shape=jax.ShapeDtypeStruct((19, 16, 16, 128), F32),
        in_specs=[smem, pl.BlockSpec(memory_space=pl.ANY)] + [vmem] * 5,
        out_specs=vmem,
        scratch_shapes=[
            pltpu.VMEM((19, EXT, 32, 128), F32),
            pltpu.VMEM((2, 18, 32, 128), F32),
            pltpu.VMEM((19, 18, 24, 128), F32),
            pltpu.SemaphoreType.DMA,
        ],
        compiler_params=pltpu.CompilerParams(vmem_limit_bytes=VMEM_LIMIT),
        cost_estimate=pl.CostEstimate(flops=10_000_000, bytes_accessed=8_000_000, transcendentals=0),
    )(force, post, coef, left, right, below, above)


def ring(axis, step):
    n = lax.axis_size(axis)
    return [(i, (i + step) % n) for i in range(n)]


def blocks_of(porosity, relaxation):
    b = lax.axis_index("gy")
    hi, lo = b // 4, b % 4
    slab = jnp.stack([porosity, relaxation]).reshape(2, 2, 8, 16, 128)
    other = lax.dynamic_slice_in_dim(slab, (1 - hi) * 4, 4, axis=2)
    mine = lax.dynamic_slice_in_dim(slab, hi * 4, 4, axis=2)
    came = lax.ppermute(other, "gy", [(i, i ^ 4) for i in range(8)])
    first_ = jnp.where(hi == 0, mine, came)
    last = jnp.where(hi == 0, came, mine)
    both = jnp.stack([first_, last])
    parts = [lax.dynamic_index_in_dim(both, lo, axis=3, keepdims=False)]
    for k in range(1, 4):
        message = lax.dynamic_index_in_dim(both, (lo + k) % 4, axis=3, keepdims=False)
        pairs = [(i, (i // 4) * 4 + (i % 4 + k) % 4) for i in range(8)]
        parts.append(lax.ppermute(message, "gy", pairs))
    stacked = jnp.stack(parts)
    ordered = [
        lax.dynamic_index_in_dim(stacked, (lo - y + 4) % 4, axis=0, keepdims=False)
        for y in range(4)
    ]
    whole = jnp.stack(ordered)
    return whole.transpose(2, 1, 0, 3, 4, 5).reshape(2, 16, 16, 128)


def local(pdf_old, tile_target, porosity, relaxation, solid_mask, force):
    packed = pack(tile_target, pdf_old.transpose(1, 0, 2))
    arrived = lax.all_to_all(
        packed.reshape(DEVICES, CAP * ROWS, 128),
        ("gx", "gy"),
        split_axis=0,
        concat_axis=0,
        tiled=True,
    ).reshape(DEVICES * CAP * ROWS, 128)
    block = blocks_of(porosity, relaxation)
    solid = block[0] + solid_mask.astype(F32) * (1.0 - block[0])
    coef = jnp.stack([solid, block[1]])
    label = arrived.reshape(DEVICES * CAP, ROWS, 128)[:, 38, 0]
    hit = label[:, None] == jnp.arange(HELD, dtype=F32)[None, :]
    number = jnp.arange(DEVICES * CAP, dtype=jnp.int32)[:, None]
    source = jnp.sum(jnp.where(hit, number, 0), axis=0)
    post, xup, xdn, yup, ydn = first(source, force, arrived, coef)
    left = lax.ppermute(xup, "gx", ring("gx", 1))
    right = lax.ppermute(xdn, "gx", ring("gx", -1))
    up, dn = join(left, right, yup, ydn)
    below = lax.ppermute(up, "gy", ring("gy", 1))
    above = lax.ppermute(dn, "gy", ring("gy", -1))
    return second(force, post, coef, left, right, below, above)


def solution(mesh):
    return jax.shard_map(
        local,
        mesh=mesh,
        in_specs=(
            P(("gx", "gy"), None, None),
            P(("gx", "gy")),
            P(("gx", "gy"), None, None),
            P(("gx", "gy"), None, None),
            P("gx", "gy", None),
            P(),
        ),
        out_specs=P(None, "gx", "gy", None),
        check_vma=False,
    )
```

time: 211 us -> 121 us (0.57)
  local copies, waits for them, and re-layouts: 41.1 us -> 4.7 us
  starting transfers between devices: 45.6 us -> 28.2 us
  Pallas kernels: 0 us -> 15.2 us
  between operations: 14.3 us -> 0.19 us
  other arithmetic: 13.9 us -> 0.27 us
  matrix products: 11.8 us -> 0 us
  waiting for transfers between devices: 82.9 us -> 71.9 us
    all_to_all x4 -> x1, waiting for transfers between devices: 61.2 us -> 0.01 us  [local(): lax.all_to_all(packed.reshape(DEVICES, CAP * ROWS, 128), ('gx', 'gy'), sp...]
    ppermute x8, waiting for transfers between devices: 21.7 us -> 71.9 us  [the longest x1 58.8 us: blocks_of(): came = lax.ppermute(other, 'gy', [(i, i ^ 4) for i in range(8)])]
    reshape x3 -> x0, local copies, waits for them, and re-layouts: 20.8 us -> none  [the longest x2 13.5 us: local(): outgoing.reshape(devices_all, capacity, 19, tile_cells)]
    all_to_all x4 -> x1, starting transfers between devices: 27.2 us -> 11.6 us  [local(): lax.all_to_all(packed.reshape(DEVICES, CAP * ROWS, 128), ('gx', 'gy'), sp...]
    pallas_call x0 -> x4, Pallas kernels: none -> 15.2 us  [the longest x1 5.86 us: second(): pl.pallas_call(second_kernel, out_shape=jax.ShapeDtypeStruct((19, 16, 16,...]
    dot_general x3 -> x0, matrix products: 11.8 us -> none  [the longest x1 6.62 us: local(): jnp.einsum('rs,rqc->qsc', place_table, arrived, precision=lax.Precision.H...]
    all_to_all x4 -> x0, local copies, waits for them, and re-layouts: 8.16 us -> none  [the longest x1 7.3 us: local(): lax.all_to_all(outgoing.reshape(devices_all, capacity, 19, tile_cells), (...]
    add x4 -> x1, other arithmetic: 5 us -> 0.02 us  [local(): solid = block[0] + solid_mask.astype(F32) * (1.0 - block[0])]
  transfers between devices with their start and end apart: 12 -> 9, of which waited for: 8 -> 6; matrix products, arithmetic and copies ran while one was open for 11% -> 0% of each run, Pallas kernels for 0% -> 0%
where the time goes in v1:
time: 121 us; the launch traced here: 120 us
  waiting for transfers between devices  71.9 us (59%)
  starting transfers between devices  28.2 us (23%)
  Pallas kernels  15.2 us (13%)
  local copies, waits for them, and re-layouts  4.7 us (4%)
    ppermute x1, waiting for transfers between devices, blocks_of(): came = lax.ppermute(other, 'gy', [(i, i ^ 4) for i in range(8)])  58.8 us
    all_to_all x1, starting transfers between devices, local(): lax.all_to_all(packed.reshape(DEVICES, CAP * ROWS, 128), ('gx', 'gy'), sp...  11.6 us
    pallas_call x1, Pallas kernels, second(): pl.pallas_call(second_kernel, out_shape=jax.ShapeDtypeStruct((19, 16, 16,...  5.86 us
    ppermute x1, starting transfers between devices, local(): above = lax.ppermute(dn, 'gy', ring('gy', -1))  5.63 us
    ppermute x1, waiting for transfers between devices, local(): below = lax.ppermute(up, 'gy', ring('gy', 1))  5.25 us
    pallas_call x1, Pallas kernels, pack(): pl.pallas_call(pack_kernel, out_shape=jax.ShapeDtypeStruct((DEVICES * CAP...  5.15 us
    ppermute x3, waiting for transfers between devices, blocks_of(): parts.append(lax.ppermute(message, 'gy', pairs))  4.81 us
    ppermute x3, starting transfers between devices, blocks_of(): parts.append(lax.ppermute(message, 'gy', pairs))  4.47 us
  transfers between devices with their start and end apart: 9, of which 6 were waited for; matrix products, arithmetic and copies ran while one was open for 0% of the time, Pallas kernels for 0%

profile of v1, /device:TPU:0, one launch (start us, length us, event | category | flops | bytes accessed | tf_op | source)
XLA Modules:
  0.0 120.5 jit_solution(10057684181750022392)
XLA Ops:
  0.0 1.7 %copy-done = f32[128,19,256]{2,0,1:T(8,128)S(1)} copy-done((f32[128,19,256]{2,0,1:T(8,128)S(1)}, f32[128,19,256]{2,0,1:T(8,128)}, u32[]{:S(2)}) %copy-start) | copy-done | bytes 2490392
  1.7 0.7 copy-done.2
  2.4 5.1 %shard_map.64 = f32[10240,128]{1,0:T(8,128)} custom-call(s32[128]{0:T(128)S(1)} %copy-done.2, f32[19,128,256]{2,1,0:T(8,128)S(1)} %bitcast.36), custom_call_target="tpu_custom_call" | custom-call | bytes 8000000 | tf_op jit(solution)/shard_map/pallas_call | solution.py:140
  7.5 11.6 %all-to-all-start = ((f32[128,80,128]{2,1,0:T(8,128)}), f32[128,80,128]{2,1,0:T(8,128)}, u32[]{:S(2)}, u32[]{:S(2)}) async-start(f32[128,80,128]{2,1,0:T(8,128)} %bitcast.37), calls=%async_computation | async-start | bytes 10485760 | tf_op jit(solution)/shard_map/all_to_all | solution.py:350
  19.1 0.0 copy-start.1
  19.2 2.5 %collective-permute-start = (f32[2,2,4,16,128]{4,3,2,1,0:T(8,128)S(1)}, f32[2,2,4,16,128]{4,3,2,1,0:T(8,128)S(1)}, u32[]{:S(2)}, u32[]{:S(2)}) collective-permute-start(f32[2,2,4,16,128]{4,3,2,1,0:T(8,128)S(1)} %fusion), channel_id=1, source_target_pairs={{0,4},{1,5},{2,6},{3,7},{4,0},{5,1},{6,2},{7,3},{8,12},{9,13},{10,... | collective-permute-start | bytes 393224 | tf_op jit(solution)/shard_map/ppermute | solution.py:330
  21.7 58.8 %collective-permute-done = f32[2,2,4,16,128]{4,3,2,1,0:T(8,128)S(1)} collective-permute-done((f32[2,2,4,16,128]{4,3,2,1,0:T(8,128)S(1)}, f32[2,2,4,16,128]{4,3,2,1,0:T(8,128)S(1)}, u32[]{:S(2)}, u32[]{:S(2)}) %collective-permute-start) | collective-permute-done | bytes 131104 | tf_op jit(solution)/shard_map/ppermute | solution.py:330
  80.5 2.8 %collective-permute-start.3 = (f32[2,2,2,16,128]{4,3,2,0,1:T(8,128)S(1)}, f32[2,2,2,16,128]{4,3,2,0,1:T(8,128)S(1)}, u32[]{:S(2)}, u32[]{:S(2)}) collective-permute-start(f32[2,2,2,16,128]{4,3,2,0,1:T(8,128)S(1)} %bitcast.45), channel_id=1, source_target_pairs={{0,3},{1,0},{2,1},{3,2},{4,7},{5,4},{6,5},{7,6},{8,11},{9,8},{10,9... | collective-permute-start | bytes 196616 | tf_op jit(solution)/shard_map/ppermute | solution.py:338
  83.4 0.8 collective-permute-start.2
  84.2 0.8 collective-permute-start.1
  85.0 0.4 collective-permute-done.3
  85.5 3.7 %collective-permute-done.2 = f32[2,2,2,16,128]{4,3,2,0,1:T(8,128)S(1)} collective-permute-done((f32[2,2,2,16,128]{4,3,2,0,1:T(8,128)S(1)}, f32[2,2,2,16,128]{4,3,2,0,1:T(8,128)S(1)}, u32[]{:S(2)}, u32[]{:S(2)}) %collective-permute-start.2) | collective-permute-done | bytes 65568 | tf_op jit(solution)/shard_map/ppermute | solution.py:338
  89.2 0.7 collective-permute-done.1
  90.0 2.3 %slice_reduce_fusion = f32[256]{0:T(256)S(1)} fusion(f32[256,40,128]{2,1,0:T(8,128)} %bitcast.2), kind=kLoop, calls=%fused_computation.17 | loop fusion | bytes 2048 | tf_op jit(solution)/shard_map/slice | solution.py:360
  92.3 0.1 select_reduce_fusion.source
  92.4 4.1 %shard_map.65 = (f32[19,16,16,128]{3,2,1,0:T(8,128)S(1)}, f32[21,16,128]{2,1,0:T(8,128)S(1)}, f32[21,16,128]{2,1,0:T(8,128)S(1)}, f32[21,16,128]{2,1,0:T(8,128)S(1)}, f32[21,16,128]{2,1,0:T(8,128)S(1)}) custom-call(s32[128]{0:T(128)S(1)} %select_reduce_fusion.source, f32[3]{0:T(128)S(1)} %copy-done.1, f32[10240,128]{1,0:T(8,128)} %bitcast.3.arrived, ...), custom_call_target="tpu_custom_call" | custom-call | flops 10000000 | bytes 8000000 | tf_op jit(solution)/shard_map/pallas_call | solution.py:205
  96.5 0.1 collective-permute-start.4
  96.6 3.8 %collective-permute-start.5 = (f32[21,16,128]{2,1,0:T(8,128)S(1)}, f32[21,16,128]{2,1,0:T(8,128)S(1)}, u32[]{:S(2)}, u32[]{:S(2)}) collective-permute-start(f32[21,16,128]{2,1,0:T(8,128)S(1)} %get-tuple-element.14), channel_id=1, source_target_pairs={{0,120},{8,0},{16,8},{24,16},{32,24},{40,32},{48,40},{56,48},{64,5... | collective-permute-start | bytes 516104 | tf_op jit(solution)/shard_map/ppermute | solution.py:366
  100.5 3.1 %collective-permute-done.4.left = f32[21,16,128]{2,1,0:T(8,128)S(1)} collective-permute-done((f32[21,16,128]{2,1,0:T(8,128)S(1)}, f32[21,16,128]{2,1,0:T(8,128)S(1)}, u32[]{:S(2)}, u32[]{:S(2)}) %collective-permute-start.4) | collective-permute-done | bytes 172064 | tf_op jit(solution)/shard_map/ppermute | solution.py:365
  103.5 0.1 shard_map.66
  103.6 0.1 collective-permute-start.6
  103.7 5.6 %collective-permute-start.7 = (f32[424,128]{1,0:T(8,128)S(1)}, f32[424,128]{1,0:T(8,128)S(1)}, u32[]{:S(2)}, u32[]{:S(2)}) collective-permute-start(f32[424,128]{1,0:T(8,128)S(1)} %get-tuple-element.18), channel_id=1, source_target_pairs={{0,7},{1,0},{2,1},{3,2},{4,3},{5,4},{6,5},{7,6},{8,15},{9,8},{10,9... | collective-permute-start | bytes 651272 | tf_op jit(solution)/shard_map/ppermute | solution.py:369
  109.3 5.3 %collective-permute-done.6.below = f32[424,128]{1,0:T(8,128)S(1)} collective-permute-done((f32[424,128]{1,0:T(8,128)S(1)}, f32[424,128]{1,0:T(8,128)S(1)}, u32[]{:S(2)}, u32[]{:S(2)}) %collective-permute-start.6) | collective-permute-done | bytes 217120 | tf_op jit(solution)/shard_map/ppermute | solution.py:368
  114.6 5.9 %shard_map.67 = f32[19,16,16,128]{3,2,1,0:T(8,128)} custom-call(f32[3]{0:T(128)S(1)} %copy-done.1, f32[19,16,16,128]{3,2,1,0:T(8,128)S(1)} %get-tuple-element.12.post, f32[2,16,16,128]{3,2,1,0:T(8,128)S(1)} %pad_maximum_fusion.1.coef, f32[21,16,128]{2,1,0:T(8,128)S(1)} %collective-permute-done.4.left, f32[21,16,128]{2,1,0:T(8,128)S(1)} %collective-permute-done.5.right, ...), custom_call_target="tpu_custom_call" | custom-call | flops 10000000 | bytes 8000000 | tf_op jit(solution)/shard_map/pallas_call | solution.py:303
  (25 shorter events, 0.2 us)
Async XLA Ops:
  0.0 1.7 %copy-start = (f32[128,19,256]{2,0,1:T(8,128)S(1)}, f32[128,19,256]{2,0,1:T(8,128)}, u32[]{:S(2)}) copy-start(f32[128,19,256]{2,0,1:T(8,128)} %param.6) | copy-start | bytes 7471108
  1.7 0.7 copy-start.2
  7.5 11.7 %copy-start.3 = (f32[2,128,128]{2,1,0:T(8,128)S(1)}, f32[2,128,128]{2,1,0:T(8,128)}, u32[]{:S(2)}) copy-start(f32[2,128,128]{2,1,0:T(8,128)} %param.8) | copy-start | bytes 393220
  7.5 11.7 %copy-start.4 = (f32[2,128,128]{2,1,0:T(8,128)S(1)}, f32[2,128,128]{2,1,0:T(8,128)}, u32[]{:S(2)}) copy-start(f32[2,128,128]{2,1,0:T(8,128)} %param.9) | copy-start | bytes 393220
  7.5 82.4 %copy-start.5 = (s32[16,16,128]{2,1,0:T(8,128)S(1)}, s32[16,16,128]{2,1,0:T(8,128)}, u32[]{:S(2)}) copy-start(s32[16,16,128]{2,1,0:T(8,128)} %param.10) | copy-start | bytes 393220
  7.5 82.5 %all-to-all-start = ((f32[128,80,128]{2,1,0:T(8,128)}), f32[128,80,128]{2,1,0:T(8,128)}, u32[]{:S(2)}, u32[]{:S(2)}) async-start(f32[128,80,128]{2,1,0:T(8,128)} %bitcast.37), calls=%async_computation | async-start | bytes 10485760 | tf_op jit(solution)/shard_map/all_to_all | solution.py:350
  19.1 73.3 %copy-start.1 = (f32[3]{0:T(128)S(1)}, f32[3]{0:T(128)}, u32[]{:S(2)}) copy-start(f32[3]{0:T(128)} %force.3) | copy-start | bytes 40
  19.2 61.2 %collective-permute-start = (f32[2,2,4,16,128]{4,3,2,1,0:T(8,128)S(1)}, f32[2,2,4,16,128]{4,3,2,1,0:T(8,128)S(1)}, u32[]{:S(2)}, u32[]{:S(2)}) collective-permute-start(f32[2,2,4,16,128]{4,3,2,1,0:T(8,128)S(1)} %fusion), channel_id=1, source_target_pairs={{0,4},{1,5},{2,6},{3,7},{4,0},{5,1},{6,2},{7,3},{8,12},{9,13},{10,... | collective-permute-start | bytes 393224 | tf_op jit(solution)/shard_map/ppermute | solution.py:330
  80.5 4.9 %collective-permute-start.3 = (f32[2,2,2,16,128]{4,3,2,0,1:T(8,128)S(1)}, f32[2,2,2,16,128]{4,3,2,0,1:T(8,128)S(1)}, u32[]{:S(2)}, u32[]{:S(2)}) collective-permute-start(f32[2,2,2,16,128]{4,3,2,0,1:T(8,128)S(1)} %bitcast.45), channel_id=1, source_target_pairs={{0,3},{1,0},{2,1},{3,2},{4,7},{5,4},{6,5},{7,6},{8,11},{9,8},{10,9... | collective-permute-start | bytes 196616 | tf_op jit(solution)/shard_map/ppermute | solution.py:338
  83.4 5.8 %collective-permute-start.2 = (f32[2,2,2,16,128]{4,3,2,0,1:T(8,128)S(1)}, f32[2,2,2,16,128]{4,3,2,0,1:T(8,128)S(1)}, u32[]{:S(2)}, u32[]{:S(2)}) collective-permute-start(f32[2,2,2,16,128]{4,3,2,0,1:T(8,128)S(1)} %bitcast.46), channel_id=1, source_target_pairs={{0,2},{1,3},{2,0},{3,1},{4,6},{5,7},{6,4},{7,5},{8,10},{9,11},{10,... | collective-permute-start | bytes 196616 | tf_op jit(solution)/shard_map/ppermute | solution.py:338
  84.2 5.6 %collective-permute-start.1 = (f32[2,2,2,16,128]{4,3,2,0,1:T(8,128)S(1)}, f32[2,2,2,16,128]{4,3,2,0,1:T(8,128)S(1)}, u32[]{:S(2)}, u32[]{:S(2)}) collective-permute-start(f32[2,2,2,16,128]{4,3,2,0,1:T(8,128)S(1)} %bitcast.47), channel_id=1, source_target_pairs={{0,1},{1,2},{2,3},{3,0},{4,5},{5,6},{6,7},{7,4},{8,9},{9,10},{10,1... | collective-permute-start | bytes 196616 | tf_op jit(solution)/shard_map/ppermute | solution.py:338
  96.5 7.0 %collective-permute-start.4 = (f32[21,16,128]{2,1,0:T(8,128)S(1)}, f32[21,16,128]{2,1,0:T(8,128)S(1)}, u32[]{:S(2)}, u32[]{:S(2)}) collective-permute-start(f32[21,16,128]{2,1,0:T(8,128)S(1)} %get-tuple-element.13), channel_id=1, source_target_pairs={{0,8},{8,16},{16,24},{24,32},{32,40},{40,48},{48,56},{56,64},{64,7... | collective-permute-start | bytes 516104 | tf_op jit(solution)/shard_map/ppermute | solution.py:365
  96.6 6.9 %collective-permute-start.5 = (f32[21,16,128]{2,1,0:T(8,128)S(1)}, f32[21,16,128]{2,1,0:T(8,128)S(1)}, u32[]{:S(2)}, u32[]{:S(2)}) collective-permute-start(f32[21,16,128]{2,1,0:T(8,128)S(1)} %get-tuple-element.14), channel_id=1, source_target_pairs={{0,120},{8,0},{16,8},{24,16},{32,24},{40,32},{48,40},{56,48},{64,5... | collective-permute-start | bytes 516104 | tf_op jit(solution)/shard_map/ppermute | solution.py:366
  103.6 11.0 %collective-permute-start.6 = (f32[424,128]{1,0:T(8,128)S(1)}, f32[424,128]{1,0:T(8,128)S(1)}, u32[]{:S(2)}, u32[]{:S(2)}) collective-permute-start(f32[424,128]{1,0:T(8,128)S(1)} %get-tuple-element.17), channel_id=1, source_target_pairs={{0,1},{1,2},{2,3},{3,4},{4,5},{5,6},{6,7},{7,0},{8,9},{9,10},{10,1... | collective-permute-start | bytes 651272 | tf_op jit(solution)/shard_map/ppermute | solution.py:368
  103.7 10.9 %collective-permute-start.7 = (f32[424,128]{1,0:T(8,128)S(1)}, f32[424,128]{1,0:T(8,128)S(1)}, u32[]{:S(2)}, u32[]{:S(2)}) collective-permute-start(f32[424,128]{1,0:T(8,128)S(1)} %get-tuple-element.18), channel_id=1, source_target_pairs={{0,7},{1,0},{2,1},{3,2},{4,3},{5,4},{6,5},{7,6},{8,15},{9,8},{10,9... | collective-permute-start | bytes 651272 | tf_op jit(solution)/shard_map/ppermute | solution.py:369

commit v2 on v1

--- a/solution.py
+++ b/solution.py
@@ -31,9 +31,12 @@
 DEVICES = 128
 HELD = 128
 CAP = 2
+TILE = 38
+PAIR = 2 * TILE + 1
 ROWS = 40
 EXT = 20
 VMEM_LIMIT = 48 * 1024 * 1024
+VMEM_MOST = 61 * 1024 * 1024
 F32 = jnp.float32
 
 
@@ -104,59 +107,98 @@
     return value if c == 0 else pltpu.roll(value, c % 128, 1)
 
 
-def pack_kernel(target, pdf, out, used):
+def pack_kernel(target_hbm, pdf_hbm, out_hbm, target, used, pdf, out3, sems, small):
+    listing = pltpu.make_async_copy(target_hbm, target, small.at[0])
+    listing.start()
+    quarters = []
+    for part in range(4):
+        rows = pl.ds(part * 64, 64)
+        copy = pltpu.make_async_copy(pdf_hbm.at[:, rows, :], pdf.at[:, rows, :], sems.at[part])
+        copy.start()
+        quarters.append(copy)
+    flat = pdf.reshape(19 * 256, 128)
+    out = out3.reshape(DEVICES * PAIR, 128)
+
+    empty = jnp.full((1, 128), -1.0, F32)
+
     def clear(i, _):
         used[i] = 0
+        out[pl.ds(i * PAIR + 2 * TILE, 1), :] = empty
         return 0
 
     lax.fori_loop(0, DEVICES, clear, 0, unroll=8)
-    empty = jnp.full((1, 128), -1.0, F32)
-
-    def blank(i, _):
-        out[pl.ds(i * ROWS + 38, 1), :] = empty
-        return 0
-
-    lax.fori_loop(0, DEVICES * CAP, blank, 0, unroll=8)
-
-    def place(group, _):
-        near = pdf.at[:, pl.ds(pl.multiple_of(group * 8, 8), 8), :]
-        for i in range(8):
-            t = target[group * 8 + i]
-            owner = lax.shift_right_logical(t, 7)
-            rank = used[owner]
-            used[owner] = rank + 1
-            start = (owner * CAP + rank) * ROWS
-            for q in range(19):
-                for r in range(2):
-                    value = near[q, i : i + 1, r * 128 : (r + 1) * 128]
-                    out[pl.ds(start + 2 * q + r, 1), :] = value
-            out[pl.ds(start + 38, 1), :] = jnp.full((1, 128), (t & 127).astype(F32), F32)
-        return 0
-
-    lax.fori_loop(0, HELD // 8, place, 0)
+    half = lax.broadcasted_iota(jnp.int32, (1, 128), 1) // 64
+    listing.wait()
+
+    def place(k, _):
+        t = target[k]
+        owner = lax.shift_right_logical(t, 7)
+        rank = used[owner]
+        used[owner] = rank + 1
+        start = owner * PAIR + rank * TILE
+        near = lax.shift_right_logical(k, 3) * 16 + (k & 7)
+        for r in range(2):
+            for q in (0, 8, 16):
+                n = min(8, 19 - q)
+                value = flat[pl.ds(near + r * 8 + q * 256, n, stride=256), :]
+                out[pl.ds(start + r * 19 + q, n), :] = value
+        line = pl.ds(owner * PAIR + 2 * TILE, 1)
+        out[line, :] = jnp.where(half == rank, (t & 127).astype(F32), out[line, :])
+        return 0
+
+    for part in range(4):
+        quarters[part].wait()
+        lax.fori_loop(part * 32, part * 32 + 32, place, 0, unroll=4)
+    done = pltpu.make_async_copy(out3, out_hbm, small.at[1])
+    done.start()
+    done.wait()
 
 
 def pack(target, pdf):
+    hbm = pl.BlockSpec(memory_space=pltpu.HBM)
     return pl.pallas_call(
         pack_kernel,
-        out_shape=jax.ShapeDtypeStruct((DEVICES * CAP * ROWS, 128), F32),
-        in_specs=[
-            pl.BlockSpec(memory_space=pltpu.SMEM),
-            pl.BlockSpec(memory_space=pltpu.VMEM),
+        out_shape=jax.ShapeDtypeStruct((DEVICES * PAIR, 1, 128), F32),
+        in_specs=[hbm, hbm],
+        out_specs=hbm,
+        scratch_shapes=[
+            pltpu.SMEM((HELD,), jnp.int32),
+            pltpu.SMEM((DEVICES,), jnp.int32),
+            pltpu.VMEM((19, 256, 128), F32),
+            pltpu.VMEM((DEVICES * PAIR, 1, 128), F32),
+            pltpu.SemaphoreType.DMA((4,)),
+            pltpu.SemaphoreType.DMA((2,)),
         ],
-        out_specs=pl.BlockSpec(memory_space=pltpu.VMEM),
-        scratch_shapes=[pltpu.SMEM((DEVICES,), jnp.int32)],
-        compiler_params=pltpu.CompilerParams(vmem_limit_bytes=VMEM_LIMIT),
+        compiler_params=pltpu.CompilerParams(vmem_limit_bytes=VMEM_MOST),
         cost_estimate=pl.CostEstimate(flops=0, bytes_accessed=8_000_000, transcendentals=0),
     )(target, pdf)
 
 
-def first_kernel(source, force, arrived, coef, post, xup, xdn, yup, ydn, tiles, sems):
+def first_kernel(force, arrived, coef, post, xup, xdn, yup, ydn, tiles, labels, found, source, sems, small):
+    pull = pltpu.make_async_copy(arrived.at[:, 2 * TILE, 0, :], labels, small.at[0])
+    pull.start()
+    pull.wait()
+    lane = lax.broadcasted_iota(jnp.int32, (8, 128), 1)
+    lane_f = lane.astype(F32)
+    sub = lax.broadcasted_iota(jnp.int32, (8, 128), 0)
+    low = lane < 64
+    total = jnp.zeros((8, 128), jnp.int32)
+    for group in range(DEVICES // 8):
+        line = labels[8 * group : 8 * group + 8, :]
+        other = pltpu.roll(line, 64, 1)
+        number = (sub + 8 * group) * 2
+        total = total + jnp.where(jnp.where(low, line, other) == lane_f, number, 0)
+        total = total + jnp.where(jnp.where(low, other, line) == lane_f, number + 1, 0)
+    found[...] = jnp.broadcast_to(jnp.sum(total, axis=0, keepdims=True), (8, 128))
+    hand = pltpu.make_async_copy(found, source, small.at[1])
+    hand.start()
+    hand.wait()
+
     def fetch(s, _):
-        p = source[s]
+        p = source[0, s]
         pltpu.make_async_copy(
-            arrived.at[pl.ds(pl.multiple_of(p * ROWS, 8), ROWS), :],
-            tiles.at[pl.ds(pl.multiple_of(s * ROWS, 8), ROWS), :],
+            arrived.at[lax.shift_right_logical(p, 1), pl.ds((p & 1) * TILE, TILE), 0, :],
+            tiles.at[pl.ds(pl.multiple_of(s * ROWS, 8), TILE), :],
             sems.at[lax.shift_right_logical(s, 3)],
         ).start()
         return 0
@@ -165,14 +207,12 @@
     f = [force[axis] for axis in range(3)]
 
     def plane(x, _):
-        whole = pl.ds(pl.multiple_of(x * (8 * ROWS), 8), 8 * ROWS)
-        pltpu.make_async_copy(
-            arrived.at[pl.ds(0, 8 * ROWS), :], tiles.at[whole, :], sems.at[x]
-        ).wait()
+        whole = tiles.at[pl.ds(0, 8 * TILE), :]
+        pltpu.make_async_copy(whole, whole, sems.at[x]).wait()
         for r in range(2):
             dist = []
             for q in range(19):
-                value = tiles[pl.ds(x * (8 * ROWS) + 2 * q + r, 8, stride=ROWS), :]
+                value = tiles[pl.ds(x * (8 * ROWS) + r * 19 + q, 8, stride=ROWS), :]
                 dist.append(WEIGHT[q] * value + WEIGHT[q])
             solid = coef[0, x, pl.ds(r, 8, stride=2), :]
             omega = coef[1, x, pl.ds(r, 8, stride=2), :]
@@ -198,22 +238,26 @@
                 out[19 + j, x : x + 1, :] = coef[j, x, row : row + 1, :]
 
 
-def first(source, force, arrived, coef):
+def first(force, arrived, coef):
     face = jax.ShapeDtypeStruct((COUNT, 16, 128), F32)
     vmem = pl.BlockSpec(memory_space=pltpu.VMEM)
     smem = pl.BlockSpec(memory_space=pltpu.SMEM)
     return pl.pallas_call(
         first_kernel,
         out_shape=[jax.ShapeDtypeStruct((19, 16, 16, 128), F32)] + [face] * 4,
-        in_specs=[smem, smem, pl.BlockSpec(memory_space=pl.ANY), vmem],
+        in_specs=[smem, pl.BlockSpec(memory_space=pltpu.HBM), vmem],
         out_specs=[vmem] * 5,
         scratch_shapes=[
             pltpu.VMEM((HELD * ROWS, 128), F32),
+            pltpu.VMEM((DEVICES, 128), F32),
+            pltpu.VMEM((8, 128), jnp.int32),
+            pltpu.SMEM((8, 128), jnp.int32),
             pltpu.SemaphoreType.DMA((16,)),
+            pltpu.SemaphoreType.DMA((2,)),
         ],
         compiler_params=pltpu.CompilerParams(vmem_limit_bytes=VMEM_LIMIT),
         cost_estimate=pl.CostEstimate(flops=10_000_000, bytes_accessed=8_000_000, transcendentals=0),
-    )(source, force, arrived, coef)
+    )(force, arrived, coef)
 
 
 def join_kernel(left, right, yup, ydn, up, dn):
@@ -247,7 +291,7 @@
     )(left, right, yup, ydn)
 
 
-def second_kernel(force, post, coef, left, right, below, above, out, wide, wcoef, again, sem):
+def second_kernel(force, post, coef, left, right, below, above, out, wide, wcoef, again, result, sem, sems):
     own = pltpu.make_async_copy(post, wide.at[:, pl.ds(2, 16), pl.ds(8, 16), :], sem)
     own.start()
     for x in range(16):
@@ -291,10 +335,13 @@
             for block in range(2):
                 start = 8 * block + 1 - cy
                 value = again[q, x + 1 - cx, start : start + 8, :]
-                out[q, x, 8 * block : 8 * block + 8, :] = value * INVERSE[q] - 1.0
+                result[x, q, 8 * block : 8 * block + 8, :] = value * INVERSE[q] - 1.0
+        pltpu.make_async_copy(result.at[x], out.at[:, x], sems.at[x]).start()
         return 0
 
     lax.fori_loop(0, 16, finish, 0)
+    for x in range(16):
+        pltpu.make_async_copy(result.at[x], out.at[:, x], sems.at[x]).wait()
 
 
 def second(force, post, coef, left, right, below, above):
@@ -304,12 +351,14 @@
         second_kernel,
         out_shape=jax.ShapeDtypeStruct((19, 16, 16, 128), F32),
         in_specs=[smem, pl.BlockSpec(memory_space=pl.ANY)] + [vmem] * 5,
-        out_specs=vmem,
+        out_specs=pl.BlockSpec(memory_space=pltpu.HBM),
         scratch_shapes=[
             pltpu.VMEM((19, EXT, 32, 128), F32),
             pltpu.VMEM((2, 18, 32, 128), F32),
             pltpu.VMEM((19, 18, 24, 128), F32),
+            pltpu.VMEM((16, 19, 16, 128), F32),
             pltpu.SemaphoreType.DMA,
+            pltpu.SemaphoreType.DMA((16,)),
         ],
         compiler_params=pltpu.CompilerParams(vmem_limit_bytes=VMEM_LIMIT),
         cost_estimate=pl.CostEstimate(flops=10_000_000, bytes_accessed=8_000_000, transcendentals=0),
@@ -321,47 +370,42 @@
     return [(i, (i + step) % n) for i in range(n)]
 
 
-def blocks_of(porosity, relaxation):
-    b = lax.axis_index("gy")
-    hi, lo = b // 4, b % 4
+def halves_of(porosity, relaxation):
+    hi = lax.axis_index("gy") // 4
     slab = jnp.stack([porosity, relaxation]).reshape(2, 2, 8, 16, 128)
     other = lax.dynamic_slice_in_dim(slab, (1 - hi) * 4, 4, axis=2)
     mine = lax.dynamic_slice_in_dim(slab, hi * 4, 4, axis=2)
-    came = lax.ppermute(other, "gy", [(i, i ^ 4) for i in range(8)])
-    first_ = jnp.where(hi == 0, mine, came)
-    last = jnp.where(hi == 0, came, mine)
-    both = jnp.stack([first_, last])
+    return mine, lax.ppermute(other, "gy", [(i, i ^ 4) for i in range(8)])
+
+
+def blocks_of(mine, came):
+    b = lax.axis_index("gy")
+    hi, lo = b // 4, b % 4
+    both = jnp.stack([jnp.where(hi == 0, mine, came), jnp.where(hi == 0, came, mine)])
     parts = [lax.dynamic_index_in_dim(both, lo, axis=3, keepdims=False)]
     for k in range(1, 4):
-        message = lax.dynamic_index_in_dim(both, (lo + k) % 4, axis=3, keepdims=False)
-        pairs = [(i, (i // 4) * 4 + (i % 4 + k) % 4) for i in range(8)]
-        parts.append(lax.ppermute(message, "gy", pairs))
+        message = lax.dynamic_index_in_dim(both, lo ^ k, axis=3, keepdims=False)
+        parts.append(lax.ppermute(message, "gy", [(i, i ^ k) for i in range(8)]))
     stacked = jnp.stack(parts)
     ordered = [
-        lax.dynamic_index_in_dim(stacked, (lo - y + 4) % 4, axis=0, keepdims=False)
-        for y in range(4)
+        lax.dynamic_index_in_dim(stacked, lo ^ y, axis=0, keepdims=False) for y in range(4)
     ]
     whole = jnp.stack(ordered)
     return whole.transpose(2, 1, 0, 3, 4, 5).reshape(2, 16, 16, 128)
 
 
 def local(pdf_old, tile_target, porosity, relaxation, solid_mask, force):
-    packed = pack(tile_target, pdf_old.transpose(1, 0, 2))
+    mine, came = halves_of(porosity, relaxation)
+    rows = pdf_old.reshape(16, 8, 19, 2, 128).transpose(2, 0, 3, 1, 4).reshape(19, 256, 128)
+    packed = pack(tile_target, rows)
+    packed, came = lax.optimization_barrier((packed, came))
     arrived = lax.all_to_all(
-        packed.reshape(DEVICES, CAP * ROWS, 128),
-        ("gx", "gy"),
-        split_axis=0,
-        concat_axis=0,
-        tiled=True,
-    ).reshape(DEVICES * CAP * ROWS, 128)
-    block = blocks_of(porosity, relaxation)
+        packed.reshape(DEVICES, PAIR, 1, 128), ("gx", "gy"), split_axis=0, concat_axis=0, tiled=True
+    )
+    block = blocks_of(mine, came)
     solid = block[0] + solid_mask.astype(F32) * (1.0 - block[0])
     coef = jnp.stack([solid, block[1]])
-    label = arrived.reshape(DEVICES * CAP, ROWS, 128)[:, 38, 0]
-    hit = label[:, None] == jnp.arange(HELD, dtype=F32)[None, :]
-    number = jnp.arange(DEVICES * CAP, dtype=jnp.int32)[:, None]
-    source = jnp.sum(jnp.where(hit, number, 0), axis=0)
-    post, xup, xdn, yup, ydn = first(source, force, arrived, coef)
+    post, xup, xdn, yup, ydn = first(force, arrived, coef)
     left = lax.ppermute(xup, "gx", ring("gx", 1))
     right = lax.ppermute(xdn, "gx", ring("gx", -1))
     up, dn = join(left, right, yup, ydn)

time: 121 us -> 112 us (0.926); the launches traced: 120 us -> 110 us
  waiting for transfers between devices: 71.9 us -> 65 us
  local copies, waits for them, and re-layouts: 4.7 us -> 0.1 us
  Pallas kernels: 15.2 us -> 16.7 us
  starting transfers between devices: 28.2 us -> 26.9 us
    ppermute x4, waiting for transfers between devices: 63.6 us -> 57.8 us  [the longest x3 57.8 us: blocks_of(): parts.append(lax.ppermute(message, 'gy', [(i, i ^ k) for i in range(8)]))]
    unnamed x12 -> x8, local copies, waits for them, and re-layouts: 2.37 us -> 0.03 us
    slice x1 -> x0, local copies, waits for them, and re-layouts: 2.26 us -> none  [local(): label = arrived.reshape(DEVICES * CAP, ROWS, 128)[:, 38, 0]]
    all_to_all x1, starting transfers between devices: 11.6 us -> 9.94 us  [local(): lax.all_to_all(packed.reshape(DEVICES, PAIR, 1, 128), ('gx', 'gy'), split...]
    pallas_call x1, Pallas kernels: 4.11 us -> 5.67 us  [first(): pl.pallas_call(first_kernel, out_shape=[jax.ShapeDtypeStruct((19, 16, 16,...]
    ppermute x1, waiting for transfers between devices: 5.25 us -> 3.98 us  [local(): below = lax.ppermute(up, 'gy', ring('gy', 1))]
  transfers between devices with their start and end apart: 9 -> 9, of which waited for: 6 -> 6; matrix products, arithmetic and copies ran while one was open for 0% -> 0% of each run, Pallas kernels for 0% -> 5%
where the time goes in v2:
time: 112 us; the launch traced here: 110 us
  waiting for transfers between devices  65 us (58%)
  starting transfers between devices  26.9 us (24%)
  Pallas kernels  16.7 us (15%)
    ppermute x3, waiting for transfers between devices, blocks_of(): parts.append(lax.ppermute(message, 'gy', [(i, i ^ k) for i in range(8)]))  57.8 us
    all_to_all x1, starting transfers between devices, local(): lax.all_to_all(packed.reshape(DEVICES, PAIR, 1, 128), ('gx', 'gy'), split...  9.94 us
    pallas_call x1, Pallas kernels, second(): pl.pallas_call(second_kernel, out_shape=jax.ShapeDtypeStruct((19, 16, 16,...  5.7 us
    pallas_call x1, Pallas kernels, first(): pl.pallas_call(first_kernel, out_shape=[jax.ShapeDtypeStruct((19, 16, 16,...  5.67 us
    pallas_call x1, Pallas kernels, pack(): pl.pallas_call(pack_kernel, out_shape=jax.ShapeDtypeStruct((DEVICES * PAI...  5.27 us
    ppermute x1, starting transfers between devices, local(): above = lax.ppermute(dn, 'gy', ring('gy', -1))  4.85 us
    ppermute x3, starting transfers between devices, blocks_of(): parts.append(lax.ppermute(message, 'gy', [(i, i ^ k) for i in range(8)]))  4.17 us
    ppermute x1, waiting for transfers between devices, local(): below = lax.ppermute(up, 'gy', ring('gy', 1))  3.98 us
  transfers between devices with their start and end apart: 9, of which 6 were waited for; matrix products, arithmetic and copies ran while one was open for 0% of the time, Pallas kernels for 5%

profile of v2, /device:TPU:0, one launch (start us, length us, event | category | flops | bytes accessed | tf_op | source)
XLA Modules:
  0.0 110.0 jit_solution(1091359298572294528)
XLA Ops:
  0.0 0.9 fusion.1
  0.9 3.2 %collective-permute-start = (f32[2,2,4,16,128]{4,3,2,1,0:T(8,128)S(1)}, f32[2,2,4,16,128]{4,3,2,1,0:T(8,128)S(1)}, u32[]{:S(2)}, u32[]{:S(2)}) collective-permute-start(f32[2,2,4,16,128]{4,3,2,1,0:T(8,128)S(1)} %fusion.1), channel_id=1, source_target_pairs={{0,4},{1,5},{2,6},{3,7},{4,0},{5,1},{6,2},{7,3},{8,12},{9,13},{10,... | collective-permute-start | bytes 393224 | tf_op jit(solution)/shard_map/ppermute | solution.py:378
  4.1 5.3 %shard_map.64 = f32[9856,1,128]{2,1,0:T(1,128)} custom-call(s32[128]{0:T(128)} %target_hbm.1, f32[19,256,128]{2,1,0:T(8,128)} %bitcast.39), custom_call_target="tpu_custom_call" | custom-call | bytes 8000000 | tf_op jit(solution)/shard_map/pallas_call | solution.py:159
  9.4 0.0 copy-start.1
  9.4 0.0 copy-start.2
  9.4 9.9 %all-to-all-start = ((f32[128,77,1,128]{3,2,1,0:T(1,128)}), f32[128,77,1,128]{3,2,1,0:T(1,128)}, u32[]{:S(2)}, u32[]{:S(2)}) async-start(f32[128,77,1,128]{3,2,1,0:T(1,128)} %bitcast.38), calls=%async_computation | async-start | bytes 10092544 | tf_op jit(solution)/shard_map/all_to_all | solution.py:402
  19.3 0.0 copy-start.3
  19.3 0.0 copy-start
  19.5 2.2 %collective-permute-start.3 = (f32[2,2,2,16,128]{4,3,2,0,1:T(8,128)S(1)}, f32[2,2,2,16,128]{4,3,2,0,1:T(8,128)S(1)}, u32[]{:S(2)}, u32[]{:S(2)}) collective-permute-start(f32[2,2,2,16,128]{4,3,2,0,1:T(8,128)S(1)} %bitcast.47), channel_id=1, source_target_pairs={{0,3},{1,2},{2,1},{3,0},{4,7},{5,6},{6,5},{7,4},{8,11},{9,10},{10,... | collective-permute-start | bytes 196616 | tf_op jit(solution)/shard_map/ppermute | solution.py:388
  21.7 0.8 collective-permute-start.2
  22.6 1.1 %collective-permute-start.1 = (f32[2,2,2,16,128]{4,3,2,0,1:T(8,128)S(1)}, f32[2,2,2,16,128]{4,3,2,0,1:T(8,128)S(1)}, u32[]{:S(2)}, u32[]{:S(2)}) collective-permute-start(f32[2,2,2,16,128]{4,3,2,0,1:T(8,128)S(1)} %bitcast.49), channel_id=1, source_target_pairs={{0,1},{1,0},{2,3},{3,2},{4,5},{5,4},{6,7},{7,6},{8,9},{9,8},{10,11... | collective-permute-start | bytes 196616 | tf_op jit(solution)/shard_map/ppermute | solution.py:388
  23.7 51.4 %collective-permute-done.3 = f32[2,2,2,16,128]{4,3,2,0,1:T(8,128)S(1)} collective-permute-done((f32[2,2,2,16,128]{4,3,2,0,1:T(8,128)S(1)}, f32[2,2,2,16,128]{4,3,2,0,1:T(8,128)S(1)}, u32[]{:S(2)}, u32[]{:S(2)}) %collective-permute-start.3) | collective-permute-done | bytes 65568 | tf_op jit(solution)/shard_map/ppermute | solution.py:388
  75.1 4.0 %collective-permute-done.2 = f32[2,2,2,16,128]{4,3,2,0,1:T(8,128)S(1)} collective-permute-done((f32[2,2,2,16,128]{4,3,2,0,1:T(8,128)S(1)}, f32[2,2,2,16,128]{4,3,2,0,1:T(8,128)S(1)}, u32[]{:S(2)}, u32[]{:S(2)}) %collective-permute-start.2) | collective-permute-done | bytes 65568 | tf_op jit(solution)/shard_map/ppermute | solution.py:388
  79.1 2.4 %collective-permute-done.1 = f32[2,2,2,16,128]{4,3,2,0,1:T(8,128)S(1)} collective-permute-done((f32[2,2,2,16,128]{4,3,2,0,1:T(8,128)S(1)}, f32[2,2,2,16,128]{4,3,2,0,1:T(8,128)S(1)}, u32[]{:S(2)}, u32[]{:S(2)}) %collective-permute-start.1) | collective-permute-done | bytes 65568 | tf_op jit(solution)/shard_map/ppermute | solution.py:388
  81.7 0.2 all-to-all-done.arrived
  81.9 5.7 %shard_map.65 = (f32[19,16,16,128]{3,2,1,0:T(8,128)S(1)}, f32[21,16,128]{2,1,0:T(8,128)S(1)}, f32[21,16,128]{2,1,0:T(8,128)S(1)}, f32[21,16,128]{2,1,0:T(8,128)S(1)}, f32[21,16,128]{2,1,0:T(8,128)S(1)}) custom-call(f32[3]{0:T(128)S(1)} %copy-done, f32[128,77,1,128]{3,2,1,0:T(1,128)} %all-to-all-done.arrived, f32[2,16,16,128]{3,2,1,0:T(8,128)S(1)} %pad_maximum_fusion.1.coef), custom_call_target="tpu_custom_call" | custom-call | flops 10000000 | bytes 8000000 | tf_op jit(solution)/shard_map/pallas_call | solution.py:245
  87.5 0.1 collective-permute-start.4
  87.6 3.8 %collective-permute-start.5 = (f32[21,16,128]{2,1,0:T(8,128)S(1)}, f32[21,16,128]{2,1,0:T(8,128)S(1)}, u32[]{:S(2)}, u32[]{:S(2)}) collective-permute-start(f32[21,16,128]{2,1,0:T(8,128)S(1)} %get-tuple-element.18), channel_id=1, source_target_pairs={{0,120},{8,0},{16,8},{24,16},{32,24},{40,32},{48,40},{56,48},{64,5... | collective-permute-start | bytes 516104 | tf_op jit(solution)/shard_map/ppermute | solution.py:410
  91.5 3.1 %collective-permute-done.4.left = f32[21,16,128]{2,1,0:T(8,128)S(1)} collective-permute-done((f32[21,16,128]{2,1,0:T(8,128)S(1)}, f32[21,16,128]{2,1,0:T(8,128)S(1)}, u32[]{:S(2)}, u32[]{:S(2)}) %collective-permute-start.4) | collective-permute-done | bytes 172064 | tf_op jit(solution)/shard_map/ppermute | solution.py:409
  94.5 0.1 shard_map.66
  94.6 0.9 collective-permute-start.6
  95.5 4.8 %collective-permute-start.7 = (f32[424,128]{1,0:T(8,128)S(1)}, f32[424,128]{1,0:T(8,128)S(1)}, u32[]{:S(2)}, u32[]{:S(2)}) collective-permute-start(f32[424,128]{1,0:T(8,128)S(1)} %get-tuple-element.22), channel_id=1, source_target_pairs={{0,7},{1,0},{2,1},{3,2},{4,3},{5,4},{6,5},{7,6},{8,15},{9,8},{10,9... | collective-permute-start | bytes 651272 | tf_op jit(solution)/shard_map/ppermute | solution.py:413
  100.3 4.0 %collective-permute-done.6.below = f32[424,128]{1,0:T(8,128)S(1)} collective-permute-done((f32[424,128]{1,0:T(8,128)S(1)}, f32[424,128]{1,0:T(8,128)S(1)}, u32[]{:S(2)}, u32[]{:S(2)}) %collective-permute-start.6) | collective-permute-done | bytes 217120 | tf_op jit(solution)/shard_map/ppermute | solution.py:412
  104.3 5.7 %shard_map.67 = f32[19,16,16,128]{3,2,1,0:T(8,128)} custom-call(f32[3]{0:T(128)S(1)} %copy-done, f32[19,16,16,128]{3,2,1,0:T(8,128)S(1)} %get-tuple-element.16.post, f32[2,16,16,128]{3,2,1,0:T(8,128)S(1)} %pad_maximum_fusion.1.coef, f32[21,16,128]{2,1,0:T(8,128)S(1)} %collective-permute-done.4.left, f32[21,16,128]{2,1,0:T(8,128)S(1)} %collective-permute-done.5.right, ...), custom_call_target="tpu_custom_call" | custom-call | flops 10000000 | bytes 8000000 | tf_op jit(solution)/shard_map/pallas_call | solution.py:350
  (19 shorter events, 0.2 us)
Async XLA Ops:
  0.9 8.5 %collective-permute-start = (f32[2,2,4,16,128]{4,3,2,1,0:T(8,128)S(1)}, f32[2,2,4,16,128]{4,3,2,1,0:T(8,128)S(1)}, u32[]{:S(2)}, u32[]{:S(2)}) collective-permute-start(f32[2,2,4,16,128]{4,3,2,1,0:T(8,128)S(1)} %fusion.1), channel_id=1, source_target_pairs={{0,4},{1,5},{2,6},{3,7},{4,0},{5,1},{6,2},{7,3},{8,12},{9,13},{10,... | collective-permute-start | bytes 393224 | tf_op jit(solution)/shard_map/ppermute | solution.py:378
  9.4 10.0 %copy-start.1 = (f32[2,128,128]{2,1,0:T(8,128)S(1)}, f32[2,128,128]{2,1,0:T(8,128)}, u32[]{:S(2)}) copy-start(f32[2,128,128]{2,1,0:T(8,128)} %param.8) | copy-start | bytes 393220
  9.4 10.0 %copy-start.2 = (f32[2,128,128]{2,1,0:T(8,128)S(1)}, f32[2,128,128]{2,1,0:T(8,128)}, u32[]{:S(2)}) copy-start(f32[2,128,128]{2,1,0:T(8,128)} %param.9) | copy-start | bytes 393220
  9.4 72.5 %all-to-all-start = ((f32[128,77,1,128]{3,2,1,0:T(1,128)}), f32[128,77,1,128]{3,2,1,0:T(1,128)}, u32[]{:S(2)}, u32[]{:S(2)}) async-start(f32[128,77,1,128]{3,2,1,0:T(1,128)} %bitcast.38), calls=%async_computation | async-start | bytes 10092544 | tf_op jit(solution)/shard_map/all_to_all | solution.py:402
  19.3 62.3 %copy-start.3 = (s32[16,16,128]{2,1,0:T(8,128)S(1)}, s32[16,16,128]{2,1,0:T(8,128)}, u32[]{:S(2)}) copy-start(s32[16,16,128]{2,1,0:T(8,128)} %param.10) | copy-start | bytes 393220
  19.3 62.5 %copy-start = (f32[3]{0:T(128)S(1)}, f32[3]{0:T(128)}, u32[]{:S(2)}) copy-start(f32[3]{0:T(128)} %force.3) | copy-start | bytes 40
  19.5 55.6 %collective-permute-start.3 = (f32[2,2,2,16,128]{4,3,2,0,1:T(8,128)S(1)}, f32[2,2,2,16,128]{4,3,2,0,1:T(8,128)S(1)}, u32[]{:S(2)}, u32[]{:S(2)}) collective-permute-start(f32[2,2,2,16,128]{4,3,2,0,1:T(8,128)S(1)} %bitcast.47), channel_id=1, source_target_pairs={{0,3},{1,2},{2,1},{3,0},{4,7},{5,6},{6,5},{7,4},{8,11},{9,10},{10,... | collective-permute-start | bytes 196616 | tf_op jit(solution)/shard_map/ppermute | solution.py:388
  21.7 57.3 %collective-permute-start.2 = (f32[2,2,2,16,128]{4,3,2,0,1:T(8,128)S(1)}, f32[2,2,2,16,128]{4,3,2,0,1:T(8,128)S(1)}, u32[]{:S(2)}, u32[]{:S(2)}) collective-permute-start(f32[2,2,2,16,128]{4,3,2,0,1:T(8,128)S(1)} %bitcast.48), channel_id=1, source_target_pairs={{0,2},{1,3},{2,0},{3,1},{4,6},{5,7},{6,4},{7,5},{8,10},{9,11},{10,... | collective-permute-start | bytes 196616 | tf_op jit(solution)/shard_map/ppermute | solution.py:388
  22.6 58.9 %collective-permute-start.1 = (f32[2,2,2,16,128]{4,3,2,0,1:T(8,128)S(1)}, f32[2,2,2,16,128]{4,3,2,0,1:T(8,128)S(1)}, u32[]{:S(2)}, u32[]{:S(2)}) collective-permute-start(f32[2,2,2,16,128]{4,3,2,0,1:T(8,128)S(1)} %bitcast.49), channel_id=1, source_target_pairs={{0,1},{1,0},{2,3},{3,2},{4,5},{5,4},{6,7},{7,6},{8,9},{9,8},{10,11... | collective-permute-start | bytes 196616 | tf_op jit(solution)/shard_map/ppermute | solution.py:388
  87.5 7.0 %collective-permute-start.4 = (f32[21,16,128]{2,1,0:T(8,128)S(1)}, f32[21,16,128]{2,1,0:T(8,128)S(1)}, u32[]{:S(2)}, u32[]{:S(2)}) collective-permute-start(f32[21,16,128]{2,1,0:T(8,128)S(1)} %get-tuple-element.17), channel_id=1, source_target_pairs={{0,8},{8,16},{16,24},{24,32},{32,40},{40,48},{48,56},{56,64},{64,7... | collective-permute-start | bytes 516104 | tf_op jit(solution)/shard_map/ppermute | solution.py:409
  87.6 6.9 %collective-permute-start.5 = (f32[21,16,128]{2,1,0:T(8,128)S(1)}, f32[21,16,128]{2,1,0:T(8,128)S(1)}, u32[]{:S(2)}, u32[]{:S(2)}) collective-permute-start(f32[21,16,128]{2,1,0:T(8,128)S(1)} %get-tuple-element.18), channel_id=1, source_target_pairs={{0,120},{8,0},{16,8},{24,16},{32,24},{40,32},{48,40},{56,48},{64,5... | collective-permute-start | bytes 516104 | tf_op jit(solution)/shard_map/ppermute | solution.py:410
  94.6 9.7 %collective-permute-start.6 = (f32[424,128]{1,0:T(8,128)S(1)}, f32[424,128]{1,0:T(8,128)S(1)}, u32[]{:S(2)}, u32[]{:S(2)}) collective-permute-start(f32[424,128]{1,0:T(8,128)S(1)} %get-tuple-element.21), channel_id=1, source_target_pairs={{0,1},{1,2},{2,3},{3,4},{4,5},{5,6},{6,7},{7,0},{8,9},{9,10},{10,1... | collective-permute-start | bytes 651272 | tf_op jit(solution)/shard_map/ppermute | solution.py:412
  95.5 8.8 %collective-permute-start.7 = (f32[424,128]{1,0:T(8,128)S(1)}, f32[424,128]{1,0:T(8,128)S(1)}, u32[]{:S(2)}, u32[]{:S(2)}) collective-permute-start(f32[424,128]{1,0:T(8,128)S(1)} %get-tuple-element.22), channel_id=1, source_target_pairs={{0,7},{1,0},{2,1},{3,2},{4,3},{5,4},{6,5},{7,6},{8,15},{9,8},{10,9... | collective-permute-start | bytes 651272 | tf_op jit(solution)/shard_map/ppermute | solution.py:413

commit v3 on v2

--- a/solution.py
+++ b/solution.py
@@ -47,6 +47,7 @@
 
 
 COUNT = 21
+SIDE_ROWS = 432
 
 
 def collide(dist, solid, omega, force):
@@ -130,7 +131,7 @@
     half = lax.broadcasted_iota(jnp.int32, (1, 128), 1) // 64
     listing.wait()
 
-    def place(k, _):
+    def put(k, _):
         t = target[k]
         owner = lax.shift_right_logical(t, 7)
         rank = used[owner]
@@ -148,7 +149,7 @@
 
     for part in range(4):
         quarters[part].wait()
-        lax.fori_loop(part * 32, part * 32 + 32, place, 0, unroll=4)
+        lax.fori_loop(part * 32, part * 32 + 32, put, 0, unroll=4)
     done = pltpu.make_async_copy(out3, out_hbm, small.at[1])
     done.start()
     done.wait()
@@ -174,7 +175,7 @@
     )(target, pdf)
 
 
-def first_kernel(force, arrived, coef, post, xup, xdn, yup, ydn, tiles, labels, found, source, sems, small):
+def place_kernel(arrived, tiles, labels, found, source, sem, small):
     pull = pltpu.make_async_copy(arrived.at[:, 2 * TILE, 0, :], labels, small.at[0])
     pull.start()
     pull.wait()
@@ -199,141 +200,185 @@
         pltpu.make_async_copy(
             arrived.at[lax.shift_right_logical(p, 1), pl.ds((p & 1) * TILE, TILE), 0, :],
             tiles.at[pl.ds(pl.multiple_of(s * ROWS, 8), TILE), :],
-            sems.at[lax.shift_right_logical(s, 3)],
+            sem,
         ).start()
         return 0
 
-    lax.fori_loop(0, HELD, fetch, 0, unroll=4)
+    lax.fori_loop(0, HELD, fetch, 0, unroll=8)
+    whole = tiles.at[pl.ds(0, HELD * TILE), :]
+    pltpu.make_async_copy(whole, whole, sem).wait()
+
+
+def place(arrived):
+    return pl.pallas_call(
+        place_kernel,
+        out_shape=jax.ShapeDtypeStruct((HELD * ROWS, 128), F32),
+        in_specs=[pl.BlockSpec(memory_space=pltpu.HBM)],
+        out_specs=pl.BlockSpec(memory_space=pltpu.VMEM),
+        scratch_shapes=[
+            pltpu.VMEM((DEVICES, 128), F32),
+            pltpu.VMEM((8, 128), jnp.int32),
+            pltpu.SMEM((8, 128), jnp.int32),
+            pltpu.SemaphoreType.DMA,
+            pltpu.SemaphoreType.DMA((2,)),
+        ],
+        compiler_params=pltpu.CompilerParams(vmem_limit_bytes=VMEM_LIMIT),
+        cost_estimate=pl.CostEstimate(flops=0, bytes_accessed=8_000_000, transcendentals=0),
+    )(arrived)
+
+
+def pick(flag, even, odd):
+    return jnp.where(flag == 0, even, odd)
+
+
+def plane_step(x, at, tiles, coef, post, f):
+    for r in range(2):
+        dist = []
+        for q in range(19):
+            value = tiles[pl.ds(x * (8 * ROWS) + r * 19 + q, 8, stride=ROWS), :]
+            dist.append(WEIGHT[q] * value + WEIGHT[q])
+        solid = coef[0, x, pl.ds(r, 8, stride=2), :]
+        omega = coef[1, x, pl.ds(r, 8, stride=2), :]
+        after = collide(dist, solid, omega, f)
+        for q in range(19):
+            post[q, at, pl.ds(r, 8, stride=2), :] = shift_z(after[q], q)
+
+
+def edge_kernel(force, odd, tiles, coef, edge, xe, xo):
     f = [force[axis] for axis in range(3)]
 
-    def plane(x, _):
-        whole = tiles.at[pl.ds(0, 8 * TILE), :]
-        pltpu.make_async_copy(whole, whole, sems.at[x]).wait()
-        for r in range(2):
-            dist = []
-            for q in range(19):
-                value = tiles[pl.ds(x * (8 * ROWS) + r * 19 + q, 8, stride=ROWS), :]
-                dist.append(WEIGHT[q] * value + WEIGHT[q])
-            solid = coef[0, x, pl.ds(r, 8, stride=2), :]
-            omega = coef[1, x, pl.ds(r, 8, stride=2), :]
-            after = collide(dist, solid, omega, f)
-            for q in range(19):
-                post[q, x, pl.ds(r, 8, stride=2), :] = shift_z(after[q], q)
-        return 0
-
-    lax.fori_loop(0, 16, plane, 0)
-    for out, sign in ((xup, 1), (xdn, -1)):
-        for i, (q, layer) in enumerate(entries(0, sign)):
-            out[i] = post[q, 15 - layer if sign == 1 else layer]
-        for j in range(2):
-            out[19 + j] = coef[j, 15 if sign == 1 else 0]
+    def plane(j, _):
+        plane_step(jnp.where(j < 2, j, j + 12), j, tiles, coef, edge, f)
+        return 0
+
+    lax.fori_loop(0, 4, plane, 0)
+    flag = odd[0]
+    for i, ((qu, lu), (qd, ld)) in enumerate(zip(entries(0, 1), entries(0, -1))):
+        up, dn = edge[qu, 3 - lu], edge[qd, ld]
+        xe[i] = pick(flag, up, dn)
+        xo[i] = pick(flag, dn, up)
+    for j in range(2):
+        up, dn = coef[j, 15], coef[j, 0]
+        xe[19 + j] = pick(flag, up, dn)
+        xo[19 + j] = pick(flag, dn, up)
+
+
+def inner_kernel(force, tiles, coef, edge, inner, yup, ydn):
+    f = [force[axis] for axis in range(3)]
+
+    def plane(j, _):
+        plane_step(j + 2, j, tiles, coef, inner, f)
+        return 0
+
+    lax.fori_loop(0, 12, plane, 0)
     for out, sign in ((yup, 1), (ydn, -1)):
         for i, (q, layer) in enumerate(entries(1, sign)):
             row = 15 - layer if sign == 1 else layer
             for x in range(16):
-                out[i, x : x + 1, :] = post[q, x, row : row + 1, :]
+                if 2 <= x < 14:
+                    value = inner[q, x - 2, row : row + 1, :]
+                else:
+                    value = edge[q, x if x < 2 else x - 12, row : row + 1, :]
+                out[i, x : x + 1, :] = value
         row = 15 if sign == 1 else 0
         for j in range(2):
             for x in range(16):
                 out[19 + j, x : x + 1, :] = coef[j, x, row : row + 1, :]
 
 
-def first(force, arrived, coef):
-    face = jax.ShapeDtypeStruct((COUNT, 16, 128), F32)
-    vmem = pl.BlockSpec(memory_space=pltpu.VMEM)
-    smem = pl.BlockSpec(memory_space=pltpu.SMEM)
+VMEM_SPEC = pl.BlockSpec(memory_space=pltpu.VMEM)
+SMEM_SPEC = pl.BlockSpec(memory_space=pltpu.SMEM)
+FACE = jax.ShapeDtypeStruct((COUNT, 16, 128), F32)
+SIDE = jax.ShapeDtypeStruct((SIDE_ROWS, 128), F32)
+
+
+def call(kernel, out_shape, operands, work, scalars=1, **more):
     return pl.pallas_call(
-        first_kernel,
-        out_shape=[jax.ShapeDtypeStruct((19, 16, 16, 128), F32)] + [face] * 4,
-        in_specs=[smem, pl.BlockSpec(memory_space=pltpu.HBM), vmem],
-        out_specs=[vmem] * 5,
-        scratch_shapes=[
-            pltpu.VMEM((HELD * ROWS, 128), F32),
-            pltpu.VMEM((DEVICES, 128), F32),
-            pltpu.VMEM((8, 128), jnp.int32),
-            pltpu.SMEM((8, 128), jnp.int32),
-            pltpu.SemaphoreType.DMA((16,)),
-            pltpu.SemaphoreType.DMA((2,)),
-        ],
+        kernel,
+        out_shape=out_shape,
+        in_specs=[SMEM_SPEC] * scalars + [VMEM_SPEC] * (len(operands) - scalars),
         compiler_params=pltpu.CompilerParams(vmem_limit_bytes=VMEM_LIMIT),
-        cost_estimate=pl.CostEstimate(flops=10_000_000, bytes_accessed=8_000_000, transcendentals=0),
-    )(force, arrived, coef)
-
-
-def join_kernel(left, right, yup, ydn, up, dn):
-    zero = jnp.zeros((1, 128), F32)
-    for own, out, sign in ((yup, up, 1), (ydn, dn, -1)):
-        listed = entries(1, sign) + [(19, 0), (20, 0)]
-        for i, (q, layer) in enumerate(listed):
-            row = 15 - layer if sign == 1 else layer
-            out[i * EXT + 2 : i * EXT + 18, :] = own[i]
-            for half, toward in ((left, 1), (right, -1)):
-                have = {e: n for n, e in enumerate(entries(0, toward) + [(19, 0), (20, 0)])}
-                for deep in range(2):
-                    at = (1 - deep) if toward == 1 else 18 + deep
-                    n = have.get((q, deep))
-                    value = zero if n is None else half[n, row : row + 1, :]
-                    out[i * EXT + at : i * EXT + at + 1, :] = value
-    for out in (up, dn):
-        out[COUNT * EXT : COUNT * EXT + 4, :] = jnp.zeros((4, 128), F32)
-
-
-def join(left, right, yup, ydn):
-    side = jax.ShapeDtypeStruct((COUNT * EXT + 4, 128), F32)
-    vmem = pl.BlockSpec(memory_space=pltpu.VMEM)
-    return pl.pallas_call(
-        join_kernel,
-        out_shape=[side] * 2,
-        in_specs=[vmem] * 4,
-        out_specs=[vmem] * 2,
-        compiler_params=pltpu.CompilerParams(vmem_limit_bytes=VMEM_LIMIT),
-        cost_estimate=pl.CostEstimate(flops=0, bytes_accessed=1_000_000, transcendentals=0),
-    )(left, right, yup, ydn)
-
-
-def second_kernel(force, post, coef, left, right, below, above, out, wide, wcoef, again, result, sem, sems):
-    own = pltpu.make_async_copy(post, wide.at[:, pl.ds(2, 16), pl.ds(8, 16), :], sem)
-    own.start()
-    for x in range(16):
-        for j in range(2):
-            wcoef[j, x + 1, 8:24, :] = coef[j, x]
-    for half, sign in ((left, 1), (right, -1)):
+        cost_estimate=pl.CostEstimate(flops=work, bytes_accessed=work, transcendentals=0),
+        **more,
+    )(*operands)
+
+
+def join_kernel(odd, xe, xo, yup, ydn, ye, yo):
+    fx, fy = odd[0], odd[1]
+    lists = [entries(1, sign) + [(19, 0), (20, 0)] for sign in (1, -1)]
+    have = [
+        {e: n for n, e in enumerate(entries(0, toward) + [(19, 0), (20, 0)])} for toward in (1, -1)
+    ]
+
+    def corner(direction, i, toward, deep):
+        q, layer = lists[direction][i]
+        n = have[toward].get((q, deep))
+        if n is None:
+            return jnp.zeros((1, 128), F32)
+        row = 15 - layer if direction == 0 else layer
+        even, odd_ = (xo, xe) if toward == 0 else (xe, xo)
+        return pick(fx, even[n, row : row + 1, :], odd_[n, row : row + 1, :])
+
+    for i in range(COUNT):
+        up, dn = yup[i], ydn[i]
+        ye[i * EXT + 2 : i * EXT + 18, :] = pick(fy, up, dn)
+        yo[i * EXT + 2 : i * EXT + 18, :] = pick(fy, dn, up)
+        for toward in range(2):
+            for deep in range(2):
+                at = i * EXT + ((1 - deep) if toward == 0 else 18 + deep)
+                up, dn = corner(0, i, toward, deep), corner(1, i, toward, deep)
+                ye[at : at + 1, :] = pick(fy, up, dn)
+                yo[at : at + 1, :] = pick(fy, dn, up)
+    for out in (ye, yo):
+        out[COUNT * EXT : SIDE_ROWS, :] = jnp.zeros((SIDE_ROWS - COUNT * EXT, 128), F32)
+
+
+def middle_kernel(force, odd, edge, inner, coef, xe, xo, out, wide, again, result, sems):
+    flag = odd[0]
+    for j in range(4):
+        for q in range(19):
+            wide[q, (j if j < 2 else j + 12) + 2, 8:24, :] = edge[q, j]
+
+    def copy(x, _):
+        for q in range(19):
+            wide[q, x + 4, 8:24, :] = inner[q, x]
+        return 0
+
+    lax.fori_loop(0, 12, copy, 0)
+    sides = []
+    for toward, sign in ((0, 1), (1, -1)):
+        even, odd_ = (xo, xe) if toward == 0 else (xe, xo)
         for i, (q, layer) in enumerate(entries(0, sign)):
-            wide[q, 1 - layer if sign == 1 else 18 + layer, 8:24, :] = half[i]
-        for j in range(2):
-            wcoef[j, 0 if sign == 1 else 17, 8:24, :] = half[19 + j]
-    for half, sign in ((below, 1), (above, -1)):
-        for i, (q, layer) in enumerate(entries(1, sign)):
-            row = 7 - layer if sign == 1 else 24 + layer
-            for x in range(EXT):
-                wide[q, x, row : row + 1, :] = half[i * EXT + x : i * EXT + x + 1, :]
-        row = 7 if sign == 1 else 24
-        for j in range(2):
-            for x in range(18):
-                at = (19 + j) * EXT + x + 1
-                wcoef[j, x, row : row + 1, :] = half[at : at + 1, :]
+            at = 1 - layer if toward == 0 else 18 + layer
+            wide[q, at, 8:24, :] = pick(flag, even[i], odd_[i])
+        sides.append([pick(flag, even[19 + j], odd_[19 + j]) for j in range(2)])
     f = [force[axis] for axis in range(3)]
-    own.wait()
-
-    def plane(x, _):
-        for block in range(3):
+
+    def one(x, solids, omegas):
+        for block in range(2):
             dist = []
             for q in range(19):
                 cx, cy, _z = VELOCITY[q]
-                dist.append(wide[q, x + 1 - cx, 7 + 8 * block - cy : 15 + 8 * block - cy, :])
-            rows = slice(7 + 8 * block, 15 + 8 * block)
-            after = collide(dist, wcoef[0, x, rows, :], wcoef[1, x, rows, :], f)
+                dist.append(wide[q, x + 1 - cx, 8 + 8 * block - cy : 16 + 8 * block - cy, :])
+            after = collide(dist, solids[block], omegas[block], f)
             for q in range(19):
-                again[q, x, 8 * block : 8 * block + 8, :] = shift_z(after[q], q)
-        return 0
-
-    lax.fori_loop(0, 18, plane, 0)
+                again[q, x, 8 + 8 * block : 16 + 8 * block, :] = shift_z(after[q], q)
+
+    def plane(x, _):
+        solids = [coef[0, x - 1, 8 * block : 8 * block + 8, :] for block in range(2)]
+        omegas = [coef[1, x - 1, 8 * block : 8 * block + 8, :] for block in range(2)]
+        one(x, solids, omegas)
+        return 0
+
+    one(0, *[[v[0:8], v[8:16]] for v in sides[0]])
+    one(17, *[[v[0:8], v[8:16]] for v in sides[1]])
+    lax.fori_loop(1, 17, plane, 0)
 
     def finish(x, _):
         for q in range(19):
             cx, cy, _z = VELOCITY[q]
             for block in range(2):
-                start = 8 * block + 1 - cy
+                start = 8 + 8 * block - cy
                 value = again[q, x + 1 - cx, start : start + 8, :]
                 result[x, q, 8 * block : 8 * block + 8, :] = value * INVERSE[q] - 1.0
         pltpu.make_async_copy(result.at[x], out.at[:, x], sems.at[x]).start()
@@ -344,30 +389,62 @@
         pltpu.make_async_copy(result.at[x], out.at[:, x], sems.at[x]).wait()
 
 
-def second(force, post, coef, left, right, below, above):
-    vmem = pl.BlockSpec(memory_space=pltpu.VMEM)
-    smem = pl.BlockSpec(memory_space=pltpu.SMEM)
-    return pl.pallas_call(
-        second_kernel,
-        out_shape=jax.ShapeDtypeStruct((19, 16, 16, 128), F32),
-        in_specs=[smem, pl.BlockSpec(memory_space=pl.ANY)] + [vmem] * 5,
-        out_specs=pl.BlockSpec(memory_space=pltpu.HBM),
-        scratch_shapes=[
-            pltpu.VMEM((19, EXT, 32, 128), F32),
-            pltpu.VMEM((2, 18, 32, 128), F32),
-            pltpu.VMEM((19, 18, 24, 128), F32),
-            pltpu.VMEM((16, 19, 16, 128), F32),
-            pltpu.SemaphoreType.DMA,
-            pltpu.SemaphoreType.DMA((16,)),
-        ],
-        compiler_params=pltpu.CompilerParams(vmem_limit_bytes=VMEM_LIMIT),
-        cost_estimate=pl.CostEstimate(flops=10_000_000, bytes_accessed=8_000_000, transcendentals=0),
-    )(force, post, coef, left, right, below, above)
-
-
-def ring(axis, step):
+def last_kernel(force, odd, mine_e, mine_o, came_e, came_o, _before, out, sides, rows, patch, sem):
+    flag = odd[1]
+    for block in range(SIDE_ROWS // 8):
+        part = slice(8 * block, 8 * block + 8)
+        me, mo, ce, co = mine_e[part, :], mine_o[part, :], came_e[part, :], came_o[part, :]
+        sides[0, part, :] = pick(flag, co, ce)
+        sides[1, part, :] = pick(flag, mo, me)
+        sides[2, part, :] = pick(flag, ce, co)
+        sides[3, part, :] = pick(flag, me, mo)
+    f = [force[axis] for axis in range(3)]
+    number = 0
+    for side, sign in ((0, 1), (1, -1)):
+        came = {e: n for n, e in enumerate(entries(1, sign))}
+        mine = {e: n for n, e in enumerate(entries(1, -sign))}
+        for line in range(2):
+            for block in range(3):
+                start = 1 + 8 * block
+                dist = []
+                for q in range(19):
+                    cx, cy, _z = VELOCITY[q]
+                    if cy == sign:
+                        which, n = 0, came[(q, 1 - line)]
+                    elif cy == 0:
+                        which, n = (0, came[(q, 0)]) if line == 0 else (1, mine[(q, 0)])
+                    else:
+                        which, n = 1, mine[(q, line)]
+                    at = n * EXT + start - cx
+                    dist.append(sides[2 * side + which, at : at + 8, :])
+                fixed = [
+                    sides[2 * side + line, (19 + j) * EXT + start : (19 + j) * EXT + start + 8, :]
+                    for j in range(2)
+                ]
+                after = collide(dist, fixed[0], fixed[1], f)
+                for q in range(19):
+                    if VELOCITY[q][1] == sign or (VELOCITY[q][1] == 0 and line == 1):
+                        rows[line, q, 8 * block : 8 * block + 8, :] = shift_z(after[q], q)
+        for q in range(19):
+            cx, cy, _z = VELOCITY[q]
+            targets = []
+            if cy == sign:
+                targets = [(0, 0), (1, 1)]
+            elif cy == 0:
+                targets = [(1, 0)]
+            for line, depth in targets:
+                value = rows[line, q, 1 - cx : 17 - cx, :]
+                patch[number] = value * INVERSE[q] - 1.0
+                y = depth if sign == 1 else 15 - depth
+                pltpu.make_async_copy(patch.at[number], out.at[q, :, y, :], sem).start()
+                number += 1
+    pltpu.make_async_copy(patch, patch, sem).wait()
+
+
+def swap(value, axis, first):
     n = lax.axis_size(axis)
-    return [(i, (i + step) % n) for i in range(n)]
+    pairs = [(i, (i + 1) % n if (i % 2 == 0) == first else (i - 1) % n) for i in range(n)]
+    return lax.ppermute(value, axis, pairs)
 
 
 def halves_of(porosity, relaxation):
@@ -405,13 +482,48 @@
     block = blocks_of(mine, came)
     solid = block[0] + solid_mask.astype(F32) * (1.0 - block[0])
     coef = jnp.stack([solid, block[1]])
-    post, xup, xdn, yup, ydn = first(force, arrived, coef)
-    left = lax.ppermute(xup, "gx", ring("gx", 1))
-    right = lax.ppermute(xdn, "gx", ring("gx", -1))
-    up, dn = join(left, right, yup, ydn)
-    below = lax.ppermute(up, "gy", ring("gy", 1))
-    above = lax.ppermute(dn, "gy", ring("gy", -1))
-    return second(force, post, coef, left, right, below, above)
+    odd = jnp.stack([lax.axis_index("gx") % 2, lax.axis_index("gy") % 2]).astype(jnp.int32)
+    tiles = place(arrived)
+    posts = [jax.ShapeDtypeStruct((19, n, 16, 128), F32) for n in (4, 12)]
+    edge, xe, xo = call(
+        edge_kernel, [posts[0], FACE, FACE], (force, odd, tiles, coef), 2_000_000, scalars=2
+    )
+    from_xe, from_xo = swap(xe, "gx", True), swap(xo, "gx", False)
+    inner, yup, ydn = call(
+        inner_kernel, [posts[1], FACE, FACE], (force, tiles, coef, edge), 6_000_000
+    )
+    ye, yo = call(join_kernel, [SIDE, SIDE], (odd, from_xe, from_xo, yup, ydn), 500_000)
+    from_ye, from_yo = swap(ye, "gy", True), swap(yo, "gy", False)
+    hbm = pl.BlockSpec(memory_space=pltpu.HBM)
+    result = call(
+        middle_kernel,
+        jax.ShapeDtypeStruct((19, 16, 16, 128), F32),
+        (force, odd, edge, inner, coef, from_xe, from_xo),
+        12_000_000,
+        scalars=2,
+        out_specs=hbm,
+        scratch_shapes=[
+            pltpu.VMEM((19, EXT, 32, 128), F32),
+            pltpu.VMEM((19, 18, 32, 128), F32),
+            pltpu.VMEM((16, 19, 16, 128), F32),
+            pltpu.SemaphoreType.DMA((16,)),
+        ],
+    )
+    return pl.pallas_call(
+        last_kernel,
+        out_shape=jax.ShapeDtypeStruct((19, 16, 16, 128), F32),
+        in_specs=[SMEM_SPEC] * 2 + [VMEM_SPEC] * 4 + [hbm],
+        out_specs=hbm,
+        input_output_aliases={6: 0},
+        scratch_shapes=[
+            pltpu.VMEM((4, SIDE_ROWS, 128), F32),
+            pltpu.VMEM((2, 19, 24, 128), F32),
+            pltpu.VMEM((38, 16, 128), F32),
+            pltpu.SemaphoreType.DMA,
+        ],
+        compiler_params=pltpu.CompilerParams(vmem_limit_bytes=VMEM_LIMIT),
+        cost_estimate=pl.CostEstimate(flops=2_000_000, bytes_accessed=2_000_000, transcendentals=0),
+    )(force, odd, ye, yo, from_ye, from_yo, result)
 
 
 def solution(mesh):

time: 112 us -> 106 us (0.946); the launches traced: 110 us -> 106 us
  waiting for transfers between devices: 65 us -> 61.6 us
  starting transfers between devices: 26.9 us -> 24.2 us
  Pallas kernels: 16.7 us -> 18.9 us
    ppermute x4, waiting for transfers between devices: 7.07 us -> 3.67 us  [swap(): return lax.ppermute(value, axis, pairs)]
    ppermute x4, starting transfers between devices: 9.63 us -> 6.88 us  [swap(): return lax.ppermute(value, axis, pairs)]
    pallas_call x3 -> x6, Pallas kernels: 11.4 us -> 13.6 us  [the longest x4 8.71 us: call(): pl.pallas_call(kernel, out_shape=out_shape, in_specs=[SMEM_SPEC] * scalar...]
  transfers between devices with their start and end apart: 9 -> 9, of which waited for: 6 -> 6; matrix products, arithmetic and copies ran while one was open for 0% -> 0% of each run, Pallas kernels for 5% -> 12%
where the time goes in v3:
time: 106 us
  waiting for transfers between devices  61.6 us (58%)
  starting transfers between devices  24.2 us (23%)
  Pallas kernels  18.9 us (18%)
  other arithmetic  1.09 us (1%)
    ppermute x3, waiting for transfers between devices, blocks_of(): parts.append(lax.ppermute(message, 'gy', [(i, i ^ k) for i in range(8)]))  57.7 us
    all_to_all x1, starting transfers between devices, local(): lax.all_to_all(packed.reshape(DEVICES, PAIR, 1, 128), ('gx', 'gy'), split...  9.92 us
    pallas_call x4, Pallas kernels, call(): pl.pallas_call(kernel, out_shape=out_shape, in_specs=[SMEM_SPEC] * scalar...  8.71 us
    ppermute x4, starting transfers between devices, swap(): return lax.ppermute(value, axis, pairs)  6.88 us
    pallas_call x1, Pallas kernels, pack(): pl.pallas_call(pack_kernel, out_shape=jax.ShapeDtypeStruct((DEVICES * PAI...  5.28 us
    ppermute x3, starting transfers between devices, blocks_of(): parts.append(lax.ppermute(message, 'gy', [(i, i ^ k) for i in range(8)]))  4.17 us
    ppermute x4, waiting for transfers between devices, swap(): return lax.ppermute(value, axis, pairs)  3.67 us
    pallas_call x1, Pallas kernels, place(): pl.pallas_call(place_kernel, out_shape=jax.ShapeDtypeStruct((HELD * ROWS,...  3.28 us
  transfers between devices with their start and end apart: 9, of which 6 were waited for; matrix products, arithmetic and copies ran while one was open for 0% of the time, Pallas kernels for 12%

profile of v3, /device:TPU:0, one launch (start us, length us, event | category | flops | bytes accessed | tf_op | source)
XLA Modules:
  0.0 106.1 jit_solution(7789648098240031102)
XLA Ops:
  0.0 0.9 fusion.1
  0.9 3.2 %collective-permute-start = (f32[2,2,4,16,128]{4,3,2,1,0:T(8,128)S(1)}, f32[2,2,4,16,128]{4,3,2,1,0:T(8,128)S(1)}, u32[]{:S(2)}, u32[]{:S(2)}) collective-permute-start(f32[2,2,4,16,128]{4,3,2,1,0:T(8,128)S(1)} %fusion.1), channel_id=1, source_target_pairs={{0,4},{1,5},{2,6},{3,7},{4,0},{5,1},{6,2},{7,3},{8,12},{9,13},{10,... | collective-permute-start | bytes 393224 | tf_op jit(solution)/shard_map/ppermute | solution.py:455
  4.1 5.3 %shard_map.64 = f32[9856,1,128]{2,1,0:T(1,128)} custom-call(s32[128]{0:T(128)} %target_hbm.1, f32[19,256,128]{2,1,0:T(8,128)} %bitcast.41), custom_call_target="tpu_custom_call" | custom-call | bytes 8000000 | tf_op jit(solution)/shard_map/pallas_call | solution.py:160
  9.4 9.9 %all-to-all-start = ((f32[128,77,1,128]{3,2,1,0:T(1,128)}), f32[128,77,1,128]{3,2,1,0:T(1,128)}, u32[]{:S(2)}, u32[]{:S(2)}) async-start(f32[128,77,1,128]{3,2,1,0:T(1,128)} %bitcast.40), calls=%async_computation | async-start | bytes 10092544 | tf_op jit(solution)/shard_map/all_to_all | solution.py:479
  19.5 2.2 %collective-permute-start.3 = (f32[2,2,2,16,128]{4,3,2,0,1:T(8,128)S(1)}, f32[2,2,2,16,128]{4,3,2,0,1:T(8,128)S(1)}, u32[]{:S(2)}, u32[]{:S(2)}) collective-permute-start(f32[2,2,2,16,128]{4,3,2,0,1:T(8,128)S(1)} %bitcast.49), channel_id=1, source_target_pairs={{0,3},{1,2},{2,1},{3,0},{4,7},{5,6},{6,5},{7,4},{8,11},{9,10},{10,... | collective-permute-start | bytes 196616 | tf_op jit(solution)/shard_map/ppermute | solution.py:465
  21.8 0.8 collective-permute-start.2
  22.6 1.1 %collective-permute-start.1 = (f32[2,2,2,16,128]{4,3,2,0,1:T(8,128)S(1)}, f32[2,2,2,16,128]{4,3,2,0,1:T(8,128)S(1)}, u32[]{:S(2)}, u32[]{:S(2)}) collective-permute-start(f32[2,2,2,16,128]{4,3,2,0,1:T(8,128)S(1)} %bitcast.51), channel_id=1, source_target_pairs={{0,1},{1,0},{2,3},{3,2},{4,5},{5,4},{6,7},{7,6},{8,9},{9,8},{10,11... | collective-permute-start | bytes 196616 | tf_op jit(solution)/shard_map/ppermute | solution.py:465
  23.7 0.1 pad_add_fusion.odd
  23.8 51.3 %collective-permute-done.3 = f32[2,2,2,16,128]{4,3,2,0,1:T(8,128)S(1)} collective-permute-done((f32[2,2,2,16,128]{4,3,2,0,1:T(8,128)S(1)}, f32[2,2,2,16,128]{4,3,2,0,1:T(8,128)S(1)}, u32[]{:S(2)}, u32[]{:S(2)}) %collective-permute-start.3) | collective-permute-done | bytes 65568 | tf_op jit(solution)/shard_map/ppermute | solution.py:465
  75.1 4.0 %collective-permute-done.2 = f32[2,2,2,16,128]{4,3,2,0,1:T(8,128)S(1)} collective-permute-done((f32[2,2,2,16,128]{4,3,2,0,1:T(8,128)S(1)}, f32[2,2,2,16,128]{4,3,2,0,1:T(8,128)S(1)}, u32[]{:S(2)}, u32[]{:S(2)}) %collective-permute-start.2) | collective-permute-done | bytes 65568 | tf_op jit(solution)/shard_map/ppermute | solution.py:465
  79.1 2.4 %collective-permute-done.1 = f32[2,2,2,16,128]{4,3,2,0,1:T(8,128)S(1)} collective-permute-done((f32[2,2,2,16,128]{4,3,2,0,1:T(8,128)S(1)}, f32[2,2,2,16,128]{4,3,2,0,1:T(8,128)S(1)}, u32[]{:S(2)}, u32[]{:S(2)}) %collective-permute-start.1) | collective-permute-done | bytes 65568 | tf_op jit(solution)/shard_map/ppermute | solution.py:465
  81.7 0.2 all-to-all-done.arrived
  81.9 3.3 %shard_map.65.tiles = f32[5120,128]{1,0:T(8,128)S(1)} custom-call(f32[128,77,1,128]{3,2,1,0:T(1,128)} %all-to-all-done.arrived), custom_call_target="tpu_custom_call" | custom-call | bytes 8000000 | tf_op jit(solution)/shard_map/pallas_call | solution.py:213
  85.1 1.1 %shard_map.66 = (f32[19,4,16,128]{3,2,1,0:T(8,128)S(1)}, f32[21,16,128]{2,1,0:T(8,128)S(1)}, f32[21,16,128]{2,1,0:T(8,128)S(1)}) custom-call(f32[3]{0:T(128)S(1)} %copy-done, s32[2]{0:T(128)S(1)} %pad_add_fusion.odd, f32[5120,128]{1,0:T(8,128)S(1)} %shard_map.65.tiles, f32[2,16,16,128]{3,2,1,0:T(8,128)S(1)} %pad_maximum_fusion.1.coef), custom_call_target="tpu_custom_call" | custom-call | flops 2000000 | bytes 2000000 | tf_op jit(solution)/shard_map/pallas_call | solution.py:296
  86.3 0.1 collective-permute-start.4
  86.4 3.6 %collective-permute-start.5 = (f32[21,16,128]{2,1,0:T(8,128)S(1)}, f32[21,16,128]{2,1,0:T(8,128)S(1)}, u32[]{:S(2)}, u32[]{:S(2)}) collective-permute-start(f32[21,16,128]{2,1,0:T(8,128)S(1)} %get-tuple-element.18), channel_id=1, source_target_pairs={{0,120},{8,16},{16,8},{24,32},{32,24},{40,48},{48,40},{56,64},{64,... | collective-permute-start | bytes 516104 | tf_op jit(solution)/shard_map/ppermute | solution.py:447
  90.0 2.4 %shard_map.67 = (f32[19,12,16,128]{3,2,1,0:T(8,128)S(1)}, f32[21,16,128]{2,1,0:T(8,128)S(1)}, f32[21,16,128]{2,1,0:T(8,128)S(1)}) custom-call(f32[3]{0:T(128)S(1)} %copy-done, f32[5120,128]{1,0:T(8,128)S(1)} %shard_map.65.tiles, f32[2,16,16,128]{3,2,1,0:T(8,128)S(1)} %pad_maximum_fusion.1.coef, f32[19,4,16,128]{3,2,1,0:T(8,128)S(1)} %get-tuple-element.19.edge), custom_call_target="tpu_custom_call" | custom-call | flops 6000000 | bytes 6000000 | tf_op jit(solution)/shard_map/pallas_call | solution.py:296
  92.4 1.0 collective-permute-done.5.xo
  93.4 0.6 shard_map.68
  94.0 0.9 collective-permute-start.6
  94.9 2.4 %collective-permute-start.7 = (f32[432,128]{1,0:T(8,128)S(1)}, f32[432,128]{1,0:T(8,128)S(1)}, u32[]{:S(2)}, u32[]{:S(2)}) collective-permute-start(f32[432,128]{1,0:T(8,128)S(1)} %get-tuple-element.23.mine_o), channel_id=1, source_target_pairs={{0,7},{1,2},{2,1},{3,4},{4,3},{5,6},{6,5},{7,0},{8,15},{9,10},{10,... | collective-permute-start | bytes 663560 | tf_op jit(solution)/shard_map/ppermute | solution.py:447
  97.3 4.5 %shard_map.69._before = f32[19,16,16,128]{3,2,1,0:T(8,128)} custom-call(f32[3]{0:T(128)S(1)} %copy-done, s32[2]{0:T(128)S(1)} %pad_add_fusion.odd, f32[19,4,16,128]{3,2,1,0:T(8,128)S(1)} %get-tuple-element.19.edge, f32[19,12,16,128]{3,2,1,0:T(8,128)S(1)} %get-tuple-element.24.inner, f32[2,16,16,128]{3,2,1,0:T(8,128)S(1)} %pad_maximum_fusion.1.coef, ...), custom_call_target="tpu_custom_call" | custom-call | flops 12000000 | bytes 12000000 | tf_op jit(solution)/shard_map/pallas_call | solution.py:296
  101.8 2.6 %collective-permute-done.7.came_o = f32[432,128]{1,0:T(8,128)S(1)} collective-permute-done((f32[432,128]{1,0:T(8,128)S(1)}, f32[432,128]{1,0:T(8,128)S(1)}, u32[]{:S(2)}, u32[]{:S(2)}) %collective-permute-start.7) | collective-permute-done | bytes 221216 | tf_op jit(solution)/shard_map/ppermute | solution.py:447
  104.5 1.6 %shard_map.70 = f32[19,16,16,128]{3,2,1,0:T(8,128)} custom-call(f32[3]{0:T(128)S(1)} %copy-done, s32[2]{0:T(128)S(1)} %pad_add_fusion.odd, f32[432,128]{1,0:T(8,128)S(1)} %get-tuple-element.22.mine_e, f32[432,128]{1,0:T(8,128)S(1)} %get-tuple-element.23.mine_o, f32[432,128]{1,0:T(8,128)S(1)} %collective-permute-done.6.came_e, ...), custom_call_target="tpu_custom_call", output_to_operand_aliasing={{}: (6, {})} | custom-call | flops 2000000 | bytes 2000000 | tf_op jit(solution)/shard_map/pallas_call | solution.py:512
  (23 shorter events, 0.2 us)
Async XLA Ops:
  0.9 8.5 %collective-permute-start = (f32[2,2,4,16,128]{4,3,2,1,0:T(8,128)S(1)}, f32[2,2,4,16,128]{4,3,2,1,0:T(8,128)S(1)}, u32[]{:S(2)}, u32[]{:S(2)}) collective-permute-start(f32[2,2,4,16,128]{4,3,2,1,0:T(8,128)S(1)} %fusion.1), channel_id=1, source_target_pairs={{0,4},{1,5},{2,6},{3,7},{4,0},{5,1},{6,2},{7,3},{8,12},{9,13},{10,... | collective-permute-start | bytes 393224 | tf_op jit(solution)/shard_map/ppermute | solution.py:455
  9.4 10.0 %copy-start.1 = (f32[2,128,128]{2,1,0:T(8,128)S(1)}, f32[2,128,128]{2,1,0:T(8,128)}, u32[]{:S(2)}) copy-start(f32[2,128,128]{2,1,0:T(8,128)} %param.8) | copy-start | bytes 393220
  9.4 10.0 %copy-start.2 = (f32[2,128,128]{2,1,0:T(8,128)S(1)}, f32[2,128,128]{2,1,0:T(8,128)}, u32[]{:S(2)}) copy-start(f32[2,128,128]{2,1,0:T(8,128)} %param.9) | copy-start | bytes 393220
  9.4 72.5 %all-to-all-start = ((f32[128,77,1,128]{3,2,1,0:T(1,128)}), f32[128,77,1,128]{3,2,1,0:T(1,128)}, u32[]{:S(2)}, u32[]{:S(2)}) async-start(f32[128,77,1,128]{3,2,1,0:T(1,128)} %bitcast.40), calls=%async_computation | async-start | bytes 10092544 | tf_op jit(solution)/shard_map/all_to_all | solution.py:479
  19.3 62.3 %copy-start.3 = (s32[16,16,128]{2,1,0:T(8,128)S(1)}, s32[16,16,128]{2,1,0:T(8,128)}, u32[]{:S(2)}) copy-start(s32[16,16,128]{2,1,0:T(8,128)} %param.10) | copy-start | bytes 393220
  19.5 55.6 %collective-permute-start.3 = (f32[2,2,2,16,128]{4,3,2,0,1:T(8,128)S(1)}, f32[2,2,2,16,128]{4,3,2,0,1:T(8,128)S(1)}, u32[]{:S(2)}, u32[]{:S(2)}) collective-permute-start(f32[2,2,2,16,128]{4,3,2,0,1:T(8,128)S(1)} %bitcast.49), channel_id=1, source_target_pairs={{0,3},{1,2},{2,1},{3,0},{4,7},{5,6},{6,5},{7,4},{8,11},{9,10},{10,... | collective-permute-start | bytes 196616 | tf_op jit(solution)/shard_map/ppermute | solution.py:465
  21.8 57.3 %collective-permute-start.2 = (f32[2,2,2,16,128]{4,3,2,0,1:T(8,128)S(1)}, f32[2,2,2,16,128]{4,3,2,0,1:T(8,128)S(1)}, u32[]{:S(2)}, u32[]{:S(2)}) collective-permute-start(f32[2,2,2,16,128]{4,3,2,0,1:T(8,128)S(1)} %bitcast.50), channel_id=1, source_target_pairs={{0,2},{1,3},{2,0},{3,1},{4,6},{5,7},{6,4},{7,5},{8,10},{9,11},{10,... | collective-permute-start | bytes 196616 | tf_op jit(solution)/shard_map/ppermute | solution.py:465
  22.6 58.9 %collective-permute-start.1 = (f32[2,2,2,16,128]{4,3,2,0,1:T(8,128)S(1)}, f32[2,2,2,16,128]{4,3,2,0,1:T(8,128)S(1)}, u32[]{:S(2)}, u32[]{:S(2)}) collective-permute-start(f32[2,2,2,16,128]{4,3,2,0,1:T(8,128)S(1)} %bitcast.51), channel_id=1, source_target_pairs={{0,1},{1,0},{2,3},{3,2},{4,5},{5,4},{6,7},{7,6},{8,9},{9,8},{10,11... | collective-permute-start | bytes 196616 | tf_op jit(solution)/shard_map/ppermute | solution.py:465
  81.7 3.5 %copy-start = (f32[3]{0:T(128)S(1)}, f32[3]{0:T(128)}, u32[]{:S(2)}) copy-start(f32[3]{0:T(128)} %force.7) | copy-start | bytes 40
  86.3 6.1 %collective-permute-start.4 = (f32[21,16,128]{2,1,0:T(8,128)S(1)}, f32[21,16,128]{2,1,0:T(8,128)S(1)}, u32[]{:S(2)}, u32[]{:S(2)}) collective-permute-start(f32[21,16,128]{2,1,0:T(8,128)S(1)} %get-tuple-element.17), channel_id=1, source_target_pairs={{0,8},{8,0},{16,24},{24,16},{32,40},{40,32},{48,56},{56,48},{64,72... | collective-permute-start | bytes 516104 | tf_op jit(solution)/shard_map/ppermute | solution.py:447
  86.4 7.0 %collective-permute-start.5 = (f32[21,16,128]{2,1,0:T(8,128)S(1)}, f32[21,16,128]{2,1,0:T(8,128)S(1)}, u32[]{:S(2)}, u32[]{:S(2)}) collective-permute-start(f32[21,16,128]{2,1,0:T(8,128)S(1)} %get-tuple-element.18), channel_id=1, source_target_pairs={{0,120},{8,16},{16,8},{24,32},{32,24},{40,48},{48,40},{56,64},{64,... | collective-permute-start | bytes 516104 | tf_op jit(solution)/shard_map/ppermute | solution.py:447
  94.0 7.8 %collective-permute-start.6 = (f32[432,128]{1,0:T(8,128)S(1)}, f32[432,128]{1,0:T(8,128)S(1)}, u32[]{:S(2)}, u32[]{:S(2)}) collective-permute-start(f32[432,128]{1,0:T(8,128)S(1)} %get-tuple-element.22.mine_e), channel_id=1, source_target_pairs={{0,1},{1,0},{2,3},{3,2},{4,5},{5,4},{6,7},{7,6},{8,9},{9,8},{10,11... | collective-permute-start | bytes 663560 | tf_op jit(solution)/shard_map/ppermute | solution.py:447
  94.9 9.5 %collective-permute-start.7 = (f32[432,128]{1,0:T(8,128)S(1)}, f32[432,128]{1,0:T(8,128)S(1)}, u32[]{:S(2)}, u32[]{:S(2)}) collective-permute-start(f32[432,128]{1,0:T(8,128)S(1)} %get-tuple-element.23.mine_o), channel_id=1, source_target_pairs={{0,7},{1,2},{2,1},{3,4},{4,3},{5,6},{6,5},{7,0},{8,15},{9,10},{10,... | collective-permute-start | bytes 663560 | tf_op jit(solution)/shard_map/ppermute | solution.py:447

commit v4 on v3

--- a/solution.py
+++ b/solution.py
@@ -108,7 +108,7 @@
     return value if c == 0 else pltpu.roll(value, c % 128, 1)
 
 
-def pack_kernel(target_hbm, pdf_hbm, out_hbm, target, used, pdf, out3, sems, small):
+def pack_kernel(target_hbm, pdf_hbm, out, target, used, pdf, tiles, labels, sems, small, sent):
     listing = pltpu.make_async_copy(target_hbm, target, small.at[0])
     listing.start()
     quarters = []
@@ -118,13 +118,13 @@
         copy.start()
         quarters.append(copy)
     flat = pdf.reshape(19 * 256, 128)
-    out = out3.reshape(DEVICES * PAIR, 128)
-
-    empty = jnp.full((1, 128), -1.0, F32)
+    rows_ = tiles.reshape(HELD * TILE, 128)
+    empty = jnp.full((8, 128), -1.0, F32)
+    for block in range(DEVICES // 8):
+        labels[8 * block : 8 * block + 8, 0, :] = empty
 
     def clear(i, _):
         used[i] = 0
-        out[pl.ds(i * PAIR + 2 * TILE, 1), :] = empty
         return 0
 
     lax.fori_loop(0, DEVICES, clear, 0, unroll=8)
@@ -136,39 +136,46 @@
         owner = lax.shift_right_logical(t, 7)
         rank = used[owner]
         used[owner] = rank + 1
-        start = owner * PAIR + rank * TILE
         near = lax.shift_right_logical(k, 3) * 16 + (k & 7)
         for r in range(2):
             for q in (0, 8, 16):
                 n = min(8, 19 - q)
                 value = flat[pl.ds(near + r * 8 + q * 256, n, stride=256), :]
-                out[pl.ds(start + r * 19 + q, n), :] = value
-        line = pl.ds(owner * PAIR + 2 * TILE, 1)
-        out[line, :] = jnp.where(half == rank, (t & 127).astype(F32), out[line, :])
+                rows_[pl.ds(k * TILE + r * 19 + q, n), :] = value
+        pltpu.make_async_copy(
+            tiles.at[pl.ds(k * TILE, TILE)],
+            out.at[owner, pl.ds(rank * TILE, TILE)],
+            sent,
+        ).start()
+        line = labels[owner]
+        labels[owner] = jnp.where(half == rank, (t & 127).astype(F32), line)
         return 0
 
     for part in range(4):
         quarters[part].wait()
         lax.fori_loop(part * 32, part * 32 + 32, put, 0, unroll=4)
-    done = pltpu.make_async_copy(out3, out_hbm, small.at[1])
-    done.start()
-    done.wait()
+    named = pltpu.make_async_copy(labels, out.at[:, 2 * TILE], small.at[1])
+    named.start()
+    pltpu.make_async_copy(tiles, tiles, sent).wait()
+    named.wait()
 
 
 def pack(target, pdf):
     hbm = pl.BlockSpec(memory_space=pltpu.HBM)
     return pl.pallas_call(
         pack_kernel,
-        out_shape=jax.ShapeDtypeStruct((DEVICES * PAIR, 1, 128), F32),
+        out_shape=jax.ShapeDtypeStruct((DEVICES, PAIR, 1, 128), F32),
         in_specs=[hbm, hbm],
         out_specs=hbm,
         scratch_shapes=[
             pltpu.SMEM((HELD,), jnp.int32),
             pltpu.SMEM((DEVICES,), jnp.int32),
             pltpu.VMEM((19, 256, 128), F32),
-            pltpu.VMEM((DEVICES * PAIR, 1, 128), F32),
+            pltpu.VMEM((HELD * TILE, 1, 128), F32),
+            pltpu.VMEM((DEVICES, 1, 128), F32),
             pltpu.SemaphoreType.DMA((4,)),
             pltpu.SemaphoreType.DMA((2,)),
+            pltpu.SemaphoreType.DMA,
         ],
         compiler_params=pltpu.CompilerParams(vmem_limit_bytes=VMEM_MOST),
         cost_estimate=pl.CostEstimate(flops=0, bytes_accessed=8_000_000, transcendentals=0),
@@ -455,7 +462,7 @@
     return mine, lax.ppermute(other, "gy", [(i, i ^ 4) for i in range(8)])
 
 
-def blocks_of(mine, came):
+def pieces_of(mine, came):
     b = lax.axis_index("gy")
     hi, lo = b // 4, b % 4
     both = jnp.stack([jnp.where(hi == 0, mine, came), jnp.where(hi == 0, came, mine)])
@@ -463,6 +470,11 @@
     for k in range(1, 4):
         message = lax.dynamic_index_in_dim(both, lo ^ k, axis=3, keepdims=False)
         parts.append(lax.ppermute(message, "gy", [(i, i ^ k) for i in range(8)]))
+    return parts
+
+
+def block_of(parts):
+    lo = lax.axis_index("gy") % 4
     stacked = jnp.stack(parts)
     ordered = [
         lax.dynamic_index_in_dim(stacked, lo ^ y, axis=0, keepdims=False) for y in range(4)
@@ -477,13 +489,14 @@
     packed = pack(tile_target, rows)
     packed, came = lax.optimization_barrier((packed, came))
     arrived = lax.all_to_all(
-        packed.reshape(DEVICES, PAIR, 1, 128), ("gx", "gy"), split_axis=0, concat_axis=0, tiled=True
+        packed, ("gx", "gy"), split_axis=0, concat_axis=0, tiled=True
     )
-    block = blocks_of(mine, came)
+    parts = pieces_of(mine, came)
+    tiles, parts[0] = lax.optimization_barrier((place(arrived), parts[0]))
+    block = block_of(parts)
     solid = block[0] + solid_mask.astype(F32) * (1.0 - block[0])
     coef = jnp.stack([solid, block[1]])
     odd = jnp.stack([lax.axis_index("gx") % 2, lax.axis_index("gy") % 2]).astype(jnp.int32)
-    tiles = place(arrived)
     posts = [jax.ShapeDtypeStruct((19, n, 16, 128), F32) for n in (4, 12)]
     edge, xe, xo = call(
         edge_kernel, [posts[0], FACE, FACE], (force, odd, tiles, coef), 2_000_000, scalars=2

time: 106 us -> 107 us (level)
  waiting for transfers between devices: 61.6 us -> 64.8 us
  Pallas kernels: 18.9 us -> 17.3 us
  starting transfers between devices: 24.2 us -> 22.7 us
    all_to_all x1, waiting for transfers between devices: 0.16 us -> 58.1 us  [local(): lax.all_to_all(packed, ('gx', 'gy'), split_axis=0, concat_axis=0, tiled=T...]
    ppermute x3, waiting for transfers between devices: 57.7 us -> 0.01 us  [pieces_of(): parts.append(lax.ppermute(message, 'gy', [(i, i ^ k) for i in range(8)]))]
    ppermute x4, starting transfers between devices: 6.88 us -> 3.8 us  [swap(): return lax.ppermute(value, axis, pairs)]
    ppermute x4, waiting for transfers between devices: 3.67 us -> 6.74 us  [swap(): return lax.ppermute(value, axis, pairs)]
    pallas_call x1, Pallas kernels: 5.28 us -> 3.71 us  [pack(): pl.pallas_call(pack_kernel, out_shape=jax.ShapeDtypeStruct((DEVICES, PAIR...]
    all_to_all x1, starting transfers between devices: 9.92 us -> 11.5 us  [local(): lax.all_to_all(packed, ('gx', 'gy'), split_axis=0, concat_axis=0, tiled=T...]
  transfers between devices with their start and end apart: 9 -> 9, of which waited for: 6 -> 3; matrix products, arithmetic and copies ran while one was open for 0% -> 0% of each run, Pallas kernels for 12% -> 13%
where the time goes in v4:
time: 107 us
  waiting for transfers between devices  64.8 us (61%)
  starting transfers between devices  22.7 us (21%)
  Pallas kernels  17.3 us (16%)
  other arithmetic  1.09 us (1%)
    all_to_all x1, waiting for transfers between devices, local(): lax.all_to_all(packed, ('gx', 'gy'), split_axis=0, concat_axis=0, tiled=T...  58.1 us
    all_to_all x1, starting transfers between devices, local(): lax.all_to_all(packed, ('gx', 'gy'), split_axis=0, concat_axis=0, tiled=T...  11.5 us
    pallas_call x4, Pallas kernels, call(): pl.pallas_call(kernel, out_shape=out_shape, in_specs=[SMEM_SPEC] * scalar...  8.71 us
    ppermute x4, waiting for transfers between devices, swap(): return lax.ppermute(value, axis, pairs)  6.74 us
    ppermute x3, starting transfers between devices, pieces_of(): parts.append(lax.ppermute(message, 'gy', [(i, i ^ k) for i in range(8)]))  4.17 us
    ppermute x4, starting transfers between devices, swap(): return lax.ppermute(value, axis, pairs)  3.8 us
    pallas_call x1, Pallas kernels, pack(): pl.pallas_call(pack_kernel, out_shape=jax.ShapeDtypeStruct((DEVICES, PAIR...  3.71 us
    pallas_call x1, Pallas kernels, place(): pl.pallas_call(place_kernel, out_shape=jax.ShapeDtypeStruct((HELD * ROWS,...  3.28 us
  transfers between devices with their start and end apart: 9, of which 3 were waited for; matrix products, arithmetic and copies ran while one was open for 0% of the time, Pallas kernels for 13%

profile of v4, /device:TPU:0, one launch (start us, length us, event | category | flops | bytes accessed | tf_op | source)
XLA Modules:
  0.0 106.7 jit_solution(3513132882182513732)
XLA Ops:
  0.0 0.9 fusion.1
  0.9 3.2 %collective-permute-start = (f32[2,2,4,16,128]{4,3,2,1,0:T(8,128)S(1)}, f32[2,2,4,16,128]{4,3,2,1,0:T(8,128)S(1)}, u32[]{:S(2)}, u32[]{:S(2)}) collective-permute-start(f32[2,2,4,16,128]{4,3,2,1,0:T(8,128)S(1)} %fusion.1), channel_id=1, source_target_pairs={{0,4},{1,5},{2,6},{3,7},{4,0},{5,1},{6,2},{7,3},{8,12},{9,13},{10,... | collective-permute-start | bytes 393224 | tf_op jit(solution)/shard_map/ppermute | solution.py:462
  4.1 3.7 %shard_map.64 = f32[128,77,1,128]{3,2,1,0:T(1,128)} custom-call(s32[128]{0:T(128)} %target_hbm.1, f32[19,256,128]{2,1,0:T(8,128)} %bitcast.40), custom_call_target="tpu_custom_call" | custom-call | bytes 8000000 | tf_op jit(solution)/shard_map/pallas_call | solution.py:165
  7.8 0.0 copy-start.1
  7.8 0.0 copy-start.2
  7.8 11.5 %all-to-all-start = ((f32[128,77,1,128]{3,2,1,0:T(1,128)}), f32[128,77,1,128]{3,2,1,0:T(1,128)}, u32[]{:S(2)}, u32[]{:S(2)}) async-start(f32[128,77,1,128]{3,2,1,0:T(1,128)} %shard_map.64), calls=%async_computation | async-start | bytes 10092544 | tf_op jit(solution)/shard_map/all_to_all | solution.py:491
  19.5 2.2 %collective-permute-start.3 = (f32[2,2,2,16,128]{4,3,2,0,1:T(8,128)S(1)}, f32[2,2,2,16,128]{4,3,2,0,1:T(8,128)S(1)}, u32[]{:S(2)}, u32[]{:S(2)}) collective-permute-start(f32[2,2,2,16,128]{4,3,2,0,1:T(8,128)S(1)} %bitcast.48), channel_id=1, source_target_pairs={{0,3},{1,2},{2,1},{3,0},{4,7},{5,6},{6,5},{7,4},{8,11},{9,10},{10,... | collective-permute-start | bytes 196616 | tf_op jit(solution)/shard_map/ppermute | solution.py:472
  21.7 0.8 collective-permute-start.2
  22.5 1.1 %collective-permute-start.1 = (f32[2,2,2,16,128]{4,3,2,0,1:T(8,128)S(1)}, f32[2,2,2,16,128]{4,3,2,0,1:T(8,128)S(1)}, u32[]{:S(2)}, u32[]{:S(2)}) collective-permute-start(f32[2,2,2,16,128]{4,3,2,0,1:T(8,128)S(1)} %bitcast.50), channel_id=1, source_target_pairs={{0,1},{1,0},{2,3},{3,2},{4,5},{5,4},{6,7},{7,6},{8,9},{9,8},{10,11... | collective-permute-start | bytes 196616 | tf_op jit(solution)/shard_map/ppermute | solution.py:472
  23.7 0.1 pad_add_fusion.odd
  23.8 58.1 %all-to-all-done.arrived = f32[128,77,1,128]{3,2,1,0:T(1,128)} async-done(((f32[128,77,1,128]{3,2,1,0:T(1,128)}), f32[128,77,1,128]{3,2,1,0:T(1,128)}, u32[]{:S(2)}, u32[]{:S(2)}) %all-to-all-start) | async-done | bytes 5046304 | tf_op jit(solution)/shard_map/all_to_all | solution.py:491
  81.8 3.3 %shard_map.65.tiles = f32[5120,128]{1,0:T(8,128)S(1)} custom-call(f32[128,77,1,128]{3,2,1,0:T(1,128)} %all-to-all-done.arrived), custom_call_target="tpu_custom_call" | custom-call | bytes 8000000 | tf_op jit(solution)/shard_map/pallas_call | solution.py:220
  85.4 0.4 copy-done
  85.8 1.1 %shard_map.66 = (f32[19,4,16,128]{3,2,1,0:T(8,128)S(1)}, f32[21,16,128]{2,1,0:T(8,128)S(1)}, f32[21,16,128]{2,1,0:T(8,128)S(1)}) custom-call(f32[3]{0:T(128)S(1)} %copy-done, s32[2]{0:T(128)S(1)} %pad_add_fusion.odd, f32[5120,128]{1,0:T(8,128)S(1)} %shard_map.65.tiles, f32[2,16,16,128]{3,2,1,0:T(8,128)S(1)} %pad_maximum_fusion.1.coef), custom_call_target="tpu_custom_call" | custom-call | flops 2000000 | bytes 2000000 | tf_op jit(solution)/shard_map/pallas_call | solution.py:303
  86.9 0.1 collective-permute-start.4
  87.0 1.1 %collective-permute-start.5 = (f32[21,16,128]{2,1,0:T(8,128)S(1)}, f32[21,16,128]{2,1,0:T(8,128)S(1)}, u32[]{:S(2)}, u32[]{:S(2)}) collective-permute-start(f32[21,16,128]{2,1,0:T(8,128)S(1)} %get-tuple-element.22), channel_id=1, source_target_pairs={{0,120},{8,16},{16,8},{24,32},{32,24},{40,48},{48,40},{56,64},{64,... | collective-permute-start | bytes 516104 | tf_op jit(solution)/shard_map/ppermute | solution.py:454
  88.1 2.4 %shard_map.67 = (f32[19,12,16,128]{3,2,1,0:T(8,128)S(1)}, f32[21,16,128]{2,1,0:T(8,128)S(1)}, f32[21,16,128]{2,1,0:T(8,128)S(1)}) custom-call(f32[3]{0:T(128)S(1)} %copy-done, f32[5120,128]{1,0:T(8,128)S(1)} %shard_map.65.tiles, f32[2,16,16,128]{3,2,1,0:T(8,128)S(1)} %pad_maximum_fusion.1.coef, f32[19,4,16,128]{3,2,1,0:T(8,128)S(1)} %get-tuple-element.23.edge), custom_call_target="tpu_custom_call" | custom-call | flops 6000000 | bytes 6000000 | tf_op jit(solution)/shard_map/pallas_call | solution.py:303
  90.6 3.5 %collective-permute-done.5.xo = f32[21,16,128]{2,1,0:T(8,128)S(1)} collective-permute-done((f32[21,16,128]{2,1,0:T(8,128)S(1)}, f32[21,16,128]{2,1,0:T(8,128)S(1)}, u32[]{:S(2)}, u32[]{:S(2)}) %collective-permute-start.5) | collective-permute-done | bytes 172064 | tf_op jit(solution)/shard_map/ppermute | solution.py:454
  94.1 0.6 shard_map.68
  94.7 0.9 collective-permute-start.6
  95.6 1.7 %collective-permute-start.7 = (f32[432,128]{1,0:T(8,128)S(1)}, f32[432,128]{1,0:T(8,128)S(1)}, u32[]{:S(2)}, u32[]{:S(2)}) collective-permute-start(f32[432,128]{1,0:T(8,128)S(1)} %get-tuple-element.27.mine_o), channel_id=1, source_target_pairs={{0,7},{1,2},{2,1},{3,4},{4,3},{5,6},{6,5},{7,0},{8,15},{9,10},{10,... | collective-permute-start | bytes 663560 | tf_op jit(solution)/shard_map/ppermute | solution.py:454
  97.3 4.5 %shard_map.69._before = f32[19,16,16,128]{3,2,1,0:T(8,128)} custom-call(f32[3]{0:T(128)S(1)} %copy-done, s32[2]{0:T(128)S(1)} %pad_add_fusion.odd, f32[19,4,16,128]{3,2,1,0:T(8,128)S(1)} %get-tuple-element.23.edge, f32[19,12,16,128]{3,2,1,0:T(8,128)S(1)} %get-tuple-element.28.inner, f32[2,16,16,128]{3,2,1,0:T(8,128)S(1)} %pad_maximum_fusion.1.coef, ...), custom_call_target="tpu_custom_call" | custom-call | flops 12000000 | bytes 12000000 | tf_op jit(solution)/shard_map/pallas_call | solution.py:303
  101.8 3.3 %collective-permute-done.7.came_o = f32[432,128]{1,0:T(8,128)S(1)} collective-permute-done((f32[432,128]{1,0:T(8,128)S(1)}, f32[432,128]{1,0:T(8,128)S(1)}, u32[]{:S(2)}, u32[]{:S(2)}) %collective-permute-start.7) | collective-permute-done | bytes 221216 | tf_op jit(solution)/shard_map/ppermute | solution.py:454
  105.1 1.6 %shard_map.70 = f32[19,16,16,128]{3,2,1,0:T(8,128)} custom-call(f32[3]{0:T(128)S(1)} %copy-done, s32[2]{0:T(128)S(1)} %pad_add_fusion.odd, f32[432,128]{1,0:T(8,128)S(1)} %get-tuple-element.26.mine_e, f32[432,128]{1,0:T(8,128)S(1)} %get-tuple-element.27.mine_o, f32[432,128]{1,0:T(8,128)S(1)} %collective-permute-done.6.came_e, ...), custom_call_target="tpu_custom_call", output_to_operand_aliasing={{}: (6, {})} | custom-call | flops 2000000 | bytes 2000000 | tf_op jit(solution)/shard_map/pallas_call | solution.py:525
  (23 shorter events, 0.2 us)
Async XLA Ops:
  0.9 6.9 %collective-permute-start = (f32[2,2,4,16,128]{4,3,2,1,0:T(8,128)S(1)}, f32[2,2,4,16,128]{4,3,2,1,0:T(8,128)S(1)}, u32[]{:S(2)}, u32[]{:S(2)}) collective-permute-start(f32[2,2,4,16,128]{4,3,2,1,0:T(8,128)S(1)} %fusion.1), channel_id=1, source_target_pairs={{0,4},{1,5},{2,6},{3,7},{4,0},{5,1},{6,2},{7,3},{8,12},{9,13},{10,... | collective-permute-start | bytes 393224 | tf_op jit(solution)/shard_map/ppermute | solution.py:462
  7.8 11.6 %copy-start.1 = (f32[2,128,128]{2,1,0:T(8,128)S(1)}, f32[2,128,128]{2,1,0:T(8,128)}, u32[]{:S(2)}) copy-start(f32[2,128,128]{2,1,0:T(8,128)} %param.8) | copy-start | bytes 393220
  7.8 11.6 %copy-start.2 = (f32[2,128,128]{2,1,0:T(8,128)S(1)}, f32[2,128,128]{2,1,0:T(8,128)}, u32[]{:S(2)}) copy-start(f32[2,128,128]{2,1,0:T(8,128)} %param.9) | copy-start | bytes 393220
  7.8 74.0 %all-to-all-start = ((f32[128,77,1,128]{3,2,1,0:T(1,128)}), f32[128,77,1,128]{3,2,1,0:T(1,128)}, u32[]{:S(2)}, u32[]{:S(2)}) async-start(f32[128,77,1,128]{3,2,1,0:T(1,128)} %shard_map.64), calls=%async_computation | async-start | bytes 10092544 | tf_op jit(solution)/shard_map/all_to_all | solution.py:491
  19.5 65.7 %collective-permute-start.3 = (f32[2,2,2,16,128]{4,3,2,0,1:T(8,128)S(1)}, f32[2,2,2,16,128]{4,3,2,0,1:T(8,128)S(1)}, u32[]{:S(2)}, u32[]{:S(2)}) collective-permute-start(f32[2,2,2,16,128]{4,3,2,0,1:T(8,128)S(1)} %bitcast.48), channel_id=1, source_target_pairs={{0,3},{1,2},{2,1},{3,0},{4,7},{5,6},{6,5},{7,4},{8,11},{9,10},{10,... | collective-permute-start | bytes 196616 | tf_op jit(solution)/shard_map/ppermute | solution.py:472
  21.7 63.4 %collective-permute-start.2 = (f32[2,2,2,16,128]{4,3,2,0,1:T(8,128)S(1)}, f32[2,2,2,16,128]{4,3,2,0,1:T(8,128)S(1)}, u32[]{:S(2)}, u32[]{:S(2)}) collective-permute-start(f32[2,2,2,16,128]{4,3,2,0,1:T(8,128)S(1)} %bitcast.49), channel_id=1, source_target_pairs={{0,2},{1,3},{2,0},{3,1},{4,6},{5,7},{6,4},{7,5},{8,10},{9,11},{10,... | collective-permute-start | bytes 196616 | tf_op jit(solution)/shard_map/ppermute | solution.py:472
  22.5 62.6 %collective-permute-start.1 = (f32[2,2,2,16,128]{4,3,2,0,1:T(8,128)S(1)}, f32[2,2,2,16,128]{4,3,2,0,1:T(8,128)S(1)}, u32[]{:S(2)}, u32[]{:S(2)}) collective-permute-start(f32[2,2,2,16,128]{4,3,2,0,1:T(8,128)S(1)} %bitcast.50), channel_id=1, source_target_pairs={{0,1},{1,0},{2,3},{3,2},{4,5},{5,4},{6,7},{7,6},{8,9},{9,8},{10,11... | collective-permute-start | bytes 196616 | tf_op jit(solution)/shard_map/ppermute | solution.py:472
  23.8 61.5 %copy-start.3 = (s32[16,16,128]{2,1,0:T(8,128)S(1)}, s32[16,16,128]{2,1,0:T(8,128)}, u32[]{:S(2)}) copy-start(s32[16,16,128]{2,1,0:T(8,128)} %param.10) | copy-start | bytes 393220
  85.1 0.7 copy-start
  86.9 3.6 %collective-permute-start.4 = (f32[21,16,128]{2,1,0:T(8,128)S(1)}, f32[21,16,128]{2,1,0:T(8,128)S(1)}, u32[]{:S(2)}, u32[]{:S(2)}) collective-permute-start(f32[21,16,128]{2,1,0:T(8,128)S(1)} %get-tuple-element.21), channel_id=1, source_target_pairs={{0,8},{8,0},{16,24},{24,16},{32,40},{40,32},{48,56},{56,48},{64,72... | collective-permute-start | bytes 516104 | tf_op jit(solution)/shard_map/ppermute | solution.py:454
  87.0 7.0 %collective-permute-start.5 = (f32[21,16,128]{2,1,0:T(8,128)S(1)}, f32[21,16,128]{2,1,0:T(8,128)S(1)}, u32[]{:S(2)}, u32[]{:S(2)}) collective-permute-start(f32[21,16,128]{2,1,0:T(8,128)S(1)} %get-tuple-element.22), channel_id=1, source_target_pairs={{0,120},{8,16},{16,8},{24,32},{32,24},{40,48},{48,40},{56,64},{64,... | collective-permute-start | bytes 516104 | tf_op jit(solution)/shard_map/ppermute | solution.py:454
  94.7 7.2 %collective-permute-start.6 = (f32[432,128]{1,0:T(8,128)S(1)}, f32[432,128]{1,0:T(8,128)S(1)}, u32[]{:S(2)}, u32[]{:S(2)}) collective-permute-start(f32[432,128]{1,0:T(8,128)S(1)} %get-tuple-element.26.mine_e), channel_id=1, source_target_pairs={{0,1},{1,0},{2,3},{3,2},{4,5},{5,4},{6,7},{7,6},{8,9},{9,8},{10,11... | collective-permute-start | bytes 663560 | tf_op jit(solution)/shard_map/ppermute | solution.py:454
  95.6 9.5 %collective-permute-start.7 = (f32[432,128]{1,0:T(8,128)S(1)}, f32[432,128]{1,0:T(8,128)S(1)}, u32[]{:S(2)}, u32[]{:S(2)}) collective-permute-start(f32[432,128]{1,0:T(8,128)S(1)} %get-tuple-element.27.mine_o), channel_id=1, source_target_pairs={{0,7},{1,2},{2,1},{3,4},{4,3},{5,6},{6,5},{7,0},{8,15},{9,10},{10,... | collective-permute-start | bytes 663560 | tf_op jit(solution)/shard_map/ppermute | solution.py:454

commit v5 on v4

--- a/solution.py
+++ b/solution.py
@@ -182,58 +182,6 @@
     )(target, pdf)
 
 
-def place_kernel(arrived, tiles, labels, found, source, sem, small):
-    pull = pltpu.make_async_copy(arrived.at[:, 2 * TILE, 0, :], labels, small.at[0])
-    pull.start()
-    pull.wait()
-    lane = lax.broadcasted_iota(jnp.int32, (8, 128), 1)
-    lane_f = lane.astype(F32)
-    sub = lax.broadcasted_iota(jnp.int32, (8, 128), 0)
-    low = lane < 64
-    total = jnp.zeros((8, 128), jnp.int32)
-    for group in range(DEVICES // 8):
-        line = labels[8 * group : 8 * group + 8, :]
-        other = pltpu.roll(line, 64, 1)
-        number = (sub + 8 * group) * 2
-        total = total + jnp.where(jnp.where(low, line, other) == lane_f, number, 0)
-        total = total + jnp.where(jnp.where(low, other, line) == lane_f, number + 1, 0)
-    found[...] = jnp.broadcast_to(jnp.sum(total, axis=0, keepdims=True), (8, 128))
-    hand = pltpu.make_async_copy(found, source, small.at[1])
-    hand.start()
-    hand.wait()
-
-    def fetch(s, _):
-        p = source[0, s]
-        pltpu.make_async_copy(
-            arrived.at[lax.shift_right_logical(p, 1), pl.ds((p & 1) * TILE, TILE), 0, :],
-            tiles.at[pl.ds(pl.multiple_of(s * ROWS, 8), TILE), :],
-            sem,
-        ).start()
-        return 0
-
-    lax.fori_loop(0, HELD, fetch, 0, unroll=8)
-    whole = tiles.at[pl.ds(0, HELD * TILE), :]
-    pltpu.make_async_copy(whole, whole, sem).wait()
-
-
-def place(arrived):
-    return pl.pallas_call(
-        place_kernel,
-        out_shape=jax.ShapeDtypeStruct((HELD * ROWS, 128), F32),
-        in_specs=[pl.BlockSpec(memory_space=pltpu.HBM)],
-        out_specs=pl.BlockSpec(memory_space=pltpu.VMEM),
-        scratch_shapes=[
-            pltpu.VMEM((DEVICES, 128), F32),
-            pltpu.VMEM((8, 128), jnp.int32),
-            pltpu.SMEM((8, 128), jnp.int32),
-            pltpu.SemaphoreType.DMA,
-            pltpu.SemaphoreType.DMA((2,)),
-        ],
-        compiler_params=pltpu.CompilerParams(vmem_limit_bytes=VMEM_LIMIT),
-        cost_estimate=pl.CostEstimate(flops=0, bytes_accessed=8_000_000, transcendentals=0),
-    )(arrived)
-
-
 def pick(flag, even, odd):
     return jnp.where(flag == 0, even, odd)
 
@@ -251,11 +199,51 @@
             post[q, at, pl.ds(r, 8, stride=2), :] = shift_z(after[q], q)
 
 
-def edge_kernel(force, odd, tiles, coef, edge, xe, xo):
-    f = [force[axis] for axis in range(3)]
+def edge_kernel(
+    odd, force, arrived, coef, tiles, edge, xe, xo, labels, found, source, sems, small
+):
+    pull = pltpu.make_async_copy(arrived.at[:, 2 * TILE, 0, :], labels, small.at[0])
+    pull.start()
+    f = [force[axis : axis + 1, :] for axis in range(3)]
+    lane = lax.broadcasted_iota(jnp.int32, (8, 128), 1)
+    lane_f = lane.astype(F32)
+    sub = lax.broadcasted_iota(jnp.int32, (8, 128), 0)
+    low = lane < 64
+    total = jnp.zeros((8, 128), jnp.int32)
+    pull.wait()
+    for group in range(DEVICES // 8):
+        line = labels[8 * group : 8 * group + 8, :]
+        other = pltpu.roll(line, 64, 1)
+        number = (sub + 8 * group) * 2
+        total = total + jnp.where(jnp.where(low, line, other) == lane_f, number, 0)
+        total = total + jnp.where(jnp.where(low, other, line) == lane_f, number + 1, 0)
+    found[...] = jnp.broadcast_to(jnp.sum(total, axis=0, keepdims=True), (8, 128))
+    hand = pltpu.make_async_copy(found, source, small.at[1])
+    hand.start()
+    hand.wait()
+
+    def fetch(s):
+        p = source[0, s]
+        pltpu.make_async_copy(
+            arrived.at[lax.shift_right_logical(p, 1), pl.ds((p & 1) * TILE, TILE), 0, :],
+            tiles.at[pl.ds(pl.multiple_of(s * ROWS, 8), TILE), :],
+            sems.at[lax.shift_right_logical(s, 3)],
+        ).start()
+
+    def arrive(x):
+        whole = tiles.at[pl.ds(0, 8 * TILE), :]
+        pltpu.make_async_copy(whole, whole, sems.at[x]).wait()
+
+    for x in (0, 1, 14, 15):
+        for i in range(8):
+            fetch(8 * x + i)
 
     def plane(j, _):
-        plane_step(jnp.where(j < 2, j, j + 12), j, tiles, coef, edge, f)
+        x = jnp.where(j < 2, j, j + 12)
+        for i in range(24):
+            fetch(16 + 24 * j + i)
+        arrive(x)
+        plane_step(x, j, tiles, coef, edge, f)
         return 0
 
     lax.fori_loop(0, 4, plane, 0)
@@ -268,10 +256,12 @@
         up, dn = coef[j, 15], coef[j, 0]
         xe[19 + j] = pick(flag, up, dn)
         xo[19 + j] = pick(flag, dn, up)
+    for x in range(2, 14):
+        arrive(x)
 
 
 def inner_kernel(force, tiles, coef, edge, inner, yup, ydn):
-    f = [force[axis] for axis in range(3)]
+    f = [force[axis : axis + 1, :] for axis in range(3)]
 
     def plane(j, _):
         plane_step(j + 2, j, tiles, coef, inner, f)
@@ -340,7 +330,7 @@
         out[COUNT * EXT : SIDE_ROWS, :] = jnp.zeros((SIDE_ROWS - COUNT * EXT, 128), F32)
 
 
-def middle_kernel(force, odd, edge, inner, coef, xe, xo, out, wide, again, result, sems):
+def middle_kernel(odd, force, edge, inner, coef, xe, xo, out, wide, again, result, sems):
     flag = odd[0]
     for j in range(4):
         for q in range(19):
@@ -359,7 +349,7 @@
             at = 1 - layer if toward == 0 else 18 + layer
             wide[q, at, 8:24, :] = pick(flag, even[i], odd_[i])
         sides.append([pick(flag, even[19 + j], odd_[19 + j]) for j in range(2)])
-    f = [force[axis] for axis in range(3)]
+    f = [force[axis : axis + 1, :] for axis in range(3)]
 
     def one(x, solids, omegas):
         for block in range(2):
@@ -396,7 +386,7 @@
         pltpu.make_async_copy(result.at[x], out.at[:, x], sems.at[x]).wait()
 
 
-def last_kernel(force, odd, mine_e, mine_o, came_e, came_o, _before, out, sides, rows, patch, sem):
+def last_kernel(odd, force, mine_e, mine_o, came_e, came_o, _before, out, sides, rows, patch, sem):
     flag = odd[1]
     for block in range(SIDE_ROWS // 8):
         part = slice(8 * block, 8 * block + 8)
@@ -405,7 +395,7 @@
         sides[1, part, :] = pick(flag, mo, me)
         sides[2, part, :] = pick(flag, ce, co)
         sides[3, part, :] = pick(flag, me, mo)
-    f = [force[axis] for axis in range(3)]
+    f = [force[axis : axis + 1, :] for axis in range(3)]
     number = 0
     for side, sign in ((0, 1), (1, -1)):
         came = {e: n for n, e in enumerate(entries(1, sign))}
@@ -455,32 +445,32 @@
 
 
 def halves_of(porosity, relaxation):
-    hi = lax.axis_index("gy") // 4
-    slab = jnp.stack([porosity, relaxation]).reshape(2, 2, 8, 16, 128)
-    other = lax.dynamic_slice_in_dim(slab, (1 - hi) * 4, 4, axis=2)
-    mine = lax.dynamic_slice_in_dim(slab, hi * 4, 4, axis=2)
-    return mine, lax.ppermute(other, "gy", [(i, i ^ 4) for i in range(8)])
+    lo = lax.axis_index("gy") % 2
+    slab = jnp.stack([porosity, relaxation]).reshape(2, 2, 4, 2, 16, 128)
+    other = lax.dynamic_index_in_dim(slab, 1 - lo, axis=3, keepdims=False)
+    mine = lax.dynamic_index_in_dim(slab, lo, axis=3, keepdims=False)
+    return mine, lax.ppermute(other, "gy", [(i, i ^ 1) for i in range(8)])
 
 
 def pieces_of(mine, came):
     b = lax.axis_index("gy")
-    hi, lo = b // 4, b % 4
-    both = jnp.stack([jnp.where(hi == 0, mine, came), jnp.where(hi == 0, came, mine)])
-    parts = [lax.dynamic_index_in_dim(both, lo, axis=3, keepdims=False)]
+    hi, lo = b // 2, b % 2
+    both = jnp.stack([jnp.where(lo == 0, mine, came), jnp.where(lo == 0, came, mine)])
+    parts = [lax.dynamic_index_in_dim(both, hi, axis=3, keepdims=False)]
     for k in range(1, 4):
-        message = lax.dynamic_index_in_dim(both, lo ^ k, axis=3, keepdims=False)
-        parts.append(lax.ppermute(message, "gy", [(i, i ^ k) for i in range(8)]))
+        message = lax.dynamic_index_in_dim(both, hi ^ k, axis=3, keepdims=False)
+        parts.append(lax.ppermute(message, "gy", [(i, i ^ (2 * k)) for i in range(8)]))
     return parts
 
 
 def block_of(parts):
-    lo = lax.axis_index("gy") % 4
+    hi = lax.axis_index("gy") // 2
     stacked = jnp.stack(parts)
     ordered = [
-        lax.dynamic_index_in_dim(stacked, lo ^ y, axis=0, keepdims=False) for y in range(4)
+        lax.dynamic_index_in_dim(stacked, hi ^ y, axis=0, keepdims=False) for y in range(4)
     ]
     whole = jnp.stack(ordered)
-    return whole.transpose(2, 1, 0, 3, 4, 5).reshape(2, 16, 16, 128)
+    return whole.transpose(2, 0, 1, 3, 4, 5).reshape(2, 16, 16, 128)
 
 
 def local(pdf_old, tile_target, porosity, relaxation, solid_mask, force):
@@ -491,29 +481,40 @@
     arrived = lax.all_to_all(
         packed, ("gx", "gy"), split_axis=0, concat_axis=0, tiled=True
     )
-    parts = pieces_of(mine, came)
-    tiles, parts[0] = lax.optimization_barrier((place(arrived), parts[0]))
-    block = block_of(parts)
+    block = block_of(pieces_of(mine, came))
     solid = block[0] + solid_mask.astype(F32) * (1.0 - block[0])
     coef = jnp.stack([solid, block[1]])
     odd = jnp.stack([lax.axis_index("gx") % 2, lax.axis_index("gy") % 2]).astype(jnp.int32)
+    drive = jnp.broadcast_to(jnp.pad(force, (0, 5))[:, None], (8, 128))
+    coef, odd, drive = lax.optimization_barrier((coef, odd, drive))
+    hbm = pl.BlockSpec(memory_space=pltpu.HBM)
     posts = [jax.ShapeDtypeStruct((19, n, 16, 128), F32) for n in (4, 12)]
-    edge, xe, xo = call(
-        edge_kernel, [posts[0], FACE, FACE], (force, odd, tiles, coef), 2_000_000, scalars=2
-    )
+    tiles, edge, xe, xo = pl.pallas_call(
+        edge_kernel,
+        out_shape=[jax.ShapeDtypeStruct((HELD * ROWS, 128), F32), posts[0], FACE, FACE],
+        in_specs=[SMEM_SPEC, VMEM_SPEC, hbm, VMEM_SPEC],
+        out_specs=[VMEM_SPEC] * 4,
+        scratch_shapes=[
+            pltpu.VMEM((DEVICES, 128), F32),
+            pltpu.VMEM((8, 128), jnp.int32),
+            pltpu.SMEM((8, 128), jnp.int32),
+            pltpu.SemaphoreType.DMA((16,)),
+            pltpu.SemaphoreType.DMA((2,)),
+        ],
+        compiler_params=pltpu.CompilerParams(vmem_limit_bytes=VMEM_LIMIT),
+        cost_estimate=pl.CostEstimate(flops=2_000_000, bytes_accessed=8_000_000, transcendentals=0),
+    )(odd, drive, arrived, coef)
     from_xe, from_xo = swap(xe, "gx", True), swap(xo, "gx", False)
     inner, yup, ydn = call(
-        inner_kernel, [posts[1], FACE, FACE], (force, tiles, coef, edge), 6_000_000
+        inner_kernel, [posts[1], FACE, FACE], (drive, tiles, coef, edge), 6_000_000, scalars=0
     )
     ye, yo = call(join_kernel, [SIDE, SIDE], (odd, from_xe, from_xo, yup, ydn), 500_000)
     from_ye, from_yo = swap(ye, "gy", True), swap(yo, "gy", False)
-    hbm = pl.BlockSpec(memory_space=pltpu.HBM)
     result = call(
         middle_kernel,
         jax.ShapeDtypeStruct((19, 16, 16, 128), F32),
-        (force, odd, edge, inner, coef, from_xe, from_xo),
+        (odd, drive, edge, inner, coef, from_xe, from_xo),
         12_000_000,
-        scalars=2,
         out_specs=hbm,
         scratch_shapes=[
             pltpu.VMEM((19, EXT, 32, 128), F32),
@@ -525,7 +526,7 @@
     return pl.pallas_call(
         last_kernel,
         out_shape=jax.ShapeDtypeStruct((19, 16, 16, 128), F32),
-        in_specs=[SMEM_SPEC] * 2 + [VMEM_SPEC] * 4 + [hbm],
+        in_specs=[SMEM_SPEC] + [VMEM_SPEC] * 5 + [hbm],
         out_specs=hbm,
         input_output_aliases={6: 0},
         scratch_shapes=[
@@ -536,7 +537,7 @@
         ],
         compiler_params=pltpu.CompilerParams(vmem_limit_bytes=VMEM_LIMIT),
         cost_estimate=pl.CostEstimate(flops=2_000_000, bytes_accessed=2_000_000, transcendentals=0),
-    )(force, odd, ye, yo, from_ye, from_yo, result)
+    )(odd, drive, ye, yo, from_ye, from_yo, result)
 
 
 def solution(mesh):

time: 107 us -> 106 us (level)
  waiting for transfers between devices: 64.8 us -> 58.8 us
  starting transfers between devices: 22.7 us -> 27.5 us
    all_to_all x1, waiting for transfers between devices: 58.1 us -> 0.64 us  [local(): lax.all_to_all(packed, ('gx', 'gy'), split_axis=0, concat_axis=0, tiled=T...]
    ppermute x4, waiting for transfers between devices: 0.01 us -> 54.8 us  [the longest x3 54.8 us: pieces_of(): lax.ppermute(message, 'gy', [(i, i ^ 2 * k) for i in range(8)])]
    ppermute x4, starting transfers between devices: 3.8 us -> 7.72 us  [swap(): return lax.ppermute(value, axis, pairs)]
    ppermute x4, waiting for transfers between devices: 6.74 us -> 3.34 us  [swap(): return lax.ppermute(value, axis, pairs)]
    pallas_call x4 -> x3, Pallas kernels: 8.71 us -> 7.05 us  [call(): pl.pallas_call(kernel, out_shape=out_shape, in_specs=[SMEM_SPEC] * scalar...]
    pallas_call x1, Pallas kernels: 3.28 us -> 4.69 us  [local(): pl.pallas_call(edge_kernel, out_shape=[jax.ShapeDtypeStruct((HELD * ROWS,...]
  transfers between devices with their start and end apart: 9 -> 9, of which waited for: 3 -> 5; matrix products, arithmetic and copies ran while one was open for 0% -> 0% of each run, Pallas kernels for 13% -> 10%
where the time goes in v5:
time: 106 us; the launch traced here: 105 us
  waiting for transfers between devices  58.8 us (55%)
  starting transfers between devices  27.5 us (26%)
  Pallas kernels  17.1 us (16%)
  other arithmetic  1.1 us (1%)
    ppermute x3, waiting for transfers between devices, pieces_of(): lax.ppermute(message, 'gy', [(i, i ^ 2 * k) for i in range(8)])  54.8 us
    all_to_all x1, starting transfers between devices, local(): lax.all_to_all(packed, ('gx', 'gy'), split_axis=0, concat_axis=0, tiled=T...  11.4 us
    ppermute x4, starting transfers between devices, swap(): return lax.ppermute(value, axis, pairs)  7.72 us
    pallas_call x3, Pallas kernels, call(): pl.pallas_call(kernel, out_shape=out_shape, in_specs=[SMEM_SPEC] * scalar...  7.05 us
    ppermute x3, starting transfers between devices, pieces_of(): lax.ppermute(message, 'gy', [(i, i ^ 2 * k) for i in range(8)])  6.58 us
    pallas_call x1, Pallas kernels, local(): pl.pallas_call(edge_kernel, out_shape=[jax.ShapeDtypeStruct((HELD * ROWS,...  4.69 us
    pallas_call x1, Pallas kernels, pack(): pl.pallas_call(pack_kernel, out_shape=jax.ShapeDtypeStruct((DEVICES, PAIR...  3.7 us
    ppermute x4, waiting for transfers between devices, swap(): return lax.ppermute(value, axis, pairs)  3.34 us
  transfers between devices with their start and end apart: 9, of which 5 were waited for; matrix products, arithmetic and copies ran while one was open for 0% of the time, Pallas kernels for 10%

profile of v5, /device:TPU:0, one launch (start us, length us, event | category | flops | bytes accessed | tf_op | source)
XLA Modules:
  0.0 104.8 jit_solution(17607309907688556347)
XLA Ops:
  0.0 0.9 fusion.1
  0.9 1.7 %collective-permute-start = (f32[2,2,4,16,128]{4,3,2,1,0:T(8,128)S(1)}, f32[2,2,4,16,128]{4,3,2,1,0:T(8,128)S(1)}, u32[]{:S(2)}, u32[]{:S(2)}) collective-permute-start(f32[2,2,4,16,128]{4,3,2,1,0:T(8,128)S(1)} %fusion.1), channel_id=1, source_target_pairs={{0,1},{1,0},{2,3},{3,2},{4,5},{5,4},{6,7},{7,6},{8,9},{9,8},{10,11... | collective-permute-start | bytes 393224 | tf_op jit(solution)/shard_map/ppermute | solution.py:452
  2.6 3.7 %shard_map.64 = f32[128,77,1,128]{3,2,1,0:T(1,128)} custom-call(s32[128]{0:T(128)} %target_hbm.1, f32[19,256,128]{2,1,0:T(8,128)} %bitcast.43), custom_call_target="tpu_custom_call" | custom-call | bytes 8000000 | tf_op jit(solution)/shard_map/pallas_call | solution.py:165
  6.3 0.0 copy-start.3
  6.4 11.4 %all-to-all-start = ((f32[128,77,1,128]{3,2,1,0:T(1,128)}), f32[128,77,1,128]{3,2,1,0:T(1,128)}, u32[]{:S(2)}, u32[]{:S(2)}) async-start(f32[128,77,1,128]{3,2,1,0:T(1,128)} %shard_map.64), calls=%async_computation | async-start | bytes 10092544 | tf_op jit(solution)/shard_map/all_to_all | solution.py:481
  18.0 2.5 %collective-permute-start.1 = (f32[2,2,2,16,128]{4,3,2,1,0:T(8,128)S(1)}, f32[2,2,2,16,128]{4,3,2,1,0:T(8,128)S(1)}, u32[]{:S(2)}, u32[]{:S(2)}) collective-permute-start(f32[2,2,2,16,128]{4,3,2,1,0:T(8,128)S(1)} %get-tuple-element.42), channel_id=1, source_target_pairs={{0,2},{1,3},{2,0},{3,1},{4,6},{5,7},{6,4},{7,5},{8,10},{9,11},{10,... | collective-permute-start | bytes 196616 | tf_op jit(solution)/shard_map/ppermute | solution.py:462
  20.5 3.0 %collective-permute-start.2 = (f32[2,2,2,16,128]{4,3,2,1,0:T(8,128)S(1)}, f32[2,2,2,16,128]{4,3,2,1,0:T(8,128)S(1)}, u32[]{:S(2)}, u32[]{:S(2)}) collective-permute-start(f32[2,2,2,16,128]{4,3,2,1,0:T(8,128)S(1)} %get-tuple-element.43), channel_id=1, source_target_pairs={{0,4},{1,5},{2,6},{3,7},{4,0},{5,1},{6,2},{7,3},{8,12},{9,13},{10,... | collective-permute-start | bytes 196616 | tf_op jit(solution)/shard_map/ppermute | solution.py:462
  23.5 1.1 %collective-permute-start.3 = (f32[2,2,2,16,128]{4,3,2,1,0:T(8,128)S(1)}, f32[2,2,2,16,128]{4,3,2,1,0:T(8,128)S(1)}, u32[]{:S(2)}, u32[]{:S(2)}) collective-permute-start(f32[2,2,2,16,128]{4,3,2,1,0:T(8,128)S(1)} %get-tuple-element.44), channel_id=1, source_target_pairs={{0,6},{1,7},{2,4},{3,5},{4,2},{5,3},{6,0},{7,1},{8,14},{9,15},{10,... | collective-permute-start | bytes 196616 | tf_op jit(solution)/shard_map/ppermute | solution.py:462
  24.6 0.1 pad_add_fusion.odd
  24.7 52.4 %collective-permute-done.1 = f32[2,2,2,16,128]{4,3,2,1,0:T(8,128)S(1)} collective-permute-done((f32[2,2,2,16,128]{4,3,2,1,0:T(8,128)S(1)}, f32[2,2,2,16,128]{4,3,2,1,0:T(8,128)S(1)}, u32[]{:S(2)}, u32[]{:S(2)}) %collective-permute-start.1) | collective-permute-done | bytes 65568 | tf_op jit(solution)/shard_map/ppermute | solution.py:462
  77.1 2.3 %collective-permute-done.3 = f32[2,2,2,16,128]{4,3,2,1,0:T(8,128)S(1)} collective-permute-done((f32[2,2,2,16,128]{4,3,2,1,0:T(8,128)S(1)}, f32[2,2,2,16,128]{4,3,2,1,0:T(8,128)S(1)}, u32[]{:S(2)}, u32[]{:S(2)}) %collective-permute-start.3) | collective-permute-done | bytes 65568 | tf_op jit(solution)/shard_map/ppermute | solution.py:462
  79.6 0.1 broadcast_in_dim.2.force
  79.7 0.6 all-to-all-done.arrived
  80.3 4.7 %shard_map.65 = (f32[5120,128]{1,0:T(8,128)S(1)}, f32[19,4,16,128]{3,2,1,0:T(8,128)S(1)}, f32[21,16,128]{2,1,0:T(8,128)S(1)}, f32[21,16,128]{2,1,0:T(8,128)S(1)}) custom-call(s32[2]{0:T(128)S(1)} %pad_add_fusion.odd, f32[8,128]{1,0:T(8,128)S(1)} %broadcast_in_dim.2.force, f32[128,77,1,128]{3,2,1,0:T(1,128)} %all-to-all-done.arrived, ...), custom_call_target="tpu_custom_call" | custom-call | flops 2000000 | bytes 8000000 | tf_op jit(solution)/shard_map/pallas_call | solution.py:492
  85.0 0.1 collective-permute-start.4
  85.1 4.5 %collective-permute-start.5 = (f32[21,16,128]{2,1,0:T(8,128)S(1)}, f32[21,16,128]{2,1,0:T(8,128)S(1)}, u32[]{:S(2)}, u32[]{:S(2)}) collective-permute-start(f32[21,16,128]{2,1,0:T(8,128)S(1)} %get-tuple-element.25), channel_id=1, source_target_pairs={{0,120},{8,16},{16,8},{24,32},{32,24},{40,48},{48,40},{56,64},{64,... | collective-permute-start | bytes 516104 | tf_op jit(solution)/shard_map/ppermute | solution.py:444
  89.7 1.9 %shard_map.66 = (f32[19,12,16,128]{3,2,1,0:T(8,128)S(1)}, f32[21,16,128]{2,1,0:T(8,128)S(1)}, f32[21,16,128]{2,1,0:T(8,128)S(1)}) custom-call(f32[8,128]{1,0:T(8,128)S(1)} %broadcast_in_dim.2.force, f32[5120,128]{1,0:T(8,128)S(1)} %get-tuple-element.26.tiles, f32[2,16,16,128]{3,2,1,0:T(8,128)S(1)} %pad_maximum_fusion.1.coef, ...), custom_call_target="tpu_custom_call" | custom-call | flops 6000000 | bytes 6000000 | tf_op jit(solution)/shard_map/pallas_call | solution.py:293
  91.6 1.1 %collective-permute-done.5.xo = f32[21,16,128]{2,1,0:T(8,128)S(1)} collective-permute-done((f32[21,16,128]{2,1,0:T(8,128)S(1)}, f32[21,16,128]{2,1,0:T(8,128)S(1)}, u32[]{:S(2)}, u32[]{:S(2)}) %collective-permute-start.5) | collective-permute-done | bytes 172064 | tf_op jit(solution)/shard_map/ppermute | solution.py:444
  92.8 0.6 shard_map.67
  93.4 0.3 collective-permute-start.6
  93.6 2.8 %collective-permute-start.7 = (f32[432,128]{1,0:T(8,128)S(1)}, f32[432,128]{1,0:T(8,128)S(1)}, u32[]{:S(2)}, u32[]{:S(2)}) collective-permute-start(f32[432,128]{1,0:T(8,128)S(1)} %get-tuple-element.31.mine_o), channel_id=1, source_target_pairs={{0,7},{1,2},{2,1},{3,4},{4,3},{5,6},{6,5},{7,0},{8,15},{9,10},{10,... | collective-permute-start | bytes 663560 | tf_op jit(solution)/shard_map/ppermute | solution.py:444
  96.5 4.5 %shard_map.68._before = f32[19,16,16,128]{3,2,1,0:T(8,128)} custom-call(s32[2]{0:T(128)S(1)} %pad_add_fusion.odd, f32[8,128]{1,0:T(8,128)S(1)} %broadcast_in_dim.2.force, f32[19,4,16,128]{3,2,1,0:T(8,128)S(1)} %get-tuple-element.27.edge, f32[19,12,16,128]{3,2,1,0:T(8,128)S(1)} %get-tuple-element.32.inner, f32[2,16,16,128]{3,2,1,0:T(8,128)S(1)} %pad_maximum_fusion.1.coef, ...), custom_call_target="tpu_custom_call" | custom-call | flops 12000000 | bytes 12000000 | tf_op jit(solution)/shard_map/pallas_call | solution.py:293
  101.0 2.2 %collective-permute-done.7.came_o = f32[432,128]{1,0:T(8,128)S(1)} collective-permute-done((f32[432,128]{1,0:T(8,128)S(1)}, f32[432,128]{1,0:T(8,128)S(1)}, u32[]{:S(2)}, u32[]{:S(2)}) %collective-permute-start.7) | collective-permute-done | bytes 221216 | tf_op jit(solution)/shard_map/ppermute | solution.py:444
  103.2 1.6 %shard_map.69 = f32[19,16,16,128]{3,2,1,0:T(8,128)} custom-call(s32[2]{0:T(128)S(1)} %pad_add_fusion.odd, f32[8,128]{1,0:T(8,128)S(1)} %broadcast_in_dim.2.force, f32[432,128]{1,0:T(8,128)S(1)} %get-tuple-element.30.mine_e, f32[432,128]{1,0:T(8,128)S(1)} %get-tuple-element.31.mine_o, ...), custom_call_target="tpu_custom_call", output_to_operand_aliasing={{}: (6, {})} | custom-call | flops 2000000 | bytes 2000000 | tf_op jit(solution)/shard_map/pallas_call | solution.py:526
  (20 shorter events, 0.2 us)
Async XLA Ops:
  0.9 5.5 %collective-permute-start = (f32[2,2,4,16,128]{4,3,2,1,0:T(8,128)S(1)}, f32[2,2,4,16,128]{4,3,2,1,0:T(8,128)S(1)}, u32[]{:S(2)}, u32[]{:S(2)}) collective-permute-start(f32[2,2,4,16,128]{4,3,2,1,0:T(8,128)S(1)} %fusion.1), channel_id=1, source_target_pairs={{0,1},{1,0},{2,3},{3,2},{4,5},{5,4},{6,7},{7,6},{8,9},{9,8},{10,11... | collective-permute-start | bytes 393224 | tf_op jit(solution)/shard_map/ppermute | solution.py:452
  6.3 11.6 %copy-start.3 = (f32[3]{0:T(128)S(1)}, f32[3]{0:T(128)}, u32[]{:S(2)}) copy-start(f32[3]{0:T(128)} %param.11) | copy-start | bytes 40
  6.3 11.6 %copy-start = (f32[2,128,128]{2,1,0:T(8,128)S(1)}, f32[2,128,128]{2,1,0:T(8,128)}, u32[]{:S(2)}) copy-start(f32[2,128,128]{2,1,0:T(8,128)} %param.8) | copy-start | bytes 393220
  6.4 11.6 %copy-start.1 = (f32[2,128,128]{2,1,0:T(8,128)S(1)}, f32[2,128,128]{2,1,0:T(8,128)}, u32[]{:S(2)}) copy-start(f32[2,128,128]{2,1,0:T(8,128)} %param.9) | copy-start | bytes 393220
  6.4 74.0 %all-to-all-start = ((f32[128,77,1,128]{3,2,1,0:T(1,128)}), f32[128,77,1,128]{3,2,1,0:T(1,128)}, u32[]{:S(2)}, u32[]{:S(2)}) async-start(f32[128,77,1,128]{3,2,1,0:T(1,128)} %shard_map.64), calls=%async_computation | async-start | bytes 10092544 | tf_op jit(solution)/shard_map/all_to_all | solution.py:481
  17.8 61.8 %copy-start.2 = (s32[16,16,128]{2,1,0:T(8,128)S(1)}, s32[16,16,128]{2,1,0:T(8,128)}, u32[]{:S(2)}) copy-start(s32[16,16,128]{2,1,0:T(8,128)} %param.10) | copy-start | bytes 393220
  18.0 59.1 %collective-permute-start.1 = (f32[2,2,2,16,128]{4,3,2,1,0:T(8,128)S(1)}, f32[2,2,2,16,128]{4,3,2,1,0:T(8,128)S(1)}, u32[]{:S(2)}, u32[]{:S(2)}) collective-permute-start(f32[2,2,2,16,128]{4,3,2,1,0:T(8,128)S(1)} %get-tuple-element.42), channel_id=1, source_target_pairs={{0,2},{1,3},{2,0},{3,1},{4,6},{5,7},{6,4},{7,5},{8,10},{9,11},{10,... | collective-permute-start | bytes 196616 | tf_op jit(solution)/shard_map/ppermute | solution.py:462
  20.5 56.6 %collective-permute-start.2 = (f32[2,2,2,16,128]{4,3,2,1,0:T(8,128)S(1)}, f32[2,2,2,16,128]{4,3,2,1,0:T(8,128)S(1)}, u32[]{:S(2)}, u32[]{:S(2)}) collective-permute-start(f32[2,2,2,16,128]{4,3,2,1,0:T(8,128)S(1)} %get-tuple-element.43), channel_id=1, source_target_pairs={{0,4},{1,5},{2,6},{3,7},{4,0},{5,1},{6,2},{7,3},{8,12},{9,13},{10,... | collective-permute-start | bytes 196616 | tf_op jit(solution)/shard_map/ppermute | solution.py:462
  23.5 56.0 %collective-permute-start.3 = (f32[2,2,2,16,128]{4,3,2,1,0:T(8,128)S(1)}, f32[2,2,2,16,128]{4,3,2,1,0:T(8,128)S(1)}, u32[]{:S(2)}, u32[]{:S(2)}) collective-permute-start(f32[2,2,2,16,128]{4,3,2,1,0:T(8,128)S(1)} %get-tuple-element.44), channel_id=1, source_target_pairs={{0,6},{1,7},{2,4},{3,5},{4,2},{5,3},{6,0},{7,1},{8,14},{9,15},{10,... | collective-permute-start | bytes 196616 | tf_op jit(solution)/shard_map/ppermute | solution.py:462
  85.0 6.6 %collective-permute-start.4 = (f32[21,16,128]{2,1,0:T(8,128)S(1)}, f32[21,16,128]{2,1,0:T(8,128)S(1)}, u32[]{:S(2)}, u32[]{:S(2)}) collective-permute-start(f32[21,16,128]{2,1,0:T(8,128)S(1)} %get-tuple-element.24), channel_id=1, source_target_pairs={{0,8},{8,0},{16,24},{24,16},{32,40},{40,32},{48,56},{56,48},{64,72... | collective-permute-start | bytes 516104 | tf_op jit(solution)/shard_map/ppermute | solution.py:444
  85.1 7.6 %collective-permute-start.5 = (f32[21,16,128]{2,1,0:T(8,128)S(1)}, f32[21,16,128]{2,1,0:T(8,128)S(1)}, u32[]{:S(2)}, u32[]{:S(2)}) collective-permute-start(f32[21,16,128]{2,1,0:T(8,128)S(1)} %get-tuple-element.25), channel_id=1, source_target_pairs={{0,120},{8,16},{16,8},{24,32},{32,24},{40,48},{48,40},{56,64},{64,... | collective-permute-start | bytes 516104 | tf_op jit(solution)/shard_map/ppermute | solution.py:444
  93.4 7.6 %collective-permute-start.6 = (f32[432,128]{1,0:T(8,128)S(1)}, f32[432,128]{1,0:T(8,128)S(1)}, u32[]{:S(2)}, u32[]{:S(2)}) collective-permute-start(f32[432,128]{1,0:T(8,128)S(1)} %get-tuple-element.30.mine_e), channel_id=1, source_target_pairs={{0,1},{1,0},{2,3},{3,2},{4,5},{5,4},{6,7},{7,6},{8,9},{9,8},{10,11... | collective-permute-start | bytes 663560 | tf_op jit(solution)/shard_map/ppermute | solution.py:444
  93.6 9.5 %collective-permute-start.7 = (f32[432,128]{1,0:T(8,128)S(1)}, f32[432,128]{1,0:T(8,128)S(1)}, u32[]{:S(2)}, u32[]{:S(2)}) collective-permute-start(f32[432,128]{1,0:T(8,128)S(1)} %get-tuple-element.31.mine_o), channel_id=1, source_target_pairs={{0,7},{1,2},{2,1},{3,4},{4,3},{5,6},{6,5},{7,0},{8,15},{9,10},{10,... | collective-permute-start | bytes 663560 | tf_op jit(solution)/shard_map/ppermute | solution.py:444

commit v6 on v5

--- a/solution.py
+++ b/solution.py
@@ -33,7 +33,8 @@
 CAP = 2
 TILE = 38
 PAIR = 2 * TILE + 1
-ROWS = 40
+ROWS = 41
+APART = 257
 EXT = 20
 VMEM_LIMIT = 48 * 1024 * 1024
 VMEM_MOST = 61 * 1024 * 1024
@@ -114,10 +115,10 @@
     quarters = []
     for part in range(4):
         rows = pl.ds(part * 64, 64)
-        copy = pltpu.make_async_copy(pdf_hbm.at[:, rows, :], pdf.at[:, rows, :], sems.at[part])
+        copy = pltpu.make_async_copy(pdf_hbm.at[:, rows, :], pdf.at[:, rows, 0, :], sems.at[part])
         copy.start()
         quarters.append(copy)
-    flat = pdf.reshape(19 * 256, 128)
+    flat = pdf.reshape(19 * APART, 128)
     rows_ = tiles.reshape(HELD * TILE, 128)
     empty = jnp.full((8, 128), -1.0, F32)
     for block in range(DEVICES // 8):
@@ -140,7 +141,7 @@
         for r in range(2):
             for q in (0, 8, 16):
                 n = min(8, 19 - q)
-                value = flat[pl.ds(near + r * 8 + q * 256, n, stride=256), :]
+                value = flat[pl.ds(near + r * 8 + q * APART, n, stride=APART), :]
                 rows_[pl.ds(k * TILE + r * 19 + q, n), :] = value
         pltpu.make_async_copy(
             tiles.at[pl.ds(k * TILE, TILE)],
@@ -170,7 +171,7 @@
         scratch_shapes=[
             pltpu.SMEM((HELD,), jnp.int32),
             pltpu.SMEM((DEVICES,), jnp.int32),
-            pltpu.VMEM((19, 256, 128), F32),
+            pltpu.VMEM((19, APART, 1, 128), F32),
             pltpu.VMEM((HELD * TILE, 1, 128), F32),
             pltpu.VMEM((DEVICES, 1, 128), F32),
             pltpu.SemaphoreType.DMA((4,)),
@@ -190,7 +191,7 @@
     for r in range(2):
         dist = []
         for q in range(19):
-            value = tiles[pl.ds(x * (8 * ROWS) + r * 19 + q, 8, stride=ROWS), :]
+            value = tiles[pl.ds(at * (8 * ROWS) + r * 19 + q, 8, stride=ROWS), :]
             dist.append(WEIGHT[q] * value + WEIGHT[q])
         solid = coef[0, x, pl.ds(r, 8, stride=2), :]
         omega = coef[1, x, pl.ds(r, 8, stride=2), :]
@@ -199,8 +200,22 @@
             post[q, at, pl.ds(r, 8, stride=2), :] = shift_z(after[q], q)
 
 
+def fetch(source, arrived, tiles, sem, slot, at):
+    p = source[0, slot]
+    pltpu.make_async_copy(
+        arrived.at[lax.shift_right_logical(p, 1), pl.ds((p & 1) * TILE, TILE), 0, :],
+        tiles.at[pl.ds(at * ROWS, TILE), :],
+        sem,
+    ).start()
+
+
+def arrive(tiles, sem):
+    whole = tiles.at[pl.ds(0, 8 * TILE), :]
+    pltpu.make_async_copy(whole, whole, sem).wait()
+
+
 def edge_kernel(
-    odd, force, arrived, coef, tiles, edge, xe, xo, labels, found, source, sems, small
+    odd, force, arrived, coef, found, edge, xe, xo, tiles, labels, source, sems, small
 ):
     pull = pltpu.make_async_copy(arrived.at[:, 2 * TILE, 0, :], labels, small.at[0])
     pull.start()
@@ -221,66 +236,74 @@
     hand = pltpu.make_async_copy(found, source, small.at[1])
     hand.start()
     hand.wait()
-
-    def fetch(s):
-        p = source[0, s]
-        pltpu.make_async_copy(
-            arrived.at[lax.shift_right_logical(p, 1), pl.ds((p & 1) * TILE, TILE), 0, :],
-            tiles.at[pl.ds(pl.multiple_of(s * ROWS, 8), TILE), :],
-            sems.at[lax.shift_right_logical(s, 3)],
-        ).start()
-
-    def arrive(x):
-        whole = tiles.at[pl.ds(0, 8 * TILE), :]
-        pltpu.make_async_copy(whole, whole, sems.at[x]).wait()
-
-    for x in (0, 1, 14, 15):
+    for j, x in enumerate((0, 1, 14, 15)):
         for i in range(8):
-            fetch(8 * x + i)
+            fetch(source, arrived, tiles, sems.at[j], 8 * x + i, 8 * j + i)
 
     def plane(j, _):
-        x = jnp.where(j < 2, j, j + 12)
-        for i in range(24):
-            fetch(16 + 24 * j + i)
-        arrive(x)
-        plane_step(x, j, tiles, coef, edge, f)
+        arrive(tiles, sems.at[j])
+        plane_step(jnp.where(j < 2, j, j + 12), j, tiles, coef, edge, f)
         return 0
 
     lax.fori_loop(0, 4, plane, 0)
-    flag = odd[0]
-    for i, ((qu, lu), (qd, ld)) in enumerate(zip(entries(0, 1), entries(0, -1))):
-        up, dn = edge[qu, 3 - lu], edge[qd, ld]
-        xe[i] = pick(flag, up, dn)
-        xo[i] = pick(flag, dn, up)
-    for j in range(2):
-        up, dn = coef[j, 15], coef[j, 0]
-        xe[19 + j] = pick(flag, up, dn)
-        xo[19 + j] = pick(flag, dn, up)
-    for x in range(2, 14):
-        arrive(x)
-
-
-def inner_kernel(force, tiles, coef, edge, inner, yup, ydn):
+    for even in range(2):
+
+        @pl.when(odd[0] == even)
+        def _():
+            for out, sign in ((xe, 1 - 2 * even), (xo, 2 * even - 1)):
+                for i, (q, layer) in enumerate(entries(0, sign)):
+                    out[i] = edge[q, 3 - layer if sign == 1 else layer]
+                for j in range(2):
+                    out[19 + j] = coef[j, 15 if sign == 1 else 0]
+
+
+def inner_kernel(odd, force, found, arrived, coef, edge, inner, ye, yo, tiles, source, sems, small):
+    hand = pltpu.make_async_copy(found, source, small)
+    hand.start()
     f = [force[axis : axis + 1, :] for axis in range(3)]
-
-    def plane(j, _):
+    hand.wait()
+
+    def ask(j):
+        for i in range(8):
+            fetch(source, arrived, tiles, sems.at[j], 16 + 8 * j + i, 8 * j + i)
+
+    for j in range(4):
+        ask(j)
+
+    def plane(j, more):
+        if more:
+            ask(j + 4)
+        arrive(tiles, sems.at[j])
         plane_step(j + 2, j, tiles, coef, inner, f)
-        return 0
-
-    lax.fori_loop(0, 12, plane, 0)
-    for out, sign in ((yup, 1), (ydn, -1)):
-        for i, (q, layer) in enumerate(entries(1, sign)):
-            row = 15 - layer if sign == 1 else layer
-            for x in range(16):
-                if 2 <= x < 14:
-                    value = inner[q, x - 2, row : row + 1, :]
-                else:
-                    value = edge[q, x if x < 2 else x - 12, row : row + 1, :]
-                out[i, x : x + 1, :] = value
-        row = 15 if sign == 1 else 0
-        for j in range(2):
-            for x in range(16):
-                out[19 + j, x : x + 1, :] = coef[j, x, row : row + 1, :]
+
+    def early(j, _):
+        plane(j, True)
+        return 0
+
+    def late(j, _):
+        plane(j, False)
+        return 0
+
+    lax.fori_loop(0, 8, early, 0)
+    lax.fori_loop(8, 12, late, 0)
+    for even in range(2):
+
+        @pl.when(odd[1] == even)
+        def _():
+            for out, sign in ((ye, 1 - 2 * even), (yo, 2 * even - 1)):
+                for i, (q, layer) in enumerate(entries(1, sign)):
+                    row = 15 - layer if sign == 1 else layer
+                    for x in range(16):
+                        if 2 <= x < 14:
+                            value = inner[q, x - 2, row : row + 1, :]
+                        else:
+                            value = edge[q, x if x < 2 else x - 12, row : row + 1, :]
+                        out[i * EXT + 2 + x : i * EXT + 3 + x, :] = value
+                row = 15 if sign == 1 else 0
+                for j in range(2):
+                    for x in range(16):
+                        at = (19 + j) * EXT + 2 + x
+                        out[at : at + 1, :] = coef[j, x, row : row + 1, :]
 
 
 VMEM_SPEC = pl.BlockSpec(memory_space=pltpu.VMEM)
@@ -300,34 +323,29 @@
     )(*operands)
 
 
-def join_kernel(odd, xe, xo, yup, ydn, ye, yo):
-    fx, fy = odd[0], odd[1]
-    lists = [entries(1, sign) + [(19, 0), (20, 0)] for sign in (1, -1)]
+def join_kernel(odd, xe, xo, own_e, own_o, ye, yo):
+    for own, out in ((own_e, ye), (own_o, yo)):
+        for block in range(SIDE_ROWS // 8):
+            out[8 * block : 8 * block + 8, :] = own[8 * block : 8 * block + 8, :]
     have = [
         {e: n for n, e in enumerate(entries(0, toward) + [(19, 0), (20, 0)])} for toward in (1, -1)
     ]
-
-    def corner(direction, i, toward, deep):
-        q, layer = lists[direction][i]
-        n = have[toward].get((q, deep))
-        if n is None:
-            return jnp.zeros((1, 128), F32)
-        row = 15 - layer if direction == 0 else layer
-        even, odd_ = (xo, xe) if toward == 0 else (xe, xo)
-        return pick(fx, even[n, row : row + 1, :], odd_[n, row : row + 1, :])
-
-    for i in range(COUNT):
-        up, dn = yup[i], ydn[i]
-        ye[i * EXT + 2 : i * EXT + 18, :] = pick(fy, up, dn)
-        yo[i * EXT + 2 : i * EXT + 18, :] = pick(fy, dn, up)
-        for toward in range(2):
-            for deep in range(2):
-                at = i * EXT + ((1 - deep) if toward == 0 else 18 + deep)
-                up, dn = corner(0, i, toward, deep), corner(1, i, toward, deep)
-                ye[at : at + 1, :] = pick(fy, up, dn)
-                yo[at : at + 1, :] = pick(fy, dn, up)
-    for out in (ye, yo):
-        out[COUNT * EXT : SIDE_ROWS, :] = jnp.zeros((SIDE_ROWS - COUNT * EXT, 128), F32)
+    zero = jnp.zeros((1, 128), F32)
+    for even_x in range(2):
+        for even_y in range(2):
+
+            @pl.when((odd[0] == even_x) & (odd[1] == even_y))
+            def _():
+                halves = (xo, xe) if even_x == 0 else (xe, xo)
+                for out, sign in ((ye, 1 - 2 * even_y), (yo, 2 * even_y - 1)):
+                    for i, (q, layer) in enumerate(entries(1, sign) + [(19, 0), (20, 0)]):
+                        row = 15 - layer if sign == 1 else layer
+                        for toward in range(2):
+                            for deep in range(2):
+                                at = i * EXT + ((1 - deep) if toward == 0 else 18 + deep)
+                                n = have[toward].get((q, deep))
+                                value = zero if n is None else halves[toward][n, row : row + 1, :]
+                                out[at : at + 1, :] = value
 
 
 def middle_kernel(odd, force, edge, inner, coef, xe, xo, out, wide, again, result, sems):
@@ -386,55 +404,60 @@
         pltpu.make_async_copy(result.at[x], out.at[:, x], sems.at[x]).wait()
 
 
-def last_kernel(odd, force, mine_e, mine_o, came_e, came_o, _before, out, sides, rows, patch, sem):
-    flag = odd[1]
-    for block in range(SIDE_ROWS // 8):
-        part = slice(8 * block, 8 * block + 8)
-        me, mo, ce, co = mine_e[part, :], mine_o[part, :], came_e[part, :], came_o[part, :]
-        sides[0, part, :] = pick(flag, co, ce)
-        sides[1, part, :] = pick(flag, mo, me)
-        sides[2, part, :] = pick(flag, ce, co)
-        sides[3, part, :] = pick(flag, me, mo)
+def last_side(side, sign, own, other, out, rows, patch, sem, f):
+    came = {e: n for n, e in enumerate(entries(1, sign))}
+    mine = {e: n for n, e in enumerate(entries(1, -sign))}
+    for line in range(2):
+        for block in range(3):
+            start = 1 + 8 * block
+            dist = []
+            for q in range(19):
+                cx, cy, _z = VELOCITY[q]
+                if cy == sign:
+                    which, n = other, came[(q, 1 - line)]
+                elif cy == 0:
+                    which, n = (other, came[(q, 0)]) if line == 0 else (own, mine[(q, 0)])
+                else:
+                    which, n = own, mine[(q, line)]
+                at = n * EXT + start - cx
+                dist.append(which[at : at + 8, :])
+            where = other if line == 0 else own
+            fixed = [where[(19 + j) * EXT + start : (19 + j) * EXT + start + 8, :] for j in range(2)]
+            after = collide(dist, fixed[0], fixed[1], f)
+            for q in range(19):
+                if VELOCITY[q][1] == sign or (VELOCITY[q][1] == 0 and line == 1):
+                    rows[line, q, 8 * block : 8 * block + 8, :] = shift_z(after[q], q)
+    number = 19 * side
+    for depth in range(2):
+        listed = [q for q in range(19) if VELOCITY[q][1] in ((sign, 0) if depth == 0 else (sign,))]
+        y = depth if sign == 1 else 15 - depth
+        begin = 0
+        for n, q in enumerate(listed):
+            cx, cy, _z = VELOCITY[q]
+            line = 1 if depth == 1 or cy == 0 else 0
+            patch[number + n] = rows[line, q, 1 - cx : 17 - cx, :] * INVERSE[q] - 1.0
+            if n + 1 == len(listed) or listed[n + 1] != q + 1:
+                count = n + 1 - begin
+                pltpu.make_async_copy(
+                    patch.at[pl.ds(number + begin, count)],
+                    out.at[pl.ds(q + 1 - count, count), :, y, :],
+                    sem,
+                ).start()
+                begin = n + 1
+        number += len(listed)
+
+
+def last_kernel(odd, force, mine_e, mine_o, came_e, came_o, _before, out, rows, patch, sem):
     f = [force[axis : axis + 1, :] for axis in range(3)]
-    number = 0
-    for side, sign in ((0, 1), (1, -1)):
-        came = {e: n for n, e in enumerate(entries(1, sign))}
-        mine = {e: n for n, e in enumerate(entries(1, -sign))}
-        for line in range(2):
-            for block in range(3):
-                start = 1 + 8 * block
-                dist = []
-                for q in range(19):
-                    cx, cy, _z = VELOCITY[q]
-                    if cy == sign:
-                        which, n = 0, came[(q, 1 - line)]
-                    elif cy == 0:
-                        which, n = (0, came[(q, 0)]) if line == 0 else (1, mine[(q, 0)])
-                    else:
-                        which, n = 1, mine[(q, line)]
-                    at = n * EXT + start - cx
-                    dist.append(sides[2 * side + which, at : at + 8, :])
-                fixed = [
-                    sides[2 * side + line, (19 + j) * EXT + start : (19 + j) * EXT + start + 8, :]
-                    for j in range(2)
-                ]
-                after = collide(dist, fixed[0], fixed[1], f)
-                for q in range(19):
-                    if VELOCITY[q][1] == sign or (VELOCITY[q][1] == 0 and line == 1):
-                        rows[line, q, 8 * block : 8 * block + 8, :] = shift_z(after[q], q)
-        for q in range(19):
-            cx, cy, _z = VELOCITY[q]
-            targets = []
-            if cy == sign:
-                targets = [(0, 0), (1, 1)]
-            elif cy == 0:
-                targets = [(1, 0)]
-            for line, depth in targets:
-                value = rows[line, q, 1 - cx : 17 - cx, :]
-                patch[number] = value * INVERSE[q] - 1.0
-                y = depth if sign == 1 else 15 - depth
-                pltpu.make_async_copy(patch.at[number], out.at[q, :, y, :], sem).start()
-                number += 1
+    for even in range(2):
+
+        @pl.when(odd[1] == even)
+        def _():
+            low = (mine_o, came_o) if even == 0 else (mine_e, came_e)
+            high = (mine_e, came_e) if even == 0 else (mine_o, came_o)
+            last_side(0, 1, *low, out, rows, patch, sem, f)
+            last_side(1, -1, *high, out, rows, patch, sem, f)
+
     pltpu.make_async_copy(patch, patch, sem).wait()
 
 
@@ -489,27 +512,40 @@
     coef, odd, drive = lax.optimization_barrier((coef, odd, drive))
     hbm = pl.BlockSpec(memory_space=pltpu.HBM)
     posts = [jax.ShapeDtypeStruct((19, n, 16, 128), F32) for n in (4, 12)]
-    tiles, edge, xe, xo = pl.pallas_call(
+    found, edge, xe, xo = pl.pallas_call(
         edge_kernel,
-        out_shape=[jax.ShapeDtypeStruct((HELD * ROWS, 128), F32), posts[0], FACE, FACE],
+        out_shape=[jax.ShapeDtypeStruct((8, 128), jnp.int32), posts[0], FACE, FACE],
         in_specs=[SMEM_SPEC, VMEM_SPEC, hbm, VMEM_SPEC],
         out_specs=[VMEM_SPEC] * 4,
         scratch_shapes=[
+            pltpu.VMEM((32 * ROWS, 128), F32),
             pltpu.VMEM((DEVICES, 128), F32),
-            pltpu.VMEM((8, 128), jnp.int32),
             pltpu.SMEM((8, 128), jnp.int32),
-            pltpu.SemaphoreType.DMA((16,)),
+            pltpu.SemaphoreType.DMA((4,)),
             pltpu.SemaphoreType.DMA((2,)),
         ],
         compiler_params=pltpu.CompilerParams(vmem_limit_bytes=VMEM_LIMIT),
         cost_estimate=pl.CostEstimate(flops=2_000_000, bytes_accessed=8_000_000, transcendentals=0),
     )(odd, drive, arrived, coef)
-    from_xe, from_xo = swap(xe, "gx", True), swap(xo, "gx", False)
-    inner, yup, ydn = call(
-        inner_kernel, [posts[1], FACE, FACE], (drive, tiles, coef, edge), 6_000_000, scalars=0
-    )
-    ye, yo = call(join_kernel, [SIDE, SIDE], (odd, from_xe, from_xo, yup, ydn), 500_000)
-    from_ye, from_yo = swap(ye, "gy", True), swap(yo, "gy", False)
+    from_xo = swap(xo, "gx", False)
+    from_xe = swap(xe, "gx", True)
+    inner, own_ye, own_yo = pl.pallas_call(
+        inner_kernel,
+        out_shape=[posts[1], SIDE, SIDE],
+        in_specs=[SMEM_SPEC, VMEM_SPEC, VMEM_SPEC, hbm, VMEM_SPEC, VMEM_SPEC],
+        out_specs=[VMEM_SPEC] * 3,
+        scratch_shapes=[
+            pltpu.VMEM((96 * ROWS, 128), F32),
+            pltpu.SMEM((8, 128), jnp.int32),
+            pltpu.SemaphoreType.DMA((12,)),
+            pltpu.SemaphoreType.DMA,
+        ],
+        compiler_params=pltpu.CompilerParams(vmem_limit_bytes=VMEM_LIMIT),
+        cost_estimate=pl.CostEstimate(flops=6_000_000, bytes_accessed=8_000_000, transcendentals=0),
+    )(odd, drive, found, arrived, coef, edge)
+    ye, yo = call(join_kernel, [SIDE, SIDE], (odd, from_xe, from_xo, own_ye, own_yo), 500_000)
+    from_yo = swap(yo, "gy", False)
+    from_ye = swap(ye, "gy", True)
     result = call(
         middle_kernel,
         jax.ShapeDtypeStruct((19, 16, 16, 128), F32),
@@ -530,7 +566,6 @@
         out_specs=hbm,
         input_output_aliases={6: 0},
         scratch_shapes=[
-            pltpu.VMEM((4, SIDE_ROWS, 128), F32),
             pltpu.VMEM((2, 19, 24, 128), F32),
             pltpu.VMEM((38, 16, 128), F32),
             pltpu.SemaphoreType.DMA,

time: 106 us -> 106 us (level)
    pallas_call x1 -> x2, Pallas kernels: 4.69 us -> 8.16 us  [the longest x1 4.6 us: local(): pl.pallas_call(inner_kernel, out_shape=[posts[1], SIDE, SIDE], in_specs=[...]
    pallas_call x3 -> x2, Pallas kernels: 7.05 us -> 5.15 us  [call(): pl.pallas_call(kernel, out_shape=out_shape, in_specs=[SMEM_SPEC] * scalar...]
    ppermute x4, waiting for transfers between devices: 3.34 us -> 2.13 us  [swap(): return lax.ppermute(value, axis, pairs)]
  transfers between devices with their start and end apart: 9 -> 9, of which waited for: 5 -> 5; matrix products, arithmetic and copies ran while one was open for 0% -> 0% of each run, Pallas kernels for 10% -> 11%
where the time goes in v6:
time: 106 us; the launch traced here: 105 us
  waiting for transfers between devices  58.3 us (55%)
  starting transfers between devices  27.7 us (26%)
  Pallas kernels  17.6 us (17%)
  other arithmetic  1.1 us (1%)
    ppermute x3, waiting for transfers between devices, pieces_of(): lax.ppermute(message, 'gy', [(i, i ^ 2 * k) for i in range(8)])  54.8 us
    all_to_all x1, starting transfers between devices, local(): lax.all_to_all(packed, ('gx', 'gy'), split_axis=0, concat_axis=0, tiled=T...  11.7 us
    ppermute x4, starting transfers between devices, swap(): return lax.ppermute(value, axis, pairs)  7.71 us
    ppermute x3, starting transfers between devices, pieces_of(): lax.ppermute(message, 'gy', [(i, i ^ 2 * k) for i in range(8)])  6.58 us
    pallas_call x2, Pallas kernels, call(): pl.pallas_call(kernel, out_shape=out_shape, in_specs=[SMEM_SPEC] * scalar...  5.15 us
    pallas_call x1, Pallas kernels, local(): pl.pallas_call(inner_kernel, out_shape=[posts[1], SIDE, SIDE], in_specs=[...  4.6 us
    pallas_call x1, Pallas kernels, local(): pl.pallas_call(edge_kernel, out_shape=[jax.ShapeDtypeStruct((8, 128), jnp...  3.56 us
    pallas_call x1, Pallas kernels, pack(): pl.pallas_call(pack_kernel, out_shape=jax.ShapeDtypeStruct((DEVICES, PAIR...  2.75 us
  transfers between devices with their start and end apart: 9, of which 5 were waited for; matrix products, arithmetic and copies ran while one was open for 0% of the time, Pallas kernels for 11%

profile of v6, /device:TPU:0, one launch (start us, length us, event | category | flops | bytes accessed | tf_op | source)
XLA Modules:
  0.0 105.1 jit_solution(3231419777374083339)
XLA Ops:
  0.0 0.9 fusion.1
  0.9 1.7 %collective-permute-start = (f32[2,2,4,16,128]{4,3,2,1,0:T(8,128)S(1)}, f32[2,2,4,16,128]{4,3,2,1,0:T(8,128)S(1)}, u32[]{:S(2)}, u32[]{:S(2)}) collective-permute-start(f32[2,2,4,16,128]{4,3,2,1,0:T(8,128)S(1)} %fusion.1), channel_id=1, source_target_pairs={{0,1},{1,0},{2,3},{3,2},{4,5},{5,4},{6,7},{7,6},{8,9},{9,8},{10,11... | collective-permute-start | bytes 393224 | tf_op jit(solution)/shard_map/ppermute | solution.py:475
  2.6 2.7 %shard_map.64 = f32[128,77,1,128]{3,2,1,0:T(1,128)} custom-call(s32[128]{0:T(128)} %target_hbm.1, f32[19,256,128]{2,1,0:T(8,128)} %bitcast.43), custom_call_target="tpu_custom_call" | custom-call | bytes 8000000 | tf_op jit(solution)/shard_map/pallas_call | solution.py:166
  5.4 0.0 copy-start
  5.4 0.7 collective-permute-done
  6.1 11.7 %all-to-all-start = ((f32[128,77,1,128]{3,2,1,0:T(1,128)}), f32[128,77,1,128]{3,2,1,0:T(1,128)}, u32[]{:S(2)}, u32[]{:S(2)}) async-start(f32[128,77,1,128]{3,2,1,0:T(1,128)} %shard_map.64), calls=%async_computation | async-start | bytes 10092544 | tf_op jit(solution)/shard_map/all_to_all | solution.py:504
  18.0 2.5 %collective-permute-start.1 = (f32[2,2,2,16,128]{4,3,2,1,0:T(8,128)S(1)}, f32[2,2,2,16,128]{4,3,2,1,0:T(8,128)S(1)}, u32[]{:S(2)}, u32[]{:S(2)}) collective-permute-start(f32[2,2,2,16,128]{4,3,2,1,0:T(8,128)S(1)} %get-tuple-element.42), channel_id=1, source_target_pairs={{0,2},{1,3},{2,0},{3,1},{4,6},{5,7},{6,4},{7,5},{8,10},{9,11},{10,... | collective-permute-start | bytes 196616 | tf_op jit(solution)/shard_map/ppermute | solution.py:485
  20.5 3.0 %collective-permute-start.2 = (f32[2,2,2,16,128]{4,3,2,1,0:T(8,128)S(1)}, f32[2,2,2,16,128]{4,3,2,1,0:T(8,128)S(1)}, u32[]{:S(2)}, u32[]{:S(2)}) collective-permute-start(f32[2,2,2,16,128]{4,3,2,1,0:T(8,128)S(1)} %get-tuple-element.43), channel_id=1, source_target_pairs={{0,4},{1,5},{2,6},{3,7},{4,0},{5,1},{6,2},{7,3},{8,12},{9,13},{10,... | collective-permute-start | bytes 196616 | tf_op jit(solution)/shard_map/ppermute | solution.py:485
  23.5 1.1 %collective-permute-start.3 = (f32[2,2,2,16,128]{4,3,2,1,0:T(8,128)S(1)}, f32[2,2,2,16,128]{4,3,2,1,0:T(8,128)S(1)}, u32[]{:S(2)}, u32[]{:S(2)}) collective-permute-start(f32[2,2,2,16,128]{4,3,2,1,0:T(8,128)S(1)} %get-tuple-element.44), channel_id=1, source_target_pairs={{0,6},{1,7},{2,4},{3,5},{4,2},{5,3},{6,0},{7,1},{8,14},{9,15},{10,... | collective-permute-start | bytes 196616 | tf_op jit(solution)/shard_map/ppermute | solution.py:485
  24.6 0.1 pad_add_fusion.odd
  24.7 52.4 %collective-permute-done.1 = f32[2,2,2,16,128]{4,3,2,1,0:T(8,128)S(1)} collective-permute-done((f32[2,2,2,16,128]{4,3,2,1,0:T(8,128)S(1)}, f32[2,2,2,16,128]{4,3,2,1,0:T(8,128)S(1)}, u32[]{:S(2)}, u32[]{:S(2)}) %collective-permute-start.1) | collective-permute-done | bytes 65568 | tf_op jit(solution)/shard_map/ppermute | solution.py:485
  77.1 2.3 %collective-permute-done.3 = f32[2,2,2,16,128]{4,3,2,1,0:T(8,128)S(1)} collective-permute-done((f32[2,2,2,16,128]{4,3,2,1,0:T(8,128)S(1)}, f32[2,2,2,16,128]{4,3,2,1,0:T(8,128)S(1)}, u32[]{:S(2)}, u32[]{:S(2)}) %collective-permute-start.3) | collective-permute-done | bytes 65568 | tf_op jit(solution)/shard_map/ppermute | solution.py:485
  79.6 0.1 broadcast_in_dim.2.force
  79.7 0.6 all-to-all-done.arrived
  80.3 3.6 %shard_map.65 = (s32[8,128]{1,0:T(8,128)S(1)}, f32[19,4,16,128]{3,2,1,0:T(8,128)S(1)}, f32[21,16,128]{2,1,0:T(8,128)S(1)}, f32[21,16,128]{2,1,0:T(8,128)S(1)}) custom-call(s32[2]{0:T(128)S(1)} %pad_add_fusion.odd, f32[8,128]{1,0:T(8,128)S(1)} %broadcast_in_dim.2.force, f32[128,77,1,128]{3,2,1,0:T(1,128)} %all-to-all-done.arrived, ...), custom_call_target="tpu_custom_call" | custom-call | flops 2000000 | bytes 8000000 | tf_op jit(solution)/shard_map/pallas_call | solution.py:515
  83.9 0.1 collective-permute-start.4
  84.0 4.5 %collective-permute-start.5 = (f32[21,16,128]{2,1,0:T(8,128)S(1)}, f32[21,16,128]{2,1,0:T(8,128)S(1)}, u32[]{:S(2)}, u32[]{:S(2)}) collective-permute-start(f32[21,16,128]{2,1,0:T(8,128)S(1)} %get-tuple-element.25), channel_id=1, source_target_pairs={{0,120},{8,16},{16,8},{24,32},{32,24},{40,48},{48,40},{56,64},{64,... | collective-permute-start | bytes 516104 | tf_op jit(solution)/shard_map/ppermute | solution.py:467
  88.5 4.6 %shard_map.66 = (f32[19,12,16,128]{3,2,1,0:T(8,128)S(1)}, f32[432,128]{1,0:T(8,128)S(1)}, f32[432,128]{1,0:T(8,128)S(1)}) custom-call(s32[2]{0:T(128)S(1)} %pad_add_fusion.odd, f32[8,128]{1,0:T(8,128)S(1)} %broadcast_in_dim.2.force, s32[8,128]{1,0:T(8,128)S(1)} %get-tuple-element.26.found, f32[128,77,1,128]{3,2,1,0:T(1,128)} %all-to-all-done.arrived, ...), custom_call_target="tpu_custom_call" | custom-call | flops 6000000 | bytes 8000000 | tf_op jit(solution)/shard_map/pallas_call | solution.py:532
  93.2 0.6 shard_map.67
  93.8 0.2 collective-permute-start.6
  94.0 2.9 %collective-permute-start.7 = (f32[432,128]{1,0:T(8,128)S(1)}, f32[432,128]{1,0:T(8,128)S(1)}, u32[]{:S(2)}, u32[]{:S(2)}) collective-permute-start(f32[432,128]{1,0:T(8,128)S(1)} %get-tuple-element.31.mine_o), channel_id=1, source_target_pairs={{0,7},{1,2},{2,1},{3,4},{4,3},{5,6},{6,5},{7,0},{8,15},{9,10},{10,... | collective-permute-start | bytes 663560 | tf_op jit(solution)/shard_map/ppermute | solution.py:467
  96.9 4.5 %shard_map.68._before = f32[19,16,16,128]{3,2,1,0:T(8,128)} custom-call(s32[2]{0:T(128)S(1)} %pad_add_fusion.odd, f32[8,128]{1,0:T(8,128)S(1)} %broadcast_in_dim.2.force, f32[19,4,16,128]{3,2,1,0:T(8,128)S(1)} %get-tuple-element.27.edge, f32[19,12,16,128]{3,2,1,0:T(8,128)S(1)} %get-tuple-element.32.inner, f32[2,16,16,128]{3,2,1,0:T(8,128)S(1)} %pad_maximum_fusion.1.coef, ...), custom_call_target="tpu_custom_call" | custom-call | flops 12000000 | bytes 12000000 | tf_op jit(solution)/shard_map/pallas_call | solution.py:316
  101.4 2.1 %collective-permute-done.7.came_o = f32[432,128]{1,0:T(8,128)S(1)} collective-permute-done((f32[432,128]{1,0:T(8,128)S(1)}, f32[432,128]{1,0:T(8,128)S(1)}, u32[]{:S(2)}, u32[]{:S(2)}) %collective-permute-start.7) | collective-permute-done | bytes 221216 | tf_op jit(solution)/shard_map/ppermute | solution.py:467
  103.6 1.5 %shard_map.69 = f32[19,16,16,128]{3,2,1,0:T(8,128)} custom-call(s32[2]{0:T(128)S(1)} %pad_add_fusion.odd, f32[8,128]{1,0:T(8,128)S(1)} %broadcast_in_dim.2.force, f32[432,128]{1,0:T(8,128)S(1)} %get-tuple-element.30.mine_e, f32[432,128]{1,0:T(8,128)S(1)} %get-tuple-element.31.mine_o, ...), custom_call_target="tpu_custom_call", output_to_operand_aliasing={{}: (6, {})} | custom-call | flops 2000000 | bytes 2000000 | tf_op jit(solution)/shard_map/pallas_call | solution.py:562
  (20 shorter events, 0.2 us)
Async XLA Ops:
  0.9 5.2 %collective-permute-start = (f32[2,2,4,16,128]{4,3,2,1,0:T(8,128)S(1)}, f32[2,2,4,16,128]{4,3,2,1,0:T(8,128)S(1)}, u32[]{:S(2)}, u32[]{:S(2)}) collective-permute-start(f32[2,2,4,16,128]{4,3,2,1,0:T(8,128)S(1)} %fusion.1), channel_id=1, source_target_pairs={{0,1},{1,0},{2,3},{3,2},{4,5},{5,4},{6,7},{7,6},{8,9},{9,8},{10,11... | collective-permute-start | bytes 393224 | tf_op jit(solution)/shard_map/ppermute | solution.py:475
  5.4 12.5 %copy-start.3 = (f32[3]{0:T(128)S(1)}, f32[3]{0:T(128)}, u32[]{:S(2)}) copy-start(f32[3]{0:T(128)} %param.11) | copy-start | bytes 40
  5.4 12.5 %copy-start = (f32[2,128,128]{2,1,0:T(8,128)S(1)}, f32[2,128,128]{2,1,0:T(8,128)}, u32[]{:S(2)}) copy-start(f32[2,128,128]{2,1,0:T(8,128)} %param.8) | copy-start | bytes 393220
  5.4 12.5 %copy-start.1 = (f32[2,128,128]{2,1,0:T(8,128)S(1)}, f32[2,128,128]{2,1,0:T(8,128)}, u32[]{:S(2)}) copy-start(f32[2,128,128]{2,1,0:T(8,128)} %param.9) | copy-start | bytes 393220
  6.1 74.2 %all-to-all-start = ((f32[128,77,1,128]{3,2,1,0:T(1,128)}), f32[128,77,1,128]{3,2,1,0:T(1,128)}, u32[]{:S(2)}, u32[]{:S(2)}) async-start(f32[128,77,1,128]{3,2,1,0:T(1,128)} %shard_map.64), calls=%async_computation | async-start | bytes 10092544 | tf_op jit(solution)/shard_map/all_to_all | solution.py:504
  17.8 61.8 %copy-start.2 = (s32[16,16,128]{2,1,0:T(8,128)S(1)}, s32[16,16,128]{2,1,0:T(8,128)}, u32[]{:S(2)}) copy-start(s32[16,16,128]{2,1,0:T(8,128)} %param.10) | copy-start | bytes 393220
  18.0 59.1 %collective-permute-start.1 = (f32[2,2,2,16,128]{4,3,2,1,0:T(8,128)S(1)}, f32[2,2,2,16,128]{4,3,2,1,0:T(8,128)S(1)}, u32[]{:S(2)}, u32[]{:S(2)}) collective-permute-start(f32[2,2,2,16,128]{4,3,2,1,0:T(8,128)S(1)} %get-tuple-element.42), channel_id=1, source_target_pairs={{0,2},{1,3},{2,0},{3,1},{4,6},{5,7},{6,4},{7,5},{8,10},{9,11},{10,... | collective-permute-start | bytes 196616 | tf_op jit(solution)/shard_map/ppermute | solution.py:485
  20.5 56.6 %collective-permute-start.2 = (f32[2,2,2,16,128]{4,3,2,1,0:T(8,128)S(1)}, f32[2,2,2,16,128]{4,3,2,1,0:T(8,128)S(1)}, u32[]{:S(2)}, u32[]{:S(2)}) collective-permute-start(f32[2,2,2,16,128]{4,3,2,1,0:T(8,128)S(1)} %get-tuple-element.43), channel_id=1, source_target_pairs={{0,4},{1,5},{2,6},{3,7},{4,0},{5,1},{6,2},{7,3},{8,12},{9,13},{10,... | collective-permute-start | bytes 196616 | tf_op jit(solution)/shard_map/ppermute | solution.py:485
  23.5 56.0 %collective-permute-start.3 = (f32[2,2,2,16,128]{4,3,2,1,0:T(8,128)S(1)}, f32[2,2,2,16,128]{4,3,2,1,0:T(8,128)S(1)}, u32[]{:S(2)}, u32[]{:S(2)}) collective-permute-start(f32[2,2,2,16,128]{4,3,2,1,0:T(8,128)S(1)} %get-tuple-element.44), channel_id=1, source_target_pairs={{0,6},{1,7},{2,4},{3,5},{4,2},{5,3},{6,0},{7,1},{8,14},{9,15},{10,... | collective-permute-start | bytes 196616 | tf_op jit(solution)/shard_map/ppermute | solution.py:485
  83.9 9.2 %collective-permute-start.4 = (f32[21,16,128]{2,1,0:T(8,128)S(1)}, f32[21,16,128]{2,1,0:T(8,128)S(1)}, u32[]{:S(2)}, u32[]{:S(2)}) collective-permute-start(f32[21,16,128]{2,1,0:T(8,128)S(1)} %get-tuple-element.24), channel_id=1, source_target_pairs={{0,8},{8,0},{16,24},{24,16},{32,40},{40,32},{48,56},{56,48},{64,72... | collective-permute-start | bytes 516104 | tf_op jit(solution)/shard_map/ppermute | solution.py:467
  84.0 9.2 %collective-permute-start.5 = (f32[21,16,128]{2,1,0:T(8,128)S(1)}, f32[21,16,128]{2,1,0:T(8,128)S(1)}, u32[]{:S(2)}, u32[]{:S(2)}) collective-permute-start(f32[21,16,128]{2,1,0:T(8,128)S(1)} %get-tuple-element.25), channel_id=1, source_target_pairs={{0,120},{8,16},{16,8},{24,32},{32,24},{40,48},{48,40},{56,64},{64,... | collective-permute-start | bytes 516104 | tf_op jit(solution)/shard_map/ppermute | solution.py:467
  93.8 7.6 %collective-permute-start.6 = (f32[432,128]{1,0:T(8,128)S(1)}, f32[432,128]{1,0:T(8,128)S(1)}, u32[]{:S(2)}, u32[]{:S(2)}) collective-permute-start(f32[432,128]{1,0:T(8,128)S(1)} %get-tuple-element.30.mine_e), channel_id=1, source_target_pairs={{0,1},{1,0},{2,3},{3,2},{4,5},{5,4},{6,7},{7,6},{8,9},{9,8},{10,11... | collective-permute-start | bytes 663560 | tf_op jit(solution)/shard_map/ppermute | solution.py:467
  94.0 9.5 %collective-permute-start.7 = (f32[432,128]{1,0:T(8,128)S(1)}, f32[432,128]{1,0:T(8,128)S(1)}, u32[]{:S(2)}, u32[]{:S(2)}) collective-permute-start(f32[432,128]{1,0:T(8,128)S(1)} %get-tuple-element.31.mine_o), channel_id=1, source_target_pairs={{0,7},{1,2},{2,1},{3,4},{4,3},{5,6},{6,5},{7,0},{8,15},{9,10},{10,... | collective-permute-start | bytes 663560 | tf_op jit(solution)/shard_map/ppermute | solution.py:467

commit v7 on v6

--- a/solution.py
+++ b/solution.py
@@ -215,7 +215,7 @@
 
 
 def edge_kernel(
-    odd, force, arrived, coef, found, edge, xe, xo, tiles, labels, source, sems, small
+    odd, force, arrived, coef, found, edge, xo, xe, tiles, labels, source, sems, small
 ):
     pull = pltpu.make_async_copy(arrived.at[:, 2 * TILE, 0, :], labels, small.at[0])
     pull.start()
@@ -257,35 +257,22 @@
                     out[19 + j] = coef[j, 15 if sign == 1 else 0]
 
 
-def inner_kernel(odd, force, found, arrived, coef, edge, inner, ye, yo, tiles, source, sems, small):
+def inner_kernel(odd, force, found, arrived, coef, edge, inner, yo, ye, tiles, source, sems, small):
     hand = pltpu.make_async_copy(found, source, small)
     hand.start()
     f = [force[axis : axis + 1, :] for axis in range(3)]
     hand.wait()
 
-    def ask(j):
+    for j in range(12):
         for i in range(8):
             fetch(source, arrived, tiles, sems.at[j], 16 + 8 * j + i, 8 * j + i)
 
-    for j in range(4):
-        ask(j)
-
-    def plane(j, more):
-        if more:
-            ask(j + 4)
+    def plane(j, _):
         arrive(tiles, sems.at[j])
         plane_step(j + 2, j, tiles, coef, inner, f)
-
-    def early(j, _):
-        plane(j, True)
-        return 0
-
-    def late(j, _):
-        plane(j, False)
-        return 0
-
-    lax.fori_loop(0, 8, early, 0)
-    lax.fori_loop(8, 12, late, 0)
+        return 0
+
+    lax.fori_loop(0, 12, plane, 0)
     for even in range(2):
 
         @pl.when(odd[1] == even)
@@ -323,7 +310,7 @@
     )(*operands)
 
 
-def join_kernel(odd, xe, xo, own_e, own_o, ye, yo):
+def join_kernel(odd, xo, xe, own_o, own_e, yo, ye):
     for own, out in ((own_e, ye), (own_o, yo)):
         for block in range(SIDE_ROWS // 8):
             out[8 * block : 8 * block + 8, :] = own[8 * block : 8 * block + 8, :]
@@ -348,7 +335,7 @@
                                 out[at : at + 1, :] = value
 
 
-def middle_kernel(odd, force, edge, inner, coef, xe, xo, out, wide, again, result, sems):
+def middle_kernel(odd, force, edge, inner, coef, xo, xe, out, wide, again, result, sems):
     flag = odd[0]
     for j in range(4):
         for q in range(19):
@@ -447,7 +434,7 @@
         number += len(listed)
 
 
-def last_kernel(odd, force, mine_e, mine_o, came_e, came_o, _before, out, rows, patch, sem):
+def last_kernel(odd, force, mine_o, mine_e, came_o, came_e, _before, out, rows, patch, sem):
     f = [force[axis : axis + 1, :] for axis in range(3)]
     for even in range(2):
 
@@ -512,7 +499,7 @@
     coef, odd, drive = lax.optimization_barrier((coef, odd, drive))
     hbm = pl.BlockSpec(memory_space=pltpu.HBM)
     posts = [jax.ShapeDtypeStruct((19, n, 16, 128), F32) for n in (4, 12)]
-    found, edge, xe, xo = pl.pallas_call(
+    found, edge, xo, xe = pl.pallas_call(
         edge_kernel,
         out_shape=[jax.ShapeDtypeStruct((8, 128), jnp.int32), posts[0], FACE, FACE],
         in_specs=[SMEM_SPEC, VMEM_SPEC, hbm, VMEM_SPEC],
@@ -529,7 +516,7 @@
     )(odd, drive, arrived, coef)
     from_xo = swap(xo, "gx", False)
     from_xe = swap(xe, "gx", True)
-    inner, own_ye, own_yo = pl.pallas_call(
+    inner, own_yo, own_ye = pl.pallas_call(
         inner_kernel,
         out_shape=[posts[1], SIDE, SIDE],
         in_specs=[SMEM_SPEC, VMEM_SPEC, VMEM_SPEC, hbm, VMEM_SPEC, VMEM_SPEC],
@@ -543,13 +530,13 @@
         compiler_params=pltpu.CompilerParams(vmem_limit_bytes=VMEM_LIMIT),
         cost_estimate=pl.CostEstimate(flops=6_000_000, bytes_accessed=8_000_000, transcendentals=0),
     )(odd, drive, found, arrived, coef, edge)
-    ye, yo = call(join_kernel, [SIDE, SIDE], (odd, from_xe, from_xo, own_ye, own_yo), 500_000)
+    yo, ye = call(join_kernel, [SIDE, SIDE], (odd, from_xo, from_xe, own_yo, own_ye), 500_000)
     from_yo = swap(yo, "gy", False)
     from_ye = swap(ye, "gy", True)
     result = call(
         middle_kernel,
         jax.ShapeDtypeStruct((19, 16, 16, 128), F32),
-        (odd, drive, edge, inner, coef, from_xe, from_xo),
+        (odd, drive, edge, inner, coef, from_xo, from_xe),
         12_000_000,
         out_specs=hbm,
         scratch_shapes=[
@@ -572,7 +559,7 @@
         ],
         compiler_params=pltpu.CompilerParams(vmem_limit_bytes=VMEM_LIMIT),
         cost_estimate=pl.CostEstimate(flops=2_000_000, bytes_accessed=2_000_000, transcendentals=0),
-    )(odd, drive, ye, yo, from_ye, from_yo, result)
+    )(odd, drive, yo, ye, from_yo, from_ye, result)
 
 
 def solution(mesh):

time: 106 us -> 106 us (level)
  waiting for transfers between devices: 58.3 us -> 60 us
    ppermute x4, waiting for transfers between devices: 2.13 us -> 3.94 us  [swap(): return lax.ppermute(value, axis, pairs)]
where the time goes in v7:
time: 106 us; the launch traced here: 105 us
  waiting for transfers between devices  60 us (57%)
  starting transfers between devices  26.8 us (25%)
  Pallas kernels  17 us (16%)
  other arithmetic  1.1 us (1%)
    ppermute x3, waiting for transfers between devices, pieces_of(): lax.ppermute(message, 'gy', [(i, i ^ 2 * k) for i in range(8)])  54.8 us
    all_to_all x1, starting transfers between devices, local(): lax.all_to_all(packed, ('gx', 'gy'), split_axis=0, concat_axis=0, tiled=T...  11.7 us
    ppermute x4, starting transfers between devices, swap(): return lax.ppermute(value, axis, pairs)  6.83 us
    ppermute x3, starting transfers between devices, pieces_of(): lax.ppermute(message, 'gy', [(i, i ^ 2 * k) for i in range(8)])  6.58 us
    pallas_call x2, Pallas kernels, call(): pl.pallas_call(kernel, out_shape=out_shape, in_specs=[SMEM_SPEC] * scalar...  5.16 us
    pallas_call x1, Pallas kernels, local(): pl.pallas_call(inner_kernel, out_shape=[posts[1], SIDE, SIDE], in_specs=[...  3.97 us
    ppermute x4, waiting for transfers between devices, swap(): return lax.ppermute(value, axis, pairs)  3.94 us
    pallas_call x1, Pallas kernels, local(): pl.pallas_call(edge_kernel, out_shape=[jax.ShapeDtypeStruct((8, 128), jnp...  3.56 us
  transfers between devices with their start and end apart: 9, of which 5 were waited for; matrix products, arithmetic and copies ran while one was open for 0% of the time, Pallas kernels for 11%

profile of v7, /device:TPU:0, one launch (start us, length us, event | category | flops | bytes accessed | tf_op | source)
XLA Modules:
  0.0 105.4 jit_solution(10437085926999802462)
XLA Ops:
  0.0 0.9 fusion.1
  0.9 1.7 %collective-permute-start = (f32[2,2,4,16,128]{4,3,2,1,0:T(8,128)S(1)}, f32[2,2,4,16,128]{4,3,2,1,0:T(8,128)S(1)}, u32[]{:S(2)}, u32[]{:S(2)}) collective-permute-start(f32[2,2,4,16,128]{4,3,2,1,0:T(8,128)S(1)} %fusion.1), channel_id=1, source_target_pairs={{0,1},{1,0},{2,3},{3,2},{4,5},{5,4},{6,7},{7,6},{8,9},{9,8},{10,11... | collective-permute-start | bytes 393224 | tf_op jit(solution)/shard_map/ppermute | solution.py:462
  2.6 2.8 %shard_map.64 = f32[128,77,1,128]{3,2,1,0:T(1,128)} custom-call(s32[128]{0:T(128)} %target_hbm.1, f32[19,256,128]{2,1,0:T(8,128)} %bitcast.43), custom_call_target="tpu_custom_call" | custom-call | bytes 8000000 | tf_op jit(solution)/shard_map/pallas_call | solution.py:166
  5.4 0.0 copy-start.3
  5.4 0.0 copy-start.1
  5.4 0.7 collective-permute-done
  6.1 11.7 %all-to-all-start = ((f32[128,77,1,128]{3,2,1,0:T(1,128)}), f32[128,77,1,128]{3,2,1,0:T(1,128)}, u32[]{:S(2)}, u32[]{:S(2)}) async-start(f32[128,77,1,128]{3,2,1,0:T(1,128)} %shard_map.64), calls=%async_computation | async-start | bytes 10092544 | tf_op jit(solution)/shard_map/all_to_all | solution.py:491
  17.8 0.0 copy-start.2
  18.0 2.5 %collective-permute-start.1 = (f32[2,2,2,16,128]{4,3,2,1,0:T(8,128)S(1)}, f32[2,2,2,16,128]{4,3,2,1,0:T(8,128)S(1)}, u32[]{:S(2)}, u32[]{:S(2)}) collective-permute-start(f32[2,2,2,16,128]{4,3,2,1,0:T(8,128)S(1)} %get-tuple-element.42), channel_id=1, source_target_pairs={{0,2},{1,3},{2,0},{3,1},{4,6},{5,7},{6,4},{7,5},{8,10},{9,11},{10,... | collective-permute-start | bytes 196616 | tf_op jit(solution)/shard_map/ppermute | solution.py:472
  20.5 3.0 %collective-permute-start.2 = (f32[2,2,2,16,128]{4,3,2,1,0:T(8,128)S(1)}, f32[2,2,2,16,128]{4,3,2,1,0:T(8,128)S(1)}, u32[]{:S(2)}, u32[]{:S(2)}) collective-permute-start(f32[2,2,2,16,128]{4,3,2,1,0:T(8,128)S(1)} %get-tuple-element.43), channel_id=1, source_target_pairs={{0,4},{1,5},{2,6},{3,7},{4,0},{5,1},{6,2},{7,3},{8,12},{9,13},{10,... | collective-permute-start | bytes 196616 | tf_op jit(solution)/shard_map/ppermute | solution.py:472
  23.5 1.1 %collective-permute-start.3 = (f32[2,2,2,16,128]{4,3,2,1,0:T(8,128)S(1)}, f32[2,2,2,16,128]{4,3,2,1,0:T(8,128)S(1)}, u32[]{:S(2)}, u32[]{:S(2)}) collective-permute-start(f32[2,2,2,16,128]{4,3,2,1,0:T(8,128)S(1)} %get-tuple-element.44), channel_id=1, source_target_pairs={{0,6},{1,7},{2,4},{3,5},{4,2},{5,3},{6,0},{7,1},{8,14},{9,15},{10,... | collective-permute-start | bytes 196616 | tf_op jit(solution)/shard_map/ppermute | solution.py:472
  24.6 0.1 pad_add_fusion.odd
  24.7 52.4 %collective-permute-done.1 = f32[2,2,2,16,128]{4,3,2,1,0:T(8,128)S(1)} collective-permute-done((f32[2,2,2,16,128]{4,3,2,1,0:T(8,128)S(1)}, f32[2,2,2,16,128]{4,3,2,1,0:T(8,128)S(1)}, u32[]{:S(2)}, u32[]{:S(2)}) %collective-permute-start.1) | collective-permute-done | bytes 65568 | tf_op jit(solution)/shard_map/ppermute | solution.py:472
  77.1 2.3 %collective-permute-done.3 = f32[2,2,2,16,128]{4,3,2,1,0:T(8,128)S(1)} collective-permute-done((f32[2,2,2,16,128]{4,3,2,1,0:T(8,128)S(1)}, f32[2,2,2,16,128]{4,3,2,1,0:T(8,128)S(1)}, u32[]{:S(2)}, u32[]{:S(2)}) %collective-permute-start.3) | collective-permute-done | bytes 65568 | tf_op jit(solution)/shard_map/ppermute | solution.py:472
  79.6 0.1 broadcast_in_dim.2.force
  79.7 0.6 all-to-all-done.arrived
  80.3 3.6 %shard_map.65 = (s32[8,128]{1,0:T(8,128)S(1)}, f32[19,4,16,128]{3,2,1,0:T(8,128)S(1)}, f32[21,16,128]{2,1,0:T(8,128)S(1)}, f32[21,16,128]{2,1,0:T(8,128)S(1)}) custom-call(s32[2]{0:T(128)S(1)} %pad_add_fusion.odd, f32[8,128]{1,0:T(8,128)S(1)} %broadcast_in_dim.2.force, f32[128,77,1,128]{3,2,1,0:T(1,128)} %all-to-all-done.arrived, ...), custom_call_target="tpu_custom_call" | custom-call | flops 2000000 | bytes 8000000 | tf_op jit(solution)/shard_map/pallas_call | solution.py:502
  83.9 3.8 %collective-permute-start.4 = (f32[21,16,128]{2,1,0:T(8,128)S(1)}, f32[21,16,128]{2,1,0:T(8,128)S(1)}, u32[]{:S(2)}, u32[]{:S(2)}) collective-permute-start(f32[21,16,128]{2,1,0:T(8,128)S(1)} %get-tuple-element.24), channel_id=1, source_target_pairs={{0,120},{8,16},{16,8},{24,32},{32,24},{40,48},{48,40},{56,64},{64,... | collective-permute-start | bytes 516104 | tf_op jit(solution)/shard_map/ppermute | solution.py:454
  87.7 4.0 %shard_map.66 = (f32[19,12,16,128]{3,2,1,0:T(8,128)S(1)}, f32[432,128]{1,0:T(8,128)S(1)}, f32[432,128]{1,0:T(8,128)S(1)}) custom-call(s32[2]{0:T(128)S(1)} %pad_add_fusion.odd, f32[8,128]{1,0:T(8,128)S(1)} %broadcast_in_dim.2.force, s32[8,128]{1,0:T(8,128)S(1)} %get-tuple-element.26.found, f32[128,77,1,128]{3,2,1,0:T(1,128)} %all-to-all-done.arrived, ...), custom_call_target="tpu_custom_call" | custom-call | flops 6000000 | bytes 8000000 | tf_op jit(solution)/shard_map/pallas_call | solution.py:519
  91.7 0.6 shard_map.67
  92.3 3.1 %collective-permute-start.6 = (f32[432,128]{1,0:T(8,128)S(1)}, f32[432,128]{1,0:T(8,128)S(1)}, u32[]{:S(2)}, u32[]{:S(2)}) collective-permute-start(f32[432,128]{1,0:T(8,128)S(1)} %get-tuple-element.30.mine_o), channel_id=1, source_target_pairs={{0,7},{1,2},{2,1},{3,4},{4,3},{5,6},{6,5},{7,0},{8,15},{9,10},{10,... | collective-permute-start | bytes 663560 | tf_op jit(solution)/shard_map/ppermute | solution.py:454
  95.4 4.5 %shard_map.68._before = f32[19,16,16,128]{3,2,1,0:T(8,128)} custom-call(s32[2]{0:T(128)S(1)} %pad_add_fusion.odd, f32[8,128]{1,0:T(8,128)S(1)} %broadcast_in_dim.2.force, f32[19,4,16,128]{3,2,1,0:T(8,128)S(1)} %get-tuple-element.27.edge, f32[19,12,16,128]{3,2,1,0:T(8,128)S(1)} %get-tuple-element.32.inner, f32[2,16,16,128]{3,2,1,0:T(8,128)S(1)} %pad_maximum_fusion.1.coef, ...), custom_call_target="tpu_custom_call" | custom-call | flops 12000000 | bytes 12000000 | tf_op jit(solution)/shard_map/pallas_call | solution.py:303
  99.9 3.9 %collective-permute-done.6.came_o = f32[432,128]{1,0:T(8,128)S(1)} collective-permute-done((f32[432,128]{1,0:T(8,128)S(1)}, f32[432,128]{1,0:T(8,128)S(1)}, u32[]{:S(2)}, u32[]{:S(2)}) %collective-permute-start.6) | collective-permute-done | bytes 221216 | tf_op jit(solution)/shard_map/ppermute | solution.py:454
  103.8 1.5 %shard_map.69 = f32[19,16,16,128]{3,2,1,0:T(8,128)} custom-call(s32[2]{0:T(128)S(1)} %pad_add_fusion.odd, f32[8,128]{1,0:T(8,128)S(1)} %broadcast_in_dim.2.force, f32[432,128]{1,0:T(8,128)S(1)} %get-tuple-element.30.mine_o, f32[432,128]{1,0:T(8,128)S(1)} %get-tuple-element.31.mine_e, ...), custom_call_target="tpu_custom_call", output_to_operand_aliasing={{}: (6, {})} | custom-call | flops 2000000 | bytes 2000000 | tf_op jit(solution)/shard_map/pallas_call | solution.py:549
  (20 shorter events, 0.2 us)
Async XLA Ops:
  0.9 5.2 %collective-permute-start = (f32[2,2,4,16,128]{4,3,2,1,0:T(8,128)S(1)}, f32[2,2,4,16,128]{4,3,2,1,0:T(8,128)S(1)}, u32[]{:S(2)}, u32[]{:S(2)}) collective-permute-start(f32[2,2,4,16,128]{4,3,2,1,0:T(8,128)S(1)} %fusion.1), channel_id=1, source_target_pairs={{0,1},{1,0},{2,3},{3,2},{4,5},{5,4},{6,7},{7,6},{8,9},{9,8},{10,11... | collective-permute-start | bytes 393224 | tf_op jit(solution)/shard_map/ppermute | solution.py:462
  5.4 12.5 %copy-start.3 = (f32[3]{0:T(128)S(1)}, f32[3]{0:T(128)}, u32[]{:S(2)}) copy-start(f32[3]{0:T(128)} %param.11) | copy-start | bytes 40
  5.4 12.5 %copy-start = (f32[2,128,128]{2,1,0:T(8,128)S(1)}, f32[2,128,128]{2,1,0:T(8,128)}, u32[]{:S(2)}) copy-start(f32[2,128,128]{2,1,0:T(8,128)} %param.8) | copy-start | bytes 393220
  5.4 12.5 %copy-start.1 = (f32[2,128,128]{2,1,0:T(8,128)S(1)}, f32[2,128,128]{2,1,0:T(8,128)}, u32[]{:S(2)}) copy-start(f32[2,128,128]{2,1,0:T(8,128)} %param.9) | copy-start | bytes 393220
  6.1 74.2 %all-to-all-start = ((f32[128,77,1,128]{3,2,1,0:T(1,128)}), f32[128,77,1,128]{3,2,1,0:T(1,128)}, u32[]{:S(2)}, u32[]{:S(2)}) async-start(f32[128,77,1,128]{3,2,1,0:T(1,128)} %shard_map.64), calls=%async_computation | async-start | bytes 10092544 | tf_op jit(solution)/shard_map/all_to_all | solution.py:491
  17.8 61.8 %copy-start.2 = (s32[16,16,128]{2,1,0:T(8,128)S(1)}, s32[16,16,128]{2,1,0:T(8,128)}, u32[]{:S(2)}) copy-start(s32[16,16,128]{2,1,0:T(8,128)} %param.10) | copy-start | bytes 393220
  18.0 59.1 %collective-permute-start.1 = (f32[2,2,2,16,128]{4,3,2,1,0:T(8,128)S(1)}, f32[2,2,2,16,128]{4,3,2,1,0:T(8,128)S(1)}, u32[]{:S(2)}, u32[]{:S(2)}) collective-permute-start(f32[2,2,2,16,128]{4,3,2,1,0:T(8,128)S(1)} %get-tuple-element.42), channel_id=1, source_target_pairs={{0,2},{1,3},{2,0},{3,1},{4,6},{5,7},{6,4},{7,5},{8,10},{9,11},{10,... | collective-permute-start | bytes 196616 | tf_op jit(solution)/shard_map/ppermute | solution.py:472
  20.5 56.6 %collective-permute-start.2 = (f32[2,2,2,16,128]{4,3,2,1,0:T(8,128)S(1)}, f32[2,2,2,16,128]{4,3,2,1,0:T(8,128)S(1)}, u32[]{:S(2)}, u32[]{:S(2)}) collective-permute-start(f32[2,2,2,16,128]{4,3,2,1,0:T(8,128)S(1)} %get-tuple-element.43), channel_id=1, source_target_pairs={{0,4},{1,5},{2,6},{3,7},{4,0},{5,1},{6,2},{7,3},{8,12},{9,13},{10,... | collective-permute-start | bytes 196616 | tf_op jit(solution)/shard_map/ppermute | solution.py:472
  23.5 56.0 %collective-permute-start.3 = (f32[2,2,2,16,128]{4,3,2,1,0:T(8,128)S(1)}, f32[2,2,2,16,128]{4,3,2,1,0:T(8,128)S(1)}, u32[]{:S(2)}, u32[]{:S(2)}) collective-permute-start(f32[2,2,2,16,128]{4,3,2,1,0:T(8,128)S(1)} %get-tuple-element.44), channel_id=1, source_target_pairs={{0,6},{1,7},{2,4},{3,5},{4,2},{5,3},{6,0},{7,1},{8,14},{9,15},{10,... | collective-permute-start | bytes 196616 | tf_op jit(solution)/shard_map/ppermute | solution.py:472
  83.9 7.7 %collective-permute-start.4 = (f32[21,16,128]{2,1,0:T(8,128)S(1)}, f32[21,16,128]{2,1,0:T(8,128)S(1)}, u32[]{:S(2)}, u32[]{:S(2)}) collective-permute-start(f32[21,16,128]{2,1,0:T(8,128)S(1)} %get-tuple-element.24), channel_id=1, source_target_pairs={{0,120},{8,16},{16,8},{24,32},{32,24},{40,48},{48,40},{56,64},{64,... | collective-permute-start | bytes 516104 | tf_op jit(solution)/shard_map/ppermute | solution.py:454
  87.7 4.0 %collective-permute-start.5 = (f32[21,16,128]{2,1,0:T(8,128)S(1)}, f32[21,16,128]{2,1,0:T(8,128)S(1)}, u32[]{:S(2)}, u32[]{:S(2)}) collective-permute-start(f32[21,16,128]{2,1,0:T(8,128)S(1)} %get-tuple-element.25), channel_id=1, source_target_pairs={{0,8},{8,0},{16,24},{24,16},{32,40},{40,32},{48,56},{56,48},{64,72... | collective-permute-start | bytes 516104 | tf_op jit(solution)/shard_map/ppermute | solution.py:454
  92.3 11.5 %collective-permute-start.6 = (f32[432,128]{1,0:T(8,128)S(1)}, f32[432,128]{1,0:T(8,128)S(1)}, u32[]{:S(2)}, u32[]{:S(2)}) collective-permute-start(f32[432,128]{1,0:T(8,128)S(1)} %get-tuple-element.30.mine_o), channel_id=1, source_target_pairs={{0,7},{1,2},{2,1},{3,4},{4,3},{5,6},{6,5},{7,0},{8,15},{9,10},{10,... | collective-permute-start | bytes 663560 | tf_op jit(solution)/shard_map/ppermute | solution.py:454
  95.4 8.5 %collective-permute-start.7 = (f32[432,128]{1,0:T(8,128)S(1)}, f32[432,128]{1,0:T(8,128)S(1)}, u32[]{:S(2)}, u32[]{:S(2)}) collective-permute-start(f32[432,128]{1,0:T(8,128)S(1)} %get-tuple-element.31.mine_e), channel_id=1, source_target_pairs={{0,1},{1,0},{2,3},{3,2},{4,5},{5,4},{6,7},{7,6},{8,9},{9,8},{10,11... | collective-permute-start | bytes 663560 | tf_op jit(solution)/shard_map/ppermute | solution.py:454

commit v8 on v7

--- a/solution.py
+++ b/solution.py
@@ -49,6 +49,7 @@
 
 COUNT = 21
 SIDE_ROWS = 432
+CORNER_ROWS = 88
 
 
 def collide(dist, solid, omega, force):
@@ -187,11 +188,11 @@
     return jnp.where(flag == 0, even, odd)
 
 
-def plane_step(x, at, tiles, coef, post, f):
+def plane_step(x, place, at, tiles, coef, post, f):
     for r in range(2):
         dist = []
         for q in range(19):
-            value = tiles[pl.ds(at * (8 * ROWS) + r * 19 + q, 8, stride=ROWS), :]
+            value = tiles[pl.ds(place * (8 * ROWS) + r * 19 + q, 8, stride=ROWS), :]
             dist.append(WEIGHT[q] * value + WEIGHT[q])
         solid = coef[0, x, pl.ds(r, 8, stride=2), :]
         omega = coef[1, x, pl.ds(r, 8, stride=2), :]
@@ -215,7 +216,7 @@
 
 
 def edge_kernel(
-    odd, force, arrived, coef, found, edge, xo, xe, tiles, labels, source, sems, small
+    odd, force, arrived, coef, tiles, edge, xe, xo, labels, found, source, sems, small
 ):
     pull = pltpu.make_async_copy(arrived.at[:, 2 * TILE, 0, :], labels, small.at[0])
     pull.start()
@@ -236,13 +237,17 @@
     hand = pltpu.make_async_copy(found, source, small.at[1])
     hand.start()
     hand.wait()
-    for j, x in enumerate((0, 1, 14, 15)):
+    for x in (0, 1, 14, 15):
         for i in range(8):
-            fetch(source, arrived, tiles, sems.at[j], 8 * x + i, 8 * j + i)
+            fetch(source, arrived, tiles, sems.at[x], 8 * x + i, 8 * x + i)
 
     def plane(j, _):
-        arrive(tiles, sems.at[j])
-        plane_step(jnp.where(j < 2, j, j + 12), j, tiles, coef, edge, f)
+        x = jnp.where(j < 2, j, j + 12)
+        for i in range(24):
+            slot = 16 + 24 * j + i
+            fetch(source, arrived, tiles, sems.at[2 + 3 * j + i // 8], slot, slot)
+        arrive(tiles, sems.at[x])
+        plane_step(x, x, j, tiles, coef, edge, f)
         return 0
 
     lax.fori_loop(0, 4, plane, 0)
@@ -256,20 +261,15 @@
                 for j in range(2):
                     out[19 + j] = coef[j, 15 if sign == 1 else 0]
 
-
-def inner_kernel(odd, force, found, arrived, coef, edge, inner, yo, ye, tiles, source, sems, small):
-    hand = pltpu.make_async_copy(found, source, small)
-    hand.start()
+    for x in range(2, 14):
+        arrive(tiles, sems.at[x])
+
+
+def inner_kernel(odd, force, tiles, coef, edge, inner, ye, yo):
     f = [force[axis : axis + 1, :] for axis in range(3)]
-    hand.wait()
-
-    for j in range(12):
-        for i in range(8):
-            fetch(source, arrived, tiles, sems.at[j], 16 + 8 * j + i, 8 * j + i)
 
     def plane(j, _):
-        arrive(tiles, sems.at[j])
-        plane_step(j + 2, j, tiles, coef, inner, f)
+        plane_step(j + 2, j + 2, j, tiles, coef, inner, f)
         return 0
 
     lax.fori_loop(0, 12, plane, 0)
@@ -285,18 +285,18 @@
                             value = inner[q, x - 2, row : row + 1, :]
                         else:
                             value = edge[q, x if x < 2 else x - 12, row : row + 1, :]
-                        out[i * EXT + 2 + x : i * EXT + 3 + x, :] = value
+                        out[i, x : x + 1, :] = value
                 row = 15 if sign == 1 else 0
                 for j in range(2):
                     for x in range(16):
-                        at = (19 + j) * EXT + 2 + x
-                        out[at : at + 1, :] = coef[j, x, row : row + 1, :]
+                        out[19 + j, x : x + 1, :] = coef[j, x, row : row + 1, :]
 
 
 VMEM_SPEC = pl.BlockSpec(memory_space=pltpu.VMEM)
 SMEM_SPEC = pl.BlockSpec(memory_space=pltpu.SMEM)
 FACE = jax.ShapeDtypeStruct((COUNT, 16, 128), F32)
 SIDE = jax.ShapeDtypeStruct((SIDE_ROWS, 128), F32)
+CORNER = jax.ShapeDtypeStruct((CORNER_ROWS, 128), F32)
 
 
 def call(kernel, out_shape, operands, work, scalars=1, **more):
@@ -310,32 +310,41 @@
     )(*operands)
 
 
-def join_kernel(odd, xo, xe, own_o, own_e, yo, ye):
-    for own, out in ((own_e, ye), (own_o, yo)):
-        for block in range(SIDE_ROWS // 8):
-            out[8 * block : 8 * block + 8, :] = own[8 * block : 8 * block + 8, :]
+def corner_kernel(odd, xe, xo, ce, co):
     have = [
         {e: n for n, e in enumerate(entries(0, toward) + [(19, 0), (20, 0)])} for toward in (1, -1)
     ]
     zero = jnp.zeros((1, 128), F32)
+    for out in (ce, co):
+        out[CORNER_ROWS - 8 : CORNER_ROWS, :] = jnp.zeros((8, 128), F32)
     for even_x in range(2):
         for even_y in range(2):
 
             @pl.when((odd[0] == even_x) & (odd[1] == even_y))
             def _():
                 halves = (xo, xe) if even_x == 0 else (xe, xo)
-                for out, sign in ((ye, 1 - 2 * even_y), (yo, 2 * even_y - 1)):
+                for out, sign in ((ce, 1 - 2 * even_y), (co, 2 * even_y - 1)):
                     for i, (q, layer) in enumerate(entries(1, sign) + [(19, 0), (20, 0)]):
                         row = 15 - layer if sign == 1 else layer
-                        for toward in range(2):
-                            for deep in range(2):
-                                at = i * EXT + ((1 - deep) if toward == 0 else 18 + deep)
-                                n = have[toward].get((q, deep))
-                                value = zero if n is None else halves[toward][n, row : row + 1, :]
-                                out[at : at + 1, :] = value
-
-
-def middle_kernel(odd, force, edge, inner, coef, xo, xe, out, wide, again, result, sems):
+                        for column, (toward, deep) in enumerate(((0, 1), (0, 0), (1, 0), (1, 1))):
+                            n = have[toward].get((q, deep))
+                            value = zero if n is None else halves[toward][n, row : row + 1, :]
+                            at = 4 * i + column
+                            out[at : at + 1, :] = value
+
+
+def widen(rows, ends, out):
+    for i in range(COUNT):
+        at = i * EXT
+        out[at : at + 2, :] = ends[4 * i : 4 * i + 2, :]
+        out[at + 2 : at + 18, :] = rows[i]
+        out[at + 18 : at + 20, :] = ends[4 * i + 2 : 4 * i + 4, :]
+    out[COUNT * EXT : SIDE_ROWS, :] = jnp.zeros((SIDE_ROWS - COUNT * EXT, 128), F32)
+
+
+def middle_kernel(
+    odd, force, edge, inner, coef, xe, xo, ye, yo, ce, co, out, own_e, own_o, wide, again, result, sems
+):
     flag = odd[0]
     for j in range(4):
         for q in range(19):
@@ -387,6 +396,8 @@
         return 0
 
     lax.fori_loop(0, 16, finish, 0)
+    widen(ye, ce, own_e)
+    widen(yo, co, own_o)
     for x in range(16):
         pltpu.make_async_copy(result.at[x], out.at[:, x], sems.at[x]).wait()
 
@@ -434,7 +445,11 @@
         number += len(listed)
 
 
-def last_kernel(odd, force, mine_o, mine_e, came_o, came_e, _before, out, rows, patch, sem):
+def last_kernel(
+    odd, force, mine_e, mine_o, rows_e, rows_o, ends_e, ends_o, _before, out, came_e, came_o, rows, patch, sem
+):
+    widen(rows_e, ends_e, came_e)
+    widen(rows_o, ends_o, came_o)
     f = [force[axis : axis + 1, :] for axis in range(3)]
     for even in range(2):
 
@@ -499,46 +514,34 @@
     coef, odd, drive = lax.optimization_barrier((coef, odd, drive))
     hbm = pl.BlockSpec(memory_space=pltpu.HBM)
     posts = [jax.ShapeDtypeStruct((19, n, 16, 128), F32) for n in (4, 12)]
-    found, edge, xo, xe = pl.pallas_call(
+    tiles, edge, xe, xo = pl.pallas_call(
         edge_kernel,
-        out_shape=[jax.ShapeDtypeStruct((8, 128), jnp.int32), posts[0], FACE, FACE],
+        out_shape=[jax.ShapeDtypeStruct((HELD * ROWS, 128), F32), posts[0], FACE, FACE],
         in_specs=[SMEM_SPEC, VMEM_SPEC, hbm, VMEM_SPEC],
         out_specs=[VMEM_SPEC] * 4,
         scratch_shapes=[
-            pltpu.VMEM((32 * ROWS, 128), F32),
             pltpu.VMEM((DEVICES, 128), F32),
+            pltpu.VMEM((8, 128), jnp.int32),
             pltpu.SMEM((8, 128), jnp.int32),
-            pltpu.SemaphoreType.DMA((4,)),
+            pltpu.SemaphoreType.DMA((16,)),
             pltpu.SemaphoreType.DMA((2,)),
         ],
         compiler_params=pltpu.CompilerParams(vmem_limit_bytes=VMEM_LIMIT),
         cost_estimate=pl.CostEstimate(flops=2_000_000, bytes_accessed=8_000_000, transcendentals=0),
     )(odd, drive, arrived, coef)
-    from_xo = swap(xo, "gx", False)
-    from_xe = swap(xe, "gx", True)
-    inner, own_yo, own_ye = pl.pallas_call(
-        inner_kernel,
-        out_shape=[posts[1], SIDE, SIDE],
-        in_specs=[SMEM_SPEC, VMEM_SPEC, VMEM_SPEC, hbm, VMEM_SPEC, VMEM_SPEC],
-        out_specs=[VMEM_SPEC] * 3,
-        scratch_shapes=[
-            pltpu.VMEM((96 * ROWS, 128), F32),
-            pltpu.SMEM((8, 128), jnp.int32),
-            pltpu.SemaphoreType.DMA((12,)),
-            pltpu.SemaphoreType.DMA,
-        ],
-        compiler_params=pltpu.CompilerParams(vmem_limit_bytes=VMEM_LIMIT),
-        cost_estimate=pl.CostEstimate(flops=6_000_000, bytes_accessed=8_000_000, transcendentals=0),
-    )(odd, drive, found, arrived, coef, edge)
-    yo, ye = call(join_kernel, [SIDE, SIDE], (odd, from_xo, from_xe, own_yo, own_ye), 500_000)
-    from_yo = swap(yo, "gy", False)
-    from_ye = swap(ye, "gy", True)
-    result = call(
+    from_xe, from_xo = swap(xe, "gx", True), swap(xo, "gx", False)
+    inner, ye, yo = call(
+        inner_kernel, [posts[1], FACE, FACE], (odd, drive, tiles, coef, edge), 6_000_000
+    )
+    from_ye, from_yo = swap(ye, "gy", True), swap(yo, "gy", False)
+    ce, co = call(corner_kernel, [CORNER, CORNER], (odd, from_xe, from_xo), 200_000)
+    from_ce, from_co = swap(ce, "gy", True), swap(co, "gy", False)
+    result, own_e, own_o = call(
         middle_kernel,
-        jax.ShapeDtypeStruct((19, 16, 16, 128), F32),
-        (odd, drive, edge, inner, coef, from_xo, from_xe),
+        [jax.ShapeDtypeStruct((19, 16, 16, 128), F32), SIDE, SIDE],
+        (odd, drive, edge, inner, coef, from_xe, from_xo, ye, yo, ce, co),
         12_000_000,
-        out_specs=hbm,
+        out_specs=[hbm, VMEM_SPEC, VMEM_SPEC],
         scratch_shapes=[
             pltpu.VMEM((19, EXT, 32, 128), F32),
             pltpu.VMEM((19, 18, 32, 128), F32),
@@ -549,17 +552,19 @@
     return pl.pallas_call(
         last_kernel,
         out_shape=jax.ShapeDtypeStruct((19, 16, 16, 128), F32),
-        in_specs=[SMEM_SPEC] + [VMEM_SPEC] * 5 + [hbm],
+        in_specs=[SMEM_SPEC] + [VMEM_SPEC] * 7 + [hbm],
         out_specs=hbm,
-        input_output_aliases={6: 0},
+        input_output_aliases={8: 0},
         scratch_shapes=[
+            pltpu.VMEM((SIDE_ROWS, 128), F32),
+            pltpu.VMEM((SIDE_ROWS, 128), F32),
             pltpu.VMEM((2, 19, 24, 128), F32),
             pltpu.VMEM((38, 16, 128), F32),
             pltpu.SemaphoreType.DMA,
         ],
         compiler_params=pltpu.CompilerParams(vmem_limit_bytes=VMEM_LIMIT),
         cost_estimate=pl.CostEstimate(flops=2_000_000, bytes_accessed=2_000_000, transcendentals=0),
-    )(odd, drive, yo, ye, from_yo, from_ye, result)
+    )(odd, drive, own_e, own_o, from_ye, from_yo, from_ce, from_co, result)
 
 
 def solution(mesh):

time: 106 us -> 106 us (level)
  starting transfers between devices: 26.8 us -> 31 us
  waiting for transfers between devices: 60 us -> 56.1 us
    ppermute x4 -> x6, starting transfers between devices: 6.83 us -> 11 us  [swap(): return lax.ppermute(value, axis, pairs)]
    ppermute x4 -> x6, waiting for transfers between devices: 3.94 us -> 0.02 us  [swap(): return lax.ppermute(value, axis, pairs)]
    pallas_call x2 -> x1, Pallas kernels: 7.53 us -> 4.65 us  [local(): pl.pallas_call(edge_kernel, out_shape=[jax.ShapeDtypeStruct((HELD * ROWS,...]
    pallas_call x2 -> x3, Pallas kernels: 5.16 us -> 7.51 us  [call(): pl.pallas_call(kernel, out_shape=out_shape, in_specs=[SMEM_SPEC] * scalar...]
  transfers between devices with their start and end apart: 9 -> 11, of which waited for: 5 -> 4; matrix products, arithmetic and copies ran while one was open for 0% -> 0% of each run, Pallas kernels for 11% -> 10%
where the time goes in v8:
time: 106 us; the launch traced here: 105 us
  waiting for transfers between devices  56.1 us (53%)
  starting transfers between devices  31 us (29%)
  Pallas kernels  16.5 us (16%)
  other arithmetic  1.1 us (1%)
    ppermute x3, waiting for transfers between devices, pieces_of(): lax.ppermute(message, 'gy', [(i, i ^ 2 * k) for i in range(8)])  54.8 us
    all_to_all x1, starting transfers between devices, local(): lax.all_to_all(packed, ('gx', 'gy'), split_axis=0, concat_axis=0, tiled=T...  11.7 us
    ppermute x6, starting transfers between devices, swap(): return lax.ppermute(value, axis, pairs)  11 us
    pallas_call x3, Pallas kernels, call(): pl.pallas_call(kernel, out_shape=out_shape, in_specs=[SMEM_SPEC] * scalar...  7.51 us
    ppermute x3, starting transfers between devices, pieces_of(): lax.ppermute(message, 'gy', [(i, i ^ 2 * k) for i in range(8)])  6.58 us
    pallas_call x1, Pallas kernels, local(): pl.pallas_call(edge_kernel, out_shape=[jax.ShapeDtypeStruct((HELD * ROWS,...  4.65 us
    pallas_call x1, Pallas kernels, pack(): pl.pallas_call(pack_kernel, out_shape=jax.ShapeDtypeStruct((DEVICES, PAIR...  2.79 us
  transfers between devices with their start and end apart: 11, of which 4 were waited for; matrix products, arithmetic and copies ran while one was open for 0% of the time, Pallas kernels for 10%

profile of v8, /device:TPU:0, one launch (start us, length us, event | category | flops | bytes accessed | tf_op | source)
XLA Modules:
  0.0 105.2 jit_solution(7313365360620054151)
XLA Ops:
  0.0 0.9 fusion.1
  0.9 1.7 %collective-permute-start = (f32[2,2,4,16,128]{4,3,2,1,0:T(8,128)S(1)}, f32[2,2,4,16,128]{4,3,2,1,0:T(8,128)S(1)}, u32[]{:S(2)}, u32[]{:S(2)}) collective-permute-start(f32[2,2,4,16,128]{4,3,2,1,0:T(8,128)S(1)} %fusion.1), channel_id=1, source_target_pairs={{0,1},{1,0},{2,3},{3,2},{4,5},{5,4},{6,7},{7,6},{8,9},{9,8},{10,11... | collective-permute-start | bytes 393224 | tf_op jit(solution)/shard_map/ppermute | solution.py:477
  2.6 2.8 %shard_map.64 = f32[128,77,1,128]{3,2,1,0:T(1,128)} custom-call(s32[128]{0:T(128)} %target_hbm.1, f32[19,256,128]{2,1,0:T(8,128)} %bitcast.43), custom_call_target="tpu_custom_call" | custom-call | bytes 8000000 | tf_op jit(solution)/shard_map/pallas_call | solution.py:167
  5.5 0.7 collective-permute-done
  6.1 11.7 %all-to-all-start = ((f32[128,77,1,128]{3,2,1,0:T(1,128)}), f32[128,77,1,128]{3,2,1,0:T(1,128)}, u32[]{:S(2)}, u32[]{:S(2)}) async-start(f32[128,77,1,128]{3,2,1,0:T(1,128)} %shard_map.64), calls=%async_computation | async-start | bytes 10092544 | tf_op jit(solution)/shard_map/all_to_all | solution.py:506
  18.0 2.5 %collective-permute-start.1 = (f32[2,2,2,16,128]{4,3,2,1,0:T(8,128)S(1)}, f32[2,2,2,16,128]{4,3,2,1,0:T(8,128)S(1)}, u32[]{:S(2)}, u32[]{:S(2)}) collective-permute-start(f32[2,2,2,16,128]{4,3,2,1,0:T(8,128)S(1)} %get-tuple-element.48), channel_id=1, source_target_pairs={{0,2},{1,3},{2,0},{3,1},{4,6},{5,7},{6,4},{7,5},{8,10},{9,11},{10,... | collective-permute-start | bytes 196616 | tf_op jit(solution)/shard_map/ppermute | solution.py:487
  20.5 3.0 %collective-permute-start.2 = (f32[2,2,2,16,128]{4,3,2,1,0:T(8,128)S(1)}, f32[2,2,2,16,128]{4,3,2,1,0:T(8,128)S(1)}, u32[]{:S(2)}, u32[]{:S(2)}) collective-permute-start(f32[2,2,2,16,128]{4,3,2,1,0:T(8,128)S(1)} %get-tuple-element.49), channel_id=1, source_target_pairs={{0,4},{1,5},{2,6},{3,7},{4,0},{5,1},{6,2},{7,3},{8,12},{9,13},{10,... | collective-permute-start | bytes 196616 | tf_op jit(solution)/shard_map/ppermute | solution.py:487
  23.5 1.1 %collective-permute-start.3 = (f32[2,2,2,16,128]{4,3,2,1,0:T(8,128)S(1)}, f32[2,2,2,16,128]{4,3,2,1,0:T(8,128)S(1)}, u32[]{:S(2)}, u32[]{:S(2)}) collective-permute-start(f32[2,2,2,16,128]{4,3,2,1,0:T(8,128)S(1)} %get-tuple-element.50), channel_id=1, source_target_pairs={{0,6},{1,7},{2,4},{3,5},{4,2},{5,3},{6,0},{7,1},{8,14},{9,15},{10,... | collective-permute-start | bytes 196616 | tf_op jit(solution)/shard_map/ppermute | solution.py:487
  24.6 0.1 pad_add_fusion.odd
  24.7 52.4 %collective-permute-done.1 = f32[2,2,2,16,128]{4,3,2,1,0:T(8,128)S(1)} collective-permute-done((f32[2,2,2,16,128]{4,3,2,1,0:T(8,128)S(1)}, f32[2,2,2,16,128]{4,3,2,1,0:T(8,128)S(1)}, u32[]{:S(2)}, u32[]{:S(2)}) %collective-permute-start.1) | collective-permute-done | bytes 65568 | tf_op jit(solution)/shard_map/ppermute | solution.py:487
  77.1 2.3 %collective-permute-done.3 = f32[2,2,2,16,128]{4,3,2,1,0:T(8,128)S(1)} collective-permute-done((f32[2,2,2,16,128]{4,3,2,1,0:T(8,128)S(1)}, f32[2,2,2,16,128]{4,3,2,1,0:T(8,128)S(1)}, u32[]{:S(2)}, u32[]{:S(2)}) %collective-permute-start.3) | collective-permute-done | bytes 65568 | tf_op jit(solution)/shard_map/ppermute | solution.py:487
  79.6 0.1 broadcast_in_dim.2.force
  79.7 0.6 all-to-all-done.arrived
  80.3 4.6 %shard_map.65 = (f32[5248,128]{1,0:T(8,128)S(1)}, f32[19,4,16,128]{3,2,1,0:T(8,128)S(1)}, f32[21,16,128]{2,1,0:T(8,128)S(1)}, f32[21,16,128]{2,1,0:T(8,128)S(1)}) custom-call(s32[2]{0:T(128)S(1)} %pad_add_fusion.odd, f32[8,128]{1,0:T(8,128)S(1)} %broadcast_in_dim.2.force, f32[128,77,1,128]{3,2,1,0:T(1,128)} %all-to-all-done.arrived, ...), custom_call_target="tpu_custom_call" | custom-call | flops 2000000 | bytes 8000000 | tf_op jit(solution)/shard_map/pallas_call | solution.py:517
  85.0 0.1 collective-permute-start.4
  85.1 4.5 %collective-permute-start.5 = (f32[21,16,128]{2,1,0:T(8,128)S(1)}, f32[21,16,128]{2,1,0:T(8,128)S(1)}, u32[]{:S(2)}, u32[]{:S(2)}) collective-permute-start(f32[21,16,128]{2,1,0:T(8,128)S(1)} %get-tuple-element.31), channel_id=1, source_target_pairs={{0,120},{8,16},{16,8},{24,32},{32,24},{40,48},{48,40},{56,64},{64,... | collective-permute-start | bytes 516104 | tf_op jit(solution)/shard_map/ppermute | solution.py:469
  89.6 2.4 %shard_map.66 = (f32[19,12,16,128]{3,2,1,0:T(8,128)S(1)}, f32[21,16,128]{2,1,0:T(8,128)S(1)}, f32[21,16,128]{2,1,0:T(8,128)S(1)}) custom-call(s32[2]{0:T(128)S(1)} %pad_add_fusion.odd, f32[8,128]{1,0:T(8,128)S(1)} %broadcast_in_dim.2.force, f32[5248,128]{1,0:T(8,128)S(1)} %get-tuple-element.28.tiles, f32[2,16,16,128]{3,2,1,0:T(8,128)S(1)} %pad_maximum_fusion.1.coef, ...), custom_call_target="tpu_custom_call" | custom-call | flops 6000000 | bytes 6000000 | tf_op jit(solution)/shard_map/pallas_call | solution.py:303
  92.0 0.2 collective-permute-start.6
  92.2 2.9 %collective-permute-start.7 = (f32[21,16,128]{2,1,0:T(8,128)S(1)}, f32[21,16,128]{2,1,0:T(8,128)S(1)}, u32[]{:S(2)}, u32[]{:S(2)}) collective-permute-start(f32[21,16,128]{2,1,0:T(8,128)S(1)} %get-tuple-element.33.yo), channel_id=1, source_target_pairs={{0,7},{1,2},{2,1},{3,4},{4,3},{5,6},{6,5},{7,0},{8,15},{9,10},{10,... | collective-permute-start | bytes 516104 | tf_op jit(solution)/shard_map/ppermute | solution.py:469
  95.1 0.6 shard_map.67
  95.7 0.1 collective-permute-start.8
  95.8 3.2 %collective-permute-start.9 = (f32[88,128]{1,0:T(8,128)S(1)}, f32[88,128]{1,0:T(8,128)S(1)}, u32[]{:S(2)}, u32[]{:S(2)}) collective-permute-start(f32[88,128]{1,0:T(8,128)S(1)} %get-tuple-element.35.co), channel_id=1, source_target_pairs={{0,7},{1,2},{2,1},{3,4},{4,3},{5,6},{6,5},{7,0},{8,15},{9,10},{10,... | collective-permute-start | bytes 135176 | tf_op jit(solution)/shard_map/ppermute | solution.py:469
  99.1 4.5 %shard_map.68 = (f32[19,16,16,128]{3,2,1,0:T(8,128)}, f32[432,128]{1,0:T(8,128)S(1)}, f32[432,128]{1,0:T(8,128)S(1)}) custom-call(s32[2]{0:T(128)S(1)} %pad_add_fusion.odd, f32[8,128]{1,0:T(8,128)S(1)} %broadcast_in_dim.2.force, f32[19,4,16,128]{3,2,1,0:T(8,128)S(1)} %get-tuple-element.27.edge, f32[19,12,16,128]{3,2,1,0:T(8,128)S(1)} %get-tuple-element.29.inner, ...), custom_call_target="tpu_custom_call" | custom-call | flops 12000000 | bytes 12000000 | tf_op jit(solution)/shard_map/pallas_call | solution.py:303
  103.6 1.6 %shard_map.69 = f32[19,16,16,128]{3,2,1,0:T(8,128)} custom-call(s32[2]{0:T(128)S(1)} %pad_add_fusion.odd, f32[8,128]{1,0:T(8,128)S(1)} %broadcast_in_dim.2.force, f32[432,128]{1,0:T(8,128)S(1)} %get-tuple-element.36.mine_e, f32[432,128]{1,0:T(8,128)S(1)} %get-tuple-element.37.mine_o, ...), custom_call_target="tpu_custom_call", output_to_operand_aliasing={{}: (8, {})} | custom-call | flops 2000000 | bytes 2000000 | tf_op jit(solution)/shard_map/pallas_call | solution.py:552
  (24 shorter events, 0.2 us)
Async XLA Ops:
  0.9 5.2 %collective-permute-start = (f32[2,2,4,16,128]{4,3,2,1,0:T(8,128)S(1)}, f32[2,2,4,16,128]{4,3,2,1,0:T(8,128)S(1)}, u32[]{:S(2)}, u32[]{:S(2)}) collective-permute-start(f32[2,2,4,16,128]{4,3,2,1,0:T(8,128)S(1)} %fusion.1), channel_id=1, source_target_pairs={{0,1},{1,0},{2,3},{3,2},{4,5},{5,4},{6,7},{7,6},{8,9},{9,8},{10,11... | collective-permute-start | bytes 393224 | tf_op jit(solution)/shard_map/ppermute | solution.py:477
  5.4 12.5 %copy-start.3 = (f32[3]{0:T(128)S(1)}, f32[3]{0:T(128)}, u32[]{:S(2)}) copy-start(f32[3]{0:T(128)} %param.11) | copy-start | bytes 40
  5.4 12.5 %copy-start = (f32[2,128,128]{2,1,0:T(8,128)S(1)}, f32[2,128,128]{2,1,0:T(8,128)}, u32[]{:S(2)}) copy-start(f32[2,128,128]{2,1,0:T(8,128)} %param.8) | copy-start | bytes 393220
  5.4 12.5 %copy-start.1 = (f32[2,128,128]{2,1,0:T(8,128)S(1)}, f32[2,128,128]{2,1,0:T(8,128)}, u32[]{:S(2)}) copy-start(f32[2,128,128]{2,1,0:T(8,128)} %param.9) | copy-start | bytes 393220
  6.1 74.2 %all-to-all-start = ((f32[128,77,1,128]{3,2,1,0:T(1,128)}), f32[128,77,1,128]{3,2,1,0:T(1,128)}, u32[]{:S(2)}, u32[]{:S(2)}) async-start(f32[128,77,1,128]{3,2,1,0:T(1,128)} %shard_map.64), calls=%async_computation | async-start | bytes 10092544 | tf_op jit(solution)/shard_map/all_to_all | solution.py:506
  17.8 61.8 %copy-start.2 = (s32[16,16,128]{2,1,0:T(8,128)S(1)}, s32[16,16,128]{2,1,0:T(8,128)}, u32[]{:S(2)}) copy-start(s32[16,16,128]{2,1,0:T(8,128)} %param.10) | copy-start | bytes 393220
  18.0 59.1 %collective-permute-start.1 = (f32[2,2,2,16,128]{4,3,2,1,0:T(8,128)S(1)}, f32[2,2,2,16,128]{4,3,2,1,0:T(8,128)S(1)}, u32[]{:S(2)}, u32[]{:S(2)}) collective-permute-start(f32[2,2,2,16,128]{4,3,2,1,0:T(8,128)S(1)} %get-tuple-element.48), channel_id=1, source_target_pairs={{0,2},{1,3},{2,0},{3,1},{4,6},{5,7},{6,4},{7,5},{8,10},{9,11},{10,... | collective-permute-start | bytes 196616 | tf_op jit(solution)/shard_map/ppermute | solution.py:487
  20.5 56.6 %collective-permute-start.2 = (f32[2,2,2,16,128]{4,3,2,1,0:T(8,128)S(1)}, f32[2,2,2,16,128]{4,3,2,1,0:T(8,128)S(1)}, u32[]{:S(2)}, u32[]{:S(2)}) collective-permute-start(f32[2,2,2,16,128]{4,3,2,1,0:T(8,128)S(1)} %get-tuple-element.49), channel_id=1, source_target_pairs={{0,4},{1,5},{2,6},{3,7},{4,0},{5,1},{6,2},{7,3},{8,12},{9,13},{10,... | collective-permute-start | bytes 196616 | tf_op jit(solution)/shard_map/ppermute | solution.py:487
  23.5 56.0 %collective-permute-start.3 = (f32[2,2,2,16,128]{4,3,2,1,0:T(8,128)S(1)}, f32[2,2,2,16,128]{4,3,2,1,0:T(8,128)S(1)}, u32[]{:S(2)}, u32[]{:S(2)}) collective-permute-start(f32[2,2,2,16,128]{4,3,2,1,0:T(8,128)S(1)} %get-tuple-element.50), channel_id=1, source_target_pairs={{0,6},{1,7},{2,4},{3,5},{4,2},{5,3},{6,0},{7,1},{8,14},{9,15},{10,... | collective-permute-start | bytes 196616 | tf_op jit(solution)/shard_map/ppermute | solution.py:487
  85.0 10.1 %collective-permute-start.4 = (f32[21,16,128]{2,1,0:T(8,128)S(1)}, f32[21,16,128]{2,1,0:T(8,128)S(1)}, u32[]{:S(2)}, u32[]{:S(2)}) collective-permute-start(f32[21,16,128]{2,1,0:T(8,128)S(1)} %get-tuple-element.30), channel_id=1, source_target_pairs={{0,8},{8,0},{16,24},{24,16},{32,40},{40,32},{48,56},{56,48},{64,72... | collective-permute-start | bytes 516104 | tf_op jit(solution)/shard_map/ppermute | solution.py:469
  85.1 10.0 %collective-permute-start.5 = (f32[21,16,128]{2,1,0:T(8,128)S(1)}, f32[21,16,128]{2,1,0:T(8,128)S(1)}, u32[]{:S(2)}, u32[]{:S(2)}) collective-permute-start(f32[21,16,128]{2,1,0:T(8,128)S(1)} %get-tuple-element.31), channel_id=1, source_target_pairs={{0,120},{8,16},{16,8},{24,32},{32,24},{40,48},{48,40},{56,64},{64,... | collective-permute-start | bytes 516104 | tf_op jit(solution)/shard_map/ppermute | solution.py:469
  92.0 11.6 %collective-permute-start.6 = (f32[21,16,128]{2,1,0:T(8,128)S(1)}, f32[21,16,128]{2,1,0:T(8,128)S(1)}, u32[]{:S(2)}, u32[]{:S(2)}) collective-permute-start(f32[21,16,128]{2,1,0:T(8,128)S(1)} %get-tuple-element.32.ye), channel_id=1, source_target_pairs={{0,1},{1,0},{2,3},{3,2},{4,5},{5,4},{6,7},{7,6},{8,9},{9,8},{10,11... | collective-permute-start | bytes 516104 | tf_op jit(solution)/shard_map/ppermute | solution.py:469
  92.2 11.4 %collective-permute-start.7 = (f32[21,16,128]{2,1,0:T(8,128)S(1)}, f32[21,16,128]{2,1,0:T(8,128)S(1)}, u32[]{:S(2)}, u32[]{:S(2)}) collective-permute-start(f32[21,16,128]{2,1,0:T(8,128)S(1)} %get-tuple-element.33.yo), channel_id=1, source_target_pairs={{0,7},{1,2},{2,1},{3,4},{4,3},{5,6},{6,5},{7,0},{8,15},{9,10},{10,... | collective-permute-start | bytes 516104 | tf_op jit(solution)/shard_map/ppermute | solution.py:469
  95.7 7.9 %collective-permute-start.8 = (f32[88,128]{1,0:T(8,128)S(1)}, f32[88,128]{1,0:T(8,128)S(1)}, u32[]{:S(2)}, u32[]{:S(2)}) collective-permute-start(f32[88,128]{1,0:T(8,128)S(1)} %get-tuple-element.34.ce), channel_id=1, source_target_pairs={{0,1},{1,0},{2,3},{3,2},{4,5},{5,4},{6,7},{7,6},{8,9},{9,8},{10,11... | collective-permute-start | bytes 135176 | tf_op jit(solution)/shard_map/ppermute | solution.py:469
  95.8 7.8 %collective-permute-start.9 = (f32[88,128]{1,0:T(8,128)S(1)}, f32[88,128]{1,0:T(8,128)S(1)}, u32[]{:S(2)}, u32[]{:S(2)}) collective-permute-start(f32[88,128]{1,0:T(8,128)S(1)} %get-tuple-element.35.co), channel_id=1, source_target_pairs={{0,7},{1,2},{2,1},{3,4},{4,3},{5,6},{6,5},{7,0},{8,15},{9,10},{10,... | collective-permute-start | bytes 135176 | tf_op jit(solution)/shard_map/ppermute | solution.py:469

commit v9 on v8

--- a/solution.py
+++ b/solution.py
@@ -1,3 +1,5 @@
+from functools import partial
+
 import jax
 import jax.numpy as jnp
 from jax import lax
@@ -198,7 +200,7 @@
         omega = coef[1, x, pl.ds(r, 8, stride=2), :]
         after = collide(dist, solid, omega, f)
         for q in range(19):
-            post[q, at, pl.ds(r, 8, stride=2), :] = shift_z(after[q], q)
+            post[q, at, pl.ds(8 + r, 8, stride=2), :] = shift_z(after[q], q)
 
 
 def fetch(source, arrived, tiles, sem, slot, at):
@@ -215,8 +217,43 @@
     pltpu.make_async_copy(whole, whole, sem).wait()
 
 
+def by_parity(flag, make):
+    for even in range(2):
+
+        @pl.when(flag == even)
+        def _():
+            make(1 - 2 * even)
+
+
+def x_face(out, sign, edge, coef):
+    for i, (q, layer) in enumerate(entries(0, sign)):
+        out[i] = edge[q, 3 - layer if sign == 1 else layer, 8:24, :]
+    for j in range(2):
+        out[19 + j] = coef[j, 15 if sign == 1 else 0]
+
+
+def y_face(out, sign, planes, coef):
+    for i, (q, layer) in enumerate(entries(1, sign)):
+        row = 8 + (15 - layer if sign == 1 else layer)
+        for x in range(16):
+            ref, at = plane_of(x, planes)
+            out[i, x : x + 1, :] = ref[q, at, row : row + 1, :]
+    row = 15 if sign == 1 else 0
+    for j in range(2):
+        for x in range(16):
+            out[19 + j, x : x + 1, :] = coef[j, x, row : row + 1, :]
+
+
+def plane_of(x, planes):
+    if x < 2:
+        return planes[0], x
+    if x < 8:
+        return planes[1], x - 2
+    return (planes[2], x - 8) if x < 14 else (planes[0], x - 12)
+
+
 def edge_kernel(
-    odd, force, arrived, coef, tiles, edge, xe, xo, labels, found, source, sems, small
+    odd, force, arrived, coef, tiles, edge, xe, labels, found, source, sems, small
 ):
     pull = pltpu.make_async_copy(arrived.at[:, 2 * TILE, 0, :], labels, small.at[0])
     pull.start()
@@ -251,45 +288,24 @@
         return 0
 
     lax.fori_loop(0, 4, plane, 0)
-    for even in range(2):
-
-        @pl.when(odd[0] == even)
-        def _():
-            for out, sign in ((xe, 1 - 2 * even), (xo, 2 * even - 1)):
-                for i, (q, layer) in enumerate(entries(0, sign)):
-                    out[i] = edge[q, 3 - layer if sign == 1 else layer]
-                for j in range(2):
-                    out[19 + j] = coef[j, 15 if sign == 1 else 0]
-
+    by_parity(odd[0], lambda sign: x_face(xe, sign, edge, coef))
     for x in range(2, 14):
         arrive(tiles, sems.at[x])
 
 
-def inner_kernel(odd, force, tiles, coef, edge, inner, ye, yo):
+def inner_kernel(start, odd, force, tiles, coef, edge, *refs):
+    inner, message = refs[-2:]
     f = [force[axis : axis + 1, :] for axis in range(3)]
 
     def plane(j, _):
-        plane_step(j + 2, j + 2, j, tiles, coef, inner, f)
+        plane_step(j + start, j + start, j, tiles, coef, inner, f)
         return 0
 
-    lax.fori_loop(0, 12, plane, 0)
-    for even in range(2):
-
-        @pl.when(odd[1] == even)
-        def _():
-            for out, sign in ((ye, 1 - 2 * even), (yo, 2 * even - 1)):
-                for i, (q, layer) in enumerate(entries(1, sign)):
-                    row = 15 - layer if sign == 1 else layer
-                    for x in range(16):
-                        if 2 <= x < 14:
-                            value = inner[q, x - 2, row : row + 1, :]
-                        else:
-                            value = edge[q, x if x < 2 else x - 12, row : row + 1, :]
-                        out[i, x : x + 1, :] = value
-                row = 15 if sign == 1 else 0
-                for j in range(2):
-                    for x in range(16):
-                        out[19 + j, x : x + 1, :] = coef[j, x, row : row + 1, :]
+    lax.fori_loop(0, 6, plane, 0)
+    if start == 2:
+        by_parity(odd[0], lambda sign: x_face(message, -sign, edge, coef))
+    else:
+        by_parity(odd[1], lambda sign: y_face(message, sign, (edge, refs[0], inner), coef))
 
 
 VMEM_SPEC = pl.BlockSpec(memory_space=pltpu.VMEM)
@@ -310,27 +326,25 @@
     )(*operands)
 
 
-def corner_kernel(odd, xe, xo, ce, co):
+def corners(out, turn, odd, xe, xo):
     have = [
         {e: n for n, e in enumerate(entries(0, toward) + [(19, 0), (20, 0)])} for toward in (1, -1)
     ]
     zero = jnp.zeros((1, 128), F32)
-    for out in (ce, co):
-        out[CORNER_ROWS - 8 : CORNER_ROWS, :] = jnp.zeros((8, 128), F32)
+    out[CORNER_ROWS - 8 : CORNER_ROWS, :] = jnp.zeros((8, 128), F32)
     for even_x in range(2):
         for even_y in range(2):
 
             @pl.when((odd[0] == even_x) & (odd[1] == even_y))
             def _():
                 halves = (xo, xe) if even_x == 0 else (xe, xo)
-                for out, sign in ((ce, 1 - 2 * even_y), (co, 2 * even_y - 1)):
-                    for i, (q, layer) in enumerate(entries(1, sign) + [(19, 0), (20, 0)]):
-                        row = 15 - layer if sign == 1 else layer
-                        for column, (toward, deep) in enumerate(((0, 1), (0, 0), (1, 0), (1, 1))):
-                            n = have[toward].get((q, deep))
-                            value = zero if n is None else halves[toward][n, row : row + 1, :]
-                            at = 4 * i + column
-                            out[at : at + 1, :] = value
+                sign = turn * (1 - 2 * even_y)
+                for i, (q, layer) in enumerate(entries(1, sign) + [(19, 0), (20, 0)]):
+                    row = 15 - layer if sign == 1 else layer
+                    for column, (toward, deep) in enumerate(((0, 1), (0, 0), (1, 0), (1, 1))):
+                        n = have[toward].get((q, deep))
+                        value = zero if n is None else halves[toward][n, row : row + 1, :]
+                        out[4 * i + column : 4 * i + column + 1, :] = value
 
 
 def widen(rows, ends, out):
@@ -342,64 +356,96 @@
     out[COUNT * EXT : SIDE_ROWS, :] = jnp.zeros((SIDE_ROWS - COUNT * EXT, 128), F32)
 
 
-def middle_kernel(
-    odd, force, edge, inner, coef, xe, xo, ye, yo, ce, co, out, own_e, own_o, wide, again, result, sems
-):
-    flag = odd[0]
-    for j in range(4):
-        for q in range(19):
-            wide[q, (j if j < 2 else j + 12) + 2, 8:24, :] = edge[q, j]
-
-    def copy(x, _):
-        for q in range(19):
-            wide[q, x + 4, 8:24, :] = inner[q, x]
-        return 0
-
-    lax.fori_loop(0, 12, copy, 0)
-    sides = []
-    for toward, sign in ((0, 1), (1, -1)):
-        even, odd_ = (xo, xe) if toward == 0 else (xe, xo)
-        for i, (q, layer) in enumerate(entries(0, sign)):
-            at = 1 - layer if toward == 0 else 18 + layer
-            wide[q, at, 8:24, :] = pick(flag, even[i], odd_[i])
-        sides.append([pick(flag, even[19 + j], odd_[19 + j]) for j in range(2)])
-    f = [force[axis : axis + 1, :] for axis in range(3)]
-
-    def one(x, solids, omegas):
-        for block in range(2):
-            dist = []
-            for q in range(19):
-                cx, cy, _z = VELOCITY[q]
-                dist.append(wide[q, x + 1 - cx, 8 + 8 * block - cy : 16 + 8 * block - cy, :])
-            after = collide(dist, solids[block], omegas[block], f)
-            for q in range(19):
-                again[q, x, 8 + 8 * block : 16 + 8 * block, :] = shift_z(after[q], q)
-
-    def plane(x, _):
-        solids = [coef[0, x - 1, 8 * block : 8 * block + 8, :] for block in range(2)]
-        omegas = [coef[1, x - 1, 8 * block : 8 * block + 8, :] for block in range(2)]
-        one(x, solids, omegas)
-        return 0
-
-    one(0, *[[v[0:8], v[8:16]] for v in sides[0]])
-    one(17, *[[v[0:8], v[8:16]] for v in sides[1]])
-    lax.fori_loop(1, 17, plane, 0)
-
-    def finish(x, _):
+def second_plane(x, plane, coef, again, at, f):
+    for block in range(2):
+        dist = []
         for q in range(19):
             cx, cy, _z = VELOCITY[q]
+            ref, n = plane(x - cx)
+            dist.append(ref[q, n, 8 + 8 * block - cy : 16 + 8 * block - cy, :])
+        solid, omega = [coef(j, x, slice(8 * block, 8 * block + 8)) for j in range(2)]
+        after = collide(dist, solid, omega, f)
+        for q in range(19):
+            again[q, at, 8 + 8 * block : 16 + 8 * block, :] = shift_z(after[q], q)
+
+
+def low_kernel(odd, force, edge, inner_a, inner_b, coef, _before, again, yo):
+    f = [force[axis : axis + 1, :] for axis in range(3)]
+    planes = (edge, inner_a, inner_b)
+    for x in range(1, 8):
+        second_plane(
+            x, lambda p: plane_of(p, planes), lambda j, p, rows: coef[j, p, rows, :], again, x - 1, f
+        )
+    by_parity(odd[1], lambda sign: y_face(yo, -sign, planes, coef))
+
+
+def high_kernel(odd, force, edge, inner_a, inner_b, coef, xe, xo, _before, again, ce):
+    corners(ce, 1, odd, xe, xo)
+    f = [force[axis : axis + 1, :] for axis in range(3)]
+    planes = (edge, inner_a, inner_b)
+    for x in range(8, 15):
+        second_plane(
+            x, lambda p: plane_of(p, planes), lambda j, p, rows: coef[j, p, rows, :], again, x - 8, f
+        )
+
+
+def again_of(x, planes):
+    if 1 <= x < 8:
+        return planes[0], x - 1
+    if 8 <= x < 15:
+        return planes[1], x - 8
+    return planes[2], {-1: 0, 0: 1, 15: 2, 16: 3}[x]
+
+
+def output_planes(listed, planes, out, result, sem):
+    for n, x in enumerate(listed):
+        for q in range(19):
+            cx, cy, _z = VELOCITY[q]
+            ref, at = again_of(x - cx, planes)
             for block in range(2):
                 start = 8 + 8 * block - cy
-                value = again[q, x + 1 - cx, start : start + 8, :]
-                result[x, q, 8 * block : 8 * block + 8, :] = value * INVERSE[q] - 1.0
-        pltpu.make_async_copy(result.at[x], out.at[:, x], sems.at[x]).start()
-        return 0
-
-    lax.fori_loop(0, 16, finish, 0)
+                value = ref[q, at, start : start + 8, :]
+                result[n, q, 8 * block : 8 * block + 8, :] = value * INVERSE[q] - 1.0
+        pltpu.make_async_copy(result.at[n], out.at[:, x], sem).start()
+
+
+def outer_kernel(
+    odd, force, edge, inner_a, inner_b, coef, xe, xo, low, high, outer, co, out, halo, fixed, result, sem
+):
+    corners(co, -1, odd, xe, xo)
+    output_planes(range(2, 14), (low, high, None), out, result, sem)
+
+    def copy(sign):
+        for toward, (face, side) in enumerate(((xo, 1), (xe, -1)) if sign == 1 else ((xe, 1), (xo, -1))):
+            for i, (q, layer) in enumerate(entries(0, side)):
+                halo[q, 2 * toward + layer, 8:24, :] = face[i]
+            for j in range(2):
+                fixed[j, toward] = face[19 + j]
+
+    by_parity(odd[0], copy)
+    f = [force[axis : axis + 1, :] for axis in range(3)]
+    planes = (edge, inner_a, inner_b)
+
+    def plane(x):
+        if x < 0:
+            return halo, -1 - x
+        return (halo, x - 14) if x > 15 else plane_of(x, planes)
+
+    def coefficient(j, x, rows):
+        if x < 0:
+            return fixed[j, 0, rows, :]
+        return fixed[j, 1, rows, :] if x > 15 else coef[j, x, rows, :]
+
+    for n, x in enumerate((-1, 0, 15, 16)):
+        second_plane(x, plane, coefficient, outer, n, f)
+    pltpu.make_async_copy(result, result, sem).wait()
+
+
+def finish_kernel(low, high, outer, ye, yo, ce, co, _before, out, own_e, own_o, result, sem):
+    output_planes((0, 1, 14, 15), (low, high, outer), out, result, sem)
     widen(ye, ce, own_e)
     widen(yo, co, own_o)
-    for x in range(16):
-        pltpu.make_async_copy(result.at[x], out.at[:, x], sems.at[x]).wait()
+    pltpu.make_async_copy(result, result, sem).wait()
 
 
 def last_side(side, sign, own, other, out, rows, patch, sem, f):
@@ -446,9 +492,8 @@
 
 
 def last_kernel(
-    odd, force, mine_e, mine_o, rows_e, rows_o, ends_e, ends_o, _before, out, came_e, came_o, rows, patch, sem
+    odd, force, mine_e, mine_o, came_e, rows_o, ends_o, _before, out, came_o, rows, patch, sem
 ):
-    widen(rows_e, ends_e, came_e)
     widen(rows_o, ends_o, came_o)
     f = [force[axis : axis + 1, :] for axis in range(3)]
     for even in range(2):
@@ -513,12 +558,14 @@
     drive = jnp.broadcast_to(jnp.pad(force, (0, 5))[:, None], (8, 128))
     coef, odd, drive = lax.optimization_barrier((coef, odd, drive))
     hbm = pl.BlockSpec(memory_space=pltpu.HBM)
-    posts = [jax.ShapeDtypeStruct((19, n, 16, 128), F32) for n in (4, 12)]
-    tiles, edge, xe, xo = pl.pallas_call(
+    def planes(n):
+        return jax.ShapeDtypeStruct((19, n, 32, 128), F32)
+
+    tiles, edge, xe = pl.pallas_call(
         edge_kernel,
-        out_shape=[jax.ShapeDtypeStruct((HELD * ROWS, 128), F32), posts[0], FACE, FACE],
+        out_shape=[jax.ShapeDtypeStruct((HELD * ROWS, 128), F32), planes(4), FACE],
         in_specs=[SMEM_SPEC, VMEM_SPEC, hbm, VMEM_SPEC],
-        out_specs=[VMEM_SPEC] * 4,
+        out_specs=[VMEM_SPEC] * 3,
         scratch_shapes=[
             pltpu.VMEM((DEVICES, 128), F32),
             pltpu.VMEM((8, 128), jnp.int32),
@@ -529,34 +576,59 @@
         compiler_params=pltpu.CompilerParams(vmem_limit_bytes=VMEM_LIMIT),
         cost_estimate=pl.CostEstimate(flops=2_000_000, bytes_accessed=8_000_000, transcendentals=0),
     )(odd, drive, arrived, coef)
-    from_xe, from_xo = swap(xe, "gx", True), swap(xo, "gx", False)
-    inner, ye, yo = call(
-        inner_kernel, [posts[1], FACE, FACE], (odd, drive, tiles, coef, edge), 6_000_000
+    from_xe = swap(xe, "gx", True)
+    inner_a, xo = call(
+        partial(inner_kernel, 2), [planes(6), FACE], (odd, drive, tiles, coef, edge), 3_000_000
     )
-    from_ye, from_yo = swap(ye, "gy", True), swap(yo, "gy", False)
-    ce, co = call(corner_kernel, [CORNER, CORNER], (odd, from_xe, from_xo), 200_000)
-    from_ce, from_co = swap(ce, "gy", True), swap(co, "gy", False)
-    result, own_e, own_o = call(
-        middle_kernel,
-        [jax.ShapeDtypeStruct((19, 16, 16, 128), F32), SIDE, SIDE],
-        (odd, drive, edge, inner, coef, from_xe, from_xo, ye, yo, ce, co),
-        12_000_000,
-        out_specs=[hbm, VMEM_SPEC, VMEM_SPEC],
+    from_xo = swap(xo, "gx", False)
+    inner_b, ye = call(
+        partial(inner_kernel, 8), [planes(6), FACE], (odd, drive, tiles, coef, edge, inner_a), 3_000_000
+    )
+    from_ye = swap(ye, "gy", True)
+    low, yo = call(
+        low_kernel, [planes(7), FACE], (odd, drive, edge, inner_a, inner_b, coef, from_xe), 4_000_000
+    )
+    from_yo = swap(yo, "gy", False)
+    high, ce = call(
+        high_kernel,
+        [planes(7), CORNER],
+        (odd, drive, edge, inner_a, inner_b, coef, from_xe, from_xo, yo),
+        4_000_000,
+    )
+    from_ce = swap(ce, "gy", True)
+    whole = jax.ShapeDtypeStruct((19, 16, 16, 128), F32)
+    outer, co, result = call(
+        outer_kernel,
+        [planes(4), CORNER, whole],
+        (odd, drive, edge, inner_a, inner_b, coef, from_xe, from_xo, low, high),
+        4_000_000,
+        out_specs=[VMEM_SPEC, VMEM_SPEC, hbm],
         scratch_shapes=[
-            pltpu.VMEM((19, EXT, 32, 128), F32),
-            pltpu.VMEM((19, 18, 32, 128), F32),
-            pltpu.VMEM((16, 19, 16, 128), F32),
-            pltpu.SemaphoreType.DMA((16,)),
+            pltpu.VMEM((19, 4, 32, 128), F32),
+            pltpu.VMEM((2, 2, 16, 128), F32),
+            pltpu.VMEM((12, 19, 16, 128), F32),
+            pltpu.SemaphoreType.DMA,
         ],
     )
+    from_co = swap(co, "gy", False)
+    result, own_e, own_o = pl.pallas_call(
+        finish_kernel,
+        out_shape=[whole, SIDE, SIDE],
+        in_specs=[VMEM_SPEC] * 7 + [hbm],
+        out_specs=[hbm, VMEM_SPEC, VMEM_SPEC],
+        input_output_aliases={7: 0},
+        scratch_shapes=[pltpu.VMEM((4, 19, 16, 128), F32), pltpu.SemaphoreType.DMA],
+        compiler_params=pltpu.CompilerParams(vmem_limit_bytes=VMEM_LIMIT),
+        cost_estimate=pl.CostEstimate(flops=2_000_000, bytes_accessed=2_000_000, transcendentals=0),
+    )(low, high, outer, ye, yo, ce, co, result)
+    came_e = call(widen, SIDE, (from_ye, from_ce), 200_000, scalars=0)
     return pl.pallas_call(
         last_kernel,
         out_shape=jax.ShapeDtypeStruct((19, 16, 16, 128), F32),
-        in_specs=[SMEM_SPEC] + [VMEM_SPEC] * 7 + [hbm],
+        in_specs=[SMEM_SPEC] + [VMEM_SPEC] * 6 + [hbm],
         out_specs=hbm,
-        input_output_aliases={8: 0},
+        input_output_aliases={7: 0},
         scratch_shapes=[
-            pltpu.VMEM((SIDE_ROWS, 128), F32),
             pltpu.VMEM((SIDE_ROWS, 128), F32),
             pltpu.VMEM((2, 19, 24, 128), F32),
             pltpu.VMEM((38, 16, 128), F32),
@@ -564,7 +636,7 @@
         ],
         compiler_params=pltpu.CompilerParams(vmem_limit_bytes=VMEM_LIMIT),
         cost_estimate=pl.CostEstimate(flops=2_000_000, bytes_accessed=2_000_000, transcendentals=0),
-    )(odd, drive, own_e, own_o, from_ye, from_yo, from_ce, from_co, result)
+    )(odd, drive, own_e, own_o, came_e, from_yo, from_co, result)
 
 
 def solution(mesh):

time: 106 us -> 118 us (1.11)
  Pallas kernels: 16.5 us -> 25.8 us
  local copies, waits for them, and re-layouts: 0.15 us -> 1.67 us
  waiting for transfers between devices: 56.1 us -> 57.5 us
    pallas_call x3 -> x6, Pallas kernels: 7.51 us -> 14.4 us  [call(): pl.pallas_call(kernel, out_shape=out_shape, in_specs=[SMEM_SPEC] * scalar...]
    pallas_call x0 -> x1, Pallas kernels: none -> 2.45 us  [local(): pl.pallas_call(finish_kernel, out_shape=[whole, SIDE, SIDE], in_specs=[VM...]
    unnamed x8 -> x14, local copies, waits for them, and re-layouts: 0.03 us -> 1.55 us
    ppermute x6, waiting for transfers between devices: 0.02 us -> 1.41 us  [swap(): return lax.ppermute(value, axis, pairs)]
  transfers between devices with their start and end apart: 11 -> 11, of which waited for: 4 -> 4; matrix products, arithmetic and copies ran while one was open for 0% -> 0% of each run, Pallas kernels for 10% -> 17%
where the time goes in v9:
time: 118 us
  waiting for transfers between devices  57.5 us (49%)
  starting transfers between devices  31.5 us (27%)
  Pallas kernels  25.8 us (22%)
  local copies, waits for them, and re-layouts  1.67 us (1%)
    ppermute x3, waiting for transfers between devices, pieces_of(): lax.ppermute(message, 'gy', [(i, i ^ 2 * k) for i in range(8)])  53.9 us
    pallas_call x6, Pallas kernels, call(): pl.pallas_call(kernel, out_shape=out_shape, in_specs=[SMEM_SPEC] * scalar...  14.4 us
    all_to_all x1, starting transfers between devices, local(): lax.all_to_all(packed, ('gx', 'gy'), split_axis=0, concat_axis=0, tiled=T...  11.7 us
    ppermute x6, starting transfers between devices, swap(): return lax.ppermute(value, axis, pairs)  11.5 us
    ppermute x3, starting transfers between devices, pieces_of(): lax.ppermute(message, 'gy', [(i, i ^ 2 * k) for i in range(8)])  6.58 us
    pallas_call x1, Pallas kernels, local(): pl.pallas_call(edge_kernel, out_shape=[jax.ShapeDtypeStruct((HELD * ROWS,...  4.65 us
    pallas_call x1, Pallas kernels, pack(): pl.pallas_call(pack_kernel, out_shape=jax.ShapeDtypeStruct((DEVICES, PAIR...  2.76 us
    pallas_call x1, Pallas kernels, local(): pl.pallas_call(finish_kernel, out_shape=[whole, SIDE, SIDE], in_specs=[VM...  2.45 us
  transfers between devices with their start and end apart: 11, of which 4 were waited for; matrix products, arithmetic and copies ran while one was open for 0% of the time, Pallas kernels for 17%

profile of v9, /device:TPU:0, one launch (start us, length us, event | category | flops | bytes accessed | tf_op | source)
XLA Modules:
  0.0 117.9 jit_solution(13051539975151774699)
XLA Ops:
  0.0 0.9 fusion.1
  0.9 1.7 %collective-permute-start = (f32[2,2,4,16,128]{4,3,2,1,0:T(8,128)S(1)}, f32[2,2,4,16,128]{4,3,2,1,0:T(8,128)S(1)}, u32[]{:S(2)}, u32[]{:S(2)}) collective-permute-start(f32[2,2,4,16,128]{4,3,2,1,0:T(8,128)S(1)} %fusion.1), channel_id=1, source_target_pairs={{0,1},{1,0},{2,3},{3,2},{4,5},{5,4},{6,7},{7,6},{8,9},{9,8},{10,11... | collective-permute-start | bytes 393224 | tf_op jit(solution)/shard_map/ppermute | solution.py:522
  2.6 2.8 %shard_map.64 = f32[128,77,1,128]{3,2,1,0:T(1,128)} custom-call(s32[128]{0:T(128)} %target_hbm.1, f32[19,256,128]{2,1,0:T(8,128)} %bitcast.43), custom_call_target="tpu_custom_call" | custom-call | bytes 8000000 | tf_op jit(solution)/shard_map/pallas_call | solution.py:169
  5.4 0.7 collective-permute-done
  6.1 11.7 %all-to-all-start = ((f32[128,77,1,128]{3,2,1,0:T(1,128)}), f32[128,77,1,128]{3,2,1,0:T(1,128)}, u32[]{:S(2)}, u32[]{:S(2)}) async-start(f32[128,77,1,128]{3,2,1,0:T(1,128)} %shard_map.64), calls=%async_computation | async-start | bytes 10092544 | tf_op jit(solution)/shard_map/all_to_all | solution.py:551
  18.0 4.9 %collective-permute-start.3 = (f32[2,2,2,16,128]{4,3,2,1,0:T(8,128)S(1)}, f32[2,2,2,16,128]{4,3,2,1,0:T(8,128)S(1)}, u32[]{:S(2)}, u32[]{:S(2)}) collective-permute-start(f32[2,2,2,16,128]{4,3,2,1,0:T(8,128)S(1)} %get-tuple-element.60), channel_id=1, source_target_pairs={{0,6},{1,7},{2,4},{3,5},{4,2},{5,3},{6,0},{7,1},{8,14},{9,15},{10,... | collective-permute-start | bytes 196616 | tf_op jit(solution)/shard_map/ppermute | solution.py:532
  22.9 0.6 collective-permute-start.2
  23.5 1.1 collective-permute-start.1
  24.7 53.9 %collective-permute-done.3 = f32[2,2,2,16,128]{4,3,2,1,0:T(8,128)S(1)} collective-permute-done((f32[2,2,2,16,128]{4,3,2,1,0:T(8,128)S(1)}, f32[2,2,2,16,128]{4,3,2,1,0:T(8,128)S(1)}, u32[]{:S(2)}, u32[]{:S(2)}) %collective-permute-start.3) | collective-permute-done | bytes 65568 | tf_op jit(solution)/shard_map/ppermute | solution.py:532
  78.8 1.6 %all-to-all-done.arrived = f32[128,77,1,128]{3,2,1,0:T(1,128)} async-done(((f32[128,77,1,128]{3,2,1,0:T(1,128)}), f32[128,77,1,128]{3,2,1,0:T(1,128)}, u32[]{:S(2)}, u32[]{:S(2)}) %all-to-all-start) | async-done | bytes 5046304 | tf_op jit(solution)/shard_map/all_to_all | solution.py:551
  80.3 4.6 %shard_map.65 = (f32[5248,128]{1,0:T(8,128)S(1)}, f32[19,4,32,128]{3,2,1,0:T(8,128)S(1)}, f32[21,16,128]{2,1,0:T(8,128)S(1)}) custom-call(s32[2]{0:T(128)S(1)} %pad_add_fusion.odd, f32[8,128]{1,0:T(8,128)S(1)} %broadcast_in_dim.2.force, f32[128,77,1,128]{3,2,1,0:T(1,128)} %all-to-all-done.arrived, f32[2,16,16,128]{3,2,1,0:T(8,128)S(1)} %pad_maximum_fusion.1.coef), custom_call_target="tpu_custom_call" | custom-call | flops 2000000 | bytes 8000000 | tf_op jit(solution)/shard_map/pallas_call | solution.py:564
  85.0 1.5 %copy-done.1 = f32[5248,128]{1,0:T(8,128)} copy-done((f32[5248,128]{1,0:T(8,128)}, f32[5248,128]{1,0:T(8,128)S(1)}, u32[]{:S(2)}) %copy-start.1) | copy-done | bytes 2687000
  86.5 2.6 %shard_map.66 = (f32[19,6,32,128]{3,2,1,0:T(8,128)S(1)}, f32[21,16,128]{2,1,0:T(8,128)S(1)}) custom-call(s32[2]{0:T(128)S(1)} %pad_add_fusion.odd, f32[8,128]{1,0:T(8,128)S(1)} %broadcast_in_dim.2.force, f32[5248,128]{1,0:T(8,128)} %copy-done.1, f32[2,16,16,128]{3,2,1,0:T(8,128)S(1)} %pad_maximum_fusion.1.coef, f32[19,4,32,128]{3,2,1,0:T(8,128)S(1)} %get-tuple-element.32.edge), custom_call_target="tpu_custom_call" | custom-call | flops 3000000 | bytes 3000000 | tf_op jit(solution)/shard_map/pallas_call | solution.py:319
  89.1 4.6 %collective-permute-start.5 = (f32[21,16,128]{2,1,0:T(8,128)S(1)}, f32[21,16,128]{2,1,0:T(8,128)S(1)}, u32[]{:S(2)}, u32[]{:S(2)}) collective-permute-start(f32[21,16,128]{2,1,0:T(8,128)S(1)} %get-tuple-element.38), channel_id=1, source_target_pairs={{0,120},{8,16},{16,8},{24,32},{32,24},{40,48},{48,40},{56,64},{64,... | collective-permute-start | bytes 516104 | tf_op jit(solution)/shard_map/ppermute | solution.py:514
  93.7 2.7 %shard_map.67 = (f32[19,6,32,128]{3,2,1,0:T(8,128)S(1)}, f32[21,16,128]{2,1,0:T(8,128)S(1)}) custom-call(s32[2]{0:T(128)S(1)} %pad_add_fusion.odd, f32[8,128]{1,0:T(8,128)S(1)} %broadcast_in_dim.2.force, f32[5248,128]{1,0:T(8,128)} %copy-done.1, f32[2,16,16,128]{3,2,1,0:T(8,128)S(1)} %pad_maximum_fusion.1.coef, ...), custom_call_target="tpu_custom_call" | custom-call | flops 3000000 | bytes 3000000 | tf_op jit(solution)/shard_map/pallas_call | solution.py:319
  96.5 0.1 collective-permute-start.6
  96.6 2.4 %shard_map.68 = (f32[19,7,32,128]{3,2,1,0:T(8,128)}, f32[21,16,128]{2,1,0:T(8,128)S(1)}) custom-call(s32[2]{0:T(128)S(1)} %pad_add_fusion.odd, f32[8,128]{1,0:T(8,128)S(1)} %broadcast_in_dim.2.force, f32[19,4,32,128]{3,2,1,0:T(8,128)S(1)} %get-tuple-element.32.edge, f32[19,6,32,128]{3,2,1,0:T(8,128)S(1)} %get-tuple-element.34.refs_0_.inner_a, ...), custom_call_target="tpu_custom_call" | custom-call | flops 4000000 | bytes 4000000 | tf_op jit(solution)/shard_map/pallas_call | solution.py:319
  99.0 3.0 %collective-permute-start.8 = (f32[21,16,128]{2,1,0:T(8,128)S(1)}, f32[21,16,128]{2,1,0:T(8,128)S(1)}, u32[]{:S(2)}, u32[]{:S(2)}) collective-permute-start(f32[21,16,128]{2,1,0:T(8,128)S(1)} %get-tuple-element.39._before.yo), channel_id=1, source_target_pairs={{0,7},{1,2},{2,1},{3,4},{4,3},{5,6},{6,5},{7,0},{8,15},{9,10},{10,... | collective-permute-start | bytes 516104 | tf_op jit(solution)/shard_map/ppermute | solution.py:514
  102.0 2.4 %shard_map.69 = (f32[19,7,32,128]{3,2,1,0:T(8,128)}, f32[88,128]{1,0:T(8,128)S(1)}) custom-call(s32[2]{0:T(128)S(1)} %pad_add_fusion.odd, f32[8,128]{1,0:T(8,128)S(1)} %broadcast_in_dim.2.force, f32[19,4,32,128]{3,2,1,0:T(8,128)S(1)} %get-tuple-element.32.edge, f32[19,6,32,128]{3,2,1,0:T(8,128)S(1)} %get-tuple-element.34.refs_0_.inner_a, ...), custom_call_target="tpu_custom_call" | custom-call | flops 4000000 | bytes 4000000 | tf_op jit(solution)/shard_map/pallas_call | solution.py:319
  104.3 4.3 %shard_map.70 = (f32[19,4,32,128]{3,2,1,0:T(8,128)S(1)}, f32[88,128]{1,0:T(8,128)S(1)}, f32[19,16,16,128]{3,2,1,0:T(8,128)}) custom-call(s32[2]{0:T(128)S(1)} %pad_add_fusion.odd, f32[8,128]{1,0:T(8,128)S(1)} %broadcast_in_dim.2.force, f32[19,4,32,128]{3,2,1,0:T(8,128)S(1)} %get-tuple-element.32.edge, ...), custom_call_target="tpu_custom_call" | custom-call | flops 4000000 | bytes 4000000 | tf_op jit(solution)/shard_map/pallas_call | solution.py:319
  108.6 3.8 %collective-permute-start.9 = (f32[88,128]{1,0:T(8,128)S(1)}, f32[88,128]{1,0:T(8,128)S(1)}, u32[]{:S(2)}, u32[]{:S(2)}) collective-permute-start(f32[88,128]{1,0:T(8,128)S(1)} %get-tuple-element.44.co), channel_id=1, source_target_pairs={{0,7},{1,2},{2,1},{3,4},{4,3},{5,6},{6,5},{7,0},{8,15},{9,10},{10,... | collective-permute-start | bytes 135176 | tf_op jit(solution)/shard_map/ppermute | solution.py:514
  112.4 2.5 %shard_map.71 = (f32[19,16,16,128]{3,2,1,0:T(8,128)}, f32[432,128]{1,0:T(8,128)S(1)}, f32[432,128]{1,0:T(8,128)S(1)}) custom-call(f32[19,7,32,128]{3,2,1,0:T(8,128)S(1)} %copy-done.2, f32[19,7,32,128]{3,2,1,0:T(8,128)} %get-tuple-element.40.high, f32[19,4,32,128]{3,2,1,0:T(8,128)S(1)} %get-tuple-element.41.outer, ...), custom_call_target="tpu_custom_call", output_to_operand_aliasing={{0}: (7, {})} | custom-call | flops 2000000 | bytes 2000000 | tf_op jit(solution)/shard_map/pallas_call | solution.py:614
  115.0 1.4 %collective-permute-done.9.ends_o = f32[88,128]{1,0:T(8,128)S(1)} collective-permute-done((f32[88,128]{1,0:T(8,128)S(1)}, f32[88,128]{1,0:T(8,128)S(1)}, u32[]{:S(2)}, u32[]{:S(2)}) %collective-permute-start.9) | collective-permute-done | bytes 45088 | tf_op jit(solution)/shard_map/ppermute | solution.py:514
  116.4 1.5 %shard_map.73 = f32[19,16,16,128]{3,2,1,0:T(8,128)} custom-call(s32[2]{0:T(128)S(1)} %pad_add_fusion.odd, f32[8,128]{1,0:T(8,128)S(1)} %broadcast_in_dim.2.force, f32[432,128]{1,0:T(8,128)S(1)} %get-tuple-element.46.mine_e, f32[432,128]{1,0:T(8,128)S(1)} %get-tuple-element.47.mine_o, ...), custom_call_target="tpu_custom_call", output_to_operand_aliasing={{}: (7, {})} | custom-call | flops 2000000 | bytes 2000000 | tf_op jit(solution)/shard_map/pallas_call | solution.py:625
  (34 shorter events, 0.4 us)
Async XLA Ops:
  0.9 5.2 %collective-permute-start = (f32[2,2,4,16,128]{4,3,2,1,0:T(8,128)S(1)}, f32[2,2,4,16,128]{4,3,2,1,0:T(8,128)S(1)}, u32[]{:S(2)}, u32[]{:S(2)}) collective-permute-start(f32[2,2,4,16,128]{4,3,2,1,0:T(8,128)S(1)} %fusion.1), channel_id=1, source_target_pairs={{0,1},{1,0},{2,3},{3,2},{4,5},{5,4},{6,7},{7,6},{8,9},{9,8},{10,11... | collective-permute-start | bytes 393224 | tf_op jit(solution)/shard_map/ppermute | solution.py:522
  5.4 12.5 %copy-start.6 = (f32[3]{0:T(128)S(1)}, f32[3]{0:T(128)}, u32[]{:S(2)}) copy-start(f32[3]{0:T(128)} %param.11) | copy-start | bytes 40
  5.4 12.5 %copy-start.3 = (f32[2,128,128]{2,1,0:T(8,128)S(1)}, f32[2,128,128]{2,1,0:T(8,128)}, u32[]{:S(2)}) copy-start(f32[2,128,128]{2,1,0:T(8,128)} %param.8) | copy-start | bytes 393220
  5.4 12.5 %copy-start.4 = (f32[2,128,128]{2,1,0:T(8,128)S(1)}, f32[2,128,128]{2,1,0:T(8,128)}, u32[]{:S(2)}) copy-start(f32[2,128,128]{2,1,0:T(8,128)} %param.9) | copy-start | bytes 393220
  6.1 74.2 %all-to-all-start = ((f32[128,77,1,128]{3,2,1,0:T(1,128)}), f32[128,77,1,128]{3,2,1,0:T(1,128)}, u32[]{:S(2)}, u32[]{:S(2)}) async-start(f32[128,77,1,128]{3,2,1,0:T(1,128)} %shard_map.64), calls=%async_computation | async-start | bytes 10092544 | tf_op jit(solution)/shard_map/all_to_all | solution.py:551
  17.8 60.8 %copy-start.5 = (s32[16,16,128]{2,1,0:T(8,128)S(1)}, s32[16,16,128]{2,1,0:T(8,128)}, u32[]{:S(2)}) copy-start(s32[16,16,128]{2,1,0:T(8,128)} %param.10) | copy-start | bytes 393220
  18.0 60.5 %collective-permute-start.3 = (f32[2,2,2,16,128]{4,3,2,1,0:T(8,128)S(1)}, f32[2,2,2,16,128]{4,3,2,1,0:T(8,128)S(1)}, u32[]{:S(2)}, u32[]{:S(2)}) collective-permute-start(f32[2,2,2,16,128]{4,3,2,1,0:T(8,128)S(1)} %get-tuple-element.60), channel_id=1, source_target_pairs={{0,6},{1,7},{2,4},{3,5},{4,2},{5,3},{6,0},{7,1},{8,14},{9,15},{10,... | collective-permute-start | bytes 196616 | tf_op jit(solution)/shard_map/ppermute | solution.py:532
  22.9 55.6 %collective-permute-start.2 = (f32[2,2,2,16,128]{4,3,2,1,0:T(8,128)S(1)}, f32[2,2,2,16,128]{4,3,2,1,0:T(8,128)S(1)}, u32[]{:S(2)}, u32[]{:S(2)}) collective-permute-start(f32[2,2,2,16,128]{4,3,2,1,0:T(8,128)S(1)} %get-tuple-element.59), channel_id=1, source_target_pairs={{0,4},{1,5},{2,6},{3,7},{4,0},{5,1},{6,2},{7,3},{8,12},{9,13},{10,... | collective-permute-start | bytes 196616 | tf_op jit(solution)/shard_map/ppermute | solution.py:532
  23.5 55.1 %collective-permute-start.1 = (f32[2,2,2,16,128]{4,3,2,1,0:T(8,128)S(1)}, f32[2,2,2,16,128]{4,3,2,1,0:T(8,128)S(1)}, u32[]{:S(2)}, u32[]{:S(2)}) collective-permute-start(f32[2,2,2,16,128]{4,3,2,1,0:T(8,128)S(1)} %get-tuple-element.58), channel_id=1, source_target_pairs={{0,2},{1,3},{2,0},{3,1},{4,6},{5,7},{6,4},{7,5},{8,10},{9,11},{10,... | collective-permute-start | bytes 196616 | tf_op jit(solution)/shard_map/ppermute | solution.py:532
  85.0 1.5 %copy-start.1 = (f32[5248,128]{1,0:T(8,128)}, f32[5248,128]{1,0:T(8,128)S(1)}, u32[]{:S(2)}) copy-start(f32[5248,128]{1,0:T(8,128)S(1)} %get-tuple-element.33.tiles) | copy-start | bytes 8060932
  86.5 10.0 %collective-permute-start.4 = (f32[21,16,128]{2,1,0:T(8,128)S(1)}, f32[21,16,128]{2,1,0:T(8,128)S(1)}, u32[]{:S(2)}, u32[]{:S(2)}) collective-permute-start(f32[21,16,128]{2,1,0:T(8,128)S(1)} %get-tuple-element.36), channel_id=1, source_target_pairs={{0,8},{8,0},{16,24},{24,16},{32,40},{40,32},{48,56},{56,48},{64,72... | collective-permute-start | bytes 516104 | tf_op jit(solution)/shard_map/ppermute | solution.py:514
  89.1 12.8 %collective-permute-start.5 = (f32[21,16,128]{2,1,0:T(8,128)S(1)}, f32[21,16,128]{2,1,0:T(8,128)S(1)}, u32[]{:S(2)}, u32[]{:S(2)}) collective-permute-start(f32[21,16,128]{2,1,0:T(8,128)S(1)} %get-tuple-element.38), channel_id=1, source_target_pairs={{0,120},{8,16},{16,8},{24,32},{32,24},{40,48},{48,40},{56,64},{64,... | collective-permute-start | bytes 516104 | tf_op jit(solution)/shard_map/ppermute | solution.py:514
  96.5 5.5 %copy-start = (f32[19,6,32,128]{3,2,1,0:T(8,128)}, f32[19,6,32,128]{3,2,1,0:T(8,128)S(1)}, u32[]{:S(2)}) copy-start(f32[19,6,32,128]{3,2,1,0:T(8,128)S(1)} %get-tuple-element.35.inner_b) | copy-start | bytes 5603332
  96.5 18.5 %collective-permute-start.6 = (f32[21,16,128]{2,1,0:T(8,128)S(1)}, f32[21,16,128]{2,1,0:T(8,128)S(1)}, u32[]{:S(2)}, u32[]{:S(2)}) collective-permute-start(f32[21,16,128]{2,1,0:T(8,128)S(1)} %get-tuple-element.42.ye), channel_id=1, source_target_pairs={{0,1},{1,0},{2,3},{3,2},{4,5},{5,4},{6,7},{7,6},{8,9},{9,8},{10,11... | collective-permute-start | bytes 516104 | tf_op jit(solution)/shard_map/ppermute | solution.py:514
  99.0 17.4 %collective-permute-start.8 = (f32[21,16,128]{2,1,0:T(8,128)S(1)}, f32[21,16,128]{2,1,0:T(8,128)S(1)}, u32[]{:S(2)}, u32[]{:S(2)}) collective-permute-start(f32[21,16,128]{2,1,0:T(8,128)S(1)} %get-tuple-element.39._before.yo), channel_id=1, source_target_pairs={{0,7},{1,2},{2,1},{3,4},{4,3},{5,6},{6,5},{7,0},{8,15},{9,10},{10,... | collective-permute-start | bytes 516104 | tf_op jit(solution)/shard_map/ppermute | solution.py:514
  104.3 10.6 %collective-permute-start.7 = (f32[88,128]{1,0:T(8,128)S(1)}, f32[88,128]{1,0:T(8,128)S(1)}, u32[]{:S(2)}, u32[]{:S(2)}) collective-permute-start(f32[88,128]{1,0:T(8,128)S(1)} %get-tuple-element.43.ce), channel_id=1, source_target_pairs={{0,1},{1,0},{2,3},{3,2},{4,5},{5,4},{6,7},{7,6},{8,9},{9,8},{10,11... | collective-permute-start | bytes 135176 | tf_op jit(solution)/shard_map/ppermute | solution.py:514
  104.3 8.1 %copy-start.2 = (f32[19,7,32,128]{3,2,1,0:T(8,128)S(1)}, f32[19,7,32,128]{3,2,1,0:T(8,128)}, u32[]{:S(2)}) copy-start(f32[19,7,32,128]{3,2,1,0:T(8,128)} %get-tuple-element.37.low) | copy-start | bytes 6537220
  108.6 7.7 %collective-permute-start.9 = (f32[88,128]{1,0:T(8,128)S(1)}, f32[88,128]{1,0:T(8,128)S(1)}, u32[]{:S(2)}, u32[]{:S(2)}) collective-permute-start(f32[88,128]{1,0:T(8,128)S(1)} %get-tuple-element.44.co), channel_id=1, source_target_pairs={{0,7},{1,2},{2,1},{3,4},{4,3},{5,6},{6,5},{7,0},{8,15},{9,10},{10,... | collective-permute-start | bytes 135176 | tf_op jit(solution)/shard_map/ppermute | solution.py:514

commit v10 on v7

--- a/solution.py
+++ b/solution.py
@@ -49,6 +49,7 @@
 
 COUNT = 21
 SIDE_ROWS = 432
+SENT_ROWS = 384
 
 
 def collide(dist, solid, omega, force):
@@ -215,7 +216,7 @@
 
 
 def edge_kernel(
-    odd, force, arrived, coef, found, edge, xo, xe, tiles, labels, source, sems, small
+    odd, force, arrived, coef, found, edge, xe, xo, tiles, labels, source, sems, small
 ):
     pull = pltpu.make_async_copy(arrived.at[:, 2 * TILE, 0, :], labels, small.at[0])
     pull.start()
@@ -257,7 +258,7 @@
                     out[19 + j] = coef[j, 15 if sign == 1 else 0]
 
 
-def inner_kernel(odd, force, found, arrived, coef, edge, inner, yo, ye, tiles, source, sems, small):
+def inner_kernel(odd, force, found, arrived, coef, edge, inner, ye, yo, tiles, source, sems, small):
     hand = pltpu.make_async_copy(found, source, small)
     hand.start()
     f = [force[axis : axis + 1, :] for axis in range(3)]
@@ -285,11 +286,11 @@
                             value = inner[q, x - 2, row : row + 1, :]
                         else:
                             value = edge[q, x if x < 2 else x - 12, row : row + 1, :]
-                        out[i * EXT + 2 + x : i * EXT + 3 + x, :] = value
+                        out[16 * i + x : 16 * i + x + 1, :] = value
                 row = 15 if sign == 1 else 0
                 for j in range(2):
                     for x in range(16):
-                        at = (19 + j) * EXT + 2 + x
+                        at = (19 + j) * 16 + x
                         out[at : at + 1, :] = coef[j, x, row : row + 1, :]
 
 
@@ -297,6 +298,7 @@
 SMEM_SPEC = pl.BlockSpec(memory_space=pltpu.SMEM)
 FACE = jax.ShapeDtypeStruct((COUNT, 16, 128), F32)
 SIDE = jax.ShapeDtypeStruct((SIDE_ROWS, 128), F32)
+SENT = jax.ShapeDtypeStruct((SENT_ROWS, 128), F32)
 
 
 def call(kernel, out_shape, operands, work, scalars=1, **more):
@@ -310,14 +312,24 @@
     )(*operands)
 
 
-def join_kernel(odd, xo, xe, own_o, own_e, yo, ye):
+def corners(sign):
+    listed = []
+    for toward, side in enumerate((1, -1)):
+        have = {e: n for n, e in enumerate(entries(0, side) + [(19, 0), (20, 0)])}
+        for deep in range(2):
+            column = 1 - deep if toward == 0 else 18 + deep
+            for i, (q, layer) in enumerate(entries(1, sign) + [(19, 0), (20, 0)]):
+                if (q, deep) in have:
+                    row = 15 - layer if sign == 1 else layer
+                    listed.append((i, column, toward, have[(q, deep)], row))
+    return listed
+
+
+def join_kernel(odd, xe, xo, own_e, own_o, ye, yo):
     for own, out in ((own_e, ye), (own_o, yo)):
-        for block in range(SIDE_ROWS // 8):
+        for block in range(COUNT * 2):
             out[8 * block : 8 * block + 8, :] = own[8 * block : 8 * block + 8, :]
-    have = [
-        {e: n for n, e in enumerate(entries(0, toward) + [(19, 0), (20, 0)])} for toward in (1, -1)
-    ]
-    zero = jnp.zeros((1, 128), F32)
+        out[SENT_ROWS - 8 : SENT_ROWS, :] = jnp.zeros((8, 128), F32)
     for even_x in range(2):
         for even_y in range(2):
 
@@ -325,17 +337,22 @@
             def _():
                 halves = (xo, xe) if even_x == 0 else (xe, xo)
                 for out, sign in ((ye, 1 - 2 * even_y), (yo, 2 * even_y - 1)):
-                    for i, (q, layer) in enumerate(entries(1, sign) + [(19, 0), (20, 0)]):
-                        row = 15 - layer if sign == 1 else layer
-                        for toward in range(2):
-                            for deep in range(2):
-                                at = i * EXT + ((1 - deep) if toward == 0 else 18 + deep)
-                                n = have[toward].get((q, deep))
-                                value = zero if n is None else halves[toward][n, row : row + 1, :]
-                                out[at : at + 1, :] = value
-
-
-def middle_kernel(odd, force, edge, inner, coef, xo, xe, out, wide, again, result, sems):
+                    for n, (_i, _column, toward, there, row) in enumerate(corners(sign)):
+                        at = COUNT * 16 + n
+                        out[at : at + 1, :] = halves[toward][there, row : row + 1, :]
+
+
+def widen(message, sign, out):
+    for i in range(COUNT):
+        out[i * EXT + 2 : i * EXT + 18, :] = message[16 * i : 16 * i + 16, :]
+    for n, (i, column, *_rest) in enumerate(corners(sign)):
+        at = COUNT * 16 + n
+        out[i * EXT + column : i * EXT + column + 1, :] = message[at : at + 1, :]
+
+
+def middle_kernel(
+    odd, force, edge, inner, coef, xe, xo, ye, yo, out, went_dn, went_up, wide, again, result, sems
+):
     flag = odd[0]
     for j in range(4):
         for q in range(19):
@@ -387,6 +404,13 @@
         return 0
 
     lax.fori_loop(0, 16, finish, 0)
+    for even in range(2):
+
+        @pl.when(odd[1] == even)
+        def _():
+            widen(ye if even == 0 else yo, 1, went_up)
+            widen(yo if even == 0 else ye, -1, went_dn)
+
     for x in range(16):
         pltpu.make_async_copy(result.at[x], out.at[:, x], sems.at[x]).wait()
 
@@ -434,17 +458,19 @@
         number += len(listed)
 
 
-def last_kernel(odd, force, mine_o, mine_e, came_o, came_e, _before, out, rows, patch, sem):
+def last_kernel(
+    odd, force, went_dn, went_up, came_e, came_o, _before, out, below, above, rows, patch, sem
+):
     f = [force[axis : axis + 1, :] for axis in range(3)]
     for even in range(2):
 
         @pl.when(odd[1] == even)
         def _():
-            low = (mine_o, came_o) if even == 0 else (mine_e, came_e)
-            high = (mine_e, came_e) if even == 0 else (mine_o, came_o)
-            last_side(0, 1, *low, out, rows, patch, sem, f)
-            last_side(1, -1, *high, out, rows, patch, sem, f)
-
+            widen(came_o if even == 0 else came_e, 1, below)
+            widen(came_e if even == 0 else came_o, -1, above)
+
+    last_side(0, 1, went_dn, below, out, rows, patch, sem, f)
+    last_side(1, -1, went_up, above, out, rows, patch, sem, f)
     pltpu.make_async_copy(patch, patch, sem).wait()
 
 
@@ -499,7 +525,7 @@
     coef, odd, drive = lax.optimization_barrier((coef, odd, drive))
     hbm = pl.BlockSpec(memory_space=pltpu.HBM)
     posts = [jax.ShapeDtypeStruct((19, n, 16, 128), F32) for n in (4, 12)]
-    found, edge, xo, xe = pl.pallas_call(
+    found, edge, xe, xo = pl.pallas_call(
         edge_kernel,
         out_shape=[jax.ShapeDtypeStruct((8, 128), jnp.int32), posts[0], FACE, FACE],
         in_specs=[SMEM_SPEC, VMEM_SPEC, hbm, VMEM_SPEC],
@@ -516,9 +542,9 @@
     )(odd, drive, arrived, coef)
     from_xo = swap(xo, "gx", False)
     from_xe = swap(xe, "gx", True)
-    inner, own_yo, own_ye = pl.pallas_call(
+    inner, own_ye, own_yo = pl.pallas_call(
         inner_kernel,
-        out_shape=[posts[1], SIDE, SIDE],
+        out_shape=[posts[1], SENT, SENT],
         in_specs=[SMEM_SPEC, VMEM_SPEC, VMEM_SPEC, hbm, VMEM_SPEC, VMEM_SPEC],
         out_specs=[VMEM_SPEC] * 3,
         scratch_shapes=[
@@ -530,15 +556,15 @@
         compiler_params=pltpu.CompilerParams(vmem_limit_bytes=VMEM_LIMIT),
         cost_estimate=pl.CostEstimate(flops=6_000_000, bytes_accessed=8_000_000, transcendentals=0),
     )(odd, drive, found, arrived, coef, edge)
-    yo, ye = call(join_kernel, [SIDE, SIDE], (odd, from_xo, from_xe, own_yo, own_ye), 500_000)
+    ye, yo = call(join_kernel, [SENT, SENT], (odd, from_xe, from_xo, own_ye, own_yo), 500_000)
     from_yo = swap(yo, "gy", False)
     from_ye = swap(ye, "gy", True)
-    result = call(
+    result, went_dn, went_up = call(
         middle_kernel,
-        jax.ShapeDtypeStruct((19, 16, 16, 128), F32),
-        (odd, drive, edge, inner, coef, from_xo, from_xe),
+        [jax.ShapeDtypeStruct((19, 16, 16, 128), F32), SIDE, SIDE],
+        (odd, drive, edge, inner, coef, from_xe, from_xo, ye, yo),
         12_000_000,
-        out_specs=hbm,
+        out_specs=[hbm, VMEM_SPEC, VMEM_SPEC],
         scratch_shapes=[
             pltpu.VMEM((19, EXT, 32, 128), F32),
             pltpu.VMEM((19, 18, 32, 128), F32),
@@ -553,13 +579,15 @@
         out_specs=hbm,
         input_output_aliases={6: 0},
         scratch_shapes=[
+            pltpu.VMEM((SIDE_ROWS, 128), F32),
+            pltpu.VMEM((SIDE_ROWS, 128), F32),
             pltpu.VMEM((2, 19, 24, 128), F32),
             pltpu.VMEM((38, 16, 128), F32),
             pltpu.SemaphoreType.DMA,
         ],
         compiler_params=pltpu.CompilerParams(vmem_limit_bytes=VMEM_LIMIT),
         cost_estimate=pl.CostEstimate(flops=2_000_000, bytes_accessed=2_000_000, transcendentals=0),
-    )(odd, drive, yo, ye, from_yo, from_ye, result)
+    )(odd, drive, went_dn, went_up, from_ye, from_yo, result)
 
 
 def solution(mesh):

time: 106 us -> 105 us (level)
  waiting for transfers between devices: 60 us -> 58 us
    ppermute x4, waiting for transfers between devices: 3.94 us -> 1.86 us  [swap(): return lax.ppermute(value, axis, pairs)]
where the time goes in v10:
time: 105 us; the launch traced here: 104 us
  waiting for transfers between devices  58 us (55%)
  starting transfers between devices  27.7 us (26%)
  Pallas kernels  17 us (16%)
  other arithmetic  1.1 us (1%)
    ppermute x3, waiting for transfers between devices, pieces_of(): lax.ppermute(message, 'gy', [(i, i ^ 2 * k) for i in range(8)])  54.8 us
    all_to_all x1, starting transfers between devices, local(): lax.all_to_all(packed, ('gx', 'gy'), split_axis=0, concat_axis=0, tiled=T...  11.7 us
    ppermute x4, starting transfers between devices, swap(): return lax.ppermute(value, axis, pairs)  7.71 us
    ppermute x3, starting transfers between devices, pieces_of(): lax.ppermute(message, 'gy', [(i, i ^ 2 * k) for i in range(8)])  6.58 us
    pallas_call x2, Pallas kernels, call(): pl.pallas_call(kernel, out_shape=out_shape, in_specs=[SMEM_SPEC] * scalar...  5.13 us
    pallas_call x1, Pallas kernels, local(): pl.pallas_call(inner_kernel, out_shape=[posts[1], SENT, SENT], in_specs=[...  3.97 us
    pallas_call x1, Pallas kernels, local(): pl.pallas_call(edge_kernel, out_shape=[jax.ShapeDtypeStruct((8, 128), jnp...  3.56 us
    pallas_call x1, Pallas kernels, pack(): pl.pallas_call(pack_kernel, out_shape=jax.ShapeDtypeStruct((DEVICES, PAIR...  2.75 us
  transfers between devices with their start and end apart: 9, of which 5 were waited for; matrix products, arithmetic and copies ran while one was open for 0% of the time, Pallas kernels for 11%

profile of v10, /device:TPU:0, one launch (start us, length us, event | category | flops | bytes accessed | tf_op | source)
XLA Modules:
  0.0 104.2 jit_solution(16601449504743701051)
XLA Ops:
  0.0 0.9 fusion.1
  0.9 1.7 %collective-permute-start = (f32[2,2,4,16,128]{4,3,2,1,0:T(8,128)S(1)}, f32[2,2,4,16,128]{4,3,2,1,0:T(8,128)S(1)}, u32[]{:S(2)}, u32[]{:S(2)}) collective-permute-start(f32[2,2,4,16,128]{4,3,2,1,0:T(8,128)S(1)} %fusion.1), channel_id=1, source_target_pairs={{0,1},{1,0},{2,3},{3,2},{4,5},{5,4},{6,7},{7,6},{8,9},{9,8},{10,11... | collective-permute-start | bytes 393224 | tf_op jit(solution)/shard_map/ppermute | solution.py:488
  2.6 2.7 %shard_map.64 = f32[128,77,1,128]{3,2,1,0:T(1,128)} custom-call(s32[128]{0:T(128)} %target_hbm.1, f32[19,256,128]{2,1,0:T(8,128)} %bitcast.43), custom_call_target="tpu_custom_call" | custom-call | bytes 8000000 | tf_op jit(solution)/shard_map/pallas_call | solution.py:167
  5.4 0.0 copy-start.3
  5.4 0.7 collective-permute-done
  6.1 11.7 %all-to-all-start = ((f32[128,77,1,128]{3,2,1,0:T(1,128)}), f32[128,77,1,128]{3,2,1,0:T(1,128)}, u32[]{:S(2)}, u32[]{:S(2)}) async-start(f32[128,77,1,128]{3,2,1,0:T(1,128)} %shard_map.64), calls=%async_computation | async-start | bytes 10092544 | tf_op jit(solution)/shard_map/all_to_all | solution.py:517
  18.0 2.5 %collective-permute-start.1 = (f32[2,2,2,16,128]{4,3,2,1,0:T(8,128)S(1)}, f32[2,2,2,16,128]{4,3,2,1,0:T(8,128)S(1)}, u32[]{:S(2)}, u32[]{:S(2)}) collective-permute-start(f32[2,2,2,16,128]{4,3,2,1,0:T(8,128)S(1)} %get-tuple-element.48), channel_id=1, source_target_pairs={{0,2},{1,3},{2,0},{3,1},{4,6},{5,7},{6,4},{7,5},{8,10},{9,11},{10,... | collective-permute-start | bytes 196616 | tf_op jit(solution)/shard_map/ppermute | solution.py:498
  20.5 3.0 %collective-permute-start.2 = (f32[2,2,2,16,128]{4,3,2,1,0:T(8,128)S(1)}, f32[2,2,2,16,128]{4,3,2,1,0:T(8,128)S(1)}, u32[]{:S(2)}, u32[]{:S(2)}) collective-permute-start(f32[2,2,2,16,128]{4,3,2,1,0:T(8,128)S(1)} %get-tuple-element.49), channel_id=1, source_target_pairs={{0,4},{1,5},{2,6},{3,7},{4,0},{5,1},{6,2},{7,3},{8,12},{9,13},{10,... | collective-permute-start | bytes 196616 | tf_op jit(solution)/shard_map/ppermute | solution.py:498
  23.5 1.1 %collective-permute-start.3 = (f32[2,2,2,16,128]{4,3,2,1,0:T(8,128)S(1)}, f32[2,2,2,16,128]{4,3,2,1,0:T(8,128)S(1)}, u32[]{:S(2)}, u32[]{:S(2)}) collective-permute-start(f32[2,2,2,16,128]{4,3,2,1,0:T(8,128)S(1)} %get-tuple-element.50), channel_id=1, source_target_pairs={{0,6},{1,7},{2,4},{3,5},{4,2},{5,3},{6,0},{7,1},{8,14},{9,15},{10,... | collective-permute-start | bytes 196616 | tf_op jit(solution)/shard_map/ppermute | solution.py:498
  24.6 0.1 pad_add_fusion.odd
  24.7 52.4 %collective-permute-done.1 = f32[2,2,2,16,128]{4,3,2,1,0:T(8,128)S(1)} collective-permute-done((f32[2,2,2,16,128]{4,3,2,1,0:T(8,128)S(1)}, f32[2,2,2,16,128]{4,3,2,1,0:T(8,128)S(1)}, u32[]{:S(2)}, u32[]{:S(2)}) %collective-permute-start.1) | collective-permute-done | bytes 65568 | tf_op jit(solution)/shard_map/ppermute | solution.py:498
  77.1 2.3 %collective-permute-done.3 = f32[2,2,2,16,128]{4,3,2,1,0:T(8,128)S(1)} collective-permute-done((f32[2,2,2,16,128]{4,3,2,1,0:T(8,128)S(1)}, f32[2,2,2,16,128]{4,3,2,1,0:T(8,128)S(1)}, u32[]{:S(2)}, u32[]{:S(2)}) %collective-permute-start.3) | collective-permute-done | bytes 65568 | tf_op jit(solution)/shard_map/ppermute | solution.py:498
  79.6 0.1 broadcast_in_dim.2.force
  79.7 0.6 all-to-all-done.arrived
  80.3 3.6 %shard_map.65 = (s32[8,128]{1,0:T(8,128)S(1)}, f32[19,4,16,128]{3,2,1,0:T(8,128)S(1)}, f32[21,16,128]{2,1,0:T(8,128)S(1)}, f32[21,16,128]{2,1,0:T(8,128)S(1)}) custom-call(s32[2]{0:T(128)S(1)} %pad_add_fusion.odd, f32[8,128]{1,0:T(8,128)S(1)} %broadcast_in_dim.2.force, f32[128,77,1,128]{3,2,1,0:T(1,128)} %all-to-all-done.arrived, ...), custom_call_target="tpu_custom_call" | custom-call | flops 2000000 | bytes 8000000 | tf_op jit(solution)/shard_map/pallas_call | solution.py:528
  83.9 0.1 collective-permute-start.4
  84.0 4.5 %collective-permute-start.5 = (f32[21,16,128]{2,1,0:T(8,128)S(1)}, f32[21,16,128]{2,1,0:T(8,128)S(1)}, u32[]{:S(2)}, u32[]{:S(2)}) collective-permute-start(f32[21,16,128]{2,1,0:T(8,128)S(1)} %get-tuple-element.31), channel_id=1, source_target_pairs={{0,120},{8,16},{16,8},{24,32},{32,24},{40,48},{48,40},{56,64},{64,... | collective-permute-start | bytes 516104 | tf_op jit(solution)/shard_map/ppermute | solution.py:480
  88.5 4.0 %shard_map.66 = (f32[19,12,16,128]{3,2,1,0:T(8,128)S(1)}, f32[384,128]{1,0:T(8,128)S(1)}, f32[384,128]{1,0:T(8,128)S(1)}) custom-call(s32[2]{0:T(128)S(1)} %pad_add_fusion.odd, f32[8,128]{1,0:T(8,128)S(1)} %broadcast_in_dim.2.force, s32[8,128]{1,0:T(8,128)S(1)} %get-tuple-element.28.found, f32[128,77,1,128]{3,2,1,0:T(1,128)} %all-to-all-done.arrived, ...), custom_call_target="tpu_custom_call" | custom-call | flops 6000000 | bytes 8000000 | tf_op jit(solution)/shard_map/pallas_call | solution.py:545
  92.5 0.6 shard_map.67
  93.2 0.2 collective-permute-start.6
  93.4 2.9 %collective-permute-start.7 = (f32[384,128]{1,0:T(8,128)S(1)}, f32[384,128]{1,0:T(8,128)S(1)}, u32[]{:S(2)}, u32[]{:S(2)}) collective-permute-start(f32[384,128]{1,0:T(8,128)S(1)} %get-tuple-element.35.yo), channel_id=1, source_target_pairs={{0,7},{1,2},{2,1},{3,4},{4,3},{5,6},{6,5},{7,0},{8,15},{9,10},{10,... | collective-permute-start | bytes 589832 | tf_op jit(solution)/shard_map/ppermute | solution.py:480
  96.3 4.5 %shard_map.68 = (f32[19,16,16,128]{3,2,1,0:T(8,128)}, f32[432,128]{1,0:T(8,128)S(1)}, f32[432,128]{1,0:T(8,128)S(1)}) custom-call(s32[2]{0:T(128)S(1)} %pad_add_fusion.odd, f32[8,128]{1,0:T(8,128)S(1)} %broadcast_in_dim.2.force, f32[19,4,16,128]{3,2,1,0:T(8,128)S(1)} %get-tuple-element.27.edge, f32[19,12,16,128]{3,2,1,0:T(8,128)S(1)} %get-tuple-element.29.inner, ...), custom_call_target="tpu_custom_call" | custom-call | flops 12000000 | bytes 12000000 | tf_op jit(solution)/shard_map/pallas_call | solution.py:305
  100.8 1.9 %collective-permute-done.7.came_o = f32[384,128]{1,0:T(8,128)S(1)} collective-permute-done((f32[384,128]{1,0:T(8,128)S(1)}, f32[384,128]{1,0:T(8,128)S(1)}, u32[]{:S(2)}, u32[]{:S(2)}) %collective-permute-start.7) | collective-permute-done | bytes 196640 | tf_op jit(solution)/shard_map/ppermute | solution.py:480
  102.6 1.6 %shard_map.69 = f32[19,16,16,128]{3,2,1,0:T(8,128)} custom-call(s32[2]{0:T(128)S(1)} %pad_add_fusion.odd, f32[8,128]{1,0:T(8,128)S(1)} %broadcast_in_dim.2.force, f32[432,128]{1,0:T(8,128)S(1)} %get-tuple-element.36.went_dn, f32[432,128]{1,0:T(8,128)S(1)} %get-tuple-element.37.went_up, ...), custom_call_target="tpu_custom_call", output_to_operand_aliasing={{}: (6, {})} | custom-call | flops 2000000 | bytes 2000000 | tf_op jit(solution)/shard_map/pallas_call | solution.py:575
  (20 shorter events, 0.2 us)
Async XLA Ops:
  0.9 5.2 %collective-permute-start = (f32[2,2,4,16,128]{4,3,2,1,0:T(8,128)S(1)}, f32[2,2,4,16,128]{4,3,2,1,0:T(8,128)S(1)}, u32[]{:S(2)}, u32[]{:S(2)}) collective-permute-start(f32[2,2,4,16,128]{4,3,2,1,0:T(8,128)S(1)} %fusion.1), channel_id=1, source_target_pairs={{0,1},{1,0},{2,3},{3,2},{4,5},{5,4},{6,7},{7,6},{8,9},{9,8},{10,11... | collective-permute-start | bytes 393224 | tf_op jit(solution)/shard_map/ppermute | solution.py:488
  5.4 12.5 %copy-start.3 = (f32[3]{0:T(128)S(1)}, f32[3]{0:T(128)}, u32[]{:S(2)}) copy-start(f32[3]{0:T(128)} %param.11) | copy-start | bytes 40
  5.4 12.5 %copy-start = (f32[2,128,128]{2,1,0:T(8,128)S(1)}, f32[2,128,128]{2,1,0:T(8,128)}, u32[]{:S(2)}) copy-start(f32[2,128,128]{2,1,0:T(8,128)} %param.8) | copy-start | bytes 393220
  5.4 12.5 %copy-start.1 = (f32[2,128,128]{2,1,0:T(8,128)S(1)}, f32[2,128,128]{2,1,0:T(8,128)}, u32[]{:S(2)}) copy-start(f32[2,128,128]{2,1,0:T(8,128)} %param.9) | copy-start | bytes 393220
  6.1 74.2 %all-to-all-start = ((f32[128,77,1,128]{3,2,1,0:T(1,128)}), f32[128,77,1,128]{3,2,1,0:T(1,128)}, u32[]{:S(2)}, u32[]{:S(2)}) async-start(f32[128,77,1,128]{3,2,1,0:T(1,128)} %shard_map.64), calls=%async_computation | async-start | bytes 10092544 | tf_op jit(solution)/shard_map/all_to_all | solution.py:517
  17.8 61.8 %copy-start.2 = (s32[16,16,128]{2,1,0:T(8,128)S(1)}, s32[16,16,128]{2,1,0:T(8,128)}, u32[]{:S(2)}) copy-start(s32[16,16,128]{2,1,0:T(8,128)} %param.10) | copy-start | bytes 393220
  18.0 59.1 %collective-permute-start.1 = (f32[2,2,2,16,128]{4,3,2,1,0:T(8,128)S(1)}, f32[2,2,2,16,128]{4,3,2,1,0:T(8,128)S(1)}, u32[]{:S(2)}, u32[]{:S(2)}) collective-permute-start(f32[2,2,2,16,128]{4,3,2,1,0:T(8,128)S(1)} %get-tuple-element.48), channel_id=1, source_target_pairs={{0,2},{1,3},{2,0},{3,1},{4,6},{5,7},{6,4},{7,5},{8,10},{9,11},{10,... | collective-permute-start | bytes 196616 | tf_op jit(solution)/shard_map/ppermute | solution.py:498
  20.5 56.6 %collective-permute-start.2 = (f32[2,2,2,16,128]{4,3,2,1,0:T(8,128)S(1)}, f32[2,2,2,16,128]{4,3,2,1,0:T(8,128)S(1)}, u32[]{:S(2)}, u32[]{:S(2)}) collective-permute-start(f32[2,2,2,16,128]{4,3,2,1,0:T(8,128)S(1)} %get-tuple-element.49), channel_id=1, source_target_pairs={{0,4},{1,5},{2,6},{3,7},{4,0},{5,1},{6,2},{7,3},{8,12},{9,13},{10,... | collective-permute-start | bytes 196616 | tf_op jit(solution)/shard_map/ppermute | solution.py:498
  23.5 56.0 %collective-permute-start.3 = (f32[2,2,2,16,128]{4,3,2,1,0:T(8,128)S(1)}, f32[2,2,2,16,128]{4,3,2,1,0:T(8,128)S(1)}, u32[]{:S(2)}, u32[]{:S(2)}) collective-permute-start(f32[2,2,2,16,128]{4,3,2,1,0:T(8,128)S(1)} %get-tuple-element.50), channel_id=1, source_target_pairs={{0,6},{1,7},{2,4},{3,5},{4,2},{5,3},{6,0},{7,1},{8,14},{9,15},{10,... | collective-permute-start | bytes 196616 | tf_op jit(solution)/shard_map/ppermute | solution.py:498
  83.9 8.6 %collective-permute-start.4 = (f32[21,16,128]{2,1,0:T(8,128)S(1)}, f32[21,16,128]{2,1,0:T(8,128)S(1)}, u32[]{:S(2)}, u32[]{:S(2)}) collective-permute-start(f32[21,16,128]{2,1,0:T(8,128)S(1)} %get-tuple-element.30), channel_id=1, source_target_pairs={{0,8},{8,0},{16,24},{24,16},{32,40},{40,32},{48,56},{56,48},{64,72... | collective-permute-start | bytes 516104 | tf_op jit(solution)/shard_map/ppermute | solution.py:480
  84.0 8.5 %collective-permute-start.5 = (f32[21,16,128]{2,1,0:T(8,128)S(1)}, f32[21,16,128]{2,1,0:T(8,128)S(1)}, u32[]{:S(2)}, u32[]{:S(2)}) collective-permute-start(f32[21,16,128]{2,1,0:T(8,128)S(1)} %get-tuple-element.31), channel_id=1, source_target_pairs={{0,120},{8,16},{16,8},{24,32},{32,24},{40,48},{48,40},{56,64},{64,... | collective-permute-start | bytes 516104 | tf_op jit(solution)/shard_map/ppermute | solution.py:480
  93.2 7.6 %collective-permute-start.6 = (f32[384,128]{1,0:T(8,128)S(1)}, f32[384,128]{1,0:T(8,128)S(1)}, u32[]{:S(2)}, u32[]{:S(2)}) collective-permute-start(f32[384,128]{1,0:T(8,128)S(1)} %get-tuple-element.34.ye), channel_id=1, source_target_pairs={{0,1},{1,0},{2,3},{3,2},{4,5},{5,4},{6,7},{7,6},{8,9},{9,8},{10,11... | collective-permute-start | bytes 589832 | tf_op jit(solution)/shard_map/ppermute | solution.py:480
  93.4 9.3 %collective-permute-start.7 = (f32[384,128]{1,0:T(8,128)S(1)}, f32[384,128]{1,0:T(8,128)S(1)}, u32[]{:S(2)}, u32[]{:S(2)}) collective-permute-start(f32[384,128]{1,0:T(8,128)S(1)} %get-tuple-element.35.yo), channel_id=1, source_target_pairs={{0,7},{1,2},{2,1},{3,4},{4,3},{5,6},{6,5},{7,0},{8,15},{9,10},{10,... | collective-permute-start | bytes 589832 | tf_op jit(solution)/shard_map/ppermute | solution.py:480

commit v11 on v10

--- a/solution.py
+++ b/solution.py
@@ -50,6 +50,10 @@
 COUNT = 21
 SIDE_ROWS = 432
 SENT_ROWS = 384
+
+
+def parity(axis):
+    return lax.rem(lax.axis_index(axis), 2)
 
 
 def collide(dist, solid, omega, force):
@@ -216,7 +220,7 @@
 
 
 def edge_kernel(
-    odd, force, arrived, coef, found, edge, xe, xo, tiles, labels, source, sems, small
+    force, arrived, coef, found, edge, xe, xo, tiles, labels, source, sems, small
 ):
     pull = pltpu.make_async_copy(arrived.at[:, 2 * TILE, 0, :], labels, small.at[0])
     pull.start()
@@ -249,7 +253,7 @@
     lax.fori_loop(0, 4, plane, 0)
     for even in range(2):
 
-        @pl.when(odd[0] == even)
+        @pl.when(parity("gx") == even)
         def _():
             for out, sign in ((xe, 1 - 2 * even), (xo, 2 * even - 1)):
                 for i, (q, layer) in enumerate(entries(0, sign)):
@@ -258,7 +262,7 @@
                     out[19 + j] = coef[j, 15 if sign == 1 else 0]
 
 
-def inner_kernel(odd, force, found, arrived, coef, edge, inner, ye, yo, tiles, source, sems, small):
+def inner_kernel(force, found, arrived, coef, edge, inner, ye, yo, tiles, source, sems, small):
     hand = pltpu.make_async_copy(found, source, small)
     hand.start()
     f = [force[axis : axis + 1, :] for axis in range(3)]
@@ -276,7 +280,7 @@
     lax.fori_loop(0, 12, plane, 0)
     for even in range(2):
 
-        @pl.when(odd[1] == even)
+        @pl.when(parity("gy") == even)
         def _():
             for out, sign in ((ye, 1 - 2 * even), (yo, 2 * even - 1)):
                 for i, (q, layer) in enumerate(entries(1, sign)):
@@ -295,17 +299,16 @@
 
 
 VMEM_SPEC = pl.BlockSpec(memory_space=pltpu.VMEM)
-SMEM_SPEC = pl.BlockSpec(memory_space=pltpu.SMEM)
 FACE = jax.ShapeDtypeStruct((COUNT, 16, 128), F32)
 SIDE = jax.ShapeDtypeStruct((SIDE_ROWS, 128), F32)
 SENT = jax.ShapeDtypeStruct((SENT_ROWS, 128), F32)
 
 
-def call(kernel, out_shape, operands, work, scalars=1, **more):
+def call(kernel, out_shape, operands, work, **more):
     return pl.pallas_call(
         kernel,
         out_shape=out_shape,
-        in_specs=[SMEM_SPEC] * scalars + [VMEM_SPEC] * (len(operands) - scalars),
+        in_specs=[VMEM_SPEC] * len(operands),
         compiler_params=pltpu.CompilerParams(vmem_limit_bytes=VMEM_LIMIT),
         cost_estimate=pl.CostEstimate(flops=work, bytes_accessed=work, transcendentals=0),
         **more,
@@ -325,7 +328,7 @@
     return listed
 
 
-def join_kernel(odd, xe, xo, own_e, own_o, ye, yo):
+def join_kernel(xe, xo, own_e, own_o, ye, yo):
     for own, out in ((own_e, ye), (own_o, yo)):
         for block in range(COUNT * 2):
             out[8 * block : 8 * block + 8, :] = own[8 * block : 8 * block + 8, :]
@@ -333,7 +336,7 @@
     for even_x in range(2):
         for even_y in range(2):
 
-            @pl.when((odd[0] == even_x) & (odd[1] == even_y))
+            @pl.when((parity("gx") == even_x) & (parity("gy") == even_y))
             def _():
                 halves = (xo, xe) if even_x == 0 else (xe, xo)
                 for out, sign in ((ye, 1 - 2 * even_y), (yo, 2 * even_y - 1)):
@@ -351,9 +354,9 @@
 
 
 def middle_kernel(
-    odd, force, edge, inner, coef, xe, xo, ye, yo, out, went_dn, went_up, wide, again, result, sems
+    force, edge, inner, coef, xe, xo, ye, yo, out, went_dn, went_up, wide, again, result, sems
 ):
-    flag = odd[0]
+    flag = parity("gx")
     for j in range(4):
         for q in range(19):
             wide[q, (j if j < 2 else j + 12) + 2, 8:24, :] = edge[q, j]
@@ -406,7 +409,7 @@
     lax.fori_loop(0, 16, finish, 0)
     for even in range(2):
 
-        @pl.when(odd[1] == even)
+        @pl.when(parity("gy") == even)
         def _():
             widen(ye if even == 0 else yo, 1, went_up)
             widen(yo if even == 0 else ye, -1, went_dn)
@@ -459,12 +462,12 @@
 
 
 def last_kernel(
-    odd, force, went_dn, went_up, came_e, came_o, _before, out, below, above, rows, patch, sem
+    force, went_dn, went_up, came_e, came_o, _before, out, below, above, rows, patch, sem
 ):
     f = [force[axis : axis + 1, :] for axis in range(3)]
     for even in range(2):
 
-        @pl.when(odd[1] == even)
+        @pl.when(parity("gy") == even)
         def _():
             widen(came_o if even == 0 else came_e, 1, below)
             widen(came_e if even == 0 else came_o, -1, above)
@@ -481,32 +484,32 @@
 
 
 def halves_of(porosity, relaxation):
-    lo = lax.axis_index("gy") % 2
-    slab = jnp.stack([porosity, relaxation]).reshape(2, 2, 4, 2, 16, 128)
-    other = lax.dynamic_index_in_dim(slab, 1 - lo, axis=3, keepdims=False)
-    mine = lax.dynamic_index_in_dim(slab, lo, axis=3, keepdims=False)
-    return mine, lax.ppermute(other, "gy", [(i, i ^ 1) for i in range(8)])
+    hi = lax.axis_index("gy") // 4
+    slab = jnp.stack([porosity, relaxation]).reshape(2, 2, 8, 16, 128)
+    other = lax.dynamic_slice_in_dim(slab, (1 - hi) * 4, 4, axis=2)
+    mine = lax.dynamic_slice_in_dim(slab, hi * 4, 4, axis=2)
+    return mine, lax.ppermute(other, "gy", [(i, i ^ 4) for i in range(8)])
 
 
 def pieces_of(mine, came):
     b = lax.axis_index("gy")
-    hi, lo = b // 2, b % 2
-    both = jnp.stack([jnp.where(lo == 0, mine, came), jnp.where(lo == 0, came, mine)])
-    parts = [lax.dynamic_index_in_dim(both, hi, axis=3, keepdims=False)]
+    hi, lo = b // 4, b % 4
+    both = jnp.stack([jnp.where(hi == 0, mine, came), jnp.where(hi == 0, came, mine)])
+    parts = [lax.dynamic_index_in_dim(both, lo, axis=3, keepdims=False)]
     for k in range(1, 4):
-        message = lax.dynamic_index_in_dim(both, hi ^ k, axis=3, keepdims=False)
-        parts.append(lax.ppermute(message, "gy", [(i, i ^ (2 * k)) for i in range(8)]))
+        message = lax.dynamic_index_in_dim(both, lo ^ k, axis=3, keepdims=False)
+        parts.append(lax.ppermute(message, "gy", [(i, i ^ k) for i in range(8)]))
     return parts
 
 
 def block_of(parts):
-    hi = lax.axis_index("gy") // 2
+    lo = lax.axis_index("gy") % 4
     stacked = jnp.stack(parts)
     ordered = [
-        lax.dynamic_index_in_dim(stacked, hi ^ y, axis=0, keepdims=False) for y in range(4)
+        lax.dynamic_index_in_dim(stacked, lo ^ y, axis=0, keepdims=False) for y in range(4)
     ]
     whole = jnp.stack(ordered)
-    return whole.transpose(2, 0, 1, 3, 4, 5).reshape(2, 16, 16, 128)
+    return whole.transpose(2, 1, 0, 3, 4, 5).reshape(2, 16, 16, 128)
 
 
 def local(pdf_old, tile_target, porosity, relaxation, solid_mask, force):
@@ -520,15 +523,14 @@
     block = block_of(pieces_of(mine, came))
     solid = block[0] + solid_mask.astype(F32) * (1.0 - block[0])
     coef = jnp.stack([solid, block[1]])
-    odd = jnp.stack([lax.axis_index("gx") % 2, lax.axis_index("gy") % 2]).astype(jnp.int32)
     drive = jnp.broadcast_to(jnp.pad(force, (0, 5))[:, None], (8, 128))
-    coef, odd, drive = lax.optimization_barrier((coef, odd, drive))
+    coef, drive = lax.optimization_barrier((coef, drive))
     hbm = pl.BlockSpec(memory_space=pltpu.HBM)
     posts = [jax.ShapeDtypeStruct((19, n, 16, 128), F32) for n in (4, 12)]
     found, edge, xe, xo = pl.pallas_call(
         edge_kernel,
         out_shape=[jax.ShapeDtypeStruct((8, 128), jnp.int32), posts[0], FACE, FACE],
-        in_specs=[SMEM_SPEC, VMEM_SPEC, hbm, VMEM_SPEC],
+        in_specs=[VMEM_SPEC, hbm, VMEM_SPEC],
         out_specs=[VMEM_SPEC] * 4,
         scratch_shapes=[
             pltpu.VMEM((32 * ROWS, 128), F32),
@@ -539,13 +541,13 @@
         ],
         compiler_params=pltpu.CompilerParams(vmem_limit_bytes=VMEM_LIMIT),
         cost_estimate=pl.CostEstimate(flops=2_000_000, bytes_accessed=8_000_000, transcendentals=0),
-    )(odd, drive, arrived, coef)
+    )(drive, arrived, coef)
     from_xo = swap(xo, "gx", False)
     from_xe = swap(xe, "gx", True)
     inner, own_ye, own_yo = pl.pallas_call(
         inner_kernel,
         out_shape=[posts[1], SENT, SENT],
-        in_specs=[SMEM_SPEC, VMEM_SPEC, VMEM_SPEC, hbm, VMEM_SPEC, VMEM_SPEC],
+        in_specs=[VMEM_SPEC, VMEM_SPEC, hbm, VMEM_SPEC, VMEM_SPEC],
         out_specs=[VMEM_SPEC] * 3,
         scratch_shapes=[
             pltpu.VMEM((96 * ROWS, 128), F32),
@@ -555,14 +557,14 @@
         ],
         compiler_params=pltpu.CompilerParams(vmem_limit_bytes=VMEM_LIMIT),
         cost_estimate=pl.CostEstimate(flops=6_000_000, bytes_accessed=8_000_000, transcendentals=0),
-    )(odd, drive, found, arrived, coef, edge)
-    ye, yo = call(join_kernel, [SENT, SENT], (odd, from_xe, from_xo, own_ye, own_yo), 500_000)
+    )(drive, found, arrived, coef, edge)
+    ye, yo = call(join_kernel, [SENT, SENT], (from_xe, from_xo, own_ye, own_yo), 500_000)
     from_yo = swap(yo, "gy", False)
     from_ye = swap(ye, "gy", True)
     result, went_dn, went_up = call(
         middle_kernel,
         [jax.ShapeDtypeStruct((19, 16, 16, 128), F32), SIDE, SIDE],
-        (odd, drive, edge, inner, coef, from_xe, from_xo, ye, yo),
+        (drive, edge, inner, coef, from_xe, from_xo, ye, yo),
         12_000_000,
         out_specs=[hbm, VMEM_SPEC, VMEM_SPEC],
         scratch_shapes=[
@@ -575,9 +577,9 @@
     return pl.pallas_call(
         last_kernel,
         out_shape=jax.ShapeDtypeStruct((19, 16, 16, 128), F32),
-        in_specs=[SMEM_SPEC] + [VMEM_SPEC] * 5 + [hbm],
+        in_specs=[VMEM_SPEC] * 5 + [hbm],
         out_specs=hbm,
-        input_output_aliases={6: 0},
+        input_output_aliases={5: 0},
         scratch_shapes=[
             pltpu.VMEM((SIDE_ROWS, 128), F32),
             pltpu.VMEM((SIDE_ROWS, 128), F32),
@@ -587,7 +589,7 @@
         ],
         compiler_params=pltpu.CompilerParams(vmem_limit_bytes=VMEM_LIMIT),
         cost_estimate=pl.CostEstimate(flops=2_000_000, bytes_accessed=2_000_000, transcendentals=0),
-    )(odd, drive, went_dn, went_up, from_ye, from_yo, result)
+    )(drive, went_dn, went_up, from_ye, from_yo, result)
 
 
 def solution(mesh):

time: 105 us -> 104 us (level)
  waiting for transfers between devices: 58 us -> 61 us
  Pallas kernels: 17 us -> 14.3 us
  starting transfers between devices: 27.7 us -> 26.4 us
    ppermute x4, waiting for transfers between devices: 55.5 us -> 58.4 us  [the longest x3 57.8 us: pieces_of(): parts.append(lax.ppermute(message, 'gy', [(i, i ^ k) for i in range(8)]))]
    pallas_call x2, Pallas kernels: 5.13 us -> 4.06 us  [call(): pl.pallas_call(kernel, out_shape=out_shape, in_specs=[VMEM_SPEC] * len(op...]
  transfers between devices with their start and end apart: 9 -> 9, of which waited for: 5 -> 6; matrix products, arithmetic and copies ran while one was open for 0% -> 0% of each run, Pallas kernels for 11% -> 10%
where the time goes in v11:
time: 104 us; the launch traced here: 103 us
  waiting for transfers between devices  61 us (59%)
  starting transfers between devices  26.4 us (25%)
  Pallas kernels  14.3 us (14%)
    ppermute x3, waiting for transfers between devices, pieces_of(): parts.append(lax.ppermute(message, 'gy', [(i, i ^ k) for i in range(8)]))  57.8 us
    all_to_all x1, starting transfers between devices, local(): lax.all_to_all(packed, ('gx', 'gy'), split_axis=0, concat_axis=0, tiled=T...  11.7 us
    ppermute x4, starting transfers between devices, swap(): return lax.ppermute(value, axis, pairs)  7.3 us
    ppermute x3, starting transfers between devices, pieces_of(): parts.append(lax.ppermute(message, 'gy', [(i, i ^ k) for i in range(8)]))  4.17 us
    pallas_call x2, Pallas kernels, call(): pl.pallas_call(kernel, out_shape=out_shape, in_specs=[VMEM_SPEC] * len(op...  4.06 us
    pallas_call x1, Pallas kernels, local(): pl.pallas_call(inner_kernel, out_shape=[posts[1], SENT, SENT], in_specs=[...  3.43 us
    ppermute x1, starting transfers between devices, halves_of(): return (mine, lax.ppermute(other, 'gy', [(i, i ^ 4) for i in range(8)]))  3.19 us
    pallas_call x1, Pallas kernels, local(): pl.pallas_call(edge_kernel, out_shape=[jax.ShapeDtypeStruct((8, 128), jnp...  3.02 us
  transfers between devices with their start and end apart: 9, of which 6 were waited for; matrix products, arithmetic and copies ran while one was open for 0% of the time, Pallas kernels for 10%

profile of v11, /device:TPU:0, one launch (start us, length us, event | category | flops | bytes accessed | tf_op | source)
XLA Modules:
  0.0 103.2 jit_solution(14595055995530144678)
XLA Ops:
  0.0 0.9 fusion
  0.9 3.2 %collective-permute-start = (f32[2,2,4,16,128]{4,3,2,1,0:T(8,128)S(1)}, f32[2,2,4,16,128]{4,3,2,1,0:T(8,128)S(1)}, u32[]{:S(2)}, u32[]{:S(2)}) collective-permute-start(f32[2,2,4,16,128]{4,3,2,1,0:T(8,128)S(1)} %fusion), channel_id=1, source_target_pairs={{0,4},{1,5},{2,6},{3,7},{4,0},{5,1},{6,2},{7,3},{8,12},{9,13},{10,... | collective-permute-start | bytes 393224 | tf_op jit(solution)/shard_map/ppermute | solution.py:491
  4.1 2.8 %shard_map.64 = f32[128,77,1,128]{3,2,1,0:T(1,128)} custom-call(s32[128]{0:T(128)} %target_hbm.1, f32[19,256,128]{2,1,0:T(8,128)} %bitcast.37), custom_call_target="tpu_custom_call" | custom-call | bytes 8000000 | tf_op jit(solution)/shard_map/pallas_call | solution.py:171
  6.9 0.0 copy-start
  6.9 0.7 collective-permute-done
  7.6 11.7 %all-to-all-start = ((f32[128,77,1,128]{3,2,1,0:T(1,128)}), f32[128,77,1,128]{3,2,1,0:T(1,128)}, u32[]{:S(2)}, u32[]{:S(2)}) async-start(f32[128,77,1,128]{3,2,1,0:T(1,128)} %shard_map.64), calls=%async_computation | async-start | bytes 10092544 | tf_op jit(solution)/shard_map/all_to_all | solution.py:520
  19.5 2.2 %collective-permute-start.3 = (f32[2,2,2,16,128]{4,3,2,0,1:T(8,128)S(1)}, f32[2,2,2,16,128]{4,3,2,0,1:T(8,128)S(1)}, u32[]{:S(2)}, u32[]{:S(2)}) collective-permute-start(f32[2,2,2,16,128]{4,3,2,0,1:T(8,128)S(1)} %bitcast.47), channel_id=1, source_target_pairs={{0,3},{1,2},{2,1},{3,0},{4,7},{5,6},{6,5},{7,4},{8,11},{9,10},{10,... | collective-permute-start | bytes 196616 | tf_op jit(solution)/shard_map/ppermute | solution.py:501
  21.7 0.8 collective-permute-start.2
  22.6 1.1 %collective-permute-start.1 = (f32[2,2,2,16,128]{4,3,2,0,1:T(8,128)S(1)}, f32[2,2,2,16,128]{4,3,2,0,1:T(8,128)S(1)}, u32[]{:S(2)}, u32[]{:S(2)}) collective-permute-start(f32[2,2,2,16,128]{4,3,2,0,1:T(8,128)S(1)} %bitcast.45), channel_id=1, source_target_pairs={{0,1},{1,0},{2,3},{3,2},{4,5},{5,4},{6,7},{7,6},{8,9},{9,8},{10,11... | collective-permute-start | bytes 196616 | tf_op jit(solution)/shard_map/ppermute | solution.py:501
  23.7 51.4 %collective-permute-done.3 = f32[2,2,2,16,128]{4,3,2,0,1:T(8,128)S(1)} collective-permute-done((f32[2,2,2,16,128]{4,3,2,0,1:T(8,128)S(1)}, f32[2,2,2,16,128]{4,3,2,0,1:T(8,128)S(1)}, u32[]{:S(2)}, u32[]{:S(2)}) %collective-permute-start.3) | collective-permute-done | bytes 65568 | tf_op jit(solution)/shard_map/ppermute | solution.py:501
  75.1 4.0 %collective-permute-done.2 = f32[2,2,2,16,128]{4,3,2,0,1:T(8,128)S(1)} collective-permute-done((f32[2,2,2,16,128]{4,3,2,0,1:T(8,128)S(1)}, f32[2,2,2,16,128]{4,3,2,0,1:T(8,128)S(1)}, u32[]{:S(2)}, u32[]{:S(2)}) %collective-permute-start.2) | collective-permute-done | bytes 65568 | tf_op jit(solution)/shard_map/ppermute | solution.py:501
  79.1 2.4 %collective-permute-done.1 = f32[2,2,2,16,128]{4,3,2,0,1:T(8,128)S(1)} collective-permute-done((f32[2,2,2,16,128]{4,3,2,0,1:T(8,128)S(1)}, f32[2,2,2,16,128]{4,3,2,0,1:T(8,128)S(1)}, u32[]{:S(2)}, u32[]{:S(2)}) %collective-permute-start.1) | collective-permute-done | bytes 65568 | tf_op jit(solution)/shard_map/ppermute | solution.py:501
  81.7 0.1 broadcast_in_dim.2.force
  81.7 0.1 all-to-all-done.arrived
  81.8 3.0 %shard_map.65 = (s32[8,128]{1,0:T(8,128)S(1)}, f32[19,4,16,128]{3,2,1,0:T(8,128)S(1)}, f32[21,16,128]{2,1,0:T(8,128)S(1)}, f32[21,16,128]{2,1,0:T(8,128)S(1)}) custom-call(f32[8,128]{1,0:T(8,128)S(1)} %broadcast_in_dim.2.force, f32[128,77,1,128]{3,2,1,0:T(1,128)} %all-to-all-done.arrived, f32[2,16,16,128]{3,2,1,0:T(8,128)S(1)} %pad_maximum_fusion.1.coef), custom_call_target="tpu_custom_call" | custom-call | flops 2000000 | bytes 8000000 | tf_op jit(solution)/shard_map/pallas_call | solution.py:530
  84.9 0.1 collective-permute-start.4
  85.0 3.6 %collective-permute-start.5 = (f32[21,16,128]{2,1,0:T(8,128)S(1)}, f32[21,16,128]{2,1,0:T(8,128)S(1)}, u32[]{:S(2)}, u32[]{:S(2)}) collective-permute-start(f32[21,16,128]{2,1,0:T(8,128)S(1)} %get-tuple-element.29), channel_id=1, source_target_pairs={{0,120},{8,16},{16,8},{24,32},{32,24},{40,48},{48,40},{56,64},{64,... | collective-permute-start | bytes 516104 | tf_op jit(solution)/shard_map/ppermute | solution.py:483
  88.6 3.4 %shard_map.66 = (f32[19,12,16,128]{3,2,1,0:T(8,128)S(1)}, f32[384,128]{1,0:T(8,128)S(1)}, f32[384,128]{1,0:T(8,128)S(1)}) custom-call(f32[8,128]{1,0:T(8,128)S(1)} %broadcast_in_dim.2.force, s32[8,128]{1,0:T(8,128)S(1)} %get-tuple-element.26.found, f32[128,77,1,128]{3,2,1,0:T(1,128)} %all-to-all-done.arrived, f32[2,16,16,128]{3,2,1,0:T(8,128)S(1)} %pad_maximum_fusion.1.coef, ...), custom_call_target="tpu_custom_call" | custom-call | flops 6000000 | bytes 8000000 | tf_op jit(solution)/shard_map/pallas_call | solution.py:547
  92.0 0.1 shard_map.67
  92.1 0.8 collective-permute-start.6
  92.9 2.8 %collective-permute-start.7 = (f32[384,128]{1,0:T(8,128)S(1)}, f32[384,128]{1,0:T(8,128)S(1)}, u32[]{:S(2)}, u32[]{:S(2)}) collective-permute-start(f32[384,128]{1,0:T(8,128)S(1)} %get-tuple-element.33.yo), channel_id=1, source_target_pairs={{0,7},{1,2},{2,1},{3,4},{4,3},{5,6},{6,5},{7,0},{8,15},{9,10},{10,... | collective-permute-start | bytes 589832 | tf_op jit(solution)/shard_map/ppermute | solution.py:483
  95.7 4.0 %shard_map.68 = (f32[19,16,16,128]{3,2,1,0:T(8,128)}, f32[432,128]{1,0:T(8,128)S(1)}, f32[432,128]{1,0:T(8,128)S(1)}) custom-call(f32[8,128]{1,0:T(8,128)S(1)} %broadcast_in_dim.2.force, f32[19,4,16,128]{3,2,1,0:T(8,128)S(1)} %get-tuple-element.25.edge, f32[19,12,16,128]{3,2,1,0:T(8,128)S(1)} %get-tuple-element.27.inner, ...), custom_call_target="tpu_custom_call" | custom-call | flops 12000000 | bytes 12000000 | tf_op jit(solution)/shard_map/pallas_call | solution.py:308
  99.7 2.5 %collective-permute-done.7.came_o = f32[384,128]{1,0:T(8,128)S(1)} collective-permute-done((f32[384,128]{1,0:T(8,128)S(1)}, f32[384,128]{1,0:T(8,128)S(1)}, u32[]{:S(2)}, u32[]{:S(2)}) %collective-permute-start.7) | collective-permute-done | bytes 196640 | tf_op jit(solution)/shard_map/ppermute | solution.py:483
  102.2 1.0 shard_map.69
  (23 shorter events, 0.2 us)
Async XLA Ops:
  0.9 6.7 %collective-permute-start = (f32[2,2,4,16,128]{4,3,2,1,0:T(8,128)S(1)}, f32[2,2,4,16,128]{4,3,2,1,0:T(8,128)S(1)}, u32[]{:S(2)}, u32[]{:S(2)}) collective-permute-start(f32[2,2,4,16,128]{4,3,2,1,0:T(8,128)S(1)} %fusion), channel_id=1, source_target_pairs={{0,4},{1,5},{2,6},{3,7},{4,0},{5,1},{6,2},{7,3},{8,12},{9,13},{10,... | collective-permute-start | bytes 393224 | tf_op jit(solution)/shard_map/ppermute | solution.py:491
  6.9 12.5 %copy-start = (f32[2,128,128]{2,1,0:T(8,128)S(1)}, f32[2,128,128]{2,1,0:T(8,128)}, u32[]{:S(2)}) copy-start(f32[2,128,128]{2,1,0:T(8,128)} %param.8) | copy-start | bytes 393220
  6.9 12.5 %copy-start.1 = (f32[2,128,128]{2,1,0:T(8,128)S(1)}, f32[2,128,128]{2,1,0:T(8,128)}, u32[]{:S(2)}) copy-start(f32[2,128,128]{2,1,0:T(8,128)} %param.9) | copy-start | bytes 393220
  6.9 16.8 %copy-start.3 = (f32[3]{0:T(128)S(1)}, f32[3]{0:T(128)}, u32[]{:S(2)}) copy-start(f32[3]{0:T(128)} %param.11) | copy-start | bytes 40
  7.6 74.3 %all-to-all-start = ((f32[128,77,1,128]{3,2,1,0:T(1,128)}), f32[128,77,1,128]{3,2,1,0:T(1,128)}, u32[]{:S(2)}, u32[]{:S(2)}) async-start(f32[128,77,1,128]{3,2,1,0:T(1,128)} %shard_map.64), calls=%async_computation | async-start | bytes 10092544 | tf_op jit(solution)/shard_map/all_to_all | solution.py:520
  19.3 62.3 %copy-start.2 = (s32[16,16,128]{2,1,0:T(8,128)S(1)}, s32[16,16,128]{2,1,0:T(8,128)}, u32[]{:S(2)}) copy-start(s32[16,16,128]{2,1,0:T(8,128)} %param.10) | copy-start | bytes 393220
  19.5 55.5 %collective-permute-start.3 = (f32[2,2,2,16,128]{4,3,2,0,1:T(8,128)S(1)}, f32[2,2,2,16,128]{4,3,2,0,1:T(8,128)S(1)}, u32[]{:S(2)}, u32[]{:S(2)}) collective-permute-start(f32[2,2,2,16,128]{4,3,2,0,1:T(8,128)S(1)} %bitcast.47), channel_id=1, source_target_pairs={{0,3},{1,2},{2,1},{3,0},{4,7},{5,6},{6,5},{7,4},{8,11},{9,10},{10,... | collective-permute-start | bytes 196616 | tf_op jit(solution)/shard_map/ppermute | solution.py:501
  21.7 57.3 %collective-permute-start.2 = (f32[2,2,2,16,128]{4,3,2,0,1:T(8,128)S(1)}, f32[2,2,2,16,128]{4,3,2,0,1:T(8,128)S(1)}, u32[]{:S(2)}, u32[]{:S(2)}) collective-permute-start(f32[2,2,2,16,128]{4,3,2,0,1:T(8,128)S(1)} %bitcast.46), channel_id=1, source_target_pairs={{0,2},{1,3},{2,0},{3,1},{4,6},{5,7},{6,4},{7,5},{8,10},{9,11},{10,... | collective-permute-start | bytes 196616 | tf_op jit(solution)/shard_map/ppermute | solution.py:501
  22.6 58.9 %collective-permute-start.1 = (f32[2,2,2,16,128]{4,3,2,0,1:T(8,128)S(1)}, f32[2,2,2,16,128]{4,3,2,0,1:T(8,128)S(1)}, u32[]{:S(2)}, u32[]{:S(2)}) collective-permute-start(f32[2,2,2,16,128]{4,3,2,0,1:T(8,128)S(1)} %bitcast.45), channel_id=1, source_target_pairs={{0,1},{1,0},{2,3},{3,2},{4,5},{5,4},{6,7},{7,6},{8,9},{9,8},{10,11... | collective-permute-start | bytes 196616 | tf_op jit(solution)/shard_map/ppermute | solution.py:501
  84.9 7.1 %collective-permute-start.4 = (f32[21,16,128]{2,1,0:T(8,128)S(1)}, f32[21,16,128]{2,1,0:T(8,128)S(1)}, u32[]{:S(2)}, u32[]{:S(2)}) collective-permute-start(f32[21,16,128]{2,1,0:T(8,128)S(1)} %get-tuple-element.28), channel_id=1, source_target_pairs={{0,8},{8,0},{16,24},{24,16},{32,40},{40,32},{48,56},{56,48},{64,72... | collective-permute-start | bytes 516104 | tf_op jit(solution)/shard_map/ppermute | solution.py:483
  85.0 7.1 %collective-permute-start.5 = (f32[21,16,128]{2,1,0:T(8,128)S(1)}, f32[21,16,128]{2,1,0:T(8,128)S(1)}, u32[]{:S(2)}, u32[]{:S(2)}) collective-permute-start(f32[21,16,128]{2,1,0:T(8,128)S(1)} %get-tuple-element.29), channel_id=1, source_target_pairs={{0,120},{8,16},{16,8},{24,32},{32,24},{40,48},{48,40},{56,64},{64,... | collective-permute-start | bytes 516104 | tf_op jit(solution)/shard_map/ppermute | solution.py:483
  92.1 7.6 %collective-permute-start.6 = (f32[384,128]{1,0:T(8,128)S(1)}, f32[384,128]{1,0:T(8,128)S(1)}, u32[]{:S(2)}, u32[]{:S(2)}) collective-permute-start(f32[384,128]{1,0:T(8,128)S(1)} %get-tuple-element.32.ye), channel_id=1, source_target_pairs={{0,1},{1,0},{2,3},{3,2},{4,5},{5,4},{6,7},{7,6},{8,9},{9,8},{10,11... | collective-permute-start | bytes 589832 | tf_op jit(solution)/shard_map/ppermute | solution.py:483
  92.9 9.3 %collective-permute-start.7 = (f32[384,128]{1,0:T(8,128)S(1)}, f32[384,128]{1,0:T(8,128)S(1)}, u32[]{:S(2)}, u32[]{:S(2)}) collective-permute-start(f32[384,128]{1,0:T(8,128)S(1)} %get-tuple-element.33.yo), channel_id=1, source_target_pairs={{0,7},{1,2},{2,1},{3,4},{4,3},{5,6},{6,5},{7,0},{8,15},{9,10},{10,... | collective-permute-start | bytes 589832 | tf_op jit(solution)/shard_map/ppermute | solution.py:483

commit v12 on v11

--- a/solution.py
+++ b/solution.py
@@ -205,8 +205,7 @@
             post[q, at, pl.ds(r, 8, stride=2), :] = shift_z(after[q], q)
 
 
-def fetch(source, arrived, tiles, sem, slot, at):
-    p = source[0, slot]
+def fetch(p, arrived, tiles, sem, at):
     pltpu.make_async_copy(
         arrived.at[lax.shift_right_logical(p, 1), pl.ds((p & 1) * TILE, TILE), 0, :],
         tiles.at[pl.ds(at * ROWS, TILE), :],
@@ -220,9 +219,9 @@
 
 
 def edge_kernel(
-    force, arrived, coef, found, edge, xe, xo, tiles, labels, source, sems, small
+    force, arrived, coef, found, edge, xe, xo, tiles, labels, sems, small
 ):
-    pull = pltpu.make_async_copy(arrived.at[:, 2 * TILE, 0, :], labels, small.at[0])
+    pull = pltpu.make_async_copy(arrived.at[:, 2 * TILE, 0, :], labels, small)
     pull.start()
     f = [force[axis : axis + 1, :] for axis in range(3)]
     lane = lax.broadcasted_iota(jnp.int32, (8, 128), 1)
@@ -237,13 +236,11 @@
         number = (sub + 8 * group) * 2
         total = total + jnp.where(jnp.where(low, line, other) == lane_f, number, 0)
         total = total + jnp.where(jnp.where(low, other, line) == lane_f, number + 1, 0)
-    found[...] = jnp.broadcast_to(jnp.sum(total, axis=0, keepdims=True), (8, 128))
-    hand = pltpu.make_async_copy(found, source, small.at[1])
-    hand.start()
-    hand.wait()
+    numbers = jnp.sum(total, axis=0, keepdims=True)
+    found[...] = jnp.broadcast_to(numbers, (8, 128))
     for j, x in enumerate((0, 1, 14, 15)):
         for i in range(8):
-            fetch(source, arrived, tiles, sems.at[j], 8 * x + i, 8 * j + i)
+            fetch(numbers[0, 8 * x + i], arrived, tiles, sems.at[j], 8 * j + i)
 
     def plane(j, _):
         arrive(tiles, sems.at[j])
@@ -270,7 +267,7 @@
 
     for j in range(12):
         for i in range(8):
-            fetch(source, arrived, tiles, sems.at[j], 16 + 8 * j + i, 8 * j + i)
+            fetch(source[0, 16 + 8 * j + i], arrived, tiles, sems.at[j], 8 * j + i)
 
     def plane(j, _):
         arrive(tiles, sems.at[j])
@@ -535,9 +532,8 @@
         scratch_shapes=[
             pltpu.VMEM((32 * ROWS, 128), F32),
             pltpu.VMEM((DEVICES, 128), F32),
-            pltpu.SMEM((8, 128), jnp.int32),
             pltpu.SemaphoreType.DMA((4,)),
-            pltpu.SemaphoreType.DMA((2,)),
+            pltpu.SemaphoreType.DMA,
         ],
         compiler_params=pltpu.CompilerParams(vmem_limit_bytes=VMEM_LIMIT),
         cost_estimate=pl.CostEstimate(flops=2_000_000, bytes_accessed=8_000_000, transcendentals=0),

time: 104 us -> 103 us (level)
  no operation moved by 1% of the time
where the time goes in v12:
time: 103 us
  waiting for transfers between devices  61.1 us (59%)
  starting transfers between devices  26.4 us (26%)
  Pallas kernels  13.8 us (13%)
    ppermute x3, waiting for transfers between devices, pieces_of(): parts.append(lax.ppermute(message, 'gy', [(i, i ^ k) for i in range(8)]))  57.8 us
    all_to_all x1, starting transfers between devices, local(): lax.all_to_all(packed, ('gx', 'gy'), split_axis=0, concat_axis=0, tiled=T...  11.7 us
    ppermute x4, starting transfers between devices, swap(): return lax.ppermute(value, axis, pairs)  7.3 us
    ppermute x3, starting transfers between devices, pieces_of(): parts.append(lax.ppermute(message, 'gy', [(i, i ^ k) for i in range(8)]))  4.17 us
    pallas_call x2, Pallas kernels, call(): pl.pallas_call(kernel, out_shape=out_shape, in_specs=[VMEM_SPEC] * len(op...  4.06 us
    pallas_call x1, Pallas kernels, local(): pl.pallas_call(inner_kernel, out_shape=[posts[1], SENT, SENT], in_specs=[...  3.43 us
    ppermute x1, starting transfers between devices, halves_of(): return (mine, lax.ppermute(other, 'gy', [(i, i ^ 4) for i in range(8)]))  3.19 us
    pallas_call x1, Pallas kernels, pack(): pl.pallas_call(pack_kernel, out_shape=jax.ShapeDtypeStruct((DEVICES, PAIR...  2.76 us
  transfers between devices with their start and end apart: 9, of which 6 were waited for; matrix products, arithmetic and copies ran while one was open for 0% of the time, Pallas kernels for 10%

profile of v12, /device:TPU:0, one launch (start us, length us, event | category | flops | bytes accessed | tf_op | source)
XLA Modules:
  0.0 102.7 jit_solution(9920250566520122239)
XLA Ops:
  0.0 0.9 fusion
  0.9 3.2 %collective-permute-start = (f32[2,2,4,16,128]{4,3,2,1,0:T(8,128)S(1)}, f32[2,2,4,16,128]{4,3,2,1,0:T(8,128)S(1)}, u32[]{:S(2)}, u32[]{:S(2)}) collective-permute-start(f32[2,2,4,16,128]{4,3,2,1,0:T(8,128)S(1)} %fusion), channel_id=1, source_target_pairs={{0,4},{1,5},{2,6},{3,7},{4,0},{5,1},{6,2},{7,3},{8,12},{9,13},{10,... | collective-permute-start | bytes 393224 | tf_op jit(solution)/shard_map/ppermute | solution.py:488
  4.1 2.8 %shard_map.64 = f32[128,77,1,128]{3,2,1,0:T(1,128)} custom-call(s32[128]{0:T(128)} %target_hbm.1, f32[19,256,128]{2,1,0:T(8,128)} %bitcast.37), custom_call_target="tpu_custom_call" | custom-call | bytes 8000000 | tf_op jit(solution)/shard_map/pallas_call | solution.py:171
  6.8 0.0 copy-start
  6.9 0.7 collective-permute-done
  7.6 11.7 %all-to-all-start = ((f32[128,77,1,128]{3,2,1,0:T(1,128)}), f32[128,77,1,128]{3,2,1,0:T(1,128)}, u32[]{:S(2)}, u32[]{:S(2)}) async-start(f32[128,77,1,128]{3,2,1,0:T(1,128)} %shard_map.64), calls=%async_computation | async-start | bytes 10092544 | tf_op jit(solution)/shard_map/all_to_all | solution.py:517
  19.5 2.2 %collective-permute-start.3 = (f32[2,2,2,16,128]{4,3,2,0,1:T(8,128)S(1)}, f32[2,2,2,16,128]{4,3,2,0,1:T(8,128)S(1)}, u32[]{:S(2)}, u32[]{:S(2)}) collective-permute-start(f32[2,2,2,16,128]{4,3,2,0,1:T(8,128)S(1)} %bitcast.47), channel_id=1, source_target_pairs={{0,3},{1,2},{2,1},{3,0},{4,7},{5,6},{6,5},{7,4},{8,11},{9,10},{10,... | collective-permute-start | bytes 196616 | tf_op jit(solution)/shard_map/ppermute | solution.py:498
  21.7 0.8 collective-permute-start.2
  22.6 1.1 %collective-permute-start.1 = (f32[2,2,2,16,128]{4,3,2,0,1:T(8,128)S(1)}, f32[2,2,2,16,128]{4,3,2,0,1:T(8,128)S(1)}, u32[]{:S(2)}, u32[]{:S(2)}) collective-permute-start(f32[2,2,2,16,128]{4,3,2,0,1:T(8,128)S(1)} %bitcast.45), channel_id=1, source_target_pairs={{0,1},{1,0},{2,3},{3,2},{4,5},{5,4},{6,7},{7,6},{8,9},{9,8},{10,11... | collective-permute-start | bytes 196616 | tf_op jit(solution)/shard_map/ppermute | solution.py:498
  23.7 51.4 %collective-permute-done.3 = f32[2,2,2,16,128]{4,3,2,0,1:T(8,128)S(1)} collective-permute-done((f32[2,2,2,16,128]{4,3,2,0,1:T(8,128)S(1)}, f32[2,2,2,16,128]{4,3,2,0,1:T(8,128)S(1)}, u32[]{:S(2)}, u32[]{:S(2)}) %collective-permute-start.3) | collective-permute-done | bytes 65568 | tf_op jit(solution)/shard_map/ppermute | solution.py:498
  75.1 4.0 %collective-permute-done.2 = f32[2,2,2,16,128]{4,3,2,0,1:T(8,128)S(1)} collective-permute-done((f32[2,2,2,16,128]{4,3,2,0,1:T(8,128)S(1)}, f32[2,2,2,16,128]{4,3,2,0,1:T(8,128)S(1)}, u32[]{:S(2)}, u32[]{:S(2)}) %collective-permute-start.2) | collective-permute-done | bytes 65568 | tf_op jit(solution)/shard_map/ppermute | solution.py:498
  79.1 2.4 %collective-permute-done.1 = f32[2,2,2,16,128]{4,3,2,0,1:T(8,128)S(1)} collective-permute-done((f32[2,2,2,16,128]{4,3,2,0,1:T(8,128)S(1)}, f32[2,2,2,16,128]{4,3,2,0,1:T(8,128)S(1)}, u32[]{:S(2)}, u32[]{:S(2)}) %collective-permute-start.1) | collective-permute-done | bytes 65568 | tf_op jit(solution)/shard_map/ppermute | solution.py:498
  81.7 0.1 broadcast_in_dim.2.force
  81.7 0.1 all-to-all-done.arrived
  81.8 2.5 %shard_map.65 = (s32[8,128]{1,0:T(8,128)S(1)}, f32[19,4,16,128]{3,2,1,0:T(8,128)S(1)}, f32[21,16,128]{2,1,0:T(8,128)S(1)}, f32[21,16,128]{2,1,0:T(8,128)S(1)}) custom-call(f32[8,128]{1,0:T(8,128)S(1)} %broadcast_in_dim.2.force, f32[128,77,1,128]{3,2,1,0:T(1,128)} %all-to-all-done.arrived, f32[2,16,16,128]{3,2,1,0:T(8,128)S(1)} %pad_maximum_fusion.1.coef), custom_call_target="tpu_custom_call" | custom-call | flops 2000000 | bytes 8000000 | tf_op jit(solution)/shard_map/pallas_call | solution.py:527
  84.3 0.1 collective-permute-start.4
  84.4 3.6 %collective-permute-start.5 = (f32[21,16,128]{2,1,0:T(8,128)S(1)}, f32[21,16,128]{2,1,0:T(8,128)S(1)}, u32[]{:S(2)}, u32[]{:S(2)}) collective-permute-start(f32[21,16,128]{2,1,0:T(8,128)S(1)} %get-tuple-element.29), channel_id=1, source_target_pairs={{0,120},{8,16},{16,8},{24,32},{32,24},{40,48},{48,40},{56,64},{64,... | collective-permute-start | bytes 516104 | tf_op jit(solution)/shard_map/ppermute | solution.py:480
  88.0 3.4 %shard_map.66 = (f32[19,12,16,128]{3,2,1,0:T(8,128)S(1)}, f32[384,128]{1,0:T(8,128)S(1)}, f32[384,128]{1,0:T(8,128)S(1)}) custom-call(f32[8,128]{1,0:T(8,128)S(1)} %broadcast_in_dim.2.force, s32[8,128]{1,0:T(8,128)S(1)} %get-tuple-element.26.found, f32[128,77,1,128]{3,2,1,0:T(1,128)} %all-to-all-done.arrived, f32[2,16,16,128]{3,2,1,0:T(8,128)S(1)} %pad_maximum_fusion.1.coef, ...), custom_call_target="tpu_custom_call" | custom-call | flops 6000000 | bytes 8000000 | tf_op jit(solution)/shard_map/pallas_call | solution.py:543
  91.5 0.1 shard_map.67
  91.6 0.8 collective-permute-start.6
  92.4 2.8 %collective-permute-start.7 = (f32[384,128]{1,0:T(8,128)S(1)}, f32[384,128]{1,0:T(8,128)S(1)}, u32[]{:S(2)}, u32[]{:S(2)}) collective-permute-start(f32[384,128]{1,0:T(8,128)S(1)} %get-tuple-element.33.yo), channel_id=1, source_target_pairs={{0,7},{1,2},{2,1},{3,4},{4,3},{5,6},{6,5},{7,0},{8,15},{9,10},{10,... | collective-permute-start | bytes 589832 | tf_op jit(solution)/shard_map/ppermute | solution.py:480
  95.2 4.0 %shard_map.68 = (f32[19,16,16,128]{3,2,1,0:T(8,128)}, f32[432,128]{1,0:T(8,128)S(1)}, f32[432,128]{1,0:T(8,128)S(1)}) custom-call(f32[8,128]{1,0:T(8,128)S(1)} %broadcast_in_dim.2.force, f32[19,4,16,128]{3,2,1,0:T(8,128)S(1)} %get-tuple-element.25.edge, f32[19,12,16,128]{3,2,1,0:T(8,128)S(1)} %get-tuple-element.27.inner, ...), custom_call_target="tpu_custom_call" | custom-call | flops 12000000 | bytes 12000000 | tf_op jit(solution)/shard_map/pallas_call | solution.py:305
  99.2 2.5 %collective-permute-done.7.came_o = f32[384,128]{1,0:T(8,128)S(1)} collective-permute-done((f32[384,128]{1,0:T(8,128)S(1)}, f32[384,128]{1,0:T(8,128)S(1)}, u32[]{:S(2)}, u32[]{:S(2)}) %collective-permute-start.7) | collective-permute-done | bytes 196640 | tf_op jit(solution)/shard_map/ppermute | solution.py:480
  101.7 1.0 shard_map.69
  (23 shorter events, 0.2 us)
Async XLA Ops:
  0.9 6.7 %collective-permute-start = (f32[2,2,4,16,128]{4,3,2,1,0:T(8,128)S(1)}, f32[2,2,4,16,128]{4,3,2,1,0:T(8,128)S(1)}, u32[]{:S(2)}, u32[]{:S(2)}) collective-permute-start(f32[2,2,4,16,128]{4,3,2,1,0:T(8,128)S(1)} %fusion), channel_id=1, source_target_pairs={{0,4},{1,5},{2,6},{3,7},{4,0},{5,1},{6,2},{7,3},{8,12},{9,13},{10,... | collective-permute-start | bytes 393224 | tf_op jit(solution)/shard_map/ppermute | solution.py:488
  6.8 12.5 %copy-start = (f32[2,128,128]{2,1,0:T(8,128)S(1)}, f32[2,128,128]{2,1,0:T(8,128)}, u32[]{:S(2)}) copy-start(f32[2,128,128]{2,1,0:T(8,128)} %param.8) | copy-start | bytes 393220
  6.9 12.5 %copy-start.1 = (f32[2,128,128]{2,1,0:T(8,128)S(1)}, f32[2,128,128]{2,1,0:T(8,128)}, u32[]{:S(2)}) copy-start(f32[2,128,128]{2,1,0:T(8,128)} %param.9) | copy-start | bytes 393220
  6.9 16.8 %copy-start.3 = (f32[3]{0:T(128)S(1)}, f32[3]{0:T(128)}, u32[]{:S(2)}) copy-start(f32[3]{0:T(128)} %param.11) | copy-start | bytes 40
  7.6 74.3 %all-to-all-start = ((f32[128,77,1,128]{3,2,1,0:T(1,128)}), f32[128,77,1,128]{3,2,1,0:T(1,128)}, u32[]{:S(2)}, u32[]{:S(2)}) async-start(f32[128,77,1,128]{3,2,1,0:T(1,128)} %shard_map.64), calls=%async_computation | async-start | bytes 10092544 | tf_op jit(solution)/shard_map/all_to_all | solution.py:517
  19.3 62.3 %copy-start.2 = (s32[16,16,128]{2,1,0:T(8,128)S(1)}, s32[16,16,128]{2,1,0:T(8,128)}, u32[]{:S(2)}) copy-start(s32[16,16,128]{2,1,0:T(8,128)} %param.10) | copy-start | bytes 393220
  19.5 55.5 %collective-permute-start.3 = (f32[2,2,2,16,128]{4,3,2,0,1:T(8,128)S(1)}, f32[2,2,2,16,128]{4,3,2,0,1:T(8,128)S(1)}, u32[]{:S(2)}, u32[]{:S(2)}) collective-permute-start(f32[2,2,2,16,128]{4,3,2,0,1:T(8,128)S(1)} %bitcast.47), channel_id=1, source_target_pairs={{0,3},{1,2},{2,1},{3,0},{4,7},{5,6},{6,5},{7,4},{8,11},{9,10},{10,... | collective-permute-start | bytes 196616 | tf_op jit(solution)/shard_map/ppermute | solution.py:498
  21.7 57.3 %collective-permute-start.2 = (f32[2,2,2,16,128]{4,3,2,0,1:T(8,128)S(1)}, f32[2,2,2,16,128]{4,3,2,0,1:T(8,128)S(1)}, u32[]{:S(2)}, u32[]{:S(2)}) collective-permute-start(f32[2,2,2,16,128]{4,3,2,0,1:T(8,128)S(1)} %bitcast.46), channel_id=1, source_target_pairs={{0,2},{1,3},{2,0},{3,1},{4,6},{5,7},{6,4},{7,5},{8,10},{9,11},{10,... | collective-permute-start | bytes 196616 | tf_op jit(solution)/shard_map/ppermute | solution.py:498
  22.6 58.9 %collective-permute-start.1 = (f32[2,2,2,16,128]{4,3,2,0,1:T(8,128)S(1)}, f32[2,2,2,16,128]{4,3,2,0,1:T(8,128)S(1)}, u32[]{:S(2)}, u32[]{:S(2)}) collective-permute-start(f32[2,2,2,16,128]{4,3,2,0,1:T(8,128)S(1)} %bitcast.45), channel_id=1, source_target_pairs={{0,1},{1,0},{2,3},{3,2},{4,5},{5,4},{6,7},{7,6},{8,9},{9,8},{10,11... | collective-permute-start | bytes 196616 | tf_op jit(solution)/shard_map/ppermute | solution.py:498
  84.3 7.1 %collective-permute-start.4 = (f32[21,16,128]{2,1,0:T(8,128)S(1)}, f32[21,16,128]{2,1,0:T(8,128)S(1)}, u32[]{:S(2)}, u32[]{:S(2)}) collective-permute-start(f32[21,16,128]{2,1,0:T(8,128)S(1)} %get-tuple-element.28), channel_id=1, source_target_pairs={{0,8},{8,0},{16,24},{24,16},{32,40},{40,32},{48,56},{56,48},{64,72... | collective-permute-start | bytes 516104 | tf_op jit(solution)/shard_map/ppermute | solution.py:480
  84.4 7.1 %collective-permute-start.5 = (f32[21,16,128]{2,1,0:T(8,128)S(1)}, f32[21,16,128]{2,1,0:T(8,128)S(1)}, u32[]{:S(2)}, u32[]{:S(2)}) collective-permute-start(f32[21,16,128]{2,1,0:T(8,128)S(1)} %get-tuple-element.29), channel_id=1, source_target_pairs={{0,120},{8,16},{16,8},{24,32},{32,24},{40,48},{48,40},{56,64},{64,... | collective-permute-start | bytes 516104 | tf_op jit(solution)/shard_map/ppermute | solution.py:480
  91.6 7.6 %collective-permute-start.6 = (f32[384,128]{1,0:T(8,128)S(1)}, f32[384,128]{1,0:T(8,128)S(1)}, u32[]{:S(2)}, u32[]{:S(2)}) collective-permute-start(f32[384,128]{1,0:T(8,128)S(1)} %get-tuple-element.32.ye), channel_id=1, source_target_pairs={{0,1},{1,0},{2,3},{3,2},{4,5},{5,4},{6,7},{7,6},{8,9},{9,8},{10,11... | collective-permute-start | bytes 589832 | tf_op jit(solution)/shard_map/ppermute | solution.py:480
  92.4 9.3 %collective-permute-start.7 = (f32[384,128]{1,0:T(8,128)S(1)}, f32[384,128]{1,0:T(8,128)S(1)}, u32[]{:S(2)}, u32[]{:S(2)}) collective-permute-start(f32[384,128]{1,0:T(8,128)S(1)} %get-tuple-element.33.yo), channel_id=1, source_target_pairs={{0,7},{1,2},{2,1},{3,4},{4,3},{5,6},{6,5},{7,0},{8,15},{9,10},{10,... | collective-permute-start | bytes 589832 | tf_op jit(solution)/shard_map/ppermute | solution.py:480

commit v13 on v12

--- a/solution.py
+++ b/solution.py
@@ -481,32 +481,32 @@
 
 
 def halves_of(porosity, relaxation):
-    hi = lax.axis_index("gy") // 4
-    slab = jnp.stack([porosity, relaxation]).reshape(2, 2, 8, 16, 128)
-    other = lax.dynamic_slice_in_dim(slab, (1 - hi) * 4, 4, axis=2)
-    mine = lax.dynamic_slice_in_dim(slab, hi * 4, 4, axis=2)
-    return mine, lax.ppermute(other, "gy", [(i, i ^ 4) for i in range(8)])
+    lo = lax.axis_index("gy") % 2
+    slab = jnp.stack([porosity, relaxation]).reshape(2, 2, 4, 2, 16, 128)
+    other = lax.dynamic_index_in_dim(slab, 1 - lo, axis=3, keepdims=False)
+    mine = lax.dynamic_index_in_dim(slab, lo, axis=3, keepdims=False)
+    return mine, lax.ppermute(other, "gy", [(i, i ^ 1) for i in range(8)])
 
 
 def pieces_of(mine, came):
     b = lax.axis_index("gy")
-    hi, lo = b // 4, b % 4
-    both = jnp.stack([jnp.where(hi == 0, mine, came), jnp.where(hi == 0, came, mine)])
-    parts = [lax.dynamic_index_in_dim(both, lo, axis=3, keepdims=False)]
+    hi, lo = b // 2, b % 2
+    both = jnp.stack([jnp.where(lo == 0, mine, came), jnp.where(lo == 0, came, mine)])
+    parts = [lax.dynamic_index_in_dim(both, hi, axis=3, keepdims=False)]
     for k in range(1, 4):
-        message = lax.dynamic_index_in_dim(both, lo ^ k, axis=3, keepdims=False)
-        parts.append(lax.ppermute(message, "gy", [(i, i ^ k) for i in range(8)]))
+        message = lax.dynamic_index_in_dim(both, hi ^ k, axis=3, keepdims=False)
+        parts.append(lax.ppermute(message, "gy", [(i, i ^ (2 * k)) for i in range(8)]))
     return parts
 
 
 def block_of(parts):
-    lo = lax.axis_index("gy") % 4
+    hi = lax.axis_index("gy") // 2
     stacked = jnp.stack(parts)
     ordered = [
-        lax.dynamic_index_in_dim(stacked, lo ^ y, axis=0, keepdims=False) for y in range(4)
+        lax.dynamic_index_in_dim(stacked, hi ^ y, axis=0, keepdims=False) for y in range(4)
     ]
     whole = jnp.stack(ordered)
-    return whole.transpose(2, 1, 0, 3, 4, 5).reshape(2, 16, 16, 128)
+    return whole.transpose(2, 0, 1, 3, 4, 5).reshape(2, 16, 16, 128)
 
 
 def local(pdf_old, tile_target, porosity, relaxation, solid_mask, force):

time: 103 us -> 102 us (level)
  waiting for transfers between devices: 61.1 us -> 58.6 us
  starting transfers between devices: 26.4 us -> 27.7 us
    ppermute x4, waiting for transfers between devices: 58.5 us -> 55.6 us  [the longest x3 54.9 us: pieces_of(): lax.ppermute(message, 'gy', [(i, i ^ 2 * k) for i in range(8)])]
  transfers between devices with their start and end apart: 9 -> 9, of which waited for: 6 -> 5; matrix products, arithmetic and copies ran while one was open for 0% -> 0% of each run, Pallas kernels for 10% -> 10%
where the time goes in v13:
time: 102 us
  waiting for transfers between devices  58.6 us (57%)
  starting transfers between devices  27.7 us (27%)
  Pallas kernels  13.8 us (14%)
  other arithmetic  1.02 us (1%)
    ppermute x3, waiting for transfers between devices, pieces_of(): lax.ppermute(message, 'gy', [(i, i ^ 2 * k) for i in range(8)])  54.9 us
    all_to_all x1, starting transfers between devices, local(): lax.all_to_all(packed, ('gx', 'gy'), split_axis=0, concat_axis=0, tiled=T...  11.7 us
    ppermute x4, starting transfers between devices, swap(): return lax.ppermute(value, axis, pairs)  7.72 us
    ppermute x3, starting transfers between devices, pieces_of(): lax.ppermute(message, 'gy', [(i, i ^ 2 * k) for i in range(8)])  6.58 us
    pallas_call x2, Pallas kernels, call(): pl.pallas_call(kernel, out_shape=out_shape, in_specs=[VMEM_SPEC] * len(op...  4.06 us
    pallas_call x1, Pallas kernels, local(): pl.pallas_call(inner_kernel, out_shape=[posts[1], SENT, SENT], in_specs=[...  3.43 us
    pallas_call x1, Pallas kernels, pack(): pl.pallas_call(pack_kernel, out_shape=jax.ShapeDtypeStruct((DEVICES, PAIR...  2.8 us
    pallas_call x1, Pallas kernels, local(): pl.pallas_call(edge_kernel, out_shape=[jax.ShapeDtypeStruct((8, 128), jnp...  2.49 us
  transfers between devices with their start and end apart: 9, of which 5 were waited for; matrix products, arithmetic and copies ran while one was open for 0% of the time, Pallas kernels for 10%

profile of v13, /device:TPU:0, one launch (start us, length us, event | category | flops | bytes accessed | tf_op | source)
XLA Modules:
  0.0 101.5 jit_solution(10481281414415588348)
XLA Ops:
  0.0 0.9 fusion.1
  0.9 1.7 %collective-permute-start = (f32[2,2,4,16,128]{4,3,2,1,0:T(8,128)S(1)}, f32[2,2,4,16,128]{4,3,2,1,0:T(8,128)S(1)}, u32[]{:S(2)}, u32[]{:S(2)}) collective-permute-start(f32[2,2,4,16,128]{4,3,2,1,0:T(8,128)S(1)} %fusion.1), channel_id=1, source_target_pairs={{0,1},{1,0},{2,3},{3,2},{4,5},{5,4},{6,7},{7,6},{8,9},{9,8},{10,11... | collective-permute-start | bytes 393224 | tf_op jit(solution)/shard_map/ppermute | solution.py:488
  2.6 2.8 %shard_map.64 = f32[128,77,1,128]{3,2,1,0:T(1,128)} custom-call(s32[128]{0:T(128)} %target_hbm.1, f32[19,256,128]{2,1,0:T(8,128)} %bitcast.41), custom_call_target="tpu_custom_call" | custom-call | bytes 8000000 | tf_op jit(solution)/shard_map/pallas_call | solution.py:171
  5.4 0.0 copy-start
  5.4 0.0 copy-start.1
  5.5 0.6 collective-permute-done
  6.1 11.7 %all-to-all-start = ((f32[128,77,1,128]{3,2,1,0:T(1,128)}), f32[128,77,1,128]{3,2,1,0:T(1,128)}, u32[]{:S(2)}, u32[]{:S(2)}) async-start(f32[128,77,1,128]{3,2,1,0:T(1,128)} %shard_map.64), calls=%async_computation | async-start | bytes 10092544 | tf_op jit(solution)/shard_map/all_to_all | solution.py:517
  18.0 2.5 %collective-permute-start.1 = (f32[2,2,2,16,128]{4,3,2,1,0:T(8,128)S(1)}, f32[2,2,2,16,128]{4,3,2,1,0:T(8,128)S(1)}, u32[]{:S(2)}, u32[]{:S(2)}) collective-permute-start(f32[2,2,2,16,128]{4,3,2,1,0:T(8,128)S(1)} %get-tuple-element.46), channel_id=1, source_target_pairs={{0,2},{1,3},{2,0},{3,1},{4,6},{5,7},{6,4},{7,5},{8,10},{9,11},{10,... | collective-permute-start | bytes 196616 | tf_op jit(solution)/shard_map/ppermute | solution.py:498
  20.5 3.0 %collective-permute-start.2 = (f32[2,2,2,16,128]{4,3,2,1,0:T(8,128)S(1)}, f32[2,2,2,16,128]{4,3,2,1,0:T(8,128)S(1)}, u32[]{:S(2)}, u32[]{:S(2)}) collective-permute-start(f32[2,2,2,16,128]{4,3,2,1,0:T(8,128)S(1)} %get-tuple-element.47), channel_id=1, source_target_pairs={{0,4},{1,5},{2,6},{3,7},{4,0},{5,1},{6,2},{7,3},{8,12},{9,13},{10,... | collective-permute-start | bytes 196616 | tf_op jit(solution)/shard_map/ppermute | solution.py:498
  23.4 1.1 %collective-permute-start.3 = (f32[2,2,2,16,128]{4,3,2,1,0:T(8,128)S(1)}, f32[2,2,2,16,128]{4,3,2,1,0:T(8,128)S(1)}, u32[]{:S(2)}, u32[]{:S(2)}) collective-permute-start(f32[2,2,2,16,128]{4,3,2,1,0:T(8,128)S(1)} %get-tuple-element.48), channel_id=1, source_target_pairs={{0,6},{1,7},{2,4},{3,5},{4,2},{5,3},{6,0},{7,1},{8,14},{9,15},{10,... | collective-permute-start | bytes 196616 | tf_op jit(solution)/shard_map/ppermute | solution.py:498
  24.5 52.6 %collective-permute-done.1 = f32[2,2,2,16,128]{4,3,2,1,0:T(8,128)S(1)} collective-permute-done((f32[2,2,2,16,128]{4,3,2,1,0:T(8,128)S(1)}, f32[2,2,2,16,128]{4,3,2,1,0:T(8,128)S(1)}, u32[]{:S(2)}, u32[]{:S(2)}) %collective-permute-start.1) | collective-permute-done | bytes 65568 | tf_op jit(solution)/shard_map/ppermute | solution.py:498
  77.1 2.3 %collective-permute-done.3 = f32[2,2,2,16,128]{4,3,2,1,0:T(8,128)S(1)} collective-permute-done((f32[2,2,2,16,128]{4,3,2,1,0:T(8,128)S(1)}, f32[2,2,2,16,128]{4,3,2,1,0:T(8,128)S(1)}, u32[]{:S(2)}, u32[]{:S(2)}) %collective-permute-start.3) | collective-permute-done | bytes 65568 | tf_op jit(solution)/shard_map/ppermute | solution.py:498
  79.6 0.1 broadcast_in_dim.2.force
  79.7 0.6 all-to-all-done.arrived
  80.3 2.5 %shard_map.65 = (s32[8,128]{1,0:T(8,128)S(1)}, f32[19,4,16,128]{3,2,1,0:T(8,128)S(1)}, f32[21,16,128]{2,1,0:T(8,128)S(1)}, f32[21,16,128]{2,1,0:T(8,128)S(1)}) custom-call(f32[8,128]{1,0:T(8,128)S(1)} %broadcast_in_dim.2.force, f32[128,77,1,128]{3,2,1,0:T(1,128)} %all-to-all-done.arrived, f32[2,16,16,128]{3,2,1,0:T(8,128)S(1)} %pad_maximum_fusion.1.coef), custom_call_target="tpu_custom_call" | custom-call | flops 2000000 | bytes 8000000 | tf_op jit(solution)/shard_map/pallas_call | solution.py:527
  82.8 0.1 collective-permute-start.4
  82.9 4.5 %collective-permute-start.5 = (f32[21,16,128]{2,1,0:T(8,128)S(1)}, f32[21,16,128]{2,1,0:T(8,128)S(1)}, u32[]{:S(2)}, u32[]{:S(2)}) collective-permute-start(f32[21,16,128]{2,1,0:T(8,128)S(1)} %get-tuple-element.29), channel_id=1, source_target_pairs={{0,120},{8,16},{16,8},{24,32},{32,24},{40,48},{48,40},{56,64},{64,... | collective-permute-start | bytes 516104 | tf_op jit(solution)/shard_map/ppermute | solution.py:480
  87.5 3.4 %shard_map.66 = (f32[19,12,16,128]{3,2,1,0:T(8,128)S(1)}, f32[384,128]{1,0:T(8,128)S(1)}, f32[384,128]{1,0:T(8,128)S(1)}) custom-call(f32[8,128]{1,0:T(8,128)S(1)} %broadcast_in_dim.2.force, s32[8,128]{1,0:T(8,128)S(1)} %get-tuple-element.26.found, f32[128,77,1,128]{3,2,1,0:T(1,128)} %all-to-all-done.arrived, f32[2,16,16,128]{3,2,1,0:T(8,128)S(1)} %pad_maximum_fusion.1.coef, ...), custom_call_target="tpu_custom_call" | custom-call | flops 6000000 | bytes 8000000 | tf_op jit(solution)/shard_map/pallas_call | solution.py:543
  90.9 0.1 shard_map.67
  91.0 0.2 collective-permute-start.6
  91.2 2.9 %collective-permute-start.7 = (f32[384,128]{1,0:T(8,128)S(1)}, f32[384,128]{1,0:T(8,128)S(1)}, u32[]{:S(2)}, u32[]{:S(2)}) collective-permute-start(f32[384,128]{1,0:T(8,128)S(1)} %get-tuple-element.33.yo), channel_id=1, source_target_pairs={{0,7},{1,2},{2,1},{3,4},{4,3},{5,6},{6,5},{7,0},{8,15},{9,10},{10,... | collective-permute-start | bytes 589832 | tf_op jit(solution)/shard_map/ppermute | solution.py:480
  94.1 4.0 %shard_map.68 = (f32[19,16,16,128]{3,2,1,0:T(8,128)}, f32[432,128]{1,0:T(8,128)S(1)}, f32[432,128]{1,0:T(8,128)S(1)}) custom-call(f32[8,128]{1,0:T(8,128)S(1)} %broadcast_in_dim.2.force, f32[19,4,16,128]{3,2,1,0:T(8,128)S(1)} %get-tuple-element.25.edge, f32[19,12,16,128]{3,2,1,0:T(8,128)S(1)} %get-tuple-element.27.inner, ...), custom_call_target="tpu_custom_call" | custom-call | flops 12000000 | bytes 12000000 | tf_op jit(solution)/shard_map/pallas_call | solution.py:305
  98.1 2.4 %collective-permute-done.7.came_o = f32[384,128]{1,0:T(8,128)S(1)} collective-permute-done((f32[384,128]{1,0:T(8,128)S(1)}, f32[384,128]{1,0:T(8,128)S(1)}, u32[]{:S(2)}, u32[]{:S(2)}) %collective-permute-start.7) | collective-permute-done | bytes 196640 | tf_op jit(solution)/shard_map/ppermute | solution.py:480
  100.5 1.0 %shard_map.69 = f32[19,16,16,128]{3,2,1,0:T(8,128)} custom-call(f32[8,128]{1,0:T(8,128)S(1)} %broadcast_in_dim.2.force, f32[432,128]{1,0:T(8,128)S(1)} %get-tuple-element.34.went_dn, f32[432,128]{1,0:T(8,128)S(1)} %get-tuple-element.35.went_up, f32[384,128]{1,0:T(8,128)S(1)} %collective-permute-done.6.came_e, ...), custom_call_target="tpu_custom_call", output_to_operand_aliasing={{}: (5, {})} | custom-call | flops 2000000 | bytes 2000000 | tf_op jit(solution)/shard_map/pallas_call | solution.py:573
  (19 shorter events, 0.2 us)
Async XLA Ops:
  0.9 5.2 %collective-permute-start = (f32[2,2,4,16,128]{4,3,2,1,0:T(8,128)S(1)}, f32[2,2,4,16,128]{4,3,2,1,0:T(8,128)S(1)}, u32[]{:S(2)}, u32[]{:S(2)}) collective-permute-start(f32[2,2,4,16,128]{4,3,2,1,0:T(8,128)S(1)} %fusion.1), channel_id=1, source_target_pairs={{0,1},{1,0},{2,3},{3,2},{4,5},{5,4},{6,7},{7,6},{8,9},{9,8},{10,11... | collective-permute-start | bytes 393224 | tf_op jit(solution)/shard_map/ppermute | solution.py:488
  5.4 12.4 %copy-start = (f32[2,128,128]{2,1,0:T(8,128)S(1)}, f32[2,128,128]{2,1,0:T(8,128)}, u32[]{:S(2)}) copy-start(f32[2,128,128]{2,1,0:T(8,128)} %param.8) | copy-start | bytes 393220
  5.4 12.4 %copy-start.1 = (f32[2,128,128]{2,1,0:T(8,128)S(1)}, f32[2,128,128]{2,1,0:T(8,128)}, u32[]{:S(2)}) copy-start(f32[2,128,128]{2,1,0:T(8,128)} %param.9) | copy-start | bytes 393220
  5.5 19.1 %copy-start.3 = (f32[3]{0:T(128)S(1)}, f32[3]{0:T(128)}, u32[]{:S(2)}) copy-start(f32[3]{0:T(128)} %param.11) | copy-start | bytes 40
  6.1 74.2 %all-to-all-start = ((f32[128,77,1,128]{3,2,1,0:T(1,128)}), f32[128,77,1,128]{3,2,1,0:T(1,128)}, u32[]{:S(2)}, u32[]{:S(2)}) async-start(f32[128,77,1,128]{3,2,1,0:T(1,128)} %shard_map.64), calls=%async_computation | async-start | bytes 10092544 | tf_op jit(solution)/shard_map/all_to_all | solution.py:517
  17.8 61.8 %copy-start.2 = (s32[16,16,128]{2,1,0:T(8,128)S(1)}, s32[16,16,128]{2,1,0:T(8,128)}, u32[]{:S(2)}) copy-start(s32[16,16,128]{2,1,0:T(8,128)} %param.10) | copy-start | bytes 393220
  18.0 59.1 %collective-permute-start.1 = (f32[2,2,2,16,128]{4,3,2,1,0:T(8,128)S(1)}, f32[2,2,2,16,128]{4,3,2,1,0:T(8,128)S(1)}, u32[]{:S(2)}, u32[]{:S(2)}) collective-permute-start(f32[2,2,2,16,128]{4,3,2,1,0:T(8,128)S(1)} %get-tuple-element.46), channel_id=1, source_target_pairs={{0,2},{1,3},{2,0},{3,1},{4,6},{5,7},{6,4},{7,5},{8,10},{9,11},{10,... | collective-permute-start | bytes 196616 | tf_op jit(solution)/shard_map/ppermute | solution.py:498
  20.5 56.7 %collective-permute-start.2 = (f32[2,2,2,16,128]{4,3,2,1,0:T(8,128)S(1)}, f32[2,2,2,16,128]{4,3,2,1,0:T(8,128)S(1)}, u32[]{:S(2)}, u32[]{:S(2)}) collective-permute-start(f32[2,2,2,16,128]{4,3,2,1,0:T(8,128)S(1)} %get-tuple-element.47), channel_id=1, source_target_pairs={{0,4},{1,5},{2,6},{3,7},{4,0},{5,1},{6,2},{7,3},{8,12},{9,13},{10,... | collective-permute-start | bytes 196616 | tf_op jit(solution)/shard_map/ppermute | solution.py:498
  23.4 56.0 %collective-permute-start.3 = (f32[2,2,2,16,128]{4,3,2,1,0:T(8,128)S(1)}, f32[2,2,2,16,128]{4,3,2,1,0:T(8,128)S(1)}, u32[]{:S(2)}, u32[]{:S(2)}) collective-permute-start(f32[2,2,2,16,128]{4,3,2,1,0:T(8,128)S(1)} %get-tuple-element.48), channel_id=1, source_target_pairs={{0,6},{1,7},{2,4},{3,5},{4,2},{5,3},{6,0},{7,1},{8,14},{9,15},{10,... | collective-permute-start | bytes 196616 | tf_op jit(solution)/shard_map/ppermute | solution.py:498
  82.8 8.1 %collective-permute-start.4 = (f32[21,16,128]{2,1,0:T(8,128)S(1)}, f32[21,16,128]{2,1,0:T(8,128)S(1)}, u32[]{:S(2)}, u32[]{:S(2)}) collective-permute-start(f32[21,16,128]{2,1,0:T(8,128)S(1)} %get-tuple-element.28), channel_id=1, source_target_pairs={{0,8},{8,0},{16,24},{24,16},{32,40},{40,32},{48,56},{56,48},{64,72... | collective-permute-start | bytes 516104 | tf_op jit(solution)/shard_map/ppermute | solution.py:480
  82.9 8.0 %collective-permute-start.5 = (f32[21,16,128]{2,1,0:T(8,128)S(1)}, f32[21,16,128]{2,1,0:T(8,128)S(1)}, u32[]{:S(2)}, u32[]{:S(2)}) collective-permute-start(f32[21,16,128]{2,1,0:T(8,128)S(1)} %get-tuple-element.29), channel_id=1, source_target_pairs={{0,120},{8,16},{16,8},{24,32},{32,24},{40,48},{48,40},{56,64},{64,... | collective-permute-start | bytes 516104 | tf_op jit(solution)/shard_map/ppermute | solution.py:480
  91.0 7.1 %collective-permute-start.6 = (f32[384,128]{1,0:T(8,128)S(1)}, f32[384,128]{1,0:T(8,128)S(1)}, u32[]{:S(2)}, u32[]{:S(2)}) collective-permute-start(f32[384,128]{1,0:T(8,128)S(1)} %get-tuple-element.32.ye), channel_id=1, source_target_pairs={{0,1},{1,0},{2,3},{3,2},{4,5},{5,4},{6,7},{7,6},{8,9},{9,8},{10,11... | collective-permute-start | bytes 589832 | tf_op jit(solution)/shard_map/ppermute | solution.py:480
  91.2 9.3 %collective-permute-start.7 = (f32[384,128]{1,0:T(8,128)S(1)}, f32[384,128]{1,0:T(8,128)S(1)}, u32[]{:S(2)}, u32[]{:S(2)}) collective-permute-start(f32[384,128]{1,0:T(8,128)S(1)} %get-tuple-element.33.yo), channel_id=1, source_target_pairs={{0,7},{1,2},{2,1},{3,4},{4,3},{5,6},{6,5},{7,0},{8,15},{9,10},{10,... | collective-permute-start | bytes 589832 | tf_op jit(solution)/shard_map/ppermute | solution.py:480
